TPU v7x, 32 devices: a whole 2x2x4 slice. The times are simulated.
32 devices in a mesh: dp: 8 (over z, x), tensor: 4 (over y, core).
Axes of the slice: x: 2, y: 2, z: 4, core: 2. Of those that a mesh axis runs over, the one named last changes fastest.
Arguments:
- tokens: bfloat16 [16384, 512], P(('dp', 'tensor')), may hold values from -6 to 6
- routes: int32 [16384, 8], P('dp'), may hold values from 0 to 23, all different within a row; in each aligned block of 2048 rows (0 to 2047, 2048 to 4095, ...) at most 1024 rows name the same one
- cotangent: bfloat16 [16384, 512], P(('dp', 'tensor')), may hold values from -12 to 12
- ln1_gain: bfloat16 [512], P(('dp', 'tensor')), may hold values from 0.5 to 1.5
- ln1_bias: bfloat16 [512], P(('dp', 'tensor')), may hold values from -0.625 to 0.625
- w_key: bfloat16 [512, 64], P(('dp', 'tensor')), may hold values from -0.25 to 0.25
- w_value: bfloat16 [512, 64], P(('dp', 'tensor')), may hold values from -0.25 to 0.25
- w_router: bfloat16 [512, 24], P(('dp', 'tensor')), may hold values from -0.125 to 0.125
- w_query: bfloat16 [24, 512, 64], P('tensor', 'dp'), may hold values from -0.375 to 0.375
- w_out: bfloat16 [24, 64, 512], P('tensor', None, 'dp'), may hold values from -16 to 16
- ln2_gain: bfloat16 [512], P(('dp', 'tensor')), may hold values from 0.5 to 1.5
- ln2_bias: bfloat16 [512], P(('dp', 'tensor')), may hold values from -0.625 to 0.625
- w_up: bfloat16 [512, 2048], P('dp', 'tensor'), may hold values from -0.25 to 0.25
- b_up: bfloat16 [2048], P(('dp', 'tensor')), may hold values from -0.625 to 0.625
- w_down: bfloat16 [2048, 512], P('tensor', 'dp'), may hold values from -0.1875 to 0.1875
- b_down: bfloat16 [512], P(('dp', 'tensor')), may hold values from -0.625 to 0.625
Outputs:
- output: bfloat16 [16384, 512], P(('dp', 'tensor'))
- grad_tokens: float32 [16384, 512], P(('dp', 'tensor'))
- grad_ln1_gain: float32 [512], P(('dp', 'tensor'))
- grad_ln1_bias: float32 [512], P(('dp', 'tensor'))
- grad_w_key: float32 [512, 64], P(('dp', 'tensor'))
- grad_w_value: float32 [512, 64], P(('dp', 'tensor'))
- grad_w_router: float32 [512, 24], P(('dp', 'tensor'))
- grad_w_query: float32 [24, 512, 64], P('tensor', 'dp')
- grad_w_out: float32 [24, 64, 512], P('tensor', None, 'dp')
- grad_ln2_gain: float32 [512], P(('dp', 'tensor'))
- grad_ln2_bias: float32 [512], P(('dp', 'tensor'))
- grad_w_up: float32 [512, 2048], P('dp', 'tensor')
- grad_b_up: float32 [2048], P(('dp', 'tensor'))
- grad_w_down: float32 [2048, 512], P('tensor', 'dp')
- grad_b_down: float32 [512], P(('dp', 'tensor'))
Inputs may be any that keep to these rules, and one draw needn't show every extreme that they name: `routes`: each row names 8 different experts. Among the 2048 rows of one sequence no expert is named by more than 1024 rows, and in every draw some expert is named by exactly 1024 rows of some sequence.
All inputs are finite; a program needn't handle non-finite values.
Results may differ from a plain program's by a relative error of at most 0.019.
Values may be sent and summed in bfloat16 or wider, within the bound.
No kernel may reach another device: no remote copies, remote signals or barrier semaphores. Data moves between devices by JAX's collectives and lax.ppermute only.
A program may use at most 128 MiB of HBM per device.

v0:
```python
import jax
import jax.numpy as jnp
from jax import lax
from jax.sharding import PartitionSpec as P

ROWBLK = 512


def split_up(x, dim, length):
    shape = x.shape
    blocks = x.reshape(*shape[:dim], length, shape[dim] // length, *shape[dim + 1 :])
    return jnp.moveaxis(blocks, dim, 0)


def sum_at_owner(x, axis, dim):
    blocks = split_up(x, dim, lax.axis_size(axis))
    arrived = lax.all_to_all(blocks, axis, split_axis=0, concat_axis=0, tiled=True)
    return arrived.astype(jnp.float32).sum(axis=0)


def contract(left, right, left_dim, right_dim):
    return lax.dot_general(
        left, right, (((left_dim,), (right_dim,)), ((), ())), preferred_element_type=jnp.float32
    )


def contract_exact(left, right, left_dim, right_dim):
    return lax.dot_general(
        left,
        right,
        (((left_dim,), (right_dim,)), ((), ())),
        precision=lax.Precision.HIGHEST,
        preferred_element_type=jnp.float32,
    )


def smooth_gate(preact):
    sigmoid_part = jax.nn.sigmoid(preact)
    return (preact * sigmoid_part, sigmoid_part * (1.0 + preact * (1.0 - sigmoid_part)))


def norm_forward(operand, gain, offset):
    average = jnp.mean(operand, axis=-1, keepdims=True)
    centered = operand - average
    inverse = lax.rsqrt(jnp.mean(centered * centered, axis=-1, keepdims=True) + 1e-05)
    scaled = centered * inverse
    return (scaled * gain + offset, scaled, inverse)


def norm_backward(incoming, scaled, inverse, gain):
    weighted = incoming * gain
    back_rows = inverse * (
        weighted
        - jnp.mean(weighted, axis=-1, keepdims=True)
        - scaled * jnp.mean(weighted * scaled, axis=-1, keepdims=True)
    )
    return (back_rows, jnp.sum(incoming * scaled, axis=0), jnp.sum(incoming, axis=0))


def slot_onehot(running_col, member_col, capacity):
    slot_range = jnp.arange(capacity, dtype=jnp.int32)[:, None]
    return (running_col[None, :] == slot_range + 1) & (member_col[None, :] > 0)


def slot_position(running_col, capacity):
    slot_range = jnp.arange(capacity, dtype=jnp.int32)[:, None]
    counted = jnp.sum((running_col[None, :] <= slot_range).astype(jnp.int32), axis=1)
    return jnp.minimum(counted, running_col.shape[0] - 1)


def masked_scores(query_block, position_block, key_rows):
    key_positions = jnp.arange(key_rows.shape[0], dtype=jnp.int32)
    scores = contract(query_block, key_rows, 1, 1) * 0.125
    return jnp.where(key_positions[None, :] <= position_block[:, None], scores, -1e30)


def attend_forward(query_blocks, position_blocks, key_rows, value_rows):

    def attend(pieces):
        scores = masked_scores(pieces[0], pieces[1], key_rows)
        top_score = jnp.max(scores, axis=-1, keepdims=True)
        exponent = jnp.exp(scores - top_score)
        totals = jnp.sum(exponent, axis=-1, keepdims=True)
        prob_low = (exponent / totals).astype(jnp.bfloat16)
        return (
            jnp.dot(prob_low, value_rows, preferred_element_type=jnp.float32),
            (top_score + jnp.log(totals))[:, 0],
        )

    return lax.map(attend, (query_blocks, position_blocks))


def attend_backward(query_blocks, position_blocks, log_totals, grad_blocks, key_rows, value_rows):

    def step(carried, pieces):
        key_sum, value_sum = carried
        query_block, position_block, lse_block, grad_block = pieces
        scores = masked_scores(query_block, position_block, key_rows)
        prob_rows = jnp.exp(scores - lse_block[:, None])
        prob_low = prob_rows.astype(jnp.bfloat16)
        grad_prob = contract(grad_block, value_rows, 1, 1)
        inner_sum = jnp.sum(prob_rows * grad_prob, axis=-1, keepdims=True)
        grad_score = (prob_rows * (grad_prob - inner_sum)).astype(jnp.bfloat16)
        grad_query = jnp.dot(grad_score, key_rows, preferred_element_type=jnp.float32) * 0.125
        key_sum = key_sum + contract(grad_score, query_block, 0, 0) * 0.125
        value_sum = value_sum + contract(prob_low, grad_block, 0, 0)
        return ((key_sum, value_sum), grad_query)

    empty_rows = jnp.zeros(key_rows.shape, jnp.float32)
    return lax.scan(
        step, (empty_rows, empty_rows), (query_blocks, position_blocks, log_totals, grad_blocks)
    )


def per_device(
    tokens,
    routes,
    cotangent,
    ln1_gain,
    ln1_bias,
    w_key,
    w_value,
    w_router,
    w_query,
    w_out,
    ln2_gain,
    ln2_bias,
    w_up,
    b_up,
    w_down,
    b_down,
):
    (
        gain_one,
        bias_one,
        key_weight,
        value_weight,
        router_weight,
        gain_two,
        bias_two,
        up_bias,
        down_bias,
    ) = (
        lax.all_gather(ln1_gain, ("dp", "tensor"), axis=0, tiled=True),
        lax.all_gather(ln1_bias, ("dp", "tensor"), axis=0, tiled=True),
        lax.all_gather(w_key, ("dp", "tensor"), axis=0, tiled=True),
        lax.all_gather(w_value, ("dp", "tensor"), axis=0, tiled=True),
        lax.all_gather(w_router, ("dp", "tensor"), axis=0, tiled=True),
        lax.all_gather(ln2_gain, ("dp", "tensor"), axis=0, tiled=True),
        lax.all_gather(ln2_bias, ("dp", "tensor"), axis=0, tiled=True),
        lax.all_gather(b_up, ("dp", "tensor"), axis=0, tiled=True),
        lax.all_gather(b_down, ("dp", "tensor"), axis=0, tiled=True),
    )
    query_weight, out_weight, up_weight, down_weight = (
        lax.all_gather(w_query, "dp", axis=1, tiled=True),
        lax.all_gather(w_out, "dp", axis=2, tiled=True),
        lax.all_gather(w_up, "dp", axis=0, tiled=True),
        lax.all_gather(w_down, "dp", axis=1, tiled=True),
    )
    model_dim = tokens.shape[1]
    seq_len = routes.shape[0]
    capacity = seq_len // 2
    expert_local = query_weight.shape[0]
    head_dim = query_weight.shape[2]
    expert_total = router_weight.shape[1]
    ffn_local = up_weight.shape[1]
    tensor_rank = lax.axis_index("tensor")
    every_expert = jnp.arange(expert_total, dtype=jnp.int32)
    pair_weight = jnp.concatenate([key_weight, value_weight], axis=1)
    layer_input = tokens.astype(jnp.float32)
    grad_out = cotangent.astype(jnp.float32)
    normed_local_f, scaled_one, inverse_one = norm_forward(
        layer_input, gain_one.astype(jnp.float32), bias_one.astype(jnp.float32)
    )
    normed_local = normed_local_f.astype(jnp.bfloat16)
    normed, grad_rows = (
        lax.all_gather(normed_local, "tensor", axis=0, tiled=True),
        lax.all_gather(cotangent, "tensor", axis=0, tiled=True),
    )
    first_expert = tensor_rank * expert_local
    query_flat = query_weight.transpose(1, 0, 2).reshape(model_dim, expert_local * head_dim)
    out_flat = out_weight.reshape(expert_local * head_dim, model_dim)
    queries = jnp.dot(normed, query_flat, preferred_element_type=jnp.float32).astype(jnp.bfloat16)
    key_value = jnp.dot(normed, pair_weight, preferred_element_type=jnp.float32).astype(
        jnp.bfloat16
    )
    key_rows = key_value[:, :head_dim]
    value_rows = key_value[:, head_dim:]
    logits = jnp.dot(normed, router_weight, preferred_element_type=jnp.float32)
    picked_all = (routes[:, :, None] == every_expert[None, None, :]).astype(jnp.float32)
    own_ids = first_expert + jnp.arange(expert_local, dtype=jnp.int32)
    picked_own = (routes[:, :, None] == own_ids[None, None, :]).astype(jnp.float32)
    chosen = jnp.sum(picked_all * logits[:, None, :], axis=-1)
    gate_rows = jax.nn.softmax(chosen, axis=-1)
    token_gate = jnp.sum(gate_rows[:, :, None] * picked_own, axis=1)
    member = jnp.sum(picked_own, axis=1).astype(jnp.int32)
    running = jnp.cumsum(member, axis=0)
    running_cols = running.T
    member_cols = member.T
    queries_cols = queries.reshape(seq_len, expert_local, head_dim).transpose(1, 0, 2)

    def place(pieces):
        running_col, member_col, query_col, gate_col = pieces
        onehot = slot_onehot(running_col, member_col, capacity)
        slot_q = jnp.dot(
            onehot.astype(jnp.bfloat16), query_col, preferred_element_type=jnp.float32
        ).astype(jnp.bfloat16)
        slot_g = jnp.dot(onehot.astype(jnp.float32), gate_col, precision=lax.Precision.HIGHEST)
        return (slot_q, slot_g, slot_position(running_col, capacity))

    slot_query, slot_gate, token_of = lax.map(
        place, (running_cols, member_cols, queries_cols, token_gate.T)
    )
    block_count = expert_local * capacity // ROWBLK
    query_blocks = slot_query.reshape(block_count, ROWBLK, head_dim)
    position_blocks = token_of.reshape(block_count, ROWBLK)
    head_blocks, log_totals = attend_forward(query_blocks, position_blocks, key_rows, value_rows)
    head_out = head_blocks.reshape(expert_local, capacity, head_dim)
    weighted = (slot_gate[:, :, None] * head_out).astype(jnp.bfloat16)

    def unplace(pieces):
        running_col, member_col, slot_col = pieces
        onehot = slot_onehot(running_col, member_col, capacity)
        return contract(onehot.astype(jnp.bfloat16), slot_col, 0, 0)

    mixed_cols = lax.map(unplace, (running_cols, member_cols, weighted))
    mixed_flat = (
        mixed_cols.astype(jnp.bfloat16).transpose(1, 0, 2).reshape(seq_len, expert_local * head_dim)
    )
    attention = lax.psum_scatter(
        jnp.dot(mixed_flat, out_flat, preferred_element_type=jnp.float32).astype(jnp.bfloat16),
        "tensor",
        scatter_dimension=0,
        tiled=True,
    ).astype(jnp.float32)
    middle = layer_input + attention
    normed_two_f, scaled_two, inverse_two = norm_forward(
        middle, gain_two.astype(jnp.float32), bias_two.astype(jnp.float32)
    )
    normed_two = lax.all_gather(normed_two_f.astype(jnp.bfloat16), "tensor", axis=0, tiled=True)
    hidden_start = tensor_rank * ffn_local
    bias_piece = lax.dynamic_slice_in_dim(up_bias, hidden_start, ffn_local, 0).astype(jnp.float32)
    preact = jnp.dot(normed_two, up_weight, preferred_element_type=jnp.float32) + bias_piece
    active, slope = smooth_gate(preact)
    hidden = active.astype(jnp.bfloat16)
    ffn_out = lax.psum_scatter(
        jnp.dot(hidden, down_weight, preferred_element_type=jnp.float32).astype(jnp.bfloat16),
        "tensor",
        scatter_dimension=0,
        tiled=True,
    ).astype(jnp.float32)
    grad_hidden = contract(grad_rows, down_weight, 1, 1)
    grad_pre = (grad_hidden * slope).astype(jnp.bfloat16)
    up_grad = contract(normed_two, grad_pre, 0, 0)
    down_grad = contract(hidden, grad_rows, 0, 0)
    bias_grad_up = lax.dynamic_update_slice_in_dim(
        jnp.zeros(up_bias.shape, jnp.float32),
        jnp.sum(grad_pre.astype(jnp.float32), axis=0),
        hidden_start,
        0,
    )
    grad_normed_two = lax.psum_scatter(
        contract(grad_pre, up_weight, 1, 1).astype(jnp.bfloat16),
        "tensor",
        scatter_dimension=0,
        tiled=True,
    ).astype(jnp.float32)
    back_two, gain_grad_two, bias_grad_two = norm_backward(
        grad_normed_two, scaled_two, inverse_two, gain_two.astype(jnp.float32)
    )
    grad_middle = grad_out + back_two
    grad_attn = lax.all_gather(grad_middle.astype(jnp.bfloat16), "tensor", axis=0, tiled=True)
    out_grad = contract(mixed_flat, grad_attn, 0, 0).reshape(expert_local, head_dim, model_dim)
    grad_mixed = (
        contract(grad_attn, out_flat, 1, 1)
        .reshape(seq_len, expert_local, head_dim)
        .transpose(1, 0, 2)
    )

    def pick_grad(pieces):
        running_col, member_col, grad_col = pieces
        onehot = slot_onehot(running_col, member_col, capacity)
        return jnp.dot(onehot.astype(jnp.float32), grad_col, precision=lax.Precision.HIGHEST)

    grad_weighted = lax.map(pick_grad, (running_cols, member_cols, grad_mixed))
    grad_gate_slot = jnp.sum(grad_weighted * head_out, axis=-1)
    grad_heads = (slot_gate[:, :, None] * grad_weighted).astype(jnp.bfloat16)
    (key_grad_sum, value_grad_sum), grad_query_blocks = attend_backward(
        query_blocks,
        position_blocks,
        log_totals,
        grad_heads.reshape(block_count, ROWBLK, head_dim),
        key_rows,
        value_rows,
    )
    grad_slot_query = grad_query_blocks.reshape(expert_local, capacity, head_dim)

    def return_grad(pieces):
        running_col, member_col, query_col, gate_col = pieces
        onehot = slot_onehot(running_col, member_col, capacity).astype(jnp.float32)
        return (contract_exact(onehot, query_col, 0, 0), contract_exact(gate_col, onehot, 0, 0))

    grad_query_cols, grad_gate_cols = lax.map(
        return_grad, (running_cols, member_cols, grad_slot_query, grad_gate_slot)
    )
    grad_queries = (
        grad_query_cols.transpose(1, 0, 2)
        .astype(jnp.bfloat16)
        .reshape(seq_len, expert_local * head_dim)
    )
    grad_token_gate = grad_gate_cols.T
    grad_pair = jnp.concatenate(
        [key_grad_sum.astype(jnp.bfloat16), value_grad_sum.astype(jnp.bfloat16)], axis=1
    )
    query_grad = (
        contract(normed, grad_queries, 0, 0)
        .reshape(model_dim, expert_local, head_dim)
        .transpose(1, 0, 2)
    )
    pair_grad = contract(normed, grad_pair, 0, 0)
    grad_gates = jnp.sum(grad_token_gate[:, None, :] * picked_own, axis=-1)
    grad_chosen = gate_rows * (grad_gates - jnp.sum(gate_rows * grad_gates, axis=-1, keepdims=True))
    grad_logits = jnp.sum(grad_chosen[:, :, None] * picked_all, axis=1)
    router_grad = jnp.einsum(
        "tb,te->be",
        normed,
        grad_logits,
        precision=lax.Precision.HIGHEST,
        preferred_element_type=jnp.float32,
    )
    router_part = jnp.einsum(
        "te,be->tb",
        grad_logits,
        router_weight,
        precision=lax.Precision.HIGHEST,
        preferred_element_type=jnp.float32,
    )
    grad_normed = lax.psum_scatter(
        (
            contract(grad_queries, query_flat, 1, 1)
            + contract(grad_pair, pair_weight, 1, 1)
            + router_part
        ).astype(jnp.bfloat16),
        "tensor",
        scatter_dimension=0,
        tiled=True,
    ).astype(jnp.float32)
    key_grad = pair_grad[:, :head_dim]
    value_grad = pair_grad[:, head_dim:]
    final_rows = middle + ffn_out + down_bias.astype(jnp.float32)
    output = final_rows.astype(jnp.bfloat16)
    bias_grad_down = jnp.sum(grad_out, axis=0)
    back_one, gain_grad_one, bias_grad_one = norm_backward(
        grad_normed, scaled_one, inverse_one, gain_one.astype(jnp.float32)
    )
    grad_tokens = grad_middle + back_one
    query_grad, out_grad, up_grad, down_grad = (
        sum_at_owner(query_grad.astype(jnp.bfloat16), "dp", 1),
        sum_at_owner(out_grad.astype(jnp.bfloat16), "dp", 2),
        sum_at_owner(up_grad.astype(jnp.bfloat16), "dp", 0),
        sum_at_owner(down_grad.astype(jnp.bfloat16), "dp", 1),
    )
    shared = (
        lax.psum_scatter(gain_grad_one, ("dp", "tensor"), scatter_dimension=0, tiled=True),
        lax.psum_scatter(bias_grad_one, ("dp", "tensor"), scatter_dimension=0, tiled=True),
        lax.psum_scatter(key_grad, ("dp", "tensor"), scatter_dimension=0, tiled=True),
        lax.psum_scatter(value_grad, ("dp", "tensor"), scatter_dimension=0, tiled=True),
        lax.psum_scatter(router_grad, ("dp", "tensor"), scatter_dimension=0, tiled=True),
        lax.psum_scatter(gain_grad_two, ("dp", "tensor"), scatter_dimension=0, tiled=True),
        lax.psum_scatter(bias_grad_two, ("dp", "tensor"), scatter_dimension=0, tiled=True),
        lax.psum_scatter(bias_grad_up, ("dp", "tensor"), scatter_dimension=0, tiled=True),
        lax.psum_scatter(bias_grad_down, ("dp", "tensor"), scatter_dimension=0, tiled=True),
    )
    return (
        output,
        grad_tokens,
        shared[0],
        shared[1],
        shared[2],
        shared[3],
        shared[4],
        query_grad,
        out_grad,
        shared[5],
        shared[6],
        up_grad,
        shared[7],
        down_grad,
        shared[8],
    )


def solution(mesh):
    in_specs = (
        P(("dp", "tensor"), None),
        P("dp", None),
        P(("dp", "tensor"), None),
        P(("dp", "tensor")),
        P(("dp", "tensor")),
        P(("dp", "tensor"), None),
        P(("dp", "tensor"), None),
        P(("dp", "tensor"), None),
        P("tensor", "dp", None),
        P("tensor", None, "dp"),
        P(("dp", "tensor")),
        P(("dp", "tensor")),
        P("dp", "tensor"),
        P(("dp", "tensor")),
        P("tensor", "dp"),
        P(("dp", "tensor")),
    )
    out_specs = (
        P(("dp", "tensor"), None),
        P(("dp", "tensor"), None),
        P(("dp", "tensor")),
        P(("dp", "tensor")),
        P(("dp", "tensor"), None),
        P(("dp", "tensor"), None),
        P(("dp", "tensor"), None),
        P("tensor", "dp", None),
        P("tensor", None, "dp"),
        P(("dp", "tensor")),
        P(("dp", "tensor")),
        P("dp", "tensor"),
        P(("dp", "tensor")),
        P("tensor", "dp"),
        P(("dp", "tensor")),
    )
    return jax.shard_map(
        per_device, mesh=mesh, in_specs=in_specs, out_specs=out_specs, check_vma=False
    )
```

profile of v0, /device:TPU:0, one launch (start us, length us, event | category | flops | bytes accessed | tf_op | source)
XLA Modules:
  0.0 1364.6 jit_solution(12581046125449714229)
XLA Ops:
  14.9 42.2 %all-reduce.13 = (bf16[512]{0:T(512)(128)(2,1)S(1)}, bf16[512]{0:T(512)(128)(2,1)S(1)}, bf16[512]{0:T(512)(128)(2,1)S(1)}, bf16[512]{0:T(512)(128)(2,1)S(1)}, bf...) all-reduce(bf16[512]{0:T(512)(128)(2,1)S(1)} %dynamic-update-slice., ...), channel_id=1, replica_groups=mesh['dp'=8,'tensor'=4] {'dp','tensor'}, use_global_device_ids=true, to_apply=%add.3 | all-reduce | flops 4608 | bytes 18432
  59.6 33.0 %all_gather.58 = bf16[6,64,512]{1,0,2:T(8,128)(2,1)S(1)} all-gather(bf16[6,64,64]{1,0,2:T(8,128)(2,1)S(1)} %copy.126), channel_id=1, replica_groups=mesh['dp'=8,'tensor'=4] {'dp'}, dimensions={2}, use_global_device_ids=true | all-gather | bytes 442368 | tf_op jit(solution)/shard_map/all_gather | solution.py:156
  94.0 32.1 %all_gather.54 = bf16[6,512,64]{2,0,1:T(8,128)(2,1)S(1)} all-gather(bf16[6,64,64]{2,0,1:T(8,128)(2,1)S(1)} %copy.118), channel_id=1, replica_groups=mesh['dp'=8,'tensor'=4] {'dp'}, dimensions={1}, use_global_device_ids=true | all-gather | bytes 442368 | tf_op jit(solution)/shard_map/all_gather | solution.py:155
  127.5 41.5 %all_gather.55 = bf16[512,24]{1,0:T(8,128)(2,1)S(1)} all-gather(bf16[16,24]{1,0:T(8,128)(2,1)S(1)} %copy-done.52), channel_id=1, replica_groups=mesh['dp'=8,'tensor'=4] {'dp','tensor'}, dimensions={0}, use_global_device_ids=true | all-gather | bytes 25344 | tf_op jit(solution)/shard_map/all_gather | solution.py:148
  169.0 37.0 %all_gather.56 = bf16[512,64]{1,0:T(8,128)(2,1)S(1)} all-gather(bf16[16,64]{1,0:T(8,128)(2,1)S(1)} %copy-done.53), channel_id=1, replica_groups=mesh['dp'=8,'tensor'=4] {'dp','tensor'}, dimensions={0}, use_global_device_ids=true | all-gather | bytes 67584 | tf_op jit(solution)/shard_map/all_gather | solution.py:146
  206.0 38.3 %all_gather.57 = bf16[512,64]{1,0:T(8,128)(2,1)S(1)} all-gather(bf16[16,64]{1,0:T(8,128)(2,1)S(1)} %copy-done.54), channel_id=1, replica_groups=mesh['dp'=8,'tensor'=4] {'dp','tensor'}, dimensions={0}, use_global_device_ids=true | all-gather | bytes 67584 | tf_op jit(solution)/shard_map/all_gather | solution.py:147
  256.4 4.1 copy.120
  260.5 56.3 %while.73 = (s32[]{:T(128)}, bf16[6,1024,64]{1,2,0:T(8,128)(2,1)}, f32[6,1024]{1,0:T(8,128)S(1)}, s32[6,1024]{1,0:T(8,128)S(1)}, s32[6,2048]{1,0:T(8,128)S(1)}, ...) while((s32[]{:T(128)}, bf16[6,1024,64]{1,2,0:T(8,128)(2,1)}, ...), condition=%wide.region_11.12_spmd, body=%wide.region_9.11_spmd.sunk | while | flops 308349952 | bytes 765057 | solution.py:211
  261.5 4.7 fusion.206
  270.9 4.7 fusion.206
  280.2 4.7 fusion.206
  289.6 4.7 fusion.206
  299.0 4.7 fusion.206
  308.4 4.7 fusion.206
  318.6 100.0 %while.74 = (s32[]{:T(128)}, f32[12,512,64]{1,0,2:T(8,128)}, f32[12,512]{1,0:T(8,128)}, s32[12,512]{1,0:T(8,128)S(1)}, bf16[12,512,64]{2,1,0:T(8,128)(2,1)S(1)},...) while((s32[]{:T(128)}, f32[12,512,64]{1,0,2:T(8,128)}, ...), condition=%wide.region_15.16_spmd, body=%wide.region_12.15_spmd.sunk | while | flops 277872128 | bytes 14182517 | solution.py:90
  389.8 3.8 dynamic_update_slice.60
  398.1 3.8 dynamic_update_slice.60
  406.5 3.8 dynamic_update_slice.60
  414.8 3.8 dynamic_update_slice.60
  424.7 26.6 %while.75 = (s32[]{:T(128)}, bf16[6,2048,64]{1,2,0:T(8,128)(2,1)}, s32[6,2048]{1,0:T(8,128)S(1)}, s32[6,2048]{1,0:T(8,128)S(1)}, bf16[6,1024,64]{1,0,2:T(8,128)(2,1)}, /*index=5*/s32[]{:T(128)}) while((s32[]{:T(128)}, bf16[6,2048,64]{1,2,0:T(8,128)(2,1)}, s32[6,2048]{1,0:T(8,128)S(1)}, s32[6,2048]{1,0:T(8,128)S(1)}, ...), condition=%wide.region_17.18_spmd, body=%wide.region_16.17_spmd.sunk | while | flops 272632832 | bytes 1224797 | solution.py:226
  451.3 4.1 bitcast_convert_fusion
  455.6 27.6 %reduce-scatter.12.cloned.1.call-done = bf16[512,512]{1,0:T(8,128)(2,1)} async-done(((bf16[2048,512]{1,0:T(8,128)(2,1)}), bf16[512,512]{1,0:T(8,128)(2,1)}) %reduce-scatter.12.cloned.1.call-update) | async-done | bytes 524304 | tf_op jit(solution)/shard_map/reduce_scatter | solution.py:230
  487.8 31.4 %all_gather.62 = bf16[512,512]{1,0:T(8,128)(2,1)S(1)} all-gather(bf16[64,512]{1,0:T(8,128)(2,1)S(1)} %copy-done.38), channel_id=1, replica_groups=mesh['dp'=8,'tensor'=4] {'dp'}, dimensions={0}, use_global_device_ids=true | all-gather | bytes 589824 | tf_op jit(solution)/shard_map/all_gather | solution.py:157
  519.2 31.2 %all_gather.64 = bf16[512,512]{0,1:T(8,128)(2,1)S(1)} all-gather(bf16[512,64]{0,1:T(8,128)(2,1)S(1)} %copy-done.39), channel_id=1, replica_groups=mesh['dp'=8,'tensor'=4] {'dp'}, dimensions={1}, use_global_device_ids=true | all-gather | bytes 589824 | tf_op jit(solution)/shard_map/all_gather | solution.py:158
  550.3 6.1 multiply_convert_fusion.2
  556.5 4.8 convert_reduce_fusion.1
  565.4 31.9 %reduce-scatter.16.cloned.1.call-done = bf16[512,512]{1,0:T(8,128)(2,1)} async-done(((bf16[2048,512]{1,0:T(8,128)(2,1)}), bf16[512,512]{1,0:T(8,128)(2,1)}) %reduce-scatter.16.cloned.1.call-update) | async-done | bytes 524304 | tf_op jit(solution)/shard_map/reduce_scatter | solution.py:262
  602.0 22.7 %all-gather.11.cloned.1.call-done = bf16[2048,512]{1,0:T(8,128)(2,1)} async-done(((bf16[512,512]{1,0:T(8,128)(2,1)}), bf16[2048,512]{1,0:T(8,128)(2,1)}) %all-gather.11.cloned.1.call-update) | async-done | bytes 2097168 | tf_op jit(solution)/shard_map/all_gather | solution.py:272
  624.6 4.3 convolution_bitcast_fusion
  628.9 71.5 %while.76 = (s32[]{:T(128)}, f32[6,1024,64]{1,0,2:T(8,128)}, s32[6,2048]{1,0:T(8,128)S(1)}, s32[6,2048]{1,0:T(8,128)S(1)}, f32[6,2048,64]{1,2,0:T(8,128)}, /*index=5*/s32[]{:T(128)}, s32[]{:T(128)}) while((s32[]{:T(128)}, f32[6,1024,64]{1,0,2:T(8,128)}, s32[6,2048]{1,0:T(8,128)S(1)}, s32[6,2048]{1,0:T(8,128)S(1)}, ...), condition=%wide.region_26.27_spmd, body=%wide.region_25.26_spmd.sunk | while | flops 1614810112 | bytes 1880165 | solution.py:285
  629.2 5.5 fusion.215
  634.9 6.1 dynamic_update_slice.63
  641.1 5.5 fusion.215
  646.8 6.1 dynamic_update_slice.63
  653.0 5.5 fusion.215
  658.7 6.1 dynamic_update_slice.63
  664.8 5.5 fusion.215
  670.6 6.1 dynamic_update_slice.63
  676.7 5.5 fusion.215
  682.5 6.1 dynamic_update_slice.63
  688.6 5.5 fusion.215
  694.4 6.1 dynamic_update_slice.63
  700.4 4.3 multiply_reduce_fusion.1
  707.7 116.3 %while.78 = (s32[]{:T(128)}, f32[2048,64]{0,1:T(8,128)S(1)}, f32[2048,64]{0,1:T(8,128)S(1)}, f32[12,512,64]{1,2,0:T(8,128)}, s32[12,512]{1,0:T(8,128)S(1)}, /*in...) while((s32[]{:T(128)}, f32[2048,64]{0,1:T(8,128)S(1)}, ...), condition=%wide.region_29.30_spmd.clone, body=%wide.region_27.29_spmd.clone.sunk | while | flops 682262016 | bytes 35012768 | solution.py:110
  827.7 54.3 %while.77 = (s32[]{:T(128)}, bf16[6,2048,64]{1,2,0:T(8,128)(2,1)S(1)}, f32[6,2048]{1,0:T(8,128)S(1)}, s32[6,2048]{1,0:T(8,128)}, s32[6,2048]{1,0:T(8,128)S(1)}, ...) while((s32[]{:T(128)}, bf16[6,2048,64]{1,2,0:T(8,128)(2,1)S(1)}, ...), condition=%wide.region_32.33_spmd, body=%wide.region_31.32_spmd.sunk | while | flops 1644170240 | bytes 1137781 | solution.py:303
  832.5 4.4 fusion.218
  841.5 4.4 fusion.218
  850.6 4.4 fusion.218
  859.6 4.4 fusion.218
  868.6 4.4 fusion.218
  877.6 4.4 fusion.218
  890.5 4.2 convolution_convert_fusion.1
  896.4 4.0 convolution_convert_fusion.4
  900.3 5.9 all-to-all-start.3
  906.3 4.5 convolution_convert_fusion.5
  910.8 10.0 all-to-all-done.3
  920.8 4.2 all-to-all-start.2
  939.2 4.1 all-to-all-start.1
  954.0 3.9 fusion.142
  957.9 5.9 all-to-all-start
  982.5 39.3 %all-reduce.12 = (f32[512]{0:T(512)S(1)}, f32[512]{0:T(512)S(1)}, f32[512]{0:T(512)S(1)}, f32[512]{0:T(512)S(1)}, f32[2048]{0:T(1024)S(1)}, /*index=5*/f32[512]{0:T(512)S(1)}) all-reduce(f32[512]{0:T(512)S(1)} %get-tuple-element.528, f32[512]{0:T(512)S(1)} %get-tuple-element.533, ...), channel_id=6, replica_groups=mesh['dp'=8,'tensor'=4] {'dp','tensor'}, use_global_device_ids=true, to_apply=%region_40.41.clone | all-reduce | flops 4608 | bytes 36864
  1025.3 67.1 %reduce-scatter.20.cloned.1.call-done = f32[16,24]{1,0:T(8,128)} async-done(((f32[512,24]{1,0:T(8,128)}), f32[16,24]{1,0:T(8,128)}) %reduce-scatter.20.cloned.1.call-update) | async-done | bytes 1552 | tf_op jit(solution)/shard_map/reduce_scatter | solution.py:368
  1092.4 132.6 %reduce-scatter.24.cloned.1.call-done = f32[16,64]{1,0:T(8,128)} async-done(((f32[512,64]{1,0:T(8,128)}), f32[16,64]{1,0:T(8,128)}) %reduce-scatter.24.cloned.1.call-update) | async-done | bytes 4112
  1225.0 132.6 %reduce-scatter.22.cloned.1.call-done = f32[16,64]{1,0:T(8,128)} async-done(((f32[512,64]{1,0:T(8,128)}), f32[16,64]{1,0:T(8,128)}) %reduce-scatter.22.cloned.1.call-update) | async-done | bytes 4112
  (589 shorter events, 393.4 us)
Async XLA Ops:
  7.2 52.2 %copy-start.36 = (bf16[6,64,64]{2,1,0:T(8,128)(2,1)S(1)}, bf16[6,64,64]{2,1,0:T(8,128)(2,1)}, u32[]{:S(2)}) copy-start(bf16[6,64,64]{2,1,0:T(8,128)(2,1)} %param.36) | copy-start | bytes 147460
  7.2 52.3 %copy-start.37 = (bf16[6,64,64]{2,1,0:T(8,128)(2,1)S(1)}, bf16[6,64,64]{2,1,0:T(8,128)(2,1)}, u32[]{:S(2)}) copy-start(bf16[6,64,64]{2,1,0:T(8,128)(2,1)} %param.37) | copy-start | bytes 147460
  7.2 237.1 %all-gather.5.cloned.1.call-start = ((), (), s32[]{:S(2)}) async-start(), calls=%async_computation.11 | async-start | bytes 2621440 | tf_op jit(solution)/shard_map/all_gather | solution.py:177
  8.5 50.9 %copy-start.41 = (f32[512]{0:T(512)}, f32[512]{0:T(512)S(1)}, u32[]{:S(2)}) copy-start(f32[512]{0:T(512)S(1)} %broadcast_multiply_fusion.5) | copy-start | bytes 6148
  9.8 49.5 %copy-start.43 = (f32[512]{0:T(512)}, f32[512]{0:T(512)S(1)}, u32[]{:S(2)}) copy-start(f32[512]{0:T(512)S(1)} %add_rsqrt_fusion.1) | copy-start | bytes 6148
  59.3 424.0 %reduce-scatter.12.cloned.1.call-start = ((), (), s32[]{:S(2)}) async-start(), calls=%async_computation.12 | async-start | bytes 2621440 | tf_op jit(solution)/shard_map/reduce_scatter | solution.py:230
  92.7 34.9 %copy-start.52 = (bf16[16,24]{1,0:T(8,128)(2,1)S(1)}, bf16[16,24]{1,0:T(8,128)(2,1)}, u32[]{:S(2)}) copy-start(bf16[16,24]{1,0:T(8,128)(2,1)} %param.35) | copy-start | bytes 2308
  92.7 76.4 %copy-start.53 = (bf16[16,64]{1,0:T(8,128)(2,1)S(1)}, bf16[16,64]{1,0:T(8,128)(2,1)}, u32[]{:S(2)}) copy-start(bf16[16,64]{1,0:T(8,128)(2,1)} %param.33) | copy-start | bytes 6148
  92.7 113.3 %copy-start.54 = (bf16[16,64]{1,0:T(8,128)(2,1)S(1)}, bf16[16,64]{1,0:T(8,128)(2,1)}, u32[]{:S(2)}) copy-start(bf16[16,64]{1,0:T(8,128)(2,1)} %param.34) | copy-start | bytes 6148
  126.2 120.6 %copy-start.25 = (s32[2048,8]{0,1:T(8,128)S(1)}, s32[2048,8]{0,1:T(8,128)}, u32[]{:S(2)}) copy-start(s32[2048,8]{0,1:T(8,128)} %param.29) | copy-start | bytes 196612
  169.0 75.3 %copy-start.19 = (bf16[512,24]{1,0:T(8,128)(2,1)}, bf16[512,24]{1,0:T(8,128)(2,1)S(1)}, u32[]{:S(2)}) copy-start(bf16[512,24]{1,0:T(8,128)(2,1)S(1)} %all_gather.55) | copy-start | bytes 73732
  206.0 46.6 %copy-start.21 = (bf16[512,64]{1,0:T(8,128)(2,1)}, bf16[512,64]{1,0:T(8,128)(2,1)S(1)}, u32[]{:S(2)}) copy-start(bf16[512,64]{1,0:T(8,128)(2,1)S(1)} %all_gather.56) | copy-start | bytes 196612
  244.3 8.3 copy-start.23
  244.3 7.3 copy-start.55
  244.3 7.3 copy-start.1
  247.0 5.6 copy-start.11
  256.4 4.1 copy-start.35
  256.4 4.1 copy-start.47
  421.9 2.8 copy-start.6
  455.5 27.7 %copy-start = (bf16[512,512]{1,0:T(8,128)(2,1)S(1)}, bf16[512,512]{1,0:T(8,128)(2,1)}, u32[]{:S(2)}) copy-start(bf16[512,512]{1,0:T(8,128)(2,1)} %param.28) | copy-start | bytes 1572868
  455.5 94.8 %all-gather.7.cloned.1.call-start = ((), (), s32[]{:S(2)}) async-start(), calls=%async_computation.13 | async-start | bytes 2621440 | tf_op jit(solution)/shard_map/all_gather | solution.py:240
  483.2 2.7 copy-start.5
  484.6 3.2 copy-start.38
  484.6 34.6 %copy-start.39 = (bf16[512,64]{0,1:T(8,128)(2,1)S(1)}, bf16[512,64]{0,1:T(8,128)(2,1)}, u32[]{:S(2)}) copy-start(bf16[512,64]{0,1:T(8,128)(2,1)} %param.42) | copy-start | bytes 196612
  487.1 69.4 %all-gather.9.cloned.1.call-start = ((), (), s32[]{:S(2)}) async-start(), calls=%async_computation.15 | async-start | bytes 2621440 | tf_op jit(solution)/shard_map/all_gather | solution.py:178
  487.7 109.6 %reduce-scatter.16.cloned.1.call-start = ((), (), s32[]{:S(2)}) async-start(), calls=%async_computation.16 | async-start | bytes 2621440 | tf_op jit(solution)/shard_map/reduce_scatter | solution.py:262
  550.3 6.2 copy-start.28
  565.3 34.2 %copy-start.8 = (bf16[512,512]{1,0:T(8,128)(2,1)S(1)}, bf16[512,512]{1,0:T(8,128)(2,1)}, u32[]{:S(2)}) copy-start(bf16[512,512]{1,0:T(8,128)(2,1)} %param.30) | copy-start | bytes 1572868
  565.3 59.3 %copy-start.30 = (bf16[6,64,512]{2,1,0:T(8,128)(2,1)S(1)}, bf16[6,64,512]{2,1,0:T(8,128)(2,1)}, u32[]{:S(2)}) copy-start(bf16[6,64,512]{2,1,0:T(8,128)(2,1)} %copy.127) | copy-start | bytes 1179652
  565.3 59.3 %all-gather.11.cloned.1.call-start = ((), (), s32[]{:S(2)}) async-start(), calls=%async_computation.17 | async-start | bytes 2621440 | tf_op jit(solution)/shard_map/all_gather | solution.py:272
  599.5 29.4 %copy-start.48 = (f32[512]{0:T(512)}, f32[512]{0:T(512)S(1)}, u32[]{:S(2)}) copy-start(f32[512]{0:T(512)S(1)} %get-tuple-element.652) | copy-start | bytes 6148
  601.9 375.9 %reduce-scatter.18.cloned.1.call-start = ((), (), s32[]{:S(2)}) async-start(), calls=%async_computation.18 | async-start | bytes 2621440 | tf_op jit(solution)/shard_map/reduce_scatter | solution.py:338
  700.4 4.3 copy-start.27
  704.7 2.9 copy-start.4
  824.0 60.9 %copy-start.13 = (bf16[2048,64]{0,1:T(8,128)(2,1)}, bf16[2048,64]{0,1:T(8,128)(2,1)S(1)}, u32[]{:S(2)}) copy-start(bf16[2048,64]{0,1:T(8,128)(2,1)S(1)} %convert_element_type.188) | copy-start | bytes 786436
  824.1 3.6 copy-start.40
  827.6 54.4 %copy-start.26 = (s32[2048,8]{0,1:T(8,128)S(1)}, s32[2048,8]{0,1:T(8,128)}, u32[]{:S(2)}) copy-start(s32[2048,8]{0,1:T(8,128)} %param.29) | copy-start | bytes 196612
  827.6 54.4 %copy-start.56 = (s32[6]{0:T(128)S(1)}, s32[6]{0:T(128)}, u32[]{:S(2)}) copy-start(s32[6]{0:T(128)} %copy-done.55) | copy-start | bytes 76
  827.7 54.5 %copy-start.12 = (f32[2048,8]{0,1:T(8,128)S(1)}, f32[2048,8]{0,1:T(8,128)}, u32[]{:S(2)}) copy-start(f32[2048,8]{0,1:T(8,128)} %copy-done.11) | copy-start | bytes 196612
  827.7 54.5 %copy-start.32 = (f32[2048]{0:T(1024)S(1)}, f32[2048]{0:T(1024)}, u32[]{:S(2)}) copy-start(f32[2048]{0:T(1024)} %copy-done.31) | copy-start | bytes 24580
  827.7 54.5 %copy-start.34 = (f32[2048]{0:T(1024)S(1)}, f32[2048]{0:T(1024)}, u32[]{:S(2)}) copy-start(f32[2048]{0:T(1024)} %copy-done.33) | copy-start | bytes 24580
  882.0 3.0 copy-start.17
  882.4 3.4 copy-start.16
  889.5 89.9 %reduce-scatter.14.cloned.1.call-start = ((), (), s32[]{:S(2)}) async-start(), calls=%async_computation.14 | async-start | bytes 2621440 | tf_op jit(solution)/shard_map/reduce_scatter | solution.py:246
  900.3 20.4 %all-to-all-start.3 = ((bf16[8,512,64]{1,2,0:T(8,128)(2,1)}), bf16[8,512,64]{1,2,0:T(8,128)(2,1)S(1)}, u32[]{:S(2)}, u32[]{:S(2)}) async-start(bf16[8,512,64]{1,2,0:T(8,128)(2,1)} %bitcast.51), calls=%async_computation.8 | async-start | bytes 1048576 | tf_op jit(solution)/shard_map/all_to_all | solution.py:17
  906.3 18.7 %copy-start.18 = (bf16[6,2048,64]{1,2,0:T(8,128)(2,1)S(1)}, bf16[6,2048,64]{1,2,0:T(8,128)(2,1)}, u32[]{:S(2)}) copy-start(bf16[6,2048,64]{1,2,0:T(8,128)(2,1)} %get-tuple-element.247) | copy-start | bytes 4718596
  920.8 4.2 copy-start.14
  920.8 18.5 %all-to-all-start.2 = ((bf16[8,64,512]{2,1,0:T(8,128)(2,1)}), bf16[8,64,512]{2,1,0:T(8,128)(2,1)}, u32[]{:S(2)}, u32[]{:S(2)}) async-start(bf16[8,64,512]{2,1,0:T(8,128)(2,1)} %bitcast.49), calls=%async_computation.7 | async-start | bytes 1048576 | tf_op jit(solution)/shard_map/all_to_all | solution.py:17
  928.3 15.1 %copy-start.58 = (bf16[512]{0:T(512)(128)(2,1)S(1)}, bf16[512]{0:T(512)(128)(2,1)}, u32[]{:S(2)}) copy-start(bf16[512]{0:T(512)(128)(2,1)} %get-tuple-element.631) | copy-start | bytes 3076
  928.3 15.1 %copy-start.57 = (f32[512]{0:T(512)S(1)}, f32[512]{0:T(512)}, u32[]{:S(2)}) copy-start(f32[512]{0:T(512)} %get-tuple-element.649) | copy-start | bytes 6148
  928.3 15.4 %copy-start.2 = (bf16[2048,512]{1,0:T(8,128)(2,1)S(1)}, bf16[2048,512]{1,0:T(8,128)(2,1)}, u32[]{:S(2)}) copy-start(bf16[2048,512]{1,0:T(8,128)(2,1)} %all-gather.5.cloned.1.call-done) | copy-start | bytes 6291460
  939.2 18.7 %all-to-all-start.1 = ((bf16[8,2,12288]{2,1,0:T(2,128)(2,1)}), bf16[8,2,12288]{2,1,0:T(2,128)(2,1)}, u32[]{:S(2)}, u32[]{:S(2)}) async-start(bf16[8,2,12288]{2,1,0:T(2,128)(2,1)} %reshape.328), calls=%async_computation.6 | async-start | bytes 786432 | tf_op jit(solution)/shard_map/all_to_all | solution.py:17
  943.3 149.1 %reduce-scatter.20.cloned.1.call-start = ((), (), s32[]{:S(2)}) async-start(), calls=%async_computation.19 | async-start | bytes 270336 | tf_op jit(solution)/shard_map/reduce_scatter | solution.py:368
  957.9 16.8 %all-to-all-start = ((bf16[8,2,12288]{2,1,0:T(2,128)(2,1)}), bf16[8,2,12288]{2,1,0:T(2,128)(2,1)}, u32[]{:S(2)}, u32[]{:S(2)}) async-start(bf16[8,2,12288]{2,1,0:T(2,128)(2,1)} %reshape.326), calls=%async_computation.5 | async-start | bytes 786432 | tf_op jit(solution)/shard_map/all_to_all | solution.py:17
  963.8 261.2 %reduce-scatter.24.cloned.1.call-start = ((), (), s32[]{:S(2)}) async-start(), calls=%async_computation.21 | async-start | bytes 270336
  966.2 391.4 %reduce-scatter.22.cloned.1.call-start = ((), (), s32[]{:S(2)}) async-start(), calls=%async_computation.20 | async-start | bytes 270336
  970.9 6.8 copy-start.42
  970.9 6.8 copy-start.44
  970.9 6.8 copy-start.46
  973.0 6.5 copy-start.9
  973.0 6.5 copy-start.10
  973.0 6.5 copy-start.49
  979.4 3.1 copy-start.50
  979.4 3.1 copy-start.51
  (11 other events, 16.7 us)
Sparse Core Ops, SparseCore 0:
  59.4 22.7 all-gather.4
  455.6 27.5 reduce-scatter.11
  487.2 22.5 all-gather.6
  511.3 22.5 all-gather.8
  565.4 31.7 reduce-scatter.15
  602.0 22.5 all-gather.10
  889.6 31.4 reduce-scatter.17
  923.7 31.3 reduce-scatter.13
  958.1 134.2 reduce-scatter.19
  1095.1 129.8 reduce-scatter.23
  1227.8 129.7 reduce-scatter.21
where the time goes:
time: 1380 us; the launch traced here: 1360 us
  waiting for transfers between devices  430 us (31%)
  matrix products  335 us (24%)
  blocking collectives  326 us (24%)
  local copies, waits for them, and re-layouts  184 us (13%)
  other arithmetic  52.2 us (4%)
  starting transfers between devices  20.8 us (2%)
  between operations  15.4 us (1%)
    unnamed x13, waiting for transfers between devices  266 us
    dot_general x76, matrix products, contract(): lax.dot_general(left, right, (((left_dim,), (right_dim,)), ((), ())), pre...  143 us
    unnamed x2, blocking collectives  81.4 us
    reduce_scatter x1, waiting for transfers between devices, per_device(): lax.psum_scatter(router_grad, ('dp', 'tensor'), scatter_dimension=0, tile...  67.1 us
    dynamic_update_slice x36, local copies, waits for them, and re-layouts, attend_forward(): return lax.map(attend, (query_blocks, position_blocks))  63.1 us
    dot_general x12, matrix products, contract_exact(): lax.dot_general(left, right, (((left_dim,), (right_dim,)), ((), ())), pre...  47.5 us
    all_gather x1, blocking collectives, per_device(): lax.all_gather(w_router, ('dp', 'tensor'), axis=0, tiled=True)  41.5 us
    all_gather x1, blocking collectives, per_device(): lax.all_gather(w_value, ('dp', 'tensor'), axis=0, tiled=True)  38.3 us
  transfers between devices with their start and end apart: 15, of which 9 were waited for; matrix products, arithmetic and copies ran while one was open for 5% of the time, Pallas kernels for 0%

commit v1 on v0

v1 whole, which is shorter than its diff:
```python
import jax
import jax.numpy as jnp
from jax import lax
from jax.experimental import pallas as pl
from jax.experimental.pallas import tpu as pltpu
from jax.sharding import PartitionSpec as P

F32 = jnp.float32
BF16 = jnp.bfloat16
HEAD = 64
LANES = 128
HALF = 256
ROWS = 64
TINY = 16
CHUNK = 32
VMEM_MAX = 60 * 1024 * 1024

PLACES_A = ((0, 0, 0), (0, 0, 1), (1, 0, 0), (1, 0, 1))
PLACES_XA = tuple((y, 1, s) for y, _, s in PLACES_A)
PLACES_B = ((0, 0, 2), (0, 0, 3), (0, 1, 2), (0, 1, 3))
PLACES_YB = tuple((1, x, s) for _, x, s in PLACES_B)
LAYOUT = tuple(
    tuple((2 * y + core, 2 * s + x) for y, x, s in places)
    for core in (0, 1)
    for places in (PLACES_A, PLACES_XA, PLACES_B, PLACES_YB)
)
SLOT_AT, IN_AT, OUT_AT, POS_AT = 0, 4, 12, 20


def nn(left, right):
    return lax.dot_general(left, right, (((1,), (0,)), ((), ())), preferred_element_type=F32)


def nt(left, right):
    return lax.dot_general(left, right, (((1,), (1,)), ((), ())), preferred_element_type=F32)


def norm_parts(rows):
    average = jnp.mean(rows, axis=-1, keepdims=True)
    centered = rows - average
    inverse = lax.rsqrt(jnp.mean(centered * centered, axis=-1, keepdims=True) + 1e-05)
    return centered * inverse, inverse


def norm_backward(incoming, scaled, inverse, gain):
    weighted = incoming * gain
    return inverse * (
        weighted
        - jnp.mean(weighted, axis=-1, keepdims=True)
        - scaled * jnp.mean(weighted * scaled, axis=-1, keepdims=True)
    )


def any_spec():
    return pl.BlockSpec(memory_space=pl.ANY)


def smem_spec():
    return pl.BlockSpec(memory_space=pltpu.SMEM)


def params():
    return pltpu.CompilerParams(vmem_limit_bytes=VMEM_MAX)


def shaped(shape, kind):
    return jax.ShapeDtypeStruct(shape, kind)


def pack_kernel(
    wq, wo, wup, wdown, wk, wv, wr, g1, b1, g2, b2, bdown, bup, first_ref, second_ref, wide, square
):
    experts = wq.shape[0]
    group = experts * HEAD
    hidden = wup.shape[1]
    first_ref[...] = jnp.zeros_like(first_ref)
    for j in range(experts):
        first_ref[0:ROWS, j * HEAD : (j + 1) * HEAD] = wq[j]
    square[...] = jnp.zeros_like(square)
    for i, vector in enumerate((g1, b1, g2, b2, bdown)):
        square[24 + i : 25 + i, 0:TINY] = vector[...].astype(F32)
    columns = square[...].T
    first_ref[ROWS : ROWS + TINY, 0:HEAD] = wk[...]
    first_ref[ROWS : ROWS + TINY, HEAD : 2 * HEAD] = wv[...]
    first_ref[ROWS : ROWS + TINY, LANES : 2 * LANES] = columns[0:TINY, :].astype(BF16)
    first_ref[ROWS : ROWS + TINY, LANES : LANES + wr.shape[1]] = wr[...]
    first_ref[ROWS : ROWS + 1, 2 * LANES : 2 * LANES + HEAD] = bup[...]
    wide[...] = jnp.zeros_like(wide)
    for j in range(experts):
        wide[j * HEAD : (j + 1) * HEAD, 0:ROWS] = wo[j].astype(F32)
    second_ref[:, 0:group] = wide[0:group, :].T[0:ROWS].astype(BF16)
    second_ref[:, group : group + hidden] = wup[...]
    wide[0:hidden, 0:ROWS] = wdown[...].astype(F32)
    second_ref[:, group + hidden :] = wide[0:hidden, :].T[0:ROWS].astype(BF16)


def pack(wq, wo, wup, wdown, wk, wv, wr, vectors, bup):
    group, hidden = wq.shape[0] * HEAD, wup.shape[1]
    return pl.pallas_call(
        pack_kernel,
        out_shape=(
            shaped((ROWS + TINY, group), BF16),
            shaped((ROWS, group + 2 * hidden), BF16),
        ),
        scratch_shapes=[
            pltpu.VMEM((max(group, hidden), LANES), F32),
            pltpu.VMEM((LANES, LANES), F32),
        ],
        compiler_params=params(),
    )(wq, wo, wup, wdown, wk, wv, wr, *[v.reshape(1, -1) for v in vectors], bup.reshape(1, -1))


def sum_four(kept, one, two, three):
    return kept.astype(F32) + one.astype(F32) + two.astype(F32) + three.astype(F32)


def unpack_first_kernel(kept, one, two, three, gq, gk, gv, gr, v1, v2, v3, v4, v5, gb, total):
    total[...] = sum_four(kept[0], one[...], two[...], three[...])
    for j in range(gq.shape[0]):
        gq[j] = total[0:ROWS, j * HEAD : (j + 1) * HEAD]
    gk[...] = total[ROWS : ROWS + TINY, 0:HEAD]
    gv[...] = total[ROWS : ROWS + TINY, HEAD : 2 * HEAD]
    gr[...] = total[ROWS : ROWS + TINY, LANES : LANES + gr.shape[1]]
    square = jnp.concatenate(
        [total[ROWS : ROWS + TINY, LANES : 2 * LANES], jnp.zeros((LANES - TINY, LANES), F32)], axis=0
    ).T
    for i, out in enumerate((v1, v2, v3, v4, v5)):
        out[...] = square[24 + i : 25 + i, 0:TINY]
    gb[...] = total[ROWS : ROWS + 1, 2 * LANES : 2 * LANES + HEAD]


def unpack_first(kept, one, two, three, experts, routed):
    outs = pl.pallas_call(
        unpack_first_kernel,
        out_shape=(
            shaped((experts, ROWS, HEAD), F32),
            shaped((TINY, HEAD), F32),
            shaped((TINY, HEAD), F32),
            shaped((TINY, routed), F32),
            *[shaped((1, TINY), F32) for _ in range(5)],
            shaped((1, HEAD), F32),
        ),
        scratch_shapes=[pltpu.VMEM(kept.shape[1:], F32)],
        compiler_params=params(),
    )(kept, one, two, three)
    return outs[0], outs[1], outs[2], outs[3], [v.reshape(-1) for v in outs[4:9]], outs[9].reshape(-1)


def unpack_second_kernel(kept, one, two, three, go, gup, gdown, total, wide):
    experts = go.shape[0]
    group, hidden = experts * HEAD, gup.shape[1]
    total[...] = sum_four(kept[0], one[...], two[...], three[...])
    gup[...] = total[:, group : group + hidden]
    wide[...] = jnp.zeros_like(wide)
    wide[0:ROWS, 0:group] = total[:, 0:group]
    turned = wide[:, 0:group].T
    for j in range(experts):
        go[j] = turned[j * HEAD : (j + 1) * HEAD, 0:ROWS]
    wide[0:ROWS, 0:hidden] = total[:, group + hidden :]
    gdown[...] = wide[:, 0:hidden].T[:, 0:ROWS]


def unpack_second(kept, one, two, three, experts, hidden):
    group = experts * HEAD
    return pl.pallas_call(
        unpack_second_kernel,
        out_shape=(
            shaped((experts, HEAD, ROWS), F32),
            shaped((ROWS, hidden), F32),
            shaped((hidden, ROWS), F32),
        ),
        scratch_shapes=[
            pltpu.VMEM(kept.shape[1:], F32),
            pltpu.VMEM((LANES, max(group, hidden)), F32),
        ],
        compiler_params=params(),
    )(kept, one, two, three)


def axis_moves(dp):
    turns = [
        [(d, (d + 2 * step) % dp) for d in range(dp)] for step in range(1, dp // 2)
    ]
    return turns, [(d, d ^ 1) for d in range(dp)]


CORE = [(0, 1), (1, 0), (2, 3), (3, 2)]
ACROSS = [(0, 2), (2, 0), (1, 3), (3, 1)]
CROSSED = [(0, 3), (3, 0), (1, 2), (2, 1)]


def over_core(x):
    return lax.ppermute(x, "tensor", CORE)


def over_y(x):
    return lax.ppermute(x, "tensor", ACROSS)


def crossed(x):
    return lax.ppermute(x, "tensor", CROSSED)


def gather_blocks(own, dp):
    turns, swap = axis_moves(dp)

    def over_x(x):
        return lax.ppermute(x, "dp", swap)

    own = own[None]
    one, two, three = [lax.ppermute(own, "dp", turn) for turn in turns]
    first = jnp.concatenate([own, one, over_y(own), over_y(one)], axis=0)
    second = jnp.concatenate([two, three, over_x(two), over_x(three)], axis=0)
    mine = [first, over_x(first), second, over_y(second)]
    return mine + [over_core(x) for x in mine]


def add_low(*terms):
    total = terms[0].astype(F32)
    for term in terms[1:]:
        total = total + term.astype(F32)
    return total.astype(BF16)


def reduce_blocks(keep_a, keep_b, send_a, send_b, dp):
    turns, swap = axis_moves(dp)

    def over_x(x):
        return lax.ppermute(x, "dp", swap)

    got_a, got_b = over_core(send_a), over_core(send_b)
    next_a = over_y(add_low(keep_a[1], got_a[1]))
    next_b = over_x(add_low(keep_b[1], got_b[1]))
    last_a = over_x(add_low(keep_a[0, 1], got_a[0, 1], next_a[1]))
    last_b = over_y(add_low(keep_b[0, 1], got_b[0, 1], next_b[1]))
    done_a = add_low(keep_a[0, 0], got_a[0, 0], next_a[0], last_a)
    done_b = add_low(keep_b[0, 0], got_b[0, 0], next_b[0], last_b)
    return (
        done_a,
        lax.ppermute(done_a[1], "dp", turns[0]),
        lax.ppermute(done_b[0], "dp", turns[1]),
        lax.ppermute(done_b[1], "dp", turns[2]),
    )


def block_copies(table, pieces, row_from, rows, stride, target, sems):
    copies = []
    for a, (piece, places) in enumerate(zip(pieces, LAYOUT)):
        for i, (slot, place) in enumerate(places):
            source = piece.at[i, pl.ds(row_from, rows), :]
            block = table[IN_AT + place]
            if stride is None:
                into = target.at[slot, pl.ds(pl.multiple_of(block * rows, rows), rows), :]
            else:
                row = (block * stride + table[SLOT_AT + slot]) * rows
                into = target.at[pl.ds(pl.multiple_of(row, rows), rows), :]
            copies.append(pltpu.make_async_copy(source, into, sems.at[a, i]))
    return copies


def first_kernel(table, low_tok, high_tok, routes, *refs):
    pieces, (normed_ref, kv_ref, gates_ref, small, vectors, up_bias, sems) = refs[:8], refs[8:]
    copies = block_copies(table, pieces, ROWS, TINY, 4, small, sems)
    for copy in copies:
        copy.start()
    tokens = jnp.concatenate([low_tok[0:HALF, :], high_tok[...]], axis=0).astype(F32)
    scaled, _ = norm_parts(tokens)
    for copy in copies:
        copy.wait()
    turned = small[:, LANES : 2 * LANES].astype(F32).T
    vectors[...] = turned[24:32, :]
    for i in range(32):
        up_bias[i // 8 : i // 8 + 1, (i % 8) * HEAD : (i % 8 + 1) * HEAD] = small[
            TINY * i : TINY * i + 1, 2 * LANES : 2 * LANES + HEAD
        ].astype(F32)
    normed = (scaled * vectors[0:1, :] + vectors[1:2, :]).astype(BF16)
    normed_ref[...] = normed
    kv_ref[...] = nn(normed, small[:, 0:LANES]).astype(BF16)
    logits = nn(normed, small[:, LANES : 2 * LANES])
    lane = lax.broadcasted_iota(jnp.int32, logits.shape, 1)
    ways = routes.shape[1]
    chosen = [lane == routes[:, k : k + 1] for k in range(ways)]
    member = chosen[0]
    for k in range(1, ways):
        member = member | chosen[k]
    logits = jnp.where(member, logits, -jnp.inf)
    exponent = jnp.exp(logits - jnp.max(logits, axis=-1, keepdims=True))
    shares = exponent / jnp.sum(exponent, axis=-1, keepdims=True)
    gates = jnp.zeros_like(shares)
    for k in range(ways):
        gate = jnp.sum(jnp.where(chosen[k], shares, 0.0), axis=-1, keepdims=True)
        gates = jnp.where(lane == k, gate, gates)
    gates_ref[...] = gates


def first_stage(table, tokens, tokens_high, routes, pieces):
    rows, width = tokens.shape
    return pl.pallas_call(
        first_kernel,
        in_specs=[smem_spec()] + [pl.BlockSpec(memory_space=pltpu.VMEM)] * 3 + [any_spec()] * 8,
        out_shape=(
            shaped((rows, width), BF16),
            shaped((rows, LANES), BF16),
            shaped((rows, LANES), F32),
            shaped((width, pieces[0].shape[2]), BF16),
            shaped((8, width), F32),
            shaped((8, width), F32),
        ),
        scratch_shapes=[pltpu.SemaphoreType.DMA((8, 4))],
        compiler_params=params(),
    )(table, tokens, tokens_high, routes, *pieces)


def half_routes(routes, k, at, half):
    return jnp.broadcast_to(routes[at, k : k + 1], half.shape) - half


def query_kernel(table, normed, routes, *refs):
    pieces, (chosen, weight, queries, sems) = refs[:8], refs[8:]
    experts = weight.shape[2] // HEAD
    copies = block_copies(table, pieces, 0, ROWS, None, weight, sems)
    for copy in copies:
        copy.start()
    for copy in copies:
        copy.wait()
    for slot in range(4):
        queries[slot] = nn(normed[...], weight[slot]).astype(BF16)
    ways = routes.shape[1]
    half = (lax.broadcasted_iota(jnp.int32, (CHUNK, LANES), 1) >= HEAD).astype(jnp.int32)

    def step(c, _):
        at = pl.ds(pl.multiple_of(c * CHUNK, CHUNK), CHUNK)
        wanted = [half_routes(routes, k, at, half) for k in range(ways)]
        picked = [jnp.zeros((CHUNK, LANES), F32)] * ways
        for slot in range(4):
            for pair in range(experts // 2):
                value = queries[slot, at, pair * LANES : (pair + 1) * LANES].astype(F32)
                base = experts * table[SLOT_AT + slot] + 2 * pair
                for k in range(ways):
                    picked[k] = jnp.where(wanted[k] == base, value, picked[k])
        for k in range(ways):
            chosen[k, at, :] = picked[k].astype(BF16)
        return 0

    lax.fori_loop(0, normed.shape[0] // CHUNK, step, 0)


def query_stage(table, normed, routes, pieces):
    rows, width = normed.shape
    group = pieces[0].shape[2]
    return pl.pallas_call(
        query_kernel,
        in_specs=[smem_spec()] + [pl.BlockSpec(memory_space=pltpu.VMEM)] * 2 + [any_spec()] * 8,
        out_shape=(
            shaped((routes.shape[1], rows, LANES), BF16),
            shaped((4, width, group), BF16),
        ),
        scratch_shapes=[
            pltpu.VMEM((4, rows, group), BF16),
            pltpu.SemaphoreType.DMA((8, 4)),
        ],
        compiler_params=params(),
    )(table, normed, routes, *pieces)


def place_pair(table, pieces, key_scr, value_scr, ones):
    lower = lax.broadcasted_iota(jnp.int32, (HALF, LANES), 1) < HEAD
    for p, piece in enumerate(pieces):
        for h in range(2):
            both = piece[h * HALF : (h + 1) * HALF, :].astype(F32)
            turned = pltpu.roll(both, HEAD, 1)
            at = pl.ds(pl.multiple_of(table[POS_AT + 2 * p + h] * HALF, HALF), HALF)
            key_scr[at, :] = (jnp.where(lower, both, turned) * 0.125).astype(BF16)
            value_scr[at, 0:LANES] = jnp.where(lower, turned, both).astype(BF16)
            if ones:
                value_scr[at, LANES : 2 * LANES] = jnp.ones((HALF, LANES), BF16)


def causal_mask():
    shape = (HALF, HALF)
    return lax.broadcasted_iota(jnp.int32, shape, 1) <= lax.broadcasted_iota(jnp.int32, shape, 0)


def attend_kernel(table, query, kv0, kv1, kv2, kv3, out_ref, total_ref, keys, values, scores, tops, sums):
    block = pl.program_id(0)
    ways = query.shape[0]

    @pl.when(block == 0)
    def _():
        place_pair(table, (kv0, kv1, kv2, kv3), keys, values, True)

    last = table[POS_AT + block]
    tops[...] = jnp.full_like(tops, -jnp.inf)

    def score(at, masked):
        rows = pl.ds(pl.multiple_of(at * HALF, HALF), HALF)
        keys_here = keys[rows, :]
        for k in range(ways):
            here = nt(query[k], keys_here)
            if masked:
                here = jnp.where(causal_mask(), here, -1e30)
            scores[at, k] = here
            tops[k] = jnp.maximum(tops[k], jnp.maximum(here[:, 0:LANES], here[:, LANES:]))

    lax.fori_loop(0, last, lambda at, _: (score(at, False), 0)[1], 0)
    score(last, True)
    for k in range(ways):
        tops[k] = jnp.broadcast_to(jnp.max(tops[k], axis=-1, keepdims=True), (HALF, LANES))
    sums[...] = jnp.zeros_like(sums)

    def weigh(at, _):
        rows = pl.ds(pl.multiple_of(at * HALF, HALF), HALF)
        values_here = values[rows, :]
        for k in range(ways):
            top = tops[k]
            here = scores[at, k]
            weights = jnp.concatenate(
                [jnp.exp(here[:, 0:LANES] - top), jnp.exp(here[:, LANES:] - top)], axis=1
            ).astype(BF16)
            sums[k] += nn(weights, values_here)
        return 0

    lax.fori_loop(0, last + 1, weigh, 0)
    for k in range(ways):
        whole = sums[k]
        out_ref[k] = whole[:, 0:LANES] / whole[:, LANES:]
        total_ref[k] = tops[k] + jnp.log(whole[:, LANES:])


def attend_stage(table, query, pairs, seq):
    ways, rows, _ = query.shape
    kv_spec = pl.BlockSpec((rows, LANES), lambda b: (0, 0))
    spec = pl.BlockSpec((ways, HALF, LANES), lambda b: (0, b, 0))
    return pl.pallas_call(
        attend_kernel,
        grid=(rows // HALF,),
        in_specs=[smem_spec(), spec] + [kv_spec] * 4,
        out_specs=(spec, spec),
        out_shape=(shaped((ways, rows, LANES), F32), shaped((ways, rows, LANES), F32)),
        scratch_shapes=[
            pltpu.VMEM((seq, LANES), BF16),
            pltpu.VMEM((seq, 2 * LANES), BF16),
            pltpu.VMEM((seq // HALF, ways, HALF, HALF), F32),
            pltpu.VMEM((ways, HALF, LANES), F32),
            pltpu.VMEM((ways, HALF, 2 * LANES), F32),
        ],
        compiler_params=params(),
    )(table, query, *pairs)


def attend_back_kernel(
    table, query, grad, totals, inner, kv0, kv1, kv2, kv3, grad_query, *refs
):
    outs, (keys, values, key_sum, value_sum, query_sum, query_t, grad_t, probs, scored) = refs[:4], refs[4:]
    block = pl.program_id(0)
    ways = query.shape[0]

    @pl.when(block == 0)
    def _():
        place_pair(table, (kv0, kv1, kv2, kv3), keys, values, False)
        key_sum[...] = jnp.zeros_like(key_sum)
        value_sum[...] = jnp.zeros_like(value_sum)

    last = table[POS_AT + block]
    query_sum[...] = jnp.zeros_like(query_sum)
    for k in range(ways):
        query_t[:, k * HALF : (k + 1) * HALF] = query[k].T
        grad_t[:, k * HALF : (k + 1) * HALF] = grad[k].T

    def step(at, masked):
        rows = pl.ds(pl.multiple_of(at * HALF, HALF), HALF)
        keys_here = keys[rows, :]
        values_here = values[rows, :]
        for k in range(ways):
            score = nt(query[k], keys_here)
            total, mean = totals[k], inner[k]
            prob = jnp.concatenate(
                [jnp.exp(score[:, 0:LANES] - total), jnp.exp(score[:, LANES:] - total)], axis=1
            )
            if masked:
                prob = jnp.where(causal_mask(), prob, 0.0)
            grad_prob = nt(grad[k], values_here)
            grad_score = prob * (grad_prob - jnp.concatenate([mean, mean], axis=1))
            probs[k * HALF : (k + 1) * HALF, :] = prob.astype(BF16)
            scored[k * HALF : (k + 1) * HALF, :] = grad_score.astype(BF16)
        query_sum[...] += nn(scored[...], keys_here)
        key_sum[at] += nn(query_t[...], scored[...])
        value_sum[at] += nn(grad_t[...], probs[...])

    lax.fori_loop(0, last, lambda at, _: (step(at, False), 0)[1], 0)
    step(last, True)
    for k in range(ways):
        grad_query[k] = query_sum[k * HALF : (k + 1) * HALF, :].astype(BF16)

    @pl.when(block == pl.num_programs(0) - 1)
    def _():
        for p, out in enumerate(outs):
            for h in range(2):
                at = table[POS_AT + 2 * p + h]
                key_part, value_part = key_sum[at], value_sum[at]
                out[h, 0:HEAD, :] = ((key_part[0:HEAD] + key_part[HEAD:]) * 0.125).astype(BF16)
                out[h, HEAD:, :] = (value_part[0:HEAD] + value_part[HEAD:]).astype(BF16)


def attend_back_stage(table, query, grad, totals, inner, pairs, seq):
    ways, rows, _ = query.shape
    kv_spec = pl.BlockSpec((rows, LANES), lambda b: (0, 0))
    spec = pl.BlockSpec((ways, HALF, LANES), lambda b: (0, b, 0))
    pair_spec = pl.BlockSpec((2, LANES, HALF), lambda b: (0, 0, 0))
    return pl.pallas_call(
        attend_back_kernel,
        grid=(rows // HALF,),
        in_specs=[smem_spec()] + [spec] * 4 + [kv_spec] * 4,
        out_specs=(spec,) + (pair_spec,) * 4,
        out_shape=(shaped((ways, rows, LANES), BF16),) + (shaped((2, LANES, HALF), BF16),) * 4,
        scratch_shapes=[
            pltpu.VMEM((seq, LANES), BF16),
            pltpu.VMEM((seq, LANES), BF16),
            pltpu.VMEM((seq // HALF, LANES, HALF), F32),
            pltpu.VMEM((seq // HALF, LANES, HALF), F32),
            pltpu.VMEM((ways * HALF, LANES), F32),
            pltpu.VMEM((LANES, ways * HALF), BF16),
            pltpu.VMEM((LANES, ways * HALF), BF16),
            pltpu.VMEM((ways * HALF, HALF), BF16),
            pltpu.VMEM((ways * HALF, HALF), BF16),
        ],
        compiler_params=params(),
    )(table, query, grad, totals, inner, *pairs)


def put_blocks(table, grads, outs, slot, rows, row_to, column_to, slot_stride):
    keep_a, keep_b, send_a, send_b = outs
    y, core = slot // 2, slot % 2
    wide = grads.shape[1]
    for s in range(4):
        for x in range(2):
            at = table[OUT_AT + 2 * s + x]
            if slot_stride:
                at = at * slot_stride + table[SLOT_AT + slot]
            block = grads[pl.ds(pl.multiple_of(at * rows, rows), rows), :]
            if s < 2:
                out, place = (send_a if core else keep_a), (y, x, s)
            else:
                out, place = (send_b if core else keep_b), (x, y, s - 2)
            out[place[0], place[1], place[2], row_to : row_to + rows, column_to : column_to + wide] = block


def middle_kernel(table, low_tok, high_tok, low_cot, high_cot, heads, gates, routes, vectors, up_bias, *refs):
    pieces = refs[:8]
    output, grad_mid, grad_ref, inner, grad_gate, sums, bias_grad = refs[8:15]
    blocks = refs[15:19]
    weight, mixed, back, big, hid_scr, pre_scr, sems = refs[19:]
    ways, rows, _ = heads.shape
    width = low_tok.shape[1]
    group = mixed.shape[2]
    hidden = hid_scr.shape[1]
    experts = group // HEAD
    copies = block_copies(table, pieces, 0, ROWS, None, weight, sems)
    for copy in copies:
        copy.start()
    half = (lax.broadcasted_iota(jnp.int32, (CHUNK, LANES), 1) >= HEAD).astype(jnp.int32)
    lane = lax.broadcasted_iota(jnp.int32, (CHUNK, LANES), 1)

    def expand(c, _):
        at = pl.ds(pl.multiple_of(c * CHUNK, CHUNK), CHUNK)
        wanted = [half_routes(routes, k, at, half) for k in range(ways)]
        weighted = [
            (heads[k, at, :] * gates[at, k : k + 1]).astype(BF16).astype(F32) for k in range(ways)
        ]
        for slot in range(4):
            for pair in range(experts // 2):
                base = experts * table[SLOT_AT + slot] + 2 * pair
                value = jnp.zeros((CHUNK, LANES), F32)
                for k in range(ways):
                    value = jnp.where(wanted[k] == base, weighted[k], value)
                mixed[slot, at, pair * LANES : (pair + 1) * LANES] = value.astype(BF16)
        return 0

    lax.fori_loop(0, rows // CHUNK, expand, 0)
    for copy in copies:
        copy.wait()
    middle = jnp.concatenate([low_tok[0:HALF, :], high_tok[...]], axis=0).astype(F32)
    for slot in range(4):
        middle = middle + nt(mixed[slot], weight[slot, :, 0:group])
    scaled, inverse = norm_parts(middle)
    gain = vectors[2:3, :]
    normed = (scaled * gain + vectors[3:4, :]).astype(BF16)
    normed_t = normed.T
    cot = jnp.concatenate([low_cot[0:HALF, :], high_cot[...]], axis=0)
    cot_t = cot.T
    result = middle + vectors[4:5, :]
    grad_normed = jnp.zeros((rows, width), F32)
    up_at, down_at = group, group + hidden
    for slot in range(4):
        bias = up_bias[pl.ds(table[SLOT_AT + slot], 1), :]
        preact = nn(normed, weight[slot, :, up_at:down_at]) + bias
        share = jax.nn.sigmoid(preact)
        active = (preact * share).astype(BF16)
        hid_scr[...] = active
        slope = share * (1.0 + preact * (1.0 - share))
        grad_pre = (nn(cot, weight[slot, :, down_at:]) * slope).astype(BF16)
        pre_scr[...] = grad_pre
        bias_grad[pl.ds(table[SLOT_AT + slot], 1), :] = jnp.sum(
            grad_pre.astype(F32), axis=0, keepdims=True
        )
        result = result + nt(hid_scr[...], weight[slot, :, down_at:])
        grad_normed = grad_normed + nt(pre_scr[...], weight[slot, :, up_at:down_at])
        big[...] = nn(normed_t, pre_scr[...]).astype(BF16)
        put_blocks(table, big, blocks, slot, ROWS, 0, up_at, 0)
        big[...] = nn(cot_t, hid_scr[...]).astype(BF16)
        put_blocks(table, big, blocks, slot, ROWS, 0, down_at, 0)
    output[...] = result.astype(BF16)
    cot_wide = cot.astype(F32)
    sums[...] = jnp.zeros_like(sums)
    sums[2:3, :] = jnp.sum(grad_normed * scaled, axis=0, keepdims=True)
    sums[3:4, :] = jnp.sum(grad_normed, axis=0, keepdims=True)
    sums[4:5, :] = jnp.sum(cot_wide, axis=0, keepdims=True)
    grad_middle = cot_wide + norm_backward(grad_normed, scaled, inverse, gain)
    grad_mid[...] = grad_middle
    grad_attn = grad_middle.astype(BF16)
    grad_attn_t = grad_attn.T
    for slot in range(4):
        big[:, 0:group] = nn(grad_attn_t, mixed[slot]).astype(BF16)
        put_blocks(table, big.at[:, 0:group], blocks, slot, ROWS, 0, 0, 0)
        back[slot] = nn(grad_attn, weight[slot, :, 0:group])

    def select(c, _):
        at = pl.ds(pl.multiple_of(c * CHUNK, CHUNK), CHUNK)
        wanted = [half_routes(routes, k, at, half) for k in range(ways)]
        picked = [jnp.zeros((CHUNK, LANES), F32)] * ways
        for slot in range(4):
            for pair in range(experts // 2):
                value = back[slot, at, pair * LANES : (pair + 1) * LANES]
                base = experts * table[SLOT_AT + slot] + 2 * pair
                for k in range(ways):
                    picked[k] = jnp.where(wanted[k] == base, value, picked[k])
        gate_grads = jnp.zeros((CHUNK, LANES), F32)
        for k in range(ways):
            head = heads[k, at, :]
            gate_grad = jnp.sum(picked[k] * head, axis=-1, keepdims=True)
            gate_grads = jnp.where(lane == k, gate_grad, gate_grads)
            low = (picked[k] * gates[at, k : k + 1]).astype(BF16)
            grad_ref[k, at, :] = low
            inner[k, at, :] = jnp.broadcast_to(
                jnp.sum(low.astype(F32) * head, axis=-1, keepdims=True), (CHUNK, LANES)
            )
        grad_gate[at, :] = gate_grads
        return 0

    lax.fori_loop(0, rows // CHUNK, select, 0)


def middle_stage(table, tokens, tokens_high, cot, cot_high, heads, gates, routes, vectors, up_bias, pieces):
    rows, width = tokens.shape
    ways = heads.shape[0]
    packed = pieces[0].shape[2]
    hidden = up_bias.shape[1]
    group = packed - 2 * hidden
    block = shaped((2, 2, 2, ROWS, packed), BF16)
    vmem = pl.BlockSpec(memory_space=pltpu.VMEM)
    return pl.pallas_call(
        middle_kernel,
        in_specs=[smem_spec()] + [vmem] * 9 + [any_spec()] * 8,
        out_shape=(
            shaped((rows, width), BF16),
            shaped((rows, width), F32),
            shaped((ways, rows, LANES), BF16),
            shaped((ways, rows, LANES), F32),
            shaped((rows, LANES), F32),
            shaped((8, width), F32),
            shaped((8, hidden), F32),
            block,
            block,
            block,
            block,
        ),
        scratch_shapes=[
            pltpu.VMEM((4, width, packed), BF16),
            pltpu.VMEM((4, rows, group), BF16),
            pltpu.VMEM((4, rows, group), F32),
            pltpu.VMEM((width, hidden), BF16),
            pltpu.VMEM((rows, hidden), BF16),
            pltpu.VMEM((rows, hidden), BF16),
            pltpu.SemaphoreType.DMA((8, 4)),
        ],
        compiler_params=params(),
    )(table, tokens, tokens_high, cot, cot_high, heads, gates, routes, vectors, up_bias, *pieces)


def last_kernel(
    table, low_tok, high_tok, grad_mid, grad_query, normed, routes, gates, grad_gate, weight, small,
    vectors, sums, bias_grad, p0, p1, p2, p3, low_out, high_out, *refs
):
    blocks, (spread, pair_grad, big, tiny, wide, extra) = refs[:4], refs[4:]
    ways, rows, _ = grad_query.shape
    group = spread.shape[2]
    experts = group // HEAD
    half = (lax.broadcasted_iota(jnp.int32, (CHUNK, LANES), 1) >= HEAD).astype(jnp.int32)

    def expand(c, _):
        at = pl.ds(pl.multiple_of(c * CHUNK, CHUNK), CHUNK)
        wanted = [half_routes(routes, k, at, half) for k in range(ways)]
        held = [grad_query[k, at, :].astype(F32) for k in range(ways)]
        for slot in range(4):
            for pair in range(experts // 2):
                base = experts * table[SLOT_AT + slot] + 2 * pair
                value = jnp.zeros((CHUNK, LANES), F32)
                for k in range(ways):
                    value = jnp.where(wanted[k] == base, held[k], value)
                spread[slot, at, pair * LANES : (pair + 1) * LANES] = value.astype(BF16)
        return 0

    lax.fori_loop(0, rows // CHUNK, expand, 0)
    for h in range(2):
        total = sum_four(p0[h], p1[h], p2[h], p3[h])
        pair_grad[h * HALF : (h + 1) * HALF, :] = total.T.astype(BF16)
    gate = gates[...]
    gate_grad = grad_gate[...]
    chosen_grad = gate * (gate_grad - jnp.sum(gate * gate_grad, axis=-1, keepdims=True))
    lane = lax.broadcasted_iota(jnp.int32, (rows, LANES), 1)
    logit_grad = jnp.zeros((rows, LANES), F32)
    for k in range(ways):
        logit_grad = jnp.where(lane == routes[:, k : k + 1], chosen_grad[:, k : k + 1], logit_grad)
    logit_low = logit_grad.astype(BF16)
    normed_t = normed[...].T
    grad_normed = nt(pair_grad[...], small[:, 0:LANES]) + nt(logit_low, small[:, LANES : 2 * LANES])
    for slot in range(4):
        grad_normed = grad_normed + nt(spread[slot], weight[slot])
        big[...] = nn(normed_t, spread[slot]).astype(BF16)
        put_blocks(table, big, blocks, slot, ROWS, 0, 0, 0)
    tokens = jnp.concatenate([low_tok[0:HALF, :], high_tok[...]], axis=0).astype(F32)
    scaled, inverse = norm_parts(tokens)
    back = grad_mid[...] + norm_backward(grad_normed, scaled, inverse, vectors[0:1, :])
    low_out[...] = back[0:HALF]
    high_out[...] = back[HALF:].astype(BF16)
    wide[...] = jnp.zeros_like(wide)
    wide[24:32, :] = sums[...]
    wide[24:25, :] = jnp.sum(grad_normed * scaled, axis=0, keepdims=True)
    wide[25:26, :] = jnp.sum(grad_normed, axis=0, keepdims=True)
    tiny[:, 0:LANES] = nn(normed_t, pair_grad[...]).astype(BF16)
    tiny[:, LANES : 2 * LANES] = (nn(normed_t, logit_low) + wide[...].T).astype(BF16)
    extra[...] = jnp.zeros_like(extra)
    for i in range(32):
        extra[TINY * i : TINY * i + 1, 0:HEAD] = bias_grad[i // 8 : i // 8 + 1, (i % 8) * HEAD : (i % 8 + 1) * HEAD]
    tiny[:, 2 * LANES : 3 * LANES] = extra[...].astype(BF16)
    for slot in range(4):
        put_blocks(table, tiny, blocks, slot, TINY, ROWS, 0, 4)


def last_stage(
    table, tokens, tokens_high, grad_mid, grad_query, normed, routes, gates, grad_gate, weight, small,
    vectors, sums, bias_grad, pair_parts
):
    rows, width = tokens.shape
    group = weight.shape[2]
    block = shaped((2, 2, 2, ROWS + TINY, group), BF16)
    vmem = pl.BlockSpec(memory_space=pltpu.VMEM)
    return pl.pallas_call(
        last_kernel,
        in_specs=[smem_spec()] + [vmem] * 17,
        out_shape=(shaped((HALF, width), F32), shaped((rows - HALF, width), BF16), block, block, block, block),
        scratch_shapes=[
            pltpu.VMEM((4, rows, group), BF16),
            pltpu.VMEM((rows, LANES), BF16),
            pltpu.VMEM((width, group), BF16),
            pltpu.VMEM((width, 3 * LANES), BF16),
            pltpu.VMEM((LANES, width), F32),
            pltpu.VMEM((width, LANES), F32),
        ],
        compiler_params=params(),
    )(
        table, tokens, tokens_high, grad_mid, grad_query, normed, routes, gates, grad_gate, weight, small,
        vectors, sums, bias_grad, *pair_parts
    )


def gather_plain(x, axis, dim):
    return lax.all_gather(x, axis, axis=dim, tiled=True)


def general_pieces(wq, wo, wup, wdown, wk, wv, wr, vectors, bup):
    every = ("dp", "tensor")
    width = wup.shape[0] * lax.axis_size("dp")
    group = wq.shape[0] * HEAD

    def whole(rows):
        return lax.all_gather(gather_plain(rows, "dp", 0), "tensor", axis=0)

    queries = whole(wq.transpose(1, 0, 2).reshape(-1, group))
    second = whole(
        jnp.concatenate([wo.transpose(2, 0, 1).reshape(-1, group), wup, wdown.T], axis=1)
    )
    wide = [gather_plain(w, every, 0) for w in (wk, wv, wr)]
    columns = [gather_plain(v, every, 0)[:, None] for v in vectors]
    bias = jnp.pad(gather_plain(bup, every, 0).reshape(-1, 1, HEAD), ((0, 0), (0, TINY - 1), (0, 0)))
    left = jnp.concatenate(wide + columns, axis=1)
    small = jnp.concatenate(
        [jnp.pad(left, ((0, 0), (0, 2 * LANES - left.shape[1]))), bias.reshape(width, HEAD)], axis=1
    )
    small = jnp.pad(small, ((0, 0), (0, group - small.shape[1])))

    def block_one(slot, place):
        row = (4 * place + slot) * TINY
        return jnp.concatenate([queries[slot, place * ROWS : (place + 1) * ROWS], small[row : row + TINY]])

    first = [jnp.stack([block_one(*at) for at in places]) for places in LAYOUT]
    later = [
        jnp.stack([second[slot, place * ROWS : (place + 1) * ROWS] for slot, place in places])
        for places in LAYOUT
    ]
    return first, later


def general_sum(blocks):
    keep_a, keep_b, send_a, send_b = blocks
    slots = []
    for slot in range(4):
        y, core = slot // 2, slot % 2
        part_a, part_b = (send_a, send_b) if core else (keep_a, keep_b)
        slots.append(
            jnp.stack(
                [(part_a[y, x, s] if s < 2 else part_b[x, y, s - 2]) for s in range(4) for x in range(2)]
            )
        )
    return lax.psum(jnp.stack(slots), ("dp", "tensor")).astype(F32)


def general_grads(first, later, experts, hidden, routed):
    group = experts * HEAD
    d, t = lax.axis_index("dp"), lax.axis_index("tensor")
    dp = lax.axis_size("dp")
    width = 8 * ROWS
    first, later = general_sum(first), general_sum(later)
    mine = lax.dynamic_index_in_dim(first[:, :, 0:ROWS].reshape(4, width, group), t, 0, False)
    small = first[:, :, ROWS:].transpose(1, 0, 2, 3).reshape(width, group)
    rest = lax.dynamic_index_in_dim(later.reshape(4, width, -1), t, 0, False)
    rows = width // dp

    def own(x, length, index):
        return lax.dynamic_slice_in_dim(x, index * length, length, 0)

    query = own(mine, rows, d).reshape(rows, experts, HEAD).transpose(1, 0, 2)
    rest = own(rest, rows, d)
    index = d * 4 + t
    tiny = own(small, rows // 4, index)
    bias = small.reshape(32, TINY, group)[:, 0, 2 * LANES : 2 * LANES + HEAD].reshape(-1)
    return (
        query,
        tiny[:, 0:HEAD],
        tiny[:, HEAD : 2 * HEAD],
        tiny[:, LANES : LANES + routed],
        [tiny[:, LANES + 24 + i] for i in range(5)],
        own(bias, bias.shape[0] // (4 * dp), index),
        rest[:, 0:group].reshape(rows, experts, HEAD).transpose(1, 2, 0),
        rest[:, group : group + hidden],
        rest[:, group + hidden :].T,
    )


def per_device(
    tokens,
    routes,
    cotangent,
    ln1_gain,
    ln1_bias,
    w_key,
    w_value,
    w_router,
    w_query,
    w_out,
    ln2_gain,
    ln2_bias,
    w_up,
    b_up,
    w_down,
    b_down,
):
    dp = lax.axis_size("dp")
    tuned = dp == 8
    d, t = lax.axis_index("dp"), lax.axis_index("tensor")
    seq = routes.shape[0]
    blocks = seq // HALF
    slots = [(t ^ s) if tuned else jnp.int32(s) for s in range(4)]
    z, x = d // 2, d % 2
    if tuned:
        into = [((z + 4 - s) % 4) * 2 + (x ^ o) for s in range(4) for o in range(2)]
        out = [((z + s) % 4) * 2 + (x ^ o) for s in range(4) for o in range(2)]
    else:
        into = out = [jnp.int32(place) for place in range(8)]
    ranks = [t, t ^ 1, t ^ 2, t ^ 3]
    positions = [p for r in ranks for p in (2 * r, blocks - 1 - 2 * r)]
    table = jnp.stack([v.astype(jnp.int32) for v in slots + into + out + positions])
    own_routes = jnp.concatenate(
        [lax.dynamic_slice_in_dim(routes, p * HALF, HALF, 0) for p in positions[0:2]], axis=0
    )
    vectors_in = (ln1_gain, ln1_bias, ln2_gain, ln2_bias, b_down)

    tokens_high = crossed(tokens[HALF:])
    if tuned:
        first, second = pack(w_query, w_out, w_up, w_down, w_key, w_value, w_router, vectors_in, b_up)
        first_pieces = gather_blocks(first, dp)
        second_pieces = gather_blocks(second, dp)
    else:
        first_pieces, second_pieces = general_pieces(
            w_query, w_out, w_up, w_down, w_key, w_value, w_router, vectors_in, b_up
        )
    cot_high = crossed(cotangent[HALF:])

    normed, pair, gates, small, vectors, up_bias = first_stage(
        table, tokens, tokens_high, own_routes, first_pieces
    )
    pair_y = over_y(pair)
    pairs = (pair, over_core(pair), pair_y, over_core(pair_y))
    query, query_weight = query_stage(table, normed, own_routes, first_pieces)
    heads, totals = attend_stage(table, query, pairs, seq)
    (output, grad_mid, grad_heads, inner, grad_gate, sums, bias_grad, *later_blocks) = middle_stage(
        table, tokens, tokens_high, cotangent, cot_high, heads, gates, own_routes, vectors, up_bias, second_pieces
    )
    grad_query, part0, part1, part2, part3 = attend_back_stage(
        table, query, grad_heads, totals, inner, pairs, seq
    )
    pair_parts = (part0, over_core(part1), over_y(part2), crossed(part3))
    low_rows, high_rows, *first_blocks = last_stage(
        table, tokens, tokens_high, grad_mid, grad_query, normed, own_routes, gates, grad_gate,
        query_weight, small, vectors, sums, bias_grad, pair_parts,
    )
    experts, hidden, routed = w_query.shape[0], w_up.shape[1], w_router.shape[1]
    if tuned:
        later = reduce_blocks(*later_blocks, dp)
        out_grad, up_grad, down_grad = unpack_second(*later, experts, hidden)
        early = reduce_blocks(*first_blocks, dp)
        query_grad, key_grad, value_grad, router_grad, small_grads, up_bias_grad = unpack_first(
            *early, experts, routed
        )
    else:
        (
            query_grad, key_grad, value_grad, router_grad, small_grads, up_bias_grad,
            out_grad, up_grad, down_grad,
        ) = general_grads(first_blocks, later_blocks, experts, hidden, routed)
    result = jnp.concatenate([output[:HALF], crossed(output[HALF:])], axis=0)
    grad_tokens = jnp.concatenate([low_rows, crossed(high_rows).astype(F32)], axis=0)
    return (
        result,
        grad_tokens,
        small_grads[0],
        small_grads[1],
        key_grad,
        value_grad,
        router_grad,
        query_grad,
        out_grad,
        small_grads[2],
        small_grads[3],
        up_grad,
        up_bias_grad,
        down_grad,
        small_grads[4],
    )


def solution(mesh):
    rows = P(("dp", "tensor"), None)
    vector = P(("dp", "tensor"))
    in_specs = (
        rows,
        P("dp", None),
        rows,
        vector,
        vector,
        rows,
        rows,
        rows,
        P("tensor", "dp", None),
        P("tensor", None, "dp"),
        vector,
        vector,
        P("dp", "tensor"),
        vector,
        P("tensor", "dp"),
        vector,
    )
    out_specs = (
        rows,
        rows,
        vector,
        vector,
        rows,
        rows,
        rows,
        P("tensor", "dp", None),
        P("tensor", None, "dp"),
        vector,
        vector,
        P("dp", "tensor"),
        vector,
        P("tensor", "dp"),
        vector,
    )
    return jax.shard_map(
        per_device, mesh=mesh, in_specs=in_specs, out_specs=out_specs, check_vma=False
    )
```

time: 1380 us -> 271 us (0.20); the launches traced: 1360 us -> 270 us
  matrix products: 335 us -> 0 us
  blocking collectives: 326 us -> 0 us
  waiting for transfers between devices: 430 us -> 110 us
  local copies, waits for them, and re-layouts: 184 us -> 10.1 us
  Pallas kernels: 0 us -> 95.8 us
  other arithmetic: 52.2 us -> 4.46 us
  starting transfers between devices: 20.8 us -> 48.6 us
  between operations: 15.4 us -> 1.23 us
    dot_general x138 -> x0, matrix products: 335 us -> none  [the longest x76 143 us: contract(): lax.dot_general(left, right, (((left_dim,), (right_dim,)), ((), ())), pre...]
    unnamed x13 -> x0, waiting for transfers between devices: 266 us -> none
    all_gather x7 -> x0, blocking collectives: 244 us -> none  [the longest x1 41.5 us: per_device(): lax.all_gather(w_router, ('dp', 'tensor'), axis=0, tiled=True)]
    reduce_scatter x5 -> x0, waiting for transfers between devices: 127 us -> none  [the longest x1 67.1 us: per_device(): lax.psum_scatter(router_grad, ('dp', 'tensor'), scatter_dimension=0, tile...]
    ppermute x0 -> x54, waiting for transfers between devices: none -> 110 us  [the longest x12 53.6 us: over_y(): return lax.ppermute(x, 'tensor', ACROSS)]
    dynamic_update_slice x67 -> x0, local copies, waits for them, and re-layouts: 104 us -> none  [the longest x36 63.1 us: attend_forward(): return lax.map(attend, (query_blocks, position_blocks))]
    pallas_call x0 -> x9, Pallas kernels: none -> 95.8 us  [the longest x1 37 us: middle_stage(): pl.pallas_call(middle_kernel, in_specs=[smem_spec()] + [vmem] * 9 + [any_...]
    unnamed x2 -> x0, blocking collectives: 81.4 us -> none
  transfers between devices with their start and end apart: 15 -> 54, of which waited for: 9 -> 24; matrix products, arithmetic and copies ran while one was open for 5% -> 3% of each run, Pallas kernels for 0% -> 10%
where the time goes in v1:
time: 271 us; the launch traced here: 270 us
  waiting for transfers between devices  110 us (41%)
  Pallas kernels  95.8 us (35%)
  starting transfers between devices  48.6 us (18%)
  local copies, waits for them, and re-layouts  10.1 us (4%)
  other arithmetic  4.46 us (2%)
    ppermute x12, waiting for transfers between devices, over_y(): return lax.ppermute(x, 'tensor', ACROSS)  53.6 us
    pallas_call x1, Pallas kernels, middle_stage(): pl.pallas_call(middle_kernel, in_specs=[smem_spec()] + [vmem] * 9 + [any_...  37 us
    ppermute x10, waiting for transfers between devices, over_x(): return lax.ppermute(x, 'dp', swap)  19.2 us
    pallas_call x1, Pallas kernels, attend_back_stage(): pl.pallas_call(attend_back_kernel, grid=(rows // HALF,), in_specs=[smem_s...  15.8 us
    ppermute x10, starting transfers between devices, over_x(): return lax.ppermute(x, 'dp', swap)  14.3 us
    ppermute x6, waiting for transfers between devices, gather_blocks(): one, two, three = [lax.ppermute(own, 'dp', turn) for turn in turns]  13.8 us
    pallas_call x1, Pallas kernels, attend_stage(): pl.pallas_call(attend_kernel, grid=(rows // HALF,), in_specs=[smem_spec()...  12.3 us
    pallas_call x1, Pallas kernels, last_stage(): pl.pallas_call(last_kernel, in_specs=[smem_spec()] + [vmem] * 17, out_sha...  11.9 us
  transfers between devices with their start and end apart: 54, of which 24 were waited for; matrix products, arithmetic and copies ran while one was open for 3% of the time, Pallas kernels for 10%

profile of v1, /device:TPU:0, one launch (start us, length us, event | category | flops | bytes accessed | tf_op | source)
XLA Modules:
  0.0 270.1 jit_solution(17755486971058362105)
XLA Ops:
  0.6 1.6 copy.35.wdown
  2.2 2.0 shard_map.271
  4.2 4.0 %collective-permute-start.6 = (bf16[1,80,384]{2,1,0:T(8,128)(2,1)}, bf16[1,80,384]{2,1,0:T(8,128)(2,1)S(1)}, u32[]{:S(2)}, u32[]{:S(2)}) collective-permute-start(bf16[1,80,384]{2,1,0:T(8,128)(2,1)} %bitcast.117), channel_id=1, source_target_pairs={{0,16},{4,20},{8,24},{12,28},{16,0},{20,4},{24,8},{28,12},{1,17},{... | collective-permute-start | bytes 184328 | tf_op jit(solution)/shard_map/ppermute | solution.py:211
  8.3 1.3 collective-permute-start.7
  9.6 0.7 collective-permute-start.2
  10.3 3.1 %collective-permute-start.23 = (bf16[1,64,1408]{2,1,0:T(8,128)(2,1)}, bf16[1,64,1408]{2,1,0:T(8,128)(2,1)S(1)}, u32[]{:S(2)}, u32[]{:S(2)}) collective-permute-start(bf16[1,64,1408]{2,1,0:T(8,128)(2,1)} %bitcast.112), channel_id=1, source_target_pairs={{0,24},{4,28},{8,0},{12,4},{16,8},{20,12},{24,16},{28,20},{1,25},{... | collective-permute-start | bytes 540680 | tf_op jit(solution)/shard_map/ppermute | solution.py:211
  13.4 1.0 slice.126
  14.4 1.6 collective-permute-start.19
  16.7 13.8 %collective-permute-done.22 = bf16[1,64,1408]{2,1,0:T(8,128)(2,1)S(1)} collective-permute-done((bf16[1,64,1408]{2,1,0:T(8,128)(2,1)}, bf16[1,64,1408]{2,1,0:T(8,128)(2,1)S(1)}, u32[]{:S(2)}, u32[]{:S(2)}) %collective-permute-start.22) | collective-permute-done | bytes 180256 | tf_op jit(solution)/shard_map/ppermute | solution.py:211
  31.0 1.6 collective-permute-start.24
  32.5 5.7 %collective-permute-done.24 = bf16[1,64,1408]{2,1,0:T(8,128)(2,1)S(1)} collective-permute-done((bf16[1,64,1408]{2,1,0:T(8,128)(2,1)S(1)}, bf16[1,64,1408]{2,1,0:T(8,128)(2,1)S(1)}, u32[]{:S(2)}, u32[]{:S(2)}) %collective-permute-start.24) | collective-permute-done | bytes 180256 | tf_op jit(solution)/shard_map/ppermute | solution.py:208
  38.2 1.5 collective-permute-start.25
  40.4 5.2 %collective-permute-done.25 = bf16[1,64,1408]{2,1,0:T(8,128)(2,1)S(1)} collective-permute-done((bf16[1,64,1408]{2,1,0:T(8,128)(2,1)S(1)}, bf16[1,64,1408]{2,1,0:T(8,128)(2,1)S(1)}, u32[]{:S(2)}, u32[]{:S(2)}) %collective-permute-start.25) | collective-permute-done | bytes 180256 | tf_op jit(solution)/shard_map/ppermute | solution.py:208
  46.2 1.6 collective-permute-start.8
  47.7 3.4 %collective-permute-done.20 = bf16[1,64,1408]{2,1,0:T(8,128)(2,1)S(1)} collective-permute-done((bf16[1,64,1408]{2,1,0:T(8,128)(2,1)S(1)}, bf16[1,64,1408]{2,1,0:T(8,128)(2,1)S(1)}, u32[]{:S(2)}, u32[]{:S(2)}) %collective-permute-start.20) | collective-permute-done | bytes 180256 | tf_op jit(solution)/shard_map/ppermute | solution.py:197
  51.8 1.6 collective-permute-start.21
  53.4 1.6 collective-permute-start.3
  55.5 13.4 %collective-permute-done.3 = bf16[1,80,384]{2,1,0:T(8,128)(2,1)S(1)} collective-permute-done((bf16[1,80,384]{2,1,0:T(8,128)(2,1)S(1)}, bf16[1,80,384]{2,1,0:T(8,128)(2,1)S(1)}, u32[]{:S(2)}, u32[]{:S(2)}) %collective-permute-start.3) | collective-permute-done | bytes 61472 | tf_op jit(solution)/shard_map/ppermute | solution.py:197
  69.9 1.6 collective-permute-start.5
  71.5 5.8 %collective-permute-done.10.refs_3_ = bf16[4,80,384]{2,1,0:T(8,128)(2,1)S(1)} collective-permute-done((bf16[4,80,384]{2,1,0:T(8,128)(2,1)S(1)}, bf16[4,80,384]{2,1,0:T(8,128)(2,1)S(1)}, u32[]{:S(2)}, u32[]{:S(2)}) %collective-permute-start.10) | collective-permute-done | bytes 245792 | tf_op jit(solution)/shard_map/ppermute | solution.py:197
  77.8 0.7 constant_dynamic-slice_fusion.1
  79.6 0.8 copy.36.routes
  81.1 4.8 %shard_map.272 = (bf16[512,512]{1,0:T(8,128)(2,1)}, bf16[512,128]{1,0:T(8,128)(2,1)}, f32[512,128]{1,0:T(8,128)}, bf16[512,384]{1,0:T(8,128)(2,1)}, f32[8,512]{1,0:T(8,128)}, /*index=5*/f32[8,512]{1,0:T(8,128)}) custom-call(s32[28]{0:T(128)} %stack.97.table, bf16[512,512]{1,0:T(8,128)(2,1)} %low_tok.5, bf16[256,512]{1,0:T(8,128)(2,1)} %copy-done.1, ...), custom_call_target="tpu_custom_call" | custom-call | tf_op jit(solution)/shard_map/pallas_call | solution.py:298
  86.0 1.5 collective-permute-start.16
  87.5 4.4 %collective-permute-done.16.kv2 = bf16[512,128]{1,0:T(8,128)(2,1)S(1)} collective-permute-done((bf16[512,128]{1,0:T(8,128)(2,1)}, bf16[512,128]{1,0:T(8,128)(2,1)S(1)}, u32[]{:S(2)}, u32[]{:S(2)}) %collective-permute-start.16) | collective-permute-done | bytes 131104 | tf_op jit(solution)/shard_map/ppermute | solution.py:197
  91.9 1.6 collective-permute-done.15.kv1
  93.6 1.2 collective-permute-done.17.kv3
  94.8 1.4 collective-permute-start.1
  96.2 8.2 %shard_map.273 = (bf16[8,512,128]{2,1,0:T(8,128)(2,1)}, bf16[4,512,384]{2,1,0:T(8,128)(2,1)}) custom-call(s32[28]{0:T(128)} %stack.97.table, bf16[512,512]{1,0:T(8,128)(2,1)} %get-tuple-element.63.normed, s32[512,8]{1,0:T(8,128)} %copy.36.routes, bf16[4,80,384]{2,1,0:T(8,128)(2,1)} %copy-done.3, bf16[4,80,384]{2,1,0:T(8,128)(2,1)} %copy-done.11, ...), custom_call_target="tpu_custom_call" | custom-call | tf_op jit(solution)/shard_map/pallas_call | solution.py:351
  104.5 12.3 %shard_map.274 = (f32[8,512,128]{2,1,0:T(8,128)}, f32[8,512,128]{2,1,0:T(8,128)}) custom-call(s32[28]{0:T(128)} %stack.97.table, bf16[8,512,128]{2,1,0:T(8,128)(2,1)} %get-tuple-element.64.query, bf16[512,128]{1,0:T(8,128)(2,1)} %get-tuple-element.65.kv0, bf16[512,128]{1,0:T(8,128)(2,1)} %copy-done.16, bf16[512,128]{1,0:T(8,128)(2,1)} %copy-done.15, ...), custom_call_target="tpu_custom_call" | custom-call | tf_op jit(solution)/shard_map/pallas_call | solution.py:434
  116.8 0.7 copy-done.22
  117.4 37.0 %shard_map.275 = (bf16[512,512]{1,0:T(8,128)(2,1)}, f32[512,512]{1,0:T(8,128)}, bf16[8,512,128]{2,1,0:T(8,128)(2,1)}, f32[8,512,128]{2,1,0:T(8,128)}, f32[512,12...) custom-call(s32[28]{0:T(128)} %stack.97.table, ...), custom_call_target="tpu_custom_call" | custom-call | tf_op jit(solution)/shard_map/pallas_call | solution.py:661
  154.4 15.8 %shard_map.276 = (bf16[8,512,128]{2,1,0:T(8,128)(2,1)}, bf16[2,128,256]{2,1,0:T(8,128)(2,1)}, bf16[2,128,256]{2,1,0:T(8,128)(2,1)}, bf16[2,128,256]{2,1,0:T(8,128)(2,1)}, bf16[2,128,256]{2,1,0:T(8,128)(2,1)}) custom-call(s32[28]{0:T(128)} %stack.97.table, bf16[8,512,128]{2,1,0:T(8,128)(2,1)} %get-tuple-element.64.query, ...), custom_call_target="tpu_custom_call" | custom-call | tf_op jit(solution)/shard_map/pallas_call | solution.py:510
  171.0 1.2 collective-permute-start.34
  172.1 5.0 %collective-permute-done.33.p2 = bf16[2,128,256]{2,1,0:T(8,128)(2,1)S(1)} collective-permute-done((bf16[2,128,256]{2,1,0:T(8,128)(2,1)}, bf16[2,128,256]{2,1,0:T(8,128)(2,1)S(1)}, u32[]{:S(2)}, u32[]{:S(2)}) %collective-permute-start.33) | collective-permute-done | bytes 131104 | tf_op jit(solution)/shard_map/ppermute | solution.py:197
  177.2 1.2 collective-permute-done.34.p3
  179.1 11.9 %shard_map.277 = (f32[256,512]{1,0:T(8,128)}, bf16[256,512]{1,0:T(8,128)(2,1)}, bf16[2,2,2,80,384]{4,3,2,1,0:T(8,128)(2,1)}, bf16[2,2,2,80,384]{4,3,2,1,0:T(8,12...) custom-call(s32[28]{0:T(128)} %stack.97.table, bf16[512,512]{1,0:T(8,128)(2,1)} %low_tok.5, ...), custom_call_target="tpu_custom_call" | custom-call | tf_op jit(solution)/shard_map/pallas_call | solution.py:758
  191.0 0.7 collective-permute-start.36
  193.3 0.8 collective-permute-start.35
  194.1 1.0 fusion.8
  195.1 1.3 collective-permute-start.37
  196.5 3.3 %collective-permute-done.31 = bf16[256,512]{1,0:T(8,128)(2,1)S(1)} collective-permute-done((bf16[256,512]{1,0:T(8,128)(2,1)S(1)}, bf16[256,512]{1,0:T(8,128)(2,1)S(1)}, u32[]{:S(2)}, u32[]{:S(2)}) %collective-permute-start.31) | collective-permute-done | bytes 262176 | tf_op jit(solution)/shard_map/ppermute | solution.py:201
  199.9 1.5 collective-permute-start.41
  201.4 0.8 pad_maximum_fusion.2
  202.2 3.3 %collective-permute-done.35 = bf16[256,512]{1,0:T(8,128)(2,1)S(1)} collective-permute-done((bf16[256,512]{1,0:T(8,128)(2,1)}, bf16[256,512]{1,0:T(8,128)(2,1)S(1)}, u32[]{:S(2)}, u32[]{:S(2)}) %collective-permute-start.35) | collective-permute-done | bytes 262176 | tf_op jit(solution)/shard_map/ppermute | solution.py:201
  205.5 5.8 %collective-permute-done.37 = bf16[2,2,80,384]{3,2,1,0:T(8,128)(2,1)S(1)} collective-permute-done((bf16[2,2,80,384]{3,2,1,0:T(8,128)(2,1)S(1)}, bf16[2,2,80,384]{3,2,1,0:T(8,128)(2,1)S(1)}, u32[]{:S(2)}, u32[]{:S(2)}) %collective-permute-start.37) | collective-permute-done | bytes 245792 | tf_op jit(solution)/shard_map/ppermute | solution.py:197
  211.4 1.6 collective-permute-start.38
  213.4 2.9 %collective-permute-done.38 = bf16[2,80,384]{2,1,0:T(8,128)(2,1)S(1)} collective-permute-done((bf16[2,80,384]{2,1,0:T(8,128)(2,1)S(1)}, bf16[2,80,384]{2,1,0:T(8,128)(2,1)S(1)}, u32[]{:S(2)}, u32[]{:S(2)}) %collective-permute-start.38) | collective-permute-done | bytes 122912 | tf_op jit(solution)/shard_map/ppermute | solution.py:229
  217.3 1.6 collective-permute-start.50
  219.0 14.4 %collective-permute-done.46 = bf16[2,2,64,1408]{3,2,1,0:T(8,128)(2,1)S(1)} collective-permute-done((bf16[2,2,64,1408]{3,2,1,0:T(8,128)(2,1)S(1)}, bf16[2,2,64,1408]{3,2,1,0:T(8,128)(2,1)S(1)}, u32[]{:S(2)}, u32[]{:S(2)}) %collective-permute-start.46) | collective-permute-done | bytes 720928 | tf_op jit(solution)/shard_map/ppermute | solution.py:197
  233.5 1.4 collective-permute-start.47
  235.1 1.3 collective-permute-start.51
  236.4 5.2 %collective-permute-done.47 = bf16[2,64,1408]{2,1,0:T(8,128)(2,1)S(1)} collective-permute-done((bf16[2,64,1408]{2,1,0:T(8,128)(2,1)S(1)}, bf16[2,64,1408]{2,1,0:T(8,128)(2,1)S(1)}, u32[]{:S(2)}, u32[]{:S(2)}) %collective-permute-start.47) | collective-permute-done | bytes 360480 | tf_op jit(solution)/shard_map/ppermute | solution.py:229
  241.9 0.7 collective-permute-done.51
  242.9 3.5 %collective-permute-start.53 = (bf16[64,1408]{1,0:T(8,128)(2,1)S(1)}, bf16[64,1408]{1,0:T(8,128)(2,1)S(1)}, u32[]{:S(2)}, u32[]{:S(2)}) collective-permute-start(bf16[64,1408]{1,0:T(8,128)(2,1)S(1)} %get-tuple-element.141), channel_id=1, source_target_pairs={{0,24},{4,28},{8,0},{12,4},{16,8},{20,12},{24,16},{28,20},{1,25},{... | collective-permute-start | bytes 540680 | tf_op jit(solution)/shard_map/ppermute | solution.py:242
  246.4 1.1 collective-permute-start.44
  247.5 2.0 collective-permute-start.43
  249.5 1.0 pad_maximum_fusion
  250.6 3.7 %collective-permute-done.44.three = bf16[80,384]{1,0:T(8,128)(2,1)S(1)} collective-permute-done((bf16[80,384]{1,0:T(8,128)(2,1)S(1)}, bf16[80,384]{1,0:T(8,128)(2,1)S(1)}, u32[]{:S(2)}, u32[]{:S(2)}) %collective-permute-start.44) | collective-permute-done | bytes 61472 | tf_op jit(solution)/shard_map/ppermute | solution.py:242
  254.2 8.2 %collective-permute-done.43.two = bf16[80,384]{1,0:T(8,128)(2,1)S(1)} collective-permute-done((bf16[80,384]{1,0:T(8,128)(2,1)S(1)}, bf16[80,384]{1,0:T(8,128)(2,1)S(1)}, u32[]{:S(2)}, u32[]{:S(2)}) %collective-permute-start.43) | collective-permute-done | bytes 61472 | tf_op jit(solution)/shard_map/ppermute | solution.py:241
  263.0 1.7 shard_map.278
  265.6 0.7 copy-done.25
  266.2 2.1 shard_map.279
  268.4 1.7 copy.40
  (161 shorter events, 13.9 us)
Async XLA Ops:
  4.2 47.4 %copy-start.26 = (bf16[64,1408]{1,0:T(8,128)(2,1)S(1)}, bf16[64,1408]{1,0:T(8,128)(2,1)}, u32[]{:S(2)}) copy-start(bf16[64,1408]{1,0:T(8,128)(2,1)} %get-tuple-element.70) | copy-start | bytes 540676
  4.2 10.2 %collective-permute-start.6 = (bf16[1,80,384]{2,1,0:T(8,128)(2,1)}, bf16[1,80,384]{2,1,0:T(8,128)(2,1)S(1)}, u32[]{:S(2)}, u32[]{:S(2)}) collective-permute-start(bf16[1,80,384]{2,1,0:T(8,128)(2,1)} %bitcast.117), channel_id=1, source_target_pairs={{0,16},{4,20},{8,24},{12,28},{16,0},{20,4},{24,8},{28,12},{1,17},{... | collective-permute-start | bytes 184328 | tf_op jit(solution)/shard_map/ppermute | solution.py:211
  8.3 7.8 %collective-permute-start.7 = (bf16[1,80,384]{2,1,0:T(8,128)(2,1)}, bf16[1,80,384]{2,1,0:T(8,128)(2,1)S(1)}, u32[]{:S(2)}, u32[]{:S(2)}) collective-permute-start(bf16[1,80,384]{2,1,0:T(8,128)(2,1)} %bitcast.118), channel_id=1, source_target_pairs={{0,24},{4,28},{8,0},{12,4},{16,8},{20,12},{24,16},{28,20},{1,25},{... | collective-permute-start | bytes 184328 | tf_op jit(solution)/shard_map/ppermute | solution.py:211
  9.6 43.7 %collective-permute-start.2 = (bf16[1,80,384]{2,1,0:T(8,128)(2,1)}, bf16[1,80,384]{2,1,0:T(8,128)(2,1)S(1)}, u32[]{:S(2)}, u32[]{:S(2)}) collective-permute-start(bf16[1,80,384]{2,1,0:T(8,128)(2,1)} %bitcast.119), channel_id=1, source_target_pairs={{0,8},{4,12},{8,16},{12,20},{16,24},{20,28},{24,0},{28,4},{1,9},{5... | collective-permute-start | bytes 184328 | tf_op jit(solution)/shard_map/ppermute | solution.py:211
  10.3 20.7 %collective-permute-start.23 = (bf16[1,64,1408]{2,1,0:T(8,128)(2,1)}, bf16[1,64,1408]{2,1,0:T(8,128)(2,1)S(1)}, u32[]{:S(2)}, u32[]{:S(2)}) collective-permute-start(bf16[1,64,1408]{2,1,0:T(8,128)(2,1)} %bitcast.112), channel_id=1, source_target_pairs={{0,24},{4,28},{8,0},{12,4},{16,8},{20,12},{24,16},{28,20},{1,25},{... | collective-permute-start | bytes 540680 | tf_op jit(solution)/shard_map/ppermute | solution.py:211
  13.4 17.0 %collective-permute-start.22 = (bf16[1,64,1408]{2,1,0:T(8,128)(2,1)}, bf16[1,64,1408]{2,1,0:T(8,128)(2,1)S(1)}, u32[]{:S(2)}, u32[]{:S(2)}) collective-permute-start(bf16[1,64,1408]{2,1,0:T(8,128)(2,1)} %bitcast.113), channel_id=1, source_target_pairs={{0,16},{4,20},{8,24},{12,28},{16,0},{20,4},{24,8},{28,12},{1,17},{... | collective-permute-start | bytes 540680 | tf_op jit(solution)/shard_map/ppermute | solution.py:211
  14.4 31.7 %collective-permute-start.19 = (bf16[1,64,1408]{2,1,0:T(8,128)(2,1)}, bf16[1,64,1408]{2,1,0:T(8,128)(2,1)S(1)}, u32[]{:S(2)}, u32[]{:S(2)}) collective-permute-start(bf16[1,64,1408]{2,1,0:T(8,128)(2,1)} %bitcast.114), channel_id=1, source_target_pairs={{0,2},{2,0},{1,3},{3,1},{4,6},{6,4},{5,7},{7,5},{8,10},{10,8},{9,1... | collective-permute-start | bytes 540680 | tf_op jit(solution)/shard_map/ppermute | solution.py:197
  16.0 23.7 %collective-permute-start.18 = (bf16[1,64,1408]{2,1,0:T(8,128)(2,1)}, bf16[1,64,1408]{2,1,0:T(8,128)(2,1)S(1)}, u32[]{:S(2)}, u32[]{:S(2)}) collective-permute-start(bf16[1,64,1408]{2,1,0:T(8,128)(2,1)} %bitcast.115), channel_id=1, source_target_pairs={{0,8},{4,12},{8,16},{12,20},{16,24},{20,28},{24,0},{28,4},{1,9},{5... | collective-permute-start | bytes 540680 | tf_op jit(solution)/shard_map/ppermute | solution.py:211
  16.7 36.7 %copy-start.33 = (bf16[80,384]{1,0:T(8,128)(2,1)S(1)}, bf16[80,384]{1,0:T(8,128)(2,1)}, u32[]{:S(2)}) copy-start(bf16[80,384]{1,0:T(8,128)(2,1)} %get-tuple-element.62) | copy-start | bytes 184324
  30.5 39.4 %collective-permute-start = (bf16[256,512]{1,0:T(8,128)(2,1)S(1)}, bf16[256,512]{1,0:T(8,128)(2,1)S(1)}, u32[]{:S(2)}, u32[]{:S(2)}) collective-permute-start(bf16[256,512]{1,0:T(8,128)(2,1)S(1)} %slice.126), channel_id=1, source_target_pairs={{0,3},{3,0},{1,2},{2,1},{4,7},{7,4},{5,6},{6,5},{8,11},{11,8},{9,1... | collective-permute-start | bytes 786440 | tf_op jit(solution)/shard_map/ppermute | solution.py:201
  31.0 7.3 %collective-permute-start.24 = (bf16[1,64,1408]{2,1,0:T(8,128)(2,1)S(1)}, bf16[1,64,1408]{2,1,0:T(8,128)(2,1)S(1)}, u32[]{:S(2)}, u32[]{:S(2)}) collective-permute-start(bf16[1,64,1408]{2,1,0:T(8,128)(2,1)S(1)} %collective-permute-done.22), channel_id=1, source_target_pairs={{0,4},{4,0},{8,12},{12,8},{16,20},{20,16},{24,28},{28,24},{1,5},{5... | collective-permute-start | bytes 540680 | tf_op jit(solution)/shard_map/ppermute | solution.py:208
  38.2 7.4 %collective-permute-start.25 = (bf16[1,64,1408]{2,1,0:T(8,128)(2,1)S(1)}, bf16[1,64,1408]{2,1,0:T(8,128)(2,1)S(1)}, u32[]{:S(2)}, u32[]{:S(2)}) collective-permute-start(bf16[1,64,1408]{2,1,0:T(8,128)(2,1)S(1)} %collective-permute-done.23), channel_id=1, source_target_pairs={{0,4},{4,0},{8,12},{12,8},{16,20},{20,16},{24,28},{28,24},{1,5},{5... | collective-permute-start | bytes 540680 | tf_op jit(solution)/shard_map/ppermute | solution.py:208
  39.8 15.2 %collective-permute-start.9 = (bf16[1,80,384]{2,1,0:T(8,128)(2,1)S(1)}, bf16[1,80,384]{2,1,0:T(8,128)(2,1)S(1)}, u32[]{:S(2)}, u32[]{:S(2)}) collective-permute-start(bf16[1,80,384]{2,1,0:T(8,128)(2,1)S(1)} %collective-permute-done.7), channel_id=1, source_target_pairs={{0,4},{4,0},{8,12},{12,8},{16,20},{20,16},{24,28},{28,24},{1,5},{5... | collective-permute-start | bytes 184328 | tf_op jit(solution)/shard_map/ppermute | solution.py:208
  45.6 5.5 %collective-permute-start.20 = (bf16[1,64,1408]{2,1,0:T(8,128)(2,1)S(1)}, bf16[1,64,1408]{2,1,0:T(8,128)(2,1)S(1)}, u32[]{:S(2)}, u32[]{:S(2)}) collective-permute-start(bf16[1,64,1408]{2,1,0:T(8,128)(2,1)S(1)} %collective-permute-done.18), channel_id=1, source_target_pairs={{0,2},{2,0},{1,3},{3,1},{4,6},{6,4},{5,7},{7,5},{8,10},{10,8},{9,1... | collective-permute-start | bytes 540680 | tf_op jit(solution)/shard_map/ppermute | solution.py:197
  46.2 39.8 %copy-start.8 = (bf16[4,64,1408]{2,1,0:T(8,128)(2,1)}, bf16[4,64,1408]{2,1,0:T(8,128)(2,1)S(1)}, u32[]{:S(2)}) copy-start(bf16[4,64,1408]{2,1,0:T(8,128)(2,1)S(1)} %constant_dynamic-update-slice_fusion.4.refs_2_) | copy-start | bytes 2162692
  46.2 5.6 %collective-permute-start.8 = (bf16[1,80,384]{2,1,0:T(8,128)(2,1)S(1)}, bf16[1,80,384]{2,1,0:T(8,128)(2,1)S(1)}, u32[]{:S(2)}, u32[]{:S(2)}) collective-permute-start(bf16[1,80,384]{2,1,0:T(8,128)(2,1)S(1)} %collective-permute-done.6), channel_id=1, source_target_pairs={{0,4},{4,0},{8,12},{12,8},{16,20},{20,16},{24,28},{28,24},{1,5},{5... | collective-permute-start | bytes 184328 | tf_op jit(solution)/shard_map/ppermute | solution.py:208
  51.1 28.0 %collective-permute-start.26 = (bf16[4,64,1408]{2,1,0:T(8,128)(2,1)S(1)}, bf16[4,64,1408]{2,1,0:T(8,128)(2,1)}, u32[]{:S(2)}, u32[]{:S(2)}) collective-permute-start(bf16[4,64,1408]{2,1,0:T(8,128)(2,1)S(1)} %constant_dynamic-update-slice_fusion.4.refs_2_), channel_id=1, source_target_pairs={{0,2},{2,0},{1,3},{3,1},{4,6},{6,4},{5,7},{7,5},{8,10},{10,8},{9,1... | collective-permute-start | bytes 2162696 | tf_op jit(solution)/shard_map/ppermute | solution.py:197
  51.7 34.2 %copy-start = (bf16[4,64,1408]{2,1,0:T(8,128)(2,1)}, bf16[4,64,1408]{2,1,0:T(8,128)(2,1)S(1)}, u32[]{:S(2)}) copy-start(bf16[4,64,1408]{2,1,0:T(8,128)(2,1)S(1)} %pad_maximum_fusion.1.refs_0_) | copy-start | bytes 2162692
  51.8 27.6 %collective-permute-start.21 = (bf16[4,64,1408]{2,1,0:T(8,128)(2,1)S(1)}, bf16[4,64,1408]{2,1,0:T(8,128)(2,1)}, u32[]{:S(2)}, u32[]{:S(2)}) collective-permute-start(bf16[4,64,1408]{2,1,0:T(8,128)(2,1)S(1)} %pad_maximum_fusion.1.refs_0_), channel_id=1, source_target_pairs={{0,4},{4,0},{8,12},{12,8},{16,20},{20,16},{24,28},{28,24},{1,5},{5... | collective-permute-start | bytes 2162696 | tf_op jit(solution)/shard_map/ppermute | solution.py:208
  53.4 15.6 %collective-permute-start.3 = (bf16[1,80,384]{2,1,0:T(8,128)(2,1)S(1)}, bf16[1,80,384]{2,1,0:T(8,128)(2,1)S(1)}, u32[]{:S(2)}, u32[]{:S(2)}) collective-permute-start(bf16[1,80,384]{2,1,0:T(8,128)(2,1)S(1)} %bitcast.120), channel_id=1, source_target_pairs={{0,2},{2,0},{1,3},{3,1},{4,6},{6,4},{5,7},{7,5},{8,10},{10,8},{9,1... | collective-permute-start | bytes 184328 | tf_op jit(solution)/shard_map/ppermute | solution.py:197
  54.9 14.6 %collective-permute-start.4 = (bf16[1,80,384]{2,1,0:T(8,128)(2,1)S(1)}, bf16[1,80,384]{2,1,0:T(8,128)(2,1)S(1)}, u32[]{:S(2)}, u32[]{:S(2)}) collective-permute-start(bf16[1,80,384]{2,1,0:T(8,128)(2,1)S(1)} %collective-permute-done.2), channel_id=1, source_target_pairs={{0,2},{2,0},{1,3},{3,1},{4,6},{6,4},{5,7},{7,5},{8,10},{10,8},{9,1... | collective-permute-start | bytes 184328 | tf_op jit(solution)/shard_map/ppermute | solution.py:197
  55.5 25.6 %copy-start.6 = (bf16[4,80,384]{2,1,0:T(8,128)(2,1)}, bf16[4,80,384]{2,1,0:T(8,128)(2,1)S(1)}, u32[]{:S(2)}) copy-start(bf16[4,80,384]{2,1,0:T(8,128)(2,1)S(1)} %constant_dynamic-update-slice_fusion.refs_2_) | copy-start | bytes 737284
  68.9 2.6 collective-permute-start.13
  69.6 7.7 %collective-permute-start.10 = (bf16[4,80,384]{2,1,0:T(8,128)(2,1)S(1)}, bf16[4,80,384]{2,1,0:T(8,128)(2,1)S(1)}, u32[]{:S(2)}, u32[]{:S(2)}) collective-permute-start(bf16[4,80,384]{2,1,0:T(8,128)(2,1)S(1)} %constant_dynamic-update-slice_fusion.refs_2_), channel_id=1, source_target_pairs={{0,2},{2,0},{1,3},{3,1},{4,6},{6,4},{5,7},{7,5},{8,10},{10,8},{9,1... | collective-permute-start | bytes 737288 | tf_op jit(solution)/shard_map/ppermute | solution.py:197
  69.9 7.5 %collective-permute-start.5 = (bf16[4,80,384]{2,1,0:T(8,128)(2,1)S(1)}, bf16[4,80,384]{2,1,0:T(8,128)(2,1)S(1)}, u32[]{:S(2)}, u32[]{:S(2)}) collective-permute-start(bf16[4,80,384]{2,1,0:T(8,128)(2,1)S(1)} %pad_maximum_fusion.3.refs_0_), channel_id=1, source_target_pairs={{0,4},{4,0},{8,12},{12,8},{16,20},{20,16},{24,28},{28,24},{1,5},{5... | collective-permute-start | bytes 737288 | tf_op jit(solution)/shard_map/ppermute | solution.py:208
  71.5 7.0 %collective-permute-start.11 = (bf16[4,80,384]{2,1,0:T(8,128)(2,1)S(1)}, bf16[4,80,384]{2,1,0:T(8,128)(2,1)S(1)}, u32[]{:S(2)}, u32[]{:S(2)}) collective-permute-start(bf16[4,80,384]{2,1,0:T(8,128)(2,1)S(1)} %pad_maximum_fusion.3.refs_0_), channel_id=1, source_target_pairs={{0,1},{1,0},{2,3},{3,2},{4,5},{5,4},{6,7},{7,6},{8,9},{9,8},{10,11... | collective-permute-start | bytes 737288 | tf_op jit(solution)/shard_map/ppermute | solution.py:193
  77.3 1.5 collective-permute-start.14
  77.4 3.6 %collective-permute-start.12 = (bf16[4,80,384]{2,1,0:T(8,128)(2,1)S(1)}, bf16[4,80,384]{2,1,0:T(8,128)(2,1)}, u32[]{:S(2)}, u32[]{:S(2)}) collective-permute-start(bf16[4,80,384]{2,1,0:T(8,128)(2,1)S(1)} %collective-permute-done.5.refs_1_), channel_id=1, source_target_pairs={{0,1},{1,0},{2,3},{3,2},{4,5},{5,4},{6,7},{7,6},{8,9},{9,8},{10,11... | collective-permute-start | bytes 737288 | tf_op jit(solution)/shard_map/ppermute | solution.py:193
  78.5 38.2 %collective-permute-start.29 = (bf16[4,64,1408]{2,1,0:T(8,128)(2,1)S(1)}, bf16[4,64,1408]{2,1,0:T(8,128)(2,1)}, u32[]{:S(2)}, u32[]{:S(2)}) collective-permute-start(bf16[4,64,1408]{2,1,0:T(8,128)(2,1)S(1)} %constant_dynamic-update-slice_fusion.4.refs_2_), channel_id=1, source_target_pairs={{0,1},{1,0},{2,3},{3,2},{4,5},{5,4},{6,7},{7,6},{8,9},{9,8},{10,11... | collective-permute-start | bytes 2162696 | tf_op jit(solution)/shard_map/ppermute | solution.py:193
  78.8 37.9 %collective-permute-start.27 = (bf16[4,64,1408]{2,1,0:T(8,128)(2,1)S(1)}, bf16[4,64,1408]{2,1,0:T(8,128)(2,1)}, u32[]{:S(2)}, u32[]{:S(2)}) collective-permute-start(bf16[4,64,1408]{2,1,0:T(8,128)(2,1)S(1)} %pad_maximum_fusion.1.refs_0_), channel_id=1, source_target_pairs={{0,1},{1,0},{2,3},{3,2},{4,5},{5,4},{6,7},{7,6},{8,9},{9,8},{10,11... | collective-permute-start | bytes 2162696 | tf_op jit(solution)/shard_map/ppermute | solution.py:193
  79.1 37.7 %collective-permute-start.30 = (bf16[4,64,1408]{2,1,0:T(8,128)(2,1)}, bf16[4,64,1408]{2,1,0:T(8,128)(2,1)}, u32[]{:S(2)}, u32[]{:S(2)}) collective-permute-start(bf16[4,64,1408]{2,1,0:T(8,128)(2,1)} %collective-permute-done.26.refs_3_), channel_id=1, source_target_pairs={{0,1},{1,0},{2,3},{3,2},{4,5},{5,4},{6,7},{7,6},{8,9},{9,8},{10,11... | collective-permute-start | bytes 2162696 | tf_op jit(solution)/shard_map/ppermute | solution.py:193
  79.3 37.4 %collective-permute-start.28 = (bf16[4,64,1408]{2,1,0:T(8,128)(2,1)}, bf16[4,64,1408]{2,1,0:T(8,128)(2,1)}, u32[]{:S(2)}, u32[]{:S(2)}) collective-permute-start(bf16[4,64,1408]{2,1,0:T(8,128)(2,1)} %collective-permute-done.21.refs_1_), channel_id=1, source_target_pairs={{0,1},{1,0},{2,3},{3,2},{4,5},{5,4},{6,7},{7,6},{8,9},{9,8},{10,11... | collective-permute-start | bytes 2162696 | tf_op jit(solution)/shard_map/ppermute | solution.py:193
  86.0 5.9 %collective-permute-start.16 = (bf16[512,128]{1,0:T(8,128)(2,1)}, bf16[512,128]{1,0:T(8,128)(2,1)S(1)}, u32[]{:S(2)}, u32[]{:S(2)}) collective-permute-start(bf16[512,128]{1,0:T(8,128)(2,1)} %get-tuple-element.65.kv0), channel_id=1, source_target_pairs={{0,2},{2,0},{1,3},{3,1},{4,6},{6,4},{5,7},{7,5},{8,10},{10,8},{9,1... | collective-permute-start | bytes 393224 | tf_op jit(solution)/shard_map/ppermute | solution.py:197
  91.9 1.6 collective-permute-start.15
  93.4 1.3 collective-permute-start.17
  94.8 21.9 %collective-permute-start.1 = (bf16[256,512]{1,0:T(8,128)(2,1)S(1)}, bf16[256,512]{1,0:T(8,128)(2,1)S(1)}, u32[]{:S(2)}, u32[]{:S(2)}) collective-permute-start(bf16[256,512]{1,0:T(8,128)(2,1)S(1)} %slice.127), channel_id=1, source_target_pairs={{0,3},{3,0},{1,2},{2,1},{4,7},{7,4},{5,6},{6,5},{8,11},{11,8},{9,1... | collective-permute-start | bytes 786440 | tf_op jit(solution)/shard_map/ppermute | solution.py:201
  170.2 1.9 collective-permute-start.32
  170.6 6.6 %collective-permute-start.33 = (bf16[2,128,256]{2,1,0:T(8,128)(2,1)}, bf16[2,128,256]{2,1,0:T(8,128)(2,1)S(1)}, u32[]{:S(2)}, u32[]{:S(2)}) collective-permute-start(bf16[2,128,256]{2,1,0:T(8,128)(2,1)} %get-tuple-element.84), channel_id=1, source_target_pairs={{0,2},{2,0},{1,3},{3,1},{4,6},{6,4},{5,7},{7,5},{8,10},{10,8},{9,1... | collective-permute-start | bytes 393224 | tf_op jit(solution)/shard_map/ppermute | solution.py:197
  171.0 7.4 %collective-permute-start.34 = (bf16[2,128,256]{2,1,0:T(8,128)(2,1)}, bf16[2,128,256]{2,1,0:T(8,128)(2,1)S(1)}, u32[]{:S(2)}, u32[]{:S(2)}) collective-permute-start(bf16[2,128,256]{2,1,0:T(8,128)(2,1)} %get-tuple-element.85), channel_id=1, source_target_pairs={{0,3},{3,0},{1,2},{2,1},{4,7},{7,4},{5,6},{6,5},{8,11},{11,8},{9,1... | collective-permute-start | bytes 393224 | tf_op jit(solution)/shard_map/ppermute | solution.py:201
  179.1 12.7 %copy-start.18 = (bf16[512,512]{1,0:T(8,128)(2,1)S(1)}, bf16[512,512]{1,0:T(8,128)(2,1)}, u32[]{:S(2)}) copy-start(bf16[512,512]{1,0:T(8,128)(2,1)} %get-tuple-element.71) | copy-start | bytes 1572868
  179.1 13.3 %copy-start.34 = (bf16[2,2,2,64,1408]{4,3,2,1,0:T(8,128)(2,1)S(1)}, bf16[2,2,2,64,1408]{4,3,2,1,0:T(8,128)(2,1)}, u32[]{:S(2)}) copy-start(bf16[2,2,2,64,1408]{4,3,2,1,0:T(8,128)(2,1)} %get-tuple-element.101) | copy-start | bytes 4325380
  191.0 2.4 collective-permute-start.36
  191.6 3.5 %collective-permute-start.40 = (bf16[2,2,2,80,384]{4,3,2,1,0:T(8,128)(2,1)}, bf16[2,2,2,80,384]{4,3,2,1,0:T(8,128)(2,1)S(1)}, u32[]{:S(2)}, u32[]{:S(2)}) collective-permute-start(bf16[2,2,2,80,384]{4,3,2,1,0:T(8,128)(2,1)} %get-tuple-element.91), channel_id=1, source_target_pairs={{0,1},{1,0},{2,3},{3,2},{4,5},{5,4},{6,7},{7,6},{8,9},{9,8},{10,11... | collective-permute-start | bytes 1474568 | tf_op jit(solution)/shard_map/ppermute | solution.py:193
  191.8 8.1 %collective-permute-start.31 = (bf16[256,512]{1,0:T(8,128)(2,1)S(1)}, bf16[256,512]{1,0:T(8,128)(2,1)S(1)}, u32[]{:S(2)}, u32[]{:S(2)}) collective-permute-start(bf16[256,512]{1,0:T(8,128)(2,1)S(1)} %get-tuple-element.140), channel_id=1, source_target_pairs={{0,3},{3,0},{1,2},{2,1},{4,7},{7,4},{5,6},{6,5},{8,11},{11,8},{9,1... | collective-permute-start | bytes 786440 | tf_op jit(solution)/shard_map/ppermute | solution.py:201
  192.2 24.3 %collective-permute-start.45 = (bf16[2,2,2,64,1408]{4,3,2,1,0:T(8,128)(2,1)}, bf16[2,2,2,64,1408]{4,3,2,1,0:T(8,128)(2,1)S(1)}, u32[]{:S(2)}, u32[]{:S(2)}) collective-permute-start(bf16[2,2,2,64,1408]{4,3,2,1,0:T(8,128)(2,1)} %get-tuple-element.99), channel_id=1, source_target_pairs={{0,1},{1,0},{2,3},{3,2},{4,5},{5,4},{6,7},{7,6},{8,9},{9,8},{10,11... | collective-permute-start | bytes 4325384 | tf_op jit(solution)/shard_map/ppermute | solution.py:193
  192.3 24.8 %collective-permute-start.49 = (bf16[2,2,2,64,1408]{4,3,2,1,0:T(8,128)(2,1)S(1)}, bf16[2,2,2,64,1408]{4,3,2,1,0:T(8,128)(2,1)S(1)}, u32[]{:S(2)}, u32[]{:S(2)}) collective-permute-start(bf16[2,2,2,64,1408]{4,3,2,1,0:T(8,128)(2,1)S(1)} %copy-done.34), channel_id=1, source_target_pairs={{0,1},{1,0},{2,3},{3,2},{4,5},{5,4},{6,7},{7,6},{8,9},{9,8},{10,11... | collective-permute-start | bytes 4325384 | tf_op jit(solution)/shard_map/ppermute | solution.py:193
  193.3 12.1 %collective-permute-start.35 = (bf16[256,512]{1,0:T(8,128)(2,1)}, bf16[256,512]{1,0:T(8,128)(2,1)S(1)}, u32[]{:S(2)}, u32[]{:S(2)}) collective-permute-start(bf16[256,512]{1,0:T(8,128)(2,1)} %get-tuple-element.87), channel_id=1, source_target_pairs={{0,3},{3,0},{1,2},{2,1},{4,7},{7,4},{5,6},{6,5},{8,11},{11,8},{9,1... | collective-permute-start | bytes 786440 | tf_op jit(solution)/shard_map/ppermute | solution.py:201
  195.1 16.2 %copy-start.21 = (bf16[2,2,2,80,384]{4,3,2,1,0:T(8,128)(2,1)S(1)}, bf16[2,2,2,80,384]{4,3,2,1,0:T(8,128)(2,1)}, u32[]{:S(2)}) copy-start(bf16[2,2,2,80,384]{4,3,2,1,0:T(8,128)(2,1)} %get-tuple-element.88) | copy-start | bytes 1474564
  195.1 16.2 %collective-permute-start.37 = (bf16[2,2,80,384]{3,2,1,0:T(8,128)(2,1)S(1)}, bf16[2,2,80,384]{3,2,1,0:T(8,128)(2,1)S(1)}, u32[]{:S(2)}, u32[]{:S(2)}) collective-permute-start(bf16[2,2,80,384]{3,2,1,0:T(8,128)(2,1)S(1)} %fusion.8), channel_id=1, source_target_pairs={{0,2},{2,0},{1,3},{3,1},{4,6},{6,4},{5,7},{7,5},{8,10},{10,8},{9,1... | collective-permute-start | bytes 737288 | tf_op jit(solution)/shard_map/ppermute | solution.py:197
  199.9 13.1 %collective-permute-start.41 = (bf16[2,2,80,384]{3,2,1,0:T(8,128)(2,1)S(1)}, bf16[2,2,80,384]{3,2,1,0:T(8,128)(2,1)S(1)}, u32[]{:S(2)}, u32[]{:S(2)}) collective-permute-start(bf16[2,2,80,384]{3,2,1,0:T(8,128)(2,1)S(1)} %fusion.9), channel_id=1, source_target_pairs={{0,4},{4,0},{8,12},{12,8},{16,20},{20,16},{24,28},{28,24},{1,5},{5... | collective-permute-start | bytes 737288 | tf_op jit(solution)/shard_map/ppermute | solution.py:229
  202.2 14.3 %copy-start.5 = (bf16[2,2,2,64,1408]{4,3,2,1,0:T(8,128)(2,1)S(1)}, bf16[2,2,2,64,1408]{4,3,2,1,0:T(8,128)(2,1)}, u32[]{:S(2)}) copy-start(bf16[2,2,2,64,1408]{4,3,2,1,0:T(8,128)(2,1)} %get-tuple-element.98) | copy-start | bytes 4325380
  211.4 4.9 %collective-permute-start.38 = (bf16[2,80,384]{2,1,0:T(8,128)(2,1)S(1)}, bf16[2,80,384]{2,1,0:T(8,128)(2,1)S(1)}, u32[]{:S(2)}, u32[]{:S(2)}) collective-permute-start(bf16[2,80,384]{2,1,0:T(8,128)(2,1)S(1)} %fusion.13), channel_id=1, source_target_pairs={{0,4},{4,0},{8,12},{12,8},{16,20},{20,16},{24,28},{28,24},{1,5},{5... | collective-permute-start | bytes 368648 | tf_op jit(solution)/shard_map/ppermute | solution.py:229
  213.0 5.9 %collective-permute-start.42 = (bf16[2,80,384]{2,1,0:T(8,128)(2,1)S(1)}, bf16[2,80,384]{2,1,0:T(8,128)(2,1)S(1)}, u32[]{:S(2)}, u32[]{:S(2)}) collective-permute-start(bf16[2,80,384]{2,1,0:T(8,128)(2,1)S(1)} %fusion.10), channel_id=1, source_target_pairs={{0,2},{2,0},{1,3},{3,1},{4,6},{6,4},{5,7},{7,5},{8,10},{10,8},{9,1... | collective-permute-start | bytes 368648 | tf_op jit(solution)/shard_map/ppermute | solution.py:197
  216.4 31.1 %collective-permute-start.39 = (bf16[80,384]{1,0:T(8,128)(2,1)S(1)}, bf16[80,384]{1,0:T(8,128)(2,1)S(1)}, u32[]{:S(2)}, u32[]{:S(2)}) collective-permute-start(bf16[80,384]{1,0:T(8,128)(2,1)S(1)} %slice_bitcast_fusion.13), channel_id=1, source_target_pairs={{0,8},{4,12},{8,16},{12,20},{16,24},{20,28},{24,0},{28,4},{1,9},{5... | collective-permute-start | bytes 184328 | tf_op jit(solution)/shard_map/ppermute | solution.py:240
  216.7 16.7 %collective-permute-start.46 = (bf16[2,2,64,1408]{3,2,1,0:T(8,128)(2,1)S(1)}, bf16[2,2,64,1408]{3,2,1,0:T(8,128)(2,1)S(1)}, u32[]{:S(2)}, u32[]{:S(2)}) collective-permute-start(bf16[2,2,64,1408]{3,2,1,0:T(8,128)(2,1)S(1)} %fusion), channel_id=1, source_target_pairs={{0,2},{2,0},{1,3},{3,1},{4,6},{6,4},{5,7},{7,5},{8,10},{10,8},{9,1... | collective-permute-start | bytes 2162696 | tf_op jit(solution)/shard_map/ppermute | solution.py:197
  217.3 17.6 %collective-permute-start.50 = (bf16[2,2,64,1408]{3,2,1,0:T(8,128)(2,1)S(1)}, bf16[2,2,64,1408]{3,2,1,0:T(8,128)(2,1)S(1)}, u32[]{:S(2)}, u32[]{:S(2)}) collective-permute-start(bf16[2,2,64,1408]{3,2,1,0:T(8,128)(2,1)S(1)} %fusion.1), channel_id=1, source_target_pairs={{0,4},{4,0},{8,12},{12,8},{16,20},{20,16},{24,28},{28,24},{1,5},{5... | collective-permute-start | bytes 2162696 | tf_op jit(solution)/shard_map/ppermute | solution.py:229
  233.5 8.0 %collective-permute-start.47 = (bf16[2,64,1408]{2,1,0:T(8,128)(2,1)S(1)}, bf16[2,64,1408]{2,1,0:T(8,128)(2,1)S(1)}, u32[]{:S(2)}, u32[]{:S(2)}) collective-permute-start(bf16[2,64,1408]{2,1,0:T(8,128)(2,1)S(1)} %fusion.5), channel_id=1, source_target_pairs={{0,4},{4,0},{8,12},{12,8},{16,20},{20,16},{24,28},{28,24},{1,5},{5... | collective-permute-start | bytes 1081352 | tf_op jit(solution)/shard_map/ppermute | solution.py:229
  235.1 7.6 %collective-permute-start.51 = (bf16[2,64,1408]{2,1,0:T(8,128)(2,1)S(1)}, bf16[2,64,1408]{2,1,0:T(8,128)(2,1)S(1)}, u32[]{:S(2)}, u32[]{:S(2)}) collective-permute-start(bf16[2,64,1408]{2,1,0:T(8,128)(2,1)S(1)} %fusion.2), channel_id=1, source_target_pairs={{0,2},{2,0},{1,3},{3,1},{4,6},{6,4},{5,7},{7,5},{8,10},{10,8},{9,1... | collective-permute-start | bytes 1081352 | tf_op jit(solution)/shard_map/ppermute | solution.py:197
  241.8 23.0 %collective-permute-start.48 = (bf16[64,1408]{1,0:T(8,128)(2,1)S(1)}, bf16[64,1408]{1,0:T(8,128)(2,1)S(1)}, u32[]{:S(2)}, u32[]{:S(2)}) collective-permute-start(bf16[64,1408]{1,0:T(8,128)(2,1)S(1)} %slice_bitcast_fusion.6), channel_id=1, source_target_pairs={{0,8},{4,12},{8,16},{12,20},{16,24},{20,28},{24,0},{28,4},{1,9},{5... | collective-permute-start | bytes 540680 | tf_op jit(solution)/shard_map/ppermute | solution.py:240
  242.9 21.9 %collective-permute-start.53 = (bf16[64,1408]{1,0:T(8,128)(2,1)S(1)}, bf16[64,1408]{1,0:T(8,128)(2,1)S(1)}, u32[]{:S(2)}, u32[]{:S(2)}) collective-permute-start(bf16[64,1408]{1,0:T(8,128)(2,1)S(1)} %get-tuple-element.141), channel_id=1, source_target_pairs={{0,24},{4,28},{8,0},{12,4},{16,8},{20,12},{24,16},{28,20},{1,25},{... | collective-permute-start | bytes 540680 | tf_op jit(solution)/shard_map/ppermute | solution.py:242
  246.4 18.5 %collective-permute-start.52 = (bf16[64,1408]{1,0:T(8,128)(2,1)S(1)}, bf16[64,1408]{1,0:T(8,128)(2,1)S(1)}, u32[]{:S(2)}, u32[]{:S(2)}) collective-permute-start(bf16[64,1408]{1,0:T(8,128)(2,1)S(1)} %get-tuple-element.142), channel_id=1, source_target_pairs={{0,16},{4,20},{8,24},{12,28},{16,0},{20,4},{24,8},{28,12},{1,17},{... | collective-permute-start | bytes 540680 | tf_op jit(solution)/shard_map/ppermute | solution.py:241
  246.4 7.8 %collective-permute-start.44 = (bf16[80,384]{1,0:T(8,128)(2,1)S(1)}, bf16[80,384]{1,0:T(8,128)(2,1)S(1)}, u32[]{:S(2)}, u32[]{:S(2)}) collective-permute-start(bf16[80,384]{1,0:T(8,128)(2,1)S(1)} %get-tuple-element.143), channel_id=1, source_target_pairs={{0,24},{4,28},{8,0},{12,4},{16,8},{20,12},{24,16},{28,20},{1,25},{... | collective-permute-start | bytes 184328 | tf_op jit(solution)/shard_map/ppermute | solution.py:242
  247.5 14.9 %copy-start.30 = (bf16[80,384]{1,0:T(8,128)(2,1)}, bf16[80,384]{1,0:T(8,128)(2,1)S(1)}, u32[]{:S(2)}) copy-start(bf16[80,384]{1,0:T(8,128)(2,1)S(1)} %collective-permute-done.39.one) | copy-start | bytes 184324
  247.5 14.9 %collective-permute-start.43 = (bf16[80,384]{1,0:T(8,128)(2,1)S(1)}, bf16[80,384]{1,0:T(8,128)(2,1)S(1)}, u32[]{:S(2)}, u32[]{:S(2)}) collective-permute-start(bf16[80,384]{1,0:T(8,128)(2,1)S(1)} %get-tuple-element.144), channel_id=1, source_target_pairs={{0,16},{4,20},{8,24},{12,28},{16,0},{20,4},{24,8},{28,12},{1,17},{... | collective-permute-start | bytes 184328 | tf_op jit(solution)/shard_map/ppermute | solution.py:241
  (25 other events, 129.1 us)

commit v2 on v1

--- a/solution.py
+++ b/solution.py
@@ -63,13 +63,23 @@
     return pltpu.CompilerParams(vmem_limit_bytes=VMEM_MAX)
 
 
+def cost(microseconds):
+    return pl.CostEstimate(flops=0, bytes_accessed=int(microseconds * 3.69e5), transcendentals=0)
+
+
+def after(value, *earlier):
+    return lax.optimization_barrier((value, *earlier))[0]
+
+
 def shaped(shape, kind):
     return jax.ShapeDtypeStruct(shape, kind)
 
 
 def pack_kernel(
-    wq, wo, wup, wdown, wk, wv, wr, g1, b1, g2, b2, bdown, bup, first_ref, second_ref, wide, square
+    wq, wo, wup, wdown, wk, wv, wr, tok, cot, g1, b1, g2, b2, bdown, bup, first_ref, second_ref, cross_ref, wide, square
 ):
+    cross_ref[0:HALF, :] = tok[HALF:, :]
+    cross_ref[HALF:, :] = cot[HALF:, :]
     experts = wq.shape[0]
     group = experts * HEAD
     hidden = wup.shape[1]
@@ -88,26 +98,27 @@
     wide[...] = jnp.zeros_like(wide)
     for j in range(experts):
         wide[j * HEAD : (j + 1) * HEAD, 0:ROWS] = wo[j].astype(F32)
-    second_ref[:, 0:group] = wide[0:group, :].T[0:ROWS].astype(BF16)
+    second_ref[:, 0:group] = wide[...].T[0:ROWS].astype(BF16)
     second_ref[:, group : group + hidden] = wup[...]
-    wide[0:hidden, 0:ROWS] = wdown[...].astype(F32)
-    second_ref[:, group + hidden :] = wide[0:hidden, :].T[0:ROWS].astype(BF16)
-
-
-def pack(wq, wo, wup, wdown, wk, wv, wr, vectors, bup):
+    second_ref[:, group + hidden :] = wdown[...]
+
+
+def pack(wq, wo, wup, wdown, wk, wv, wr, tok, cot, vectors, bup):
     group, hidden = wq.shape[0] * HEAD, wup.shape[1]
     return pl.pallas_call(
         pack_kernel,
+        cost_estimate=cost(2),
         out_shape=(
             shaped((ROWS + TINY, group), BF16),
             shaped((ROWS, group + 2 * hidden), BF16),
+            shaped(tok.shape, BF16),
         ),
         scratch_shapes=[
-            pltpu.VMEM((max(group, hidden), LANES), F32),
+            pltpu.VMEM((group, LANES), F32),
             pltpu.VMEM((LANES, LANES), F32),
         ],
         compiler_params=params(),
-    )(wq, wo, wup, wdown, wk, wv, wr, *[v.reshape(1, -1) for v in vectors], bup.reshape(1, -1))
+    )(wq, wo, wup, wdown, wk, wv, wr, tok, cot, *[v.reshape(1, -1) for v in vectors], bup.reshape(1, -1))
 
 
 def sum_four(kept, one, two, three):
@@ -132,6 +143,7 @@
 def unpack_first(kept, one, two, three, experts, routed):
     outs = pl.pallas_call(
         unpack_first_kernel,
+        cost_estimate=cost(2),
         out_shape=(
             shaped((experts, ROWS, HEAD), F32),
             shaped((TINY, HEAD), F32),
@@ -152,26 +164,26 @@
     total[...] = sum_four(kept[0], one[...], two[...], three[...])
     gup[...] = total[:, group : group + hidden]
     wide[...] = jnp.zeros_like(wide)
-    wide[0:ROWS, 0:group] = total[:, 0:group]
-    turned = wide[:, 0:group].T
+    wide[0:ROWS, :] = total[:, 0:group]
+    turned = wide[...].T
     for j in range(experts):
         go[j] = turned[j * HEAD : (j + 1) * HEAD, 0:ROWS]
-    wide[0:ROWS, 0:hidden] = total[:, group + hidden :]
-    gdown[...] = wide[:, 0:hidden].T[:, 0:ROWS]
+    gdown[...] = total[:, group + hidden :]
 
 
 def unpack_second(kept, one, two, three, experts, hidden):
     group = experts * HEAD
     return pl.pallas_call(
         unpack_second_kernel,
+        cost_estimate=cost(2),
         out_shape=(
             shaped((experts, HEAD, ROWS), F32),
             shaped((ROWS, hidden), F32),
-            shaped((hidden, ROWS), F32),
+            shaped((ROWS, hidden), F32),
         ),
         scratch_shapes=[
             pltpu.VMEM(kept.shape[1:], F32),
-            pltpu.VMEM((LANES, max(group, hidden)), F32),
+            pltpu.VMEM((LANES, group), F32),
         ],
         compiler_params=params(),
     )(kept, one, two, three)
@@ -201,46 +213,11 @@
     return lax.ppermute(x, "tensor", CROSSED)
 
 
-def gather_blocks(own, dp):
-    turns, swap = axis_moves(dp)
-
-    def over_x(x):
-        return lax.ppermute(x, "dp", swap)
-
-    own = own[None]
-    one, two, three = [lax.ppermute(own, "dp", turn) for turn in turns]
-    first = jnp.concatenate([own, one, over_y(own), over_y(one)], axis=0)
-    second = jnp.concatenate([two, three, over_x(two), over_x(three)], axis=0)
-    mine = [first, over_x(first), second, over_y(second)]
-    return mine + [over_core(x) for x in mine]
-
-
 def add_low(*terms):
     total = terms[0].astype(F32)
     for term in terms[1:]:
         total = total + term.astype(F32)
     return total.astype(BF16)
-
-
-def reduce_blocks(keep_a, keep_b, send_a, send_b, dp):
-    turns, swap = axis_moves(dp)
-
-    def over_x(x):
-        return lax.ppermute(x, "dp", swap)
-
-    got_a, got_b = over_core(send_a), over_core(send_b)
-    next_a = over_y(add_low(keep_a[1], got_a[1]))
-    next_b = over_x(add_low(keep_b[1], got_b[1]))
-    last_a = over_x(add_low(keep_a[0, 1], got_a[0, 1], next_a[1]))
-    last_b = over_y(add_low(keep_b[0, 1], got_b[0, 1], next_b[1]))
-    done_a = add_low(keep_a[0, 0], got_a[0, 0], next_a[0], last_a)
-    done_b = add_low(keep_b[0, 0], got_b[0, 0], next_b[0], last_b)
-    return (
-        done_a,
-        lax.ppermute(done_a[1], "dp", turns[0]),
-        lax.ppermute(done_b[0], "dp", turns[1]),
-        lax.ppermute(done_b[1], "dp", turns[2]),
-    )
 
 
 def block_copies(table, pieces, row_from, rows, stride, target, sems):
@@ -258,12 +235,12 @@
     return copies
 
 
-def first_kernel(table, low_tok, high_tok, routes, *refs):
+def first_kernel(table, low_tok, cross, routes, *refs):
     pieces, (normed_ref, kv_ref, gates_ref, small, vectors, up_bias, sems) = refs[:8], refs[8:]
     copies = block_copies(table, pieces, ROWS, TINY, 4, small, sems)
     for copy in copies:
         copy.start()
-    tokens = jnp.concatenate([low_tok[0:HALF, :], high_tok[...]], axis=0).astype(F32)
+    tokens = jnp.concatenate([low_tok[0:HALF, :], cross[0:HALF, :]], axis=0).astype(F32)
     scaled, _ = norm_parts(tokens)
     for copy in copies:
         copy.wait()
@@ -293,10 +270,11 @@
     gates_ref[...] = gates
 
 
-def first_stage(table, tokens, tokens_high, routes, pieces):
+def first_stage(table, tokens, cross, routes, pieces):
     rows, width = tokens.shape
     return pl.pallas_call(
         first_kernel,
+        cost_estimate=cost(5),
         in_specs=[smem_spec()] + [pl.BlockSpec(memory_space=pltpu.VMEM)] * 3 + [any_spec()] * 8,
         out_shape=(
             shaped((rows, width), BF16),
@@ -308,7 +286,7 @@
         ),
         scratch_shapes=[pltpu.SemaphoreType.DMA((8, 4))],
         compiler_params=params(),
-    )(table, tokens, tokens_high, routes, *pieces)
+    )(table, tokens, cross, routes, *pieces)
 
 
 def half_routes(routes, k, at, half):
@@ -350,6 +328,7 @@
     group = pieces[0].shape[2]
     return pl.pallas_call(
         query_kernel,
+        cost_estimate=cost(8),
         in_specs=[smem_spec()] + [pl.BlockSpec(memory_space=pltpu.VMEM)] * 2 + [any_spec()] * 8,
         out_shape=(
             shaped((routes.shape[1], rows, LANES), BF16),
@@ -433,6 +412,7 @@
     spec = pl.BlockSpec((ways, HALF, LANES), lambda b: (0, b, 0))
     return pl.pallas_call(
         attend_kernel,
+        cost_estimate=cost(12),
         grid=(rows // HALF,),
         in_specs=[smem_spec(), spec] + [kv_spec] * 4,
         out_specs=(spec, spec),
@@ -509,6 +489,7 @@
     pair_spec = pl.BlockSpec((2, LANES, HALF), lambda b: (0, 0, 0))
     return pl.pallas_call(
         attend_back_kernel,
+        cost_estimate=cost(16),
         grid=(rows // HALF,),
         in_specs=[smem_spec()] + [spec] * 4 + [kv_spec] * 4,
         out_specs=(spec,) + (pair_spec,) * 4,
@@ -545,11 +526,11 @@
             out[place[0], place[1], place[2], row_to : row_to + rows, column_to : column_to + wide] = block
 
 
-def middle_kernel(table, low_tok, high_tok, low_cot, high_cot, heads, gates, routes, vectors, up_bias, *refs):
+def middle_kernel(table, low_tok, low_cot, cross, heads, gates, routes, vectors, up_bias, *refs):
     pieces = refs[:8]
-    output, grad_mid, grad_ref, inner, grad_gate, sums, bias_grad = refs[8:15]
-    blocks = refs[15:19]
-    weight, mixed, back, big, hid_scr, pre_scr, sems = refs[19:]
+    output, grad_mid, back, sums, bias_grad = refs[8:13]
+    blocks = refs[13:17]
+    weight, mixed, big, hid_scr, pre_scr, sems = refs[17:]
     ways, rows, _ = heads.shape
     width = low_tok.shape[1]
     group = mixed.shape[2]
@@ -559,7 +540,6 @@
     for copy in copies:
         copy.start()
     half = (lax.broadcasted_iota(jnp.int32, (CHUNK, LANES), 1) >= HEAD).astype(jnp.int32)
-    lane = lax.broadcasted_iota(jnp.int32, (CHUNK, LANES), 1)
 
     def expand(c, _):
         at = pl.ds(pl.multiple_of(c * CHUNK, CHUNK), CHUNK)
@@ -579,14 +559,14 @@
     lax.fori_loop(0, rows // CHUNK, expand, 0)
     for copy in copies:
         copy.wait()
-    middle = jnp.concatenate([low_tok[0:HALF, :], high_tok[...]], axis=0).astype(F32)
+    middle = jnp.concatenate([low_tok[0:HALF, :], cross[0:HALF, :]], axis=0).astype(F32)
     for slot in range(4):
         middle = middle + nt(mixed[slot], weight[slot, :, 0:group])
     scaled, inverse = norm_parts(middle)
     gain = vectors[2:3, :]
     normed = (scaled * gain + vectors[3:4, :]).astype(BF16)
     normed_t = normed.T
-    cot = jnp.concatenate([low_cot[0:HALF, :], high_cot[...]], axis=0)
+    cot = jnp.concatenate([low_cot[0:HALF, :], cross[HALF:, :]], axis=0)
     cot_t = cot.T
     result = middle + vectors[4:5, :]
     grad_normed = jnp.zeros((rows, width), F32)
@@ -622,7 +602,14 @@
     for slot in range(4):
         big[:, 0:group] = nn(grad_attn_t, mixed[slot]).astype(BF16)
         put_blocks(table, big.at[:, 0:group], blocks, slot, ROWS, 0, 0, 0)
-        back[slot] = nn(grad_attn, weight[slot, :, 0:group])
+        back[slot] = nn(grad_attn, weight[slot, :, 0:group]).astype(BF16)
+
+
+def select_kernel(table, back, heads, gates, routes, grad_ref, inner, grad_gate):
+    ways, rows, _ = heads.shape
+    experts = back.shape[2] // HEAD
+    half = (lax.broadcasted_iota(jnp.int32, (CHUNK, LANES), 1) >= HEAD).astype(jnp.int32)
+    lane = lax.broadcasted_iota(jnp.int32, (CHUNK, LANES), 1)
 
     def select(c, _):
         at = pl.ds(pl.multiple_of(c * CHUNK, CHUNK), CHUNK)
@@ -630,29 +617,42 @@
         picked = [jnp.zeros((CHUNK, LANES), F32)] * ways
         for slot in range(4):
             for pair in range(experts // 2):
-                value = back[slot, at, pair * LANES : (pair + 1) * LANES]
+                value = back[slot, at, pair * LANES : (pair + 1) * LANES].astype(F32)
                 base = experts * table[SLOT_AT + slot] + 2 * pair
                 for k in range(ways):
                     picked[k] = jnp.where(wanted[k] == base, value, picked[k])
         gate_grads = jnp.zeros((CHUNK, LANES), F32)
+        ones = jnp.ones((LANES, LANES), BF16)
         for k in range(ways):
-            head = heads[k, at, :]
-            gate_grad = jnp.sum(picked[k] * head, axis=-1, keepdims=True)
+            gate = jnp.broadcast_to(gates[at, k : k + 1], (CHUNK, LANES))
+            gate_grad = nn((picked[k] * heads[k, at, :]).astype(BF16), ones)
             gate_grads = jnp.where(lane == k, gate_grad, gate_grads)
-            low = (picked[k] * gates[at, k : k + 1]).astype(BF16)
-            grad_ref[k, at, :] = low
-            inner[k, at, :] = jnp.broadcast_to(
-                jnp.sum(low.astype(F32) * head, axis=-1, keepdims=True), (CHUNK, LANES)
-            )
+            grad_ref[k, at, :] = (picked[k] * gate).astype(BF16)
+            inner[k, at, :] = gate_grad * gate
         grad_gate[at, :] = gate_grads
         return 0
 
     lax.fori_loop(0, rows // CHUNK, select, 0)
 
 
-def middle_stage(table, tokens, tokens_high, cot, cot_high, heads, gates, routes, vectors, up_bias, pieces):
+def select_stage(table, back, heads, gates, routes):
+    ways, rows, _ = heads.shape
+    vmem = pl.BlockSpec(memory_space=pltpu.VMEM)
+    return pl.pallas_call(
+        select_kernel,
+        cost_estimate=cost(8),
+        in_specs=[smem_spec()] + [vmem] * 4,
+        out_shape=(
+            shaped((ways, rows, LANES), BF16),
+            shaped((ways, rows, LANES), F32),
+            shaped((rows, LANES), F32),
+        ),
+        compiler_params=params(),
+    )(table, back, heads, gates, routes)
+
+
+def middle_stage(table, tokens, cot, cross, heads, gates, routes, vectors, up_bias, pieces):
     rows, width = tokens.shape
-    ways = heads.shape[0]
     packed = pieces[0].shape[2]
     hidden = up_bias.shape[1]
     group = packed - 2 * hidden
@@ -660,13 +660,12 @@
     vmem = pl.BlockSpec(memory_space=pltpu.VMEM)
     return pl.pallas_call(
         middle_kernel,
-        in_specs=[smem_spec()] + [vmem] * 9 + [any_spec()] * 8,
+        cost_estimate=cost(36),
+        in_specs=[smem_spec()] + [vmem] * 8 + [any_spec()] * 8,
         out_shape=(
             shaped((rows, width), BF16),
             shaped((rows, width), F32),
-            shaped((ways, rows, LANES), BF16),
-            shaped((ways, rows, LANES), F32),
-            shaped((rows, LANES), F32),
+            shaped((4, rows, group), BF16),
             shaped((8, width), F32),
             shaped((8, hidden), F32),
             block,
@@ -677,18 +676,17 @@
         scratch_shapes=[
             pltpu.VMEM((4, width, packed), BF16),
             pltpu.VMEM((4, rows, group), BF16),
-            pltpu.VMEM((4, rows, group), F32),
             pltpu.VMEM((width, hidden), BF16),
             pltpu.VMEM((rows, hidden), BF16),
             pltpu.VMEM((rows, hidden), BF16),
             pltpu.SemaphoreType.DMA((8, 4)),
         ],
         compiler_params=params(),
-    )(table, tokens, tokens_high, cot, cot_high, heads, gates, routes, vectors, up_bias, *pieces)
+    )(table, tokens, cot, cross, heads, gates, routes, vectors, up_bias, *pieces)
 
 
 def last_kernel(
-    table, low_tok, high_tok, grad_mid, grad_query, normed, routes, gates, grad_gate, weight, small,
+    table, low_tok, cross, grad_mid, grad_query, normed, routes, gates, grad_gate, weight, small,
     vectors, sums, bias_grad, p0, p1, p2, p3, low_out, high_out, *refs
 ):
     blocks, (spread, pair_grad, big, tiny, wide, extra) = refs[:4], refs[4:]
@@ -728,7 +726,7 @@
         grad_normed = grad_normed + nt(spread[slot], weight[slot])
         big[...] = nn(normed_t, spread[slot]).astype(BF16)
         put_blocks(table, big, blocks, slot, ROWS, 0, 0, 0)
-    tokens = jnp.concatenate([low_tok[0:HALF, :], high_tok[...]], axis=0).astype(F32)
+    tokens = jnp.concatenate([low_tok[0:HALF, :], cross[0:HALF, :]], axis=0).astype(F32)
     scaled, inverse = norm_parts(tokens)
     back = grad_mid[...] + norm_backward(grad_normed, scaled, inverse, vectors[0:1, :])
     low_out[...] = back[0:HALF]
@@ -748,7 +746,7 @@
 
 
 def last_stage(
-    table, tokens, tokens_high, grad_mid, grad_query, normed, routes, gates, grad_gate, weight, small,
+    table, tokens, cross, grad_mid, grad_query, normed, routes, gates, grad_gate, weight, small,
     vectors, sums, bias_grad, pair_parts
 ):
     rows, width = tokens.shape
@@ -757,6 +755,7 @@
     vmem = pl.BlockSpec(memory_space=pltpu.VMEM)
     return pl.pallas_call(
         last_kernel,
+        cost_estimate=cost(12),
         in_specs=[smem_spec()] + [vmem] * 17,
         out_shape=(shaped((HALF, width), F32), shaped((rows - HALF, width), BF16), block, block, block, block),
         scratch_shapes=[
@@ -769,7 +768,7 @@
         ],
         compiler_params=params(),
     )(
-        table, tokens, tokens_high, grad_mid, grad_query, normed, routes, gates, grad_gate, weight, small,
+        table, tokens, cross, grad_mid, grad_query, normed, routes, gates, grad_gate, weight, small,
         vectors, sums, bias_grad, *pair_parts
     )
 
@@ -895,40 +894,105 @@
     )
     vectors_in = (ln1_gain, ln1_bias, ln2_gain, ln2_bias, b_down)
 
-    tokens_high = crossed(tokens[HALF:])
+    experts, hidden, routed = w_query.shape[0], w_up.shape[1], w_router.shape[1]
+    turns, swap = axis_moves(dp)
+
+    def over_x(x):
+        return lax.ppermute(x, "dp", swap)
+
+    def over_z(x, step):
+        return lax.ppermute(x, "dp", turns[step - 1])
+
+    def over_zx(x, step):
+        return lax.ppermute(x, "dp", [(source, target ^ 1) for source, target in turns[step - 1]])
+
     if tuned:
-        first, second = pack(w_query, w_out, w_up, w_down, w_key, w_value, w_router, vectors_in, b_up)
-        first_pieces = gather_blocks(first, dp)
-        second_pieces = gather_blocks(second, dp)
+        first, second, cross = pack(
+            w_query, w_out, w_up, w_down.T, w_key, w_value, w_router, tokens, cotangent, vectors_in, b_up
+        )
+        first, second = first[None], second[None]
+        z1, z2, z3 = [over_z(first, step) for step in (1, 2, 3)]
+        cross = crossed(cross)
+        side_a = jnp.concatenate([after(first, table, own_routes), z1], axis=0)
+        side_b = jnp.concatenate([z2, z3], axis=0)
+        next_a, next_b = over_y(side_a), over_x(side_b)
+        later_z1, later_z3 = [over_z(after(second, z1), step) for step in (1, 3)]
+        later_z2 = over_z(later_z1, 1)
+        side_a = jnp.concatenate([side_a, after(next_a, later_z1, later_z3)], axis=0)
+        side_b = jnp.concatenate([side_b, after(next_b, later_z1, later_z3)], axis=0)
+        far_a, far_b = over_x(side_a), over_y(side_b)
+        first_pieces = [side_a, after(far_a, later_z2), side_b, after(far_b, later_z2)]
+        first_pieces = first_pieces + [over_core(v) for v in first_pieces]
+        later_a = jnp.concatenate([after(second, far_a), later_z1], axis=0)
+        later_b = jnp.concatenate([after(later_z2, far_b), later_z3], axis=0)
+        next_a, next_b = over_y(later_a), over_x(later_b)
     else:
         first_pieces, second_pieces = general_pieces(
             w_query, w_out, w_up, w_down, w_key, w_value, w_router, vectors_in, b_up
         )
-    cot_high = crossed(cotangent[HALF:])
-
+        cross = crossed(jnp.concatenate([tokens[HALF:], cotangent[HALF:]], axis=0))
     normed, pair, gates, small, vectors, up_bias = first_stage(
-        table, tokens, tokens_high, own_routes, first_pieces
+        table, tokens, cross, own_routes, first_pieces
     )
     pair_y = over_y(pair)
     pairs = (pair, over_core(pair), pair_y, over_core(pair_y))
+    if tuned:
+        normed = after(normed, later_a, later_b)
     query, query_weight = query_stage(table, normed, own_routes, first_pieces)
+    if tuned:
+        side_a = jnp.concatenate([later_a, after(next_a, query, pair_y)], axis=0)
+        side_b = jnp.concatenate([later_b, after(next_b, query, pair_y)], axis=0)
+        far_a, far_b = over_x(side_a), over_y(side_b)
     heads, totals = attend_stage(table, query, pairs, seq)
-    (output, grad_mid, grad_heads, inner, grad_gate, sums, bias_grad, *later_blocks) = middle_stage(
-        table, tokens, tokens_high, cotangent, cot_high, heads, gates, own_routes, vectors, up_bias, second_pieces
-    )
+    if tuned:
+        second_pieces = [side_a, after(far_a, heads), side_b, after(far_b, heads)]
+        second_pieces = second_pieces + [over_core(v) for v in second_pieces]
+    output, grad_mid, back, sums, bias_grad, *later_blocks = middle_stage(
+        table, tokens, cotangent, cross, heads, gates, own_routes, vectors, up_bias, second_pieces
+    )
+    if tuned:
+        keep_a, keep_b, send_a, send_b = later_blocks
+        got_a, got_b = over_core(send_a), over_core(send_b)
+    output_high = crossed(output[HALF:])
+    grad_heads, inner, grad_gate = select_stage(table, back, heads, gates, own_routes)
+    if tuned:
+        part_a, part_b = add_low(keep_a[1], after(got_a, inner)[1]), add_low(keep_b[1], after(got_b, inner)[1])
+        next_a, next_b = over_y(part_a), over_x(part_b)
+        grad_heads = after(grad_heads, part_a, part_b, output_high)
     grad_query, part0, part1, part2, part3 = attend_back_stage(
         table, query, grad_heads, totals, inner, pairs, seq
     )
     pair_parts = (part0, over_core(part1), over_y(part2), crossed(part3))
+    if tuned:
+        next_a, next_b = after(next_a, *pair_parts), after(next_b, *pair_parts)
+        part_a = add_low(keep_a[0, 1], got_a[0, 1], next_a[1])
+        part_b = add_low(keep_b[0, 1], got_b[0, 1], next_b[1])
+        last_a, last_b = over_x(part_a), over_y(part_b)
+        grad_query = after(grad_query, part_a, part_b)
     low_rows, high_rows, *first_blocks = last_stage(
-        table, tokens, tokens_high, grad_mid, grad_query, normed, own_routes, gates, grad_gate,
+        table, tokens, cross, grad_mid, grad_query, normed, own_routes, gates, grad_gate,
         query_weight, small, vectors, sums, bias_grad, pair_parts,
     )
-    experts, hidden, routed = w_query.shape[0], w_up.shape[1], w_router.shape[1]
     if tuned:
-        later = reduce_blocks(*later_blocks, dp)
+        last_a, last_b = after(last_a, low_rows), after(last_b, low_rows)
+        done_a = add_low(keep_a[0, 0], got_a[0, 0], next_a[0], last_a)
+        done_b = add_low(keep_b[0, 0], got_b[0, 0], next_b[0], last_b)
+        later = (done_a, over_z(done_a[1], 1), over_z(done_b[0], 2), over_z(done_b[1], 3))
         out_grad, up_grad, down_grad = unpack_second(*later, experts, hidden)
-        early = reduce_blocks(*first_blocks, dp)
+        down_grad = down_grad.T
+
+        keep_a, keep_b, send_a, send_b = first_blocks
+        got_a, got_b = over_core(send_a), over_core(send_b)
+        got_a, got_b = after(got_a, done_a), after(got_b, done_b)
+        next_a = over_y(add_low(keep_a[1], got_a[1]))
+        next_b = over_x(add_low(keep_b[1], got_b[1]))
+        last_a = over_x(add_low(keep_a[0, 1], got_a[0, 1], next_a[1]))
+        last_b = over_y(add_low(keep_b[0, 1], got_b[0, 1], next_b[1]))
+        last_a = after(last_a, *later[1:])
+        high_rows = after(high_rows, last_a)
+        done_a = add_low(keep_a[0, 0], got_a[0, 0], next_a[0], last_a)
+        done_b = add_low(keep_b[0, 0], got_b[0, 0], next_b[0], last_b)
+        early = (done_a, over_z(done_a[1], 1), over_z(done_b[0], 2), over_z(done_b[1], 3))
         query_grad, key_grad, value_grad, router_grad, small_grads, up_bias_grad = unpack_first(
             *early, experts, routed
         )
@@ -937,7 +1001,7 @@
             query_grad, key_grad, value_grad, router_grad, small_grads, up_bias_grad,
             out_grad, up_grad, down_grad,
         ) = general_grads(first_blocks, later_blocks, experts, hidden, routed)
-    result = jnp.concatenate([output[:HALF], crossed(output[HALF:])], axis=0)
+    result = jnp.concatenate([output[:HALF], output_high], axis=0)
     grad_tokens = jnp.concatenate([low_rows, crossed(high_rows).astype(F32)], axis=0)
     return (
         result,

time: 271 us -> 205 us (0.76)
  waiting for transfers between devices: 110 us -> 49.1 us
  starting transfers between devices: 48.6 us -> 39.2 us
  other arithmetic: 4.46 us -> 13.5 us
  Pallas kernels: 95.8 us -> 89 us
    ppermute x12 -> x10, waiting for transfers between devices: 53.6 us -> 7.2 us  [over_y(): return lax.ppermute(x, 'tensor', ACROSS)]
    ppermute x10 -> x8, waiting for transfers between devices: 19.2 us -> 8.32 us  [over_x(): return lax.ppermute(x, 'dp', swap)]
    convert_element_type x12, other arithmetic: 2.39 us -> 10.8 us  [add_low(): return total.astype(BF16)]
    ppermute x10 -> x8, starting transfers between devices: 14.3 us -> 6.44 us  [over_x(): return lax.ppermute(x, 'dp', swap)]
    pallas_call x9 -> x10, Pallas kernels: 95.8 us -> 89 us  [the longest x1 21 us: middle_stage(): pl.pallas_call(middle_kernel, cost_estimate=cost(36), in_specs=[smem_spec...]
    ppermute x5 -> x4, waiting for transfers between devices: 7.86 us -> 6.28 us  [crossed(): return lax.ppermute(x, 'tensor', CROSSED)]
    ppermute x12 -> x10, starting transfers between devices: 10.3 us -> 10.9 us  [over_y(): return lax.ppermute(x, 'tensor', ACROSS)]
    unnamed x78 -> x76, local copies, waits for them, and re-layouts: 6.85 us -> 6.86 us
  transfers between devices with their start and end apart: 54 -> 49, of which waited for: 24 -> 20; matrix products, arithmetic and copies ran while one was open for 3% -> 10% of each run, Pallas kernels for 10% -> 32%
where the time goes in v2:
time: 205 us; the launch traced here: 204 us
  Pallas kernels  89 us (43%)
  waiting for transfers between devices  49.1 us (24%)
  starting transfers between devices  39.2 us (19%)
  other arithmetic  13.5 us (7%)
  local copies, waits for them, and re-layouts  12.3 us (6%)
    ppermute x12, waiting for transfers between devices, over_z(): return lax.ppermute(x, 'dp', turns[step - 1])  24 us
    pallas_call x1, Pallas kernels, middle_stage(): pl.pallas_call(middle_kernel, cost_estimate=cost(36), in_specs=[smem_spec...  21 us
    ppermute x12, starting transfers between devices, over_z(): return lax.ppermute(x, 'dp', turns[step - 1])  15.8 us
    pallas_call x1, Pallas kernels, attend_back_stage(): pl.pallas_call(attend_back_kernel, cost_estimate=cost(16), grid=(rows //...  15.7 us
    pallas_call x1, Pallas kernels, attend_stage(): pl.pallas_call(attend_kernel, cost_estimate=cost(12), grid=(rows // HALF,...  12.3 us
    pallas_call x1, Pallas kernels, last_stage(): pl.pallas_call(last_kernel, cost_estimate=cost(12), in_specs=[smem_spec()...  11.8 us
    ppermute x10, starting transfers between devices, over_y(): return lax.ppermute(x, 'tensor', ACROSS)  10.9 us
    convert_element_type x12, other arithmetic, add_low(): return total.astype(BF16)  10.8 us
  transfers between devices with their start and end apart: 49, of which 20 were waited for; matrix products, arithmetic and copies ran while one was open for 10% of the time, Pallas kernels for 32%

profile of v2, /device:TPU:0, one launch (start us, length us, event | category | flops | bytes accessed | tf_op | source)
XLA Modules:
  0.0 204.3 jit_solution(8542416634028640217)
XLA Ops:
  0.7 2.4 %shard_map.271 = (bf16[80,384]{1,0:T(8,128)(2,1)}, bf16[64,1408]{1,0:T(8,128)(2,1)}, bf16[512,512]{1,0:T(8,128)(2,1)}) custom-call(bf16[6,64,64]{2,1,0:T(8,128)(2,1)} %wq.1, bf16[6,64,64]{2,1,0:T(8,128)(2,1)} %wo.1, bf16[64,512]{1,0:T(8,128)(2,1)} %wup.1, bf16[64,512]{1,0:T(8,128)(2,1)} %bitcast.114, bf16[16,64]{1,0:T(8,128)(2,1)} %wk.1, bf16[16,64]{1,0:T(8,128)(2,1)} %wv.1, ...), custom_call_target="tpu_custom_call" | custom-call | bytes 738000 | tf_op jit(solution)/shard_map/pallas_call | solution.py:108
  3.1 5.0 %collective-permute-start.8 = (bf16[1,80,384]{2,1,0:T(8,128)(2,1)}, bf16[1,80,384]{2,1,0:T(8,128)(2,1)S(1)}, u32[]{:S(2)}, u32[]{:S(2)}) collective-permute-start(bf16[1,80,384]{2,1,0:T(8,128)(2,1)} %bitcast.106), channel_id=1, source_target_pairs={{0,24},{4,28},{8,0},{12,4},{16,8},{20,12},{24,16},{28,20},{1,25},{... | collective-permute-start | bytes 184328 | tf_op jit(solution)/shard_map/ppermute | solution.py:904
  8.1 1.0 collective-permute-start.1
  9.2 0.7 constant_dynamic-slice_fusion.1
  9.9 0.7 stack.97.table
  10.6 0.8 constant_dynamic-update-slice_fusion.2
  11.4 3.0 %collective-permute-done.1 = bf16[1,80,384]{2,1,0:T(8,128)(2,1)S(1)} collective-permute-done((bf16[1,80,384]{2,1,0:T(8,128)(2,1)}, bf16[1,80,384]{2,1,0:T(8,128)(2,1)S(1)}, u32[]{:S(2)}, u32[]{:S(2)}) %collective-permute-start.1) | collective-permute-done | bytes 61472 | tf_op jit(solution)/shard_map/ppermute | solution.py:904
  14.5 1.1 collective-permute-start.4
  15.6 0.9 collective-permute-start.3
  16.5 1.6 collective-permute-start.9
  18.1 0.8 pad_maximum_fusion.2
  18.9 1.6 collective-permute-start.2
  20.6 0.9 collective-permute-done.9
  21.5 4.3 %collective-permute-done.3 = bf16[1,64,1408]{2,1,0:T(8,128)(2,1)S(1)} collective-permute-done((bf16[1,64,1408]{2,1,0:T(8,128)(2,1)}, bf16[1,64,1408]{2,1,0:T(8,128)(2,1)S(1)}, u32[]{:S(2)}, u32[]{:S(2)}) %collective-permute-start.3) | collective-permute-done | bytes 180256 | tf_op jit(solution)/shard_map/ppermute | solution.py:904
  25.8 1.6 collective-permute-start.5
  27.4 1.6 collective-permute-start.10
  29.6 2.7 %collective-permute-done.5.refs_1_ = bf16[4,80,384]{2,1,0:T(8,128)(2,1)S(1)} collective-permute-done((bf16[4,80,384]{2,1,0:T(8,128)(2,1)S(1)}, bf16[4,80,384]{2,1,0:T(8,128)(2,1)S(1)}, u32[]{:S(2)}, u32[]{:S(2)}) %collective-permute-start.5) | collective-permute-done | bytes 245792 | tf_op jit(solution)/shard_map/ppermute | solution.py:901
  32.4 3.9 %collective-permute-done.6 = bf16[1,64,1408]{2,1,0:T(8,128)(2,1)S(1)} collective-permute-done((bf16[1,64,1408]{2,1,0:T(8,128)(2,1)S(1)}, bf16[1,64,1408]{2,1,0:T(8,128)(2,1)S(1)}, u32[]{:S(2)}, u32[]{:S(2)}) %collective-permute-start.6) | collective-permute-done | bytes 180256 | tf_op jit(solution)/shard_map/ppermute | solution.py:904
  36.8 0.7 constant_dynamic-update-slice_fusion.12
  37.5 0.7 constant_dynamic-update-slice_fusion.15
  39.5 0.7 constant_dynamic-update-slice_fusion.11
  40.2 0.9 collective-permute-start.18
  41.1 0.8 copy.33.routes
  41.9 4.4 %collective-permute-done.cross = bf16[512,512]{1,0:T(8,128)(2,1)S(1)} collective-permute-done((bf16[512,512]{1,0:T(8,128)(2,1)}, bf16[512,512]{1,0:T(8,128)(2,1)S(1)}, u32[]{:S(2)}, u32[]{:S(2)}) %collective-permute-start) | collective-permute-done | bytes 524320 | tf_op jit(solution)/shard_map/ppermute | solution.py:213
  46.4 0.7 copy-done
  47.1 4.8 %shard_map.272 = (bf16[512,512]{1,0:T(8,128)(2,1)}, bf16[512,128]{1,0:T(8,128)(2,1)}, f32[512,128]{1,0:T(8,128)}, bf16[512,384]{1,0:T(8,128)(2,1)}, f32[8,512]{1,0:T(8,128)}, /*index=5*/f32[8,512]{1,0:T(8,128)}) custom-call(s32[28]{0:T(128)} %stack.97.table, bf16[512,512]{1,0:T(8,128)(2,1)} %low_tok.5, bf16[512,512]{1,0:T(8,128)(2,1)} %copy-done, ...), custom_call_target="tpu_custom_call" | custom-call | bytes 1845000 | tf_op jit(solution)/shard_map/pallas_call | solution.py:275
  52.0 8.3 %shard_map.273 = (bf16[8,512,128]{2,1,0:T(8,128)(2,1)}, bf16[4,512,384]{2,1,0:T(8,128)(2,1)}) custom-call(s32[28]{0:T(128)} %stack.97.table, bf16[512,512]{1,0:T(8,128)(2,1)} %get-tuple-element.101.normed, s32[512,8]{1,0:T(8,128)} %copy.33.routes, bf16[4,80,384]{2,1,0:T(8,128)(2,1)} %copy-done.4, bf16[4,80,384]{2,1,0:T(8,128)(2,1)} %copy-done.8, ...), custom_call_target="tpu_custom_call" | custom-call | bytes 2952000 | tf_op jit(solution)/shard_map/pallas_call | solution.py:329
  60.4 1.1 constant_dynamic-update-slice_fusion.13.refs_2_
  61.4 2.1 %collective-permute-start.21 = (bf16[4,64,1408]{2,1,0:T(8,128)(2,1)S(1)}, bf16[4,64,1408]{2,1,0:T(8,128)(2,1)S(1)}, u32[]{:S(2)}, u32[]{:S(2)}) collective-permute-start(bf16[4,64,1408]{2,1,0:T(8,128)(2,1)S(1)} %constant_dynamic-update-slice_fusion.13.refs_2_), channel_id=1, source_target_pairs={{0,2},{2,0},{1,3},{3,1},{4,6},{6,4},{5,7},{7,5},{8,10},{10,8},{9,1... | collective-permute-start | bytes 2162696 | tf_op jit(solution)/shard_map/ppermute | solution.py:209
  63.5 1.0 constant_dynamic-update-slice_fusion.10.refs_0_
  66.8 12.3 %shard_map.274 = (f32[8,512,128]{2,1,0:T(8,128)}, f32[8,512,128]{2,1,0:T(8,128)}) custom-call(s32[28]{0:T(128)} %stack.97.table, bf16[8,512,128]{2,1,0:T(8,128)(2,1)} %get-tuple-element.102.query, bf16[512,128]{1,0:T(8,128)(2,1)} %get-tuple-element.103.kv0, bf16[512,128]{1,0:T(8,128)(2,1)} %copy-done.20, bf16[512,128]{1,0:T(8,128)(2,1)} %copy-done.19, ...), custom_call_target="tpu_custom_call" | custom-call | bytes 4428000 | tf_op jit(solution)/shard_map/pallas_call | solution.py:413
  79.7 3.5 %collective-permute-done.19.refs_1_ = bf16[4,64,1408]{2,1,0:T(8,128)(2,1)S(1)} collective-permute-done((bf16[4,64,1408]{2,1,0:T(8,128)(2,1)S(1)}, bf16[4,64,1408]{2,1,0:T(8,128)(2,1)S(1)}, u32[]{:S(2)}, u32[]{:S(2)}) %collective-permute-start.19) | collective-permute-done | bytes 720928 | tf_op jit(solution)/shard_map/ppermute | solution.py:901
  83.6 1.7 collective-permute-done.23.refs_5_
  85.3 1.0 collective-permute-done.25.refs_7_
  86.4 0.9 copy-done.17
  87.3 21.0 %shard_map.275 = (bf16[512,512]{1,0:T(8,128)(2,1)}, f32[512,512]{1,0:T(8,128)}, bf16[4,512,384]{2,1,0:T(8,128)(2,1)}, f32[8,512]{1,0:T(8,128)}, f32[8,512]{1,0:T...) custom-call(s32[28]{0:T(128)} %stack.97.table, ...), custom_call_target="tpu_custom_call" | custom-call | bytes 13284000 | tf_op jit(solution)/shard_map/pallas_call | solution.py:661
  108.8 1.1 fusion.16
  110.0 8.8 %shard_map.276 = (bf16[8,512,128]{2,1,0:T(8,128)(2,1)}, f32[8,512,128]{2,1,0:T(8,128)}, f32[512,128]{1,0:T(8,128)}) custom-call(s32[28]{0:T(128)} %stack.97.table, bf16[4,512,384]{2,1,0:T(8,128)(2,1)} %get-tuple-element.114.back, f32[8,512,128]{2,1,0:T(8,128)} %get-tuple-element.104.heads, f32[512,128]{1,0:T(8,128)} %get-tuple-element.105.gates, ...), custom_call_target="tpu_custom_call" | custom-call | bytes 2952000 | tf_op jit(solution)/shard_map/pallas_call | solution.py:641
  118.8 2.3 %fusion = bf16[2,2,64,1408]{3,2,1,0:T(8,128)(2,1)} fusion(bf16[2,2,2,64,1408]{4,3,2,1,0:T(8,128)(2,1)} %collective-permute-done.27, bf16[2,2,2,64,1408]{4,3,2,1,0:T(8,128)(2,1)S(1)} %copy-done.3), kind=kLoop, calls=%fused_computation.3 | loop fusion | flops 1441792 | bytes 2162688 | tf_op jit(solution)/shard_map/convert_element_type | solution.py:220
  121.1 1.7 collective-permute-start.29
  122.8 2.1 %fusion.1 = bf16[2,2,64,1408]{3,2,1,0:T(8,128)(2,1)} fusion(bf16[2,2,2,64,1408]{4,3,2,1,0:T(8,128)(2,1)} %collective-permute-done.28, bf16[2,2,2,64,1408]{4,3,2,1,0:T(8,128)(2,1)S(1)} %copy-done.2), kind=kLoop, calls=%fused_computation.4 | loop fusion | flops 1441792 | bytes 2162688 | tf_op jit(solution)/shard_map/convert_element_type | solution.py:220
  125.2 15.7 %shard_map.277 = (bf16[8,512,128]{2,1,0:T(8,128)(2,1)}, bf16[2,128,256]{2,1,0:T(8,128)(2,1)}, bf16[2,128,256]{2,1,0:T(8,128)(2,1)}, bf16[2,128,256]{2,1,0:T(8,128)(2,1)}, bf16[2,128,256]{2,1,0:T(8,128)(2,1)}) custom-call(s32[28]{0:T(128)} %stack.97.table, bf16[8,512,128]{2,1,0:T(8,128)(2,1)} %get-tuple-element.102.query, ...), custom_call_target="tpu_custom_call" | custom-call | bytes 5904000 | tf_op jit(solution)/shard_map/pallas_call | solution.py:490
  141.4 1.5 collective-permute-start.32
  142.9 4.7 %collective-permute-done.31.p2 = bf16[2,128,256]{2,1,0:T(8,128)(2,1)S(1)} collective-permute-done((bf16[2,128,256]{2,1,0:T(8,128)(2,1)}, bf16[2,128,256]{2,1,0:T(8,128)(2,1)S(1)}, u32[]{:S(2)}, u32[]{:S(2)}) %collective-permute-start.31) | collective-permute-done | bytes 131104 | tf_op jit(solution)/shard_map/ppermute | solution.py:209
  147.6 1.9 collective-permute-done.32.p3
  150.2 1.2 fusion.7
  151.4 1.8 collective-permute-start.35
  153.2 2.0 fusion.6
  155.5 11.8 %shard_map.278 = (f32[256,512]{1,0:T(8,128)}, bf16[256,512]{1,0:T(8,128)(2,1)}, bf16[2,2,2,80,384]{4,3,2,1,0:T(8,128)(2,1)}, bf16[2,2,2,80,384]{4,3,2,1,0:T(8,12...) custom-call(s32[28]{0:T(128)} %stack.97.table, bf16[512,512]{1,0:T(8,128)(2,1)} %low_tok.5, ...), custom_call_target="tpu_custom_call" | custom-call | bytes 4428000 | tf_op jit(solution)/shard_map/pallas_call | solution.py:756
  167.9 1.3 fusion.5.kept
  169.2 1.5 fusion.3
  170.9 1.7 collective-permute-start.36
  173.1 3.8 %collective-permute-start.41 = (bf16[64,1408]{1,0:T(8,128)(2,1)S(1)}, bf16[64,1408]{1,0:T(8,128)(2,1)S(1)}, u32[]{:S(2)}, u32[]{:S(2)}) collective-permute-start(bf16[64,1408]{1,0:T(8,128)(2,1)S(1)} %get-tuple-element.165), channel_id=1, source_target_pairs={{0,24},{4,28},{8,0},{12,4},{16,8},{20,12},{24,16},{28,20},{1,25},{... | collective-permute-start | bytes 540680 | tf_op jit(solution)/shard_map/ppermute | solution.py:904
  176.9 1.9 collective-permute-done.36
  179.2 1.2 collective-permute-done.45
  181.0 1.3 collective-permute-done.38.one
  182.4 1.7 collective-permute-done.41.three
  184.1 6.8 %collective-permute-done.40.two = bf16[64,1408]{1,0:T(8,128)(2,1)S(1)} collective-permute-done((bf16[64,1408]{1,0:T(8,128)(2,1)S(1)}, bf16[64,1408]{1,0:T(8,128)(2,1)S(1)}, u32[]{:S(2)}, u32[]{:S(2)}) %collective-permute-start.40) | collective-permute-done | bytes 180256 | tf_op jit(solution)/shard_map/ppermute | solution.py:904
  191.3 3.8 %collective-permute-start.48 = (bf16[80,384]{1,0:T(8,128)(2,1)S(1)}, bf16[80,384]{1,0:T(8,128)(2,1)S(1)}, u32[]{:S(2)}, u32[]{:S(2)}) collective-permute-start(bf16[80,384]{1,0:T(8,128)(2,1)S(1)} %get-tuple-element.175), channel_id=1, source_target_pairs={{0,24},{4,28},{8,0},{12,4},{16,8},{20,12},{24,16},{28,20},{1,25},{... | collective-permute-start | bytes 184328 | tf_op jit(solution)/shard_map/ppermute | solution.py:904
  195.1 0.8 pad_maximum_fusion.1
  195.9 2.0 %shard_map.280 = (f32[6,64,64]{2,1,0:T(8,128)}, f32[64,512]{1,0:T(8,128)}, f32[64,512]{1,0:T(8,128)}) custom-call(bf16[2,64,1408]{2,1,0:T(8,128)(2,1)} %copy-done.1, bf16[64,1408]{1,0:T(8,128)(2,1)} %copy-done.24, bf16[64,1408]{1,0:T(8,128)(2,1)} %copy-done.26, bf16[64,1408]{1,0:T(8,128)(2,1)} %copy-done.25), custom_call_target="tpu_custom_call" | custom-call | bytes 738000 | tf_op jit(solution)/shard_map/pallas_call | solution.py:176
  198.0 2.8 %collective-permute-done.47.two = bf16[80,384]{1,0:T(8,128)(2,1)S(1)} collective-permute-done((bf16[80,384]{1,0:T(8,128)(2,1)S(1)}, bf16[80,384]{1,0:T(8,128)(2,1)S(1)}, u32[]{:S(2)}, u32[]{:S(2)}) %collective-permute-start.47) | collective-permute-done | bytes 61472 | tf_op jit(solution)/shard_map/ppermute | solution.py:904
  201.4 1.7 shard_map.279
  203.2 1.0 pad_maximum_fusion
  (150 shorter events, 11.5 us)
Async XLA Ops:
  3.1 33.7 %copy-start.27 = (bf16[64,1408]{1,0:T(8,128)(2,1)S(1)}, bf16[64,1408]{1,0:T(8,128)(2,1)}, u32[]{:S(2)}) copy-start(bf16[64,1408]{1,0:T(8,128)(2,1)} %get-tuple-element.92) | copy-start | bytes 540676
  3.1 13.4 %collective-permute-start.8 = (bf16[1,80,384]{2,1,0:T(8,128)(2,1)}, bf16[1,80,384]{2,1,0:T(8,128)(2,1)S(1)}, u32[]{:S(2)}, u32[]{:S(2)}) collective-permute-start(bf16[1,80,384]{2,1,0:T(8,128)(2,1)} %bitcast.106), channel_id=1, source_target_pairs={{0,24},{4,28},{8,0},{12,4},{16,8},{20,12},{24,16},{28,20},{1,25},{... | collective-permute-start | bytes 184328 | tf_op jit(solution)/shard_map/ppermute | solution.py:904
  8.1 8.4 %collective-permute-start.7 = (bf16[1,80,384]{2,1,0:T(8,128)(2,1)}, bf16[1,80,384]{2,1,0:T(8,128)(2,1)S(1)}, u32[]{:S(2)}, u32[]{:S(2)}) collective-permute-start(bf16[1,80,384]{2,1,0:T(8,128)(2,1)} %bitcast.107), channel_id=1, source_target_pairs={{0,16},{4,20},{8,24},{12,28},{16,0},{20,4},{24,8},{28,12},{1,17},{... | collective-permute-start | bytes 184328 | tf_op jit(solution)/shard_map/ppermute | solution.py:904
  8.1 6.3 %collective-permute-start.1 = (bf16[1,80,384]{2,1,0:T(8,128)(2,1)}, bf16[1,80,384]{2,1,0:T(8,128)(2,1)S(1)}, u32[]{:S(2)}, u32[]{:S(2)}) collective-permute-start(bf16[1,80,384]{2,1,0:T(8,128)(2,1)} %bitcast.108), channel_id=1, source_target_pairs={{0,8},{4,12},{8,16},{12,20},{16,24},{20,28},{24,0},{28,4},{1,9},{5... | collective-permute-start | bytes 184328 | tf_op jit(solution)/shard_map/ppermute | solution.py:904
  14.5 7.0 %collective-permute-start.4 = (bf16[1,64,1408]{2,1,0:T(8,128)(2,1)}, bf16[1,64,1408]{2,1,0:T(8,128)(2,1)S(1)}, u32[]{:S(2)}, u32[]{:S(2)}) collective-permute-start(bf16[1,64,1408]{2,1,0:T(8,128)(2,1)} %bitcast.111), channel_id=1, source_target_pairs={{0,24},{4,28},{8,0},{12,4},{16,8},{20,12},{24,16},{28,20},{1,25},{... | collective-permute-start | bytes 540680 | tf_op jit(solution)/shard_map/ppermute | solution.py:904
  15.6 10.2 %collective-permute-start.3 = (bf16[1,64,1408]{2,1,0:T(8,128)(2,1)}, bf16[1,64,1408]{2,1,0:T(8,128)(2,1)S(1)}, u32[]{:S(2)}, u32[]{:S(2)}) collective-permute-start(bf16[1,64,1408]{2,1,0:T(8,128)(2,1)} %bitcast.112), channel_id=1, source_target_pairs={{0,8},{4,12},{8,16},{12,20},{16,24},{20,28},{24,0},{28,4},{1,9},{5... | collective-permute-start | bytes 540680 | tf_op jit(solution)/shard_map/ppermute | solution.py:904
  16.5 4.9 %collective-permute-start.9 = (bf16[2,80,384]{2,1,0:T(8,128)(2,1)S(1)}, bf16[2,80,384]{2,1,0:T(8,128)(2,1)S(1)}, u32[]{:S(2)}, u32[]{:S(2)}) collective-permute-start(bf16[2,80,384]{2,1,0:T(8,128)(2,1)S(1)} %pad_maximum_fusion.3), channel_id=1, source_target_pairs={{0,4},{4,0},{8,12},{12,8},{16,20},{20,16},{24,28},{28,24},{1,5},{5... | collective-permute-start | bytes 368648 | tf_op jit(solution)/shard_map/ppermute | solution.py:901
  18.9 6.9 %collective-permute-start.2 = (bf16[2,80,384]{2,1,0:T(8,128)(2,1)S(1)}, bf16[2,80,384]{2,1,0:T(8,128)(2,1)S(1)}, u32[]{:S(2)}, u32[]{:S(2)}) collective-permute-start(bf16[2,80,384]{2,1,0:T(8,128)(2,1)S(1)} %pad_maximum_fusion.2), channel_id=1, source_target_pairs={{0,2},{2,0},{1,3},{3,1},{4,6},{6,4},{5,7},{7,5},{8,10},{10,8},{9,1... | collective-permute-start | bytes 368648 | tf_op jit(solution)/shard_map/ppermute | solution.py:209
  25.8 20.5 %copy-start.4 = (bf16[4,80,384]{2,1,0:T(8,128)(2,1)}, bf16[4,80,384]{2,1,0:T(8,128)(2,1)S(1)}, u32[]{:S(2)}) copy-start(bf16[4,80,384]{2,1,0:T(8,128)(2,1)S(1)} %constant_dynamic-update-slice_fusion.refs_0_) | copy-start | bytes 737284
  25.8 6.5 %collective-permute-start.5 = (bf16[4,80,384]{2,1,0:T(8,128)(2,1)S(1)}, bf16[4,80,384]{2,1,0:T(8,128)(2,1)S(1)}, u32[]{:S(2)}, u32[]{:S(2)}) collective-permute-start(bf16[4,80,384]{2,1,0:T(8,128)(2,1)S(1)} %constant_dynamic-update-slice_fusion.refs_0_), channel_id=1, source_target_pairs={{0,4},{4,0},{8,12},{12,8},{16,20},{20,16},{24,28},{28,24},{1,5},{5... | collective-permute-start | bytes 737288 | tf_op jit(solution)/shard_map/ppermute | solution.py:901
  27.4 18.9 %copy-start.5 = (bf16[4,80,384]{2,1,0:T(8,128)(2,1)}, bf16[4,80,384]{2,1,0:T(8,128)(2,1)S(1)}, u32[]{:S(2)}) copy-start(bf16[4,80,384]{2,1,0:T(8,128)(2,1)S(1)} %constant_dynamic-update-slice_fusion.3.refs_2_) | copy-start | bytes 737284
  27.4 8.9 %collective-permute-start.10 = (bf16[4,80,384]{2,1,0:T(8,128)(2,1)S(1)}, bf16[4,80,384]{2,1,0:T(8,128)(2,1)S(1)}, u32[]{:S(2)}, u32[]{:S(2)}) collective-permute-start(bf16[4,80,384]{2,1,0:T(8,128)(2,1)S(1)} %constant_dynamic-update-slice_fusion.3.refs_2_), channel_id=1, source_target_pairs={{0,2},{2,0},{1,3},{3,1},{4,6},{6,4},{5,7},{7,5},{8,10},{10,8},{9,1... | collective-permute-start | bytes 737288 | tf_op jit(solution)/shard_map/ppermute | solution.py:209
  29.0 7.3 %collective-permute-start.6 = (bf16[1,64,1408]{2,1,0:T(8,128)(2,1)S(1)}, bf16[1,64,1408]{2,1,0:T(8,128)(2,1)S(1)}, u32[]{:S(2)}, u32[]{:S(2)}) collective-permute-start(bf16[1,64,1408]{2,1,0:T(8,128)(2,1)S(1)} %collective-permute-done.3), channel_id=1, source_target_pairs={{0,8},{4,12},{8,16},{12,20},{16,24},{20,28},{24,0},{28,4},{1,9},{5... | collective-permute-start | bytes 540680 | tf_op jit(solution)/shard_map/ppermute | solution.py:904
  29.0 17.3 %collective-permute-start = (bf16[512,512]{1,0:T(8,128)(2,1)}, bf16[512,512]{1,0:T(8,128)(2,1)S(1)}, u32[]{:S(2)}, u32[]{:S(2)}) collective-permute-start(bf16[512,512]{1,0:T(8,128)(2,1)} %get-tuple-element.89), channel_id=1, source_target_pairs={{0,3},{3,0},{1,2},{2,1},{4,7},{7,4},{5,6},{6,5},{8,11},{11,8},{9,1... | collective-permute-start | bytes 1572872 | tf_op jit(solution)/shard_map/ppermute | solution.py:213
  29.0 9.9 %collective-permute-start.11 = (bf16[4,80,384]{2,1,0:T(8,128)(2,1)S(1)}, bf16[4,80,384]{2,1,0:T(8,128)(2,1)S(1)}, u32[]{:S(2)}, u32[]{:S(2)}) collective-permute-start(bf16[4,80,384]{2,1,0:T(8,128)(2,1)S(1)} %constant_dynamic-update-slice_fusion.refs_0_), channel_id=1, source_target_pairs={{0,1},{1,0},{2,3},{3,2},{4,5},{5,4},{6,7},{7,6},{8,9},{9,8},{10,11... | collective-permute-start | bytes 737288 | tf_op jit(solution)/shard_map/ppermute | solution.py:205
  32.4 14.0 %copy-start.8 = (bf16[4,80,384]{2,1,0:T(8,128)(2,1)}, bf16[4,80,384]{2,1,0:T(8,128)(2,1)S(1)}, u32[]{:S(2)}) copy-start(bf16[4,80,384]{2,1,0:T(8,128)(2,1)S(1)} %collective-permute-done.5.refs_1_) | copy-start | bytes 737284
  32.4 7.8 %collective-permute-start.13 = (bf16[4,80,384]{2,1,0:T(8,128)(2,1)S(1)}, bf16[4,80,384]{2,1,0:T(8,128)(2,1)S(1)}, u32[]{:S(2)}, u32[]{:S(2)}) collective-permute-start(bf16[4,80,384]{2,1,0:T(8,128)(2,1)S(1)} %constant_dynamic-update-slice_fusion.3.refs_2_), channel_id=1, source_target_pairs={{0,1},{1,0},{2,3},{3,2},{4,5},{5,4},{6,7},{7,6},{8,9},{9,8},{10,11... | collective-permute-start | bytes 737288 | tf_op jit(solution)/shard_map/ppermute | solution.py:205
  36.3 10.0 %collective-permute-start.12 = (bf16[4,80,384]{2,1,0:T(8,128)(2,1)S(1)}, bf16[4,80,384]{2,1,0:T(8,128)(2,1)}, u32[]{:S(2)}, u32[]{:S(2)}) collective-permute-start(bf16[4,80,384]{2,1,0:T(8,128)(2,1)S(1)} %collective-permute-done.5.refs_1_), channel_id=1, source_target_pairs={{0,1},{1,0},{2,3},{3,2},{4,5},{5,4},{6,7},{7,6},{8,9},{9,8},{10,11... | collective-permute-start | bytes 737288 | tf_op jit(solution)/shard_map/ppermute | solution.py:205
  36.3 10.1 %copy-start.9 = (bf16[4,80,384]{2,1,0:T(8,128)(2,1)}, bf16[4,80,384]{2,1,0:T(8,128)(2,1)S(1)}, u32[]{:S(2)}) copy-start(bf16[4,80,384]{2,1,0:T(8,128)(2,1)S(1)} %collective-permute-done.10.refs_3_) | copy-start | bytes 737284
  36.3 10.0 %collective-permute-start.14 = (bf16[4,80,384]{2,1,0:T(8,128)(2,1)S(1)}, bf16[4,80,384]{2,1,0:T(8,128)(2,1)}, u32[]{:S(2)}, u32[]{:S(2)}) collective-permute-start(bf16[4,80,384]{2,1,0:T(8,128)(2,1)S(1)} %collective-permute-done.10.refs_3_), channel_id=1, source_target_pairs={{0,1},{1,0},{2,3},{3,2},{4,5},{5,4},{6,7},{7,6},{8,9},{9,8},{10,11... | collective-permute-start | bytes 737288 | tf_op jit(solution)/shard_map/ppermute | solution.py:205
  38.9 7.4 %copy-start.10 = (bf16[4,80,384]{2,1,0:T(8,128)(2,1)}, bf16[4,80,384]{2,1,0:T(8,128)(2,1)S(1)}, u32[]{:S(2)}) copy-start(bf16[4,80,384]{2,1,0:T(8,128)(2,1)S(1)} %collective-permute-done.11.refs_4_) | copy-start | bytes 737284
  38.9 21.4 %collective-permute-start.20 = (bf16[2,64,1408]{2,1,0:T(8,128)(2,1)}, bf16[2,64,1408]{2,1,0:T(8,128)(2,1)}, u32[]{:S(2)}, u32[]{:S(2)}) collective-permute-start(bf16[2,64,1408]{2,1,0:T(8,128)(2,1)} %get-tuple-element.168), channel_id=1, source_target_pairs={{0,4},{4,0},{8,12},{12,8},{16,20},{20,16},{24,28},{28,24},{1,5},{5... | collective-permute-start | bytes 1081352 | tf_op jit(solution)/shard_map/ppermute | solution.py:901
  40.2 20.2 %collective-permute-start.18 = (bf16[2,64,1408]{2,1,0:T(8,128)(2,1)}, bf16[2,64,1408]{2,1,0:T(8,128)(2,1)}, u32[]{:S(2)}, u32[]{:S(2)}) collective-permute-start(bf16[2,64,1408]{2,1,0:T(8,128)(2,1)} %get-tuple-element.172), channel_id=1, source_target_pairs={{0,2},{2,0},{1,3},{3,1},{4,6},{6,4},{5,7},{7,5},{8,10},{10,8},{9,1... | collective-permute-start | bytes 1081352 | tf_op jit(solution)/shard_map/ppermute | solution.py:209
  52.0 8.4 %collective-permute-start.16 = (bf16[512,128]{1,0:T(8,128)(2,1)}, bf16[512,128]{1,0:T(8,128)(2,1)S(1)}, u32[]{:S(2)}, u32[]{:S(2)}) collective-permute-start(bf16[512,128]{1,0:T(8,128)(2,1)} %get-tuple-element.103.kv0), channel_id=1, source_target_pairs={{0,2},{2,0},{1,3},{3,1},{4,6},{6,4},{5,7},{7,5},{8,10},{10,8},{9,1... | collective-permute-start | bytes 393224 | tf_op jit(solution)/shard_map/ppermute | solution.py:209
  52.0 12.6 %copy-start.18 = (bf16[512,128]{1,0:T(8,128)(2,1)S(1)}, bf16[512,128]{1,0:T(8,128)(2,1)}, u32[]{:S(2)}) copy-start(bf16[512,128]{1,0:T(8,128)(2,1)} %get-tuple-element.103.kv0) | copy-start | bytes 393220
  61.4 25.8 %copy-start.7 = (bf16[4,64,1408]{2,1,0:T(8,128)(2,1)}, bf16[4,64,1408]{2,1,0:T(8,128)(2,1)S(1)}, u32[]{:S(2)}) copy-start(bf16[4,64,1408]{2,1,0:T(8,128)(2,1)S(1)} %constant_dynamic-update-slice_fusion.13.refs_2_) | copy-start | bytes 2162692
  61.4 18.2 %collective-permute-start.21 = (bf16[4,64,1408]{2,1,0:T(8,128)(2,1)S(1)}, bf16[4,64,1408]{2,1,0:T(8,128)(2,1)S(1)}, u32[]{:S(2)}, u32[]{:S(2)}) collective-permute-start(bf16[4,64,1408]{2,1,0:T(8,128)(2,1)S(1)} %constant_dynamic-update-slice_fusion.13.refs_2_), channel_id=1, source_target_pairs={{0,2},{2,0},{1,3},{3,1},{4,6},{6,4},{5,7},{7,5},{8,10},{10,8},{9,1... | collective-permute-start | bytes 2162696 | tf_op jit(solution)/shard_map/ppermute | solution.py:209
  64.5 22.7 %copy-start.6 = (bf16[4,64,1408]{2,1,0:T(8,128)(2,1)}, bf16[4,64,1408]{2,1,0:T(8,128)(2,1)S(1)}, u32[]{:S(2)}) copy-start(bf16[4,64,1408]{2,1,0:T(8,128)(2,1)S(1)} %constant_dynamic-update-slice_fusion.10.refs_0_) | copy-start | bytes 2162692
  64.5 18.6 %collective-permute-start.19 = (bf16[4,64,1408]{2,1,0:T(8,128)(2,1)S(1)}, bf16[4,64,1408]{2,1,0:T(8,128)(2,1)S(1)}, u32[]{:S(2)}, u32[]{:S(2)}) collective-permute-start(bf16[4,64,1408]{2,1,0:T(8,128)(2,1)S(1)} %constant_dynamic-update-slice_fusion.10.refs_0_), channel_id=1, source_target_pairs={{0,4},{4,0},{8,12},{12,8},{16,20},{20,16},{24,28},{28,24},{1,5},{5... | collective-permute-start | bytes 2162696 | tf_op jit(solution)/shard_map/ppermute | solution.py:901
  64.6 1.5 collective-permute-start.15
  65.2 1.5 collective-permute-start.17
  65.3 18.4 %collective-permute-start.22 = (bf16[4,64,1408]{2,1,0:T(8,128)(2,1)S(1)}, bf16[4,64,1408]{2,1,0:T(8,128)(2,1)S(1)}, u32[]{:S(2)}, u32[]{:S(2)}) collective-permute-start(bf16[4,64,1408]{2,1,0:T(8,128)(2,1)S(1)} %constant_dynamic-update-slice_fusion.10.refs_0_), channel_id=1, source_target_pairs={{0,1},{1,0},{2,3},{3,2},{4,5},{5,4},{6,7},{7,6},{8,9},{9,8},{10,11... | collective-permute-start | bytes 2162696 | tf_op jit(solution)/shard_map/ppermute | solution.py:205
  66.2 17.5 %collective-permute-start.24 = (bf16[4,64,1408]{2,1,0:T(8,128)(2,1)S(1)}, bf16[4,64,1408]{2,1,0:T(8,128)(2,1)}, u32[]{:S(2)}, u32[]{:S(2)}) collective-permute-start(bf16[4,64,1408]{2,1,0:T(8,128)(2,1)S(1)} %constant_dynamic-update-slice_fusion.13.refs_2_), channel_id=1, source_target_pairs={{0,1},{1,0},{2,3},{3,2},{4,5},{5,4},{6,7},{7,6},{8,9},{9,8},{10,11... | collective-permute-start | bytes 2162696 | tf_op jit(solution)/shard_map/ppermute | solution.py:205
  79.7 7.6 %copy-start.13 = (bf16[4,64,1408]{2,1,0:T(8,128)(2,1)}, bf16[4,64,1408]{2,1,0:T(8,128)(2,1)S(1)}, u32[]{:S(2)}) copy-start(bf16[4,64,1408]{2,1,0:T(8,128)(2,1)S(1)} %collective-permute-done.21.refs_3_) | copy-start | bytes 2162692
  83.1 2.2 %collective-permute-start.23 = (bf16[4,64,1408]{2,1,0:T(8,128)(2,1)S(1)}, bf16[4,64,1408]{2,1,0:T(8,128)(2,1)S(1)}, u32[]{:S(2)}, u32[]{:S(2)}) collective-permute-start(bf16[4,64,1408]{2,1,0:T(8,128)(2,1)S(1)} %collective-permute-done.19.refs_1_), channel_id=1, source_target_pairs={{0,1},{1,0},{2,3},{3,2},{4,5},{5,4},{6,7},{7,6},{8,9},{9,8},{10,11... | collective-permute-start | bytes 2162696 | tf_op jit(solution)/shard_map/ppermute | solution.py:205
  83.1 3.2 %collective-permute-start.25 = (bf16[4,64,1408]{2,1,0:T(8,128)(2,1)S(1)}, bf16[4,64,1408]{2,1,0:T(8,128)(2,1)S(1)}, u32[]{:S(2)}, u32[]{:S(2)}) collective-permute-start(bf16[4,64,1408]{2,1,0:T(8,128)(2,1)S(1)} %collective-permute-done.21.refs_3_), channel_id=1, source_target_pairs={{0,1},{1,0},{2,3},{3,2},{4,5},{5,4},{6,7},{7,6},{8,9},{9,8},{10,11... | collective-permute-start | bytes 2162696 | tf_op jit(solution)/shard_map/ppermute | solution.py:205
  108.2 10.6 %collective-permute-start.27 = (bf16[2,2,2,64,1408]{4,3,2,1,0:T(8,128)(2,1)}, bf16[2,2,2,64,1408]{4,3,2,1,0:T(8,128)(2,1)}, u32[]{:S(2)}, u32[]{:S(2)}) collective-permute-start(bf16[2,2,2,64,1408]{4,3,2,1,0:T(8,128)(2,1)} %get-tuple-element.117), channel_id=1, source_target_pairs={{0,1},{1,0},{2,3},{3,2},{4,5},{5,4},{6,7},{7,6},{8,9},{9,8},{10,11... | collective-permute-start | bytes 4325384 | tf_op jit(solution)/shard_map/ppermute | solution.py:205
  108.4 14.4 %collective-permute-start.28 = (bf16[2,2,2,64,1408]{4,3,2,1,0:T(8,128)(2,1)}, bf16[2,2,2,64,1408]{4,3,2,1,0:T(8,128)(2,1)}, u32[]{:S(2)}, u32[]{:S(2)}) collective-permute-start(bf16[2,2,2,64,1408]{4,3,2,1,0:T(8,128)(2,1)} %get-tuple-element.121), channel_id=1, source_target_pairs={{0,1},{1,0},{2,3},{3,2},{4,5},{5,4},{6,7},{7,6},{8,9},{9,8},{10,11... | collective-permute-start | bytes 4325384 | tf_op jit(solution)/shard_map/ppermute | solution.py:205
  109.9 15.3 %collective-permute-start.26 = (bf16[256,512]{1,0:T(8,128)(2,1)S(1)}, bf16[256,512]{1,0:T(8,128)(2,1)S(1)}, u32[]{:S(2)}, u32[]{:S(2)}) collective-permute-start(bf16[256,512]{1,0:T(8,128)(2,1)S(1)} %get-tuple-element.164), channel_id=1, source_target_pairs={{0,3},{3,0},{1,2},{2,1},{4,7},{7,4},{5,6},{6,5},{8,11},{11,8},{9,1... | collective-permute-start | bytes 786440 | tf_op jit(solution)/shard_map/ppermute | solution.py:213
  110.0 8.8 %copy-start.3 = (bf16[2,2,2,64,1408]{4,3,2,1,0:T(8,128)(2,1)S(1)}, bf16[2,2,2,64,1408]{4,3,2,1,0:T(8,128)(2,1)}, u32[]{:S(2)}) copy-start(bf16[2,2,2,64,1408]{4,3,2,1,0:T(8,128)(2,1)} %get-tuple-element.116) | copy-start | bytes 4325380
  121.1 28.4 %collective-permute-start.29 = (bf16[2,2,64,1408]{3,2,1,0:T(8,128)(2,1)}, bf16[2,2,64,1408]{3,2,1,0:T(8,128)(2,1)}, u32[]{:S(2)}, u32[]{:S(2)}) collective-permute-start(bf16[2,2,64,1408]{3,2,1,0:T(8,128)(2,1)} %fusion), channel_id=1, source_target_pairs={{0,2},{2,0},{1,3},{3,1},{4,6},{6,4},{5,7},{7,5},{8,10},{10,8},{9,1... | collective-permute-start | bytes 2162696 | tf_op jit(solution)/shard_map/ppermute | solution.py:209
  124.9 28.3 %collective-permute-start.33 = (bf16[2,2,64,1408]{3,2,1,0:T(8,128)(2,1)}, bf16[2,2,64,1408]{3,2,1,0:T(8,128)(2,1)}, u32[]{:S(2)}, u32[]{:S(2)}) collective-permute-start(bf16[2,2,64,1408]{3,2,1,0:T(8,128)(2,1)} %fusion.1), channel_id=1, source_target_pairs={{0,4},{4,0},{8,12},{12,8},{16,20},{20,16},{24,28},{28,24},{1,5},{5... | collective-permute-start | bytes 2162696 | tf_op jit(solution)/shard_map/ppermute | solution.py:901
  140.9 1.9 collective-permute-start.30
  141.0 6.6 %collective-permute-start.31 = (bf16[2,128,256]{2,1,0:T(8,128)(2,1)}, bf16[2,128,256]{2,1,0:T(8,128)(2,1)S(1)}, u32[]{:S(2)}, u32[]{:S(2)}) collective-permute-start(bf16[2,128,256]{2,1,0:T(8,128)(2,1)} %get-tuple-element.128), channel_id=1, source_target_pairs={{0,2},{2,0},{1,3},{3,1},{4,6},{6,4},{5,7},{7,5},{8,10},{10,8},{9,1... | collective-permute-start | bytes 393224 | tf_op jit(solution)/shard_map/ppermute | solution.py:209
  141.4 8.1 %collective-permute-start.32 = (bf16[2,128,256]{2,1,0:T(8,128)(2,1)}, bf16[2,128,256]{2,1,0:T(8,128)(2,1)S(1)}, u32[]{:S(2)}, u32[]{:S(2)}) collective-permute-start(bf16[2,128,256]{2,1,0:T(8,128)(2,1)} %get-tuple-element.129), channel_id=1, source_target_pairs={{0,3},{3,0},{1,2},{2,1},{4,7},{7,4},{5,6},{6,5},{8,11},{11,8},{9,1... | collective-permute-start | bytes 393224 | tf_op jit(solution)/shard_map/ppermute | solution.py:213
  142.9 7.3 %copy-start.28 = (bf16[2,128,256]{2,1,0:T(8,128)(2,1)}, bf16[2,128,256]{2,1,0:T(8,128)(2,1)S(1)}, u32[]{:S(2)}) copy-start(bf16[2,128,256]{2,1,0:T(8,128)(2,1)S(1)} %collective-permute-done.30.p1) | copy-start | bytes 393220
  151.4 16.5 %collective-permute-start.35 = (bf16[2,64,1408]{2,1,0:T(8,128)(2,1)S(1)}, bf16[2,64,1408]{2,1,0:T(8,128)(2,1)S(1)}, u32[]{:S(2)}, u32[]{:S(2)}) collective-permute-start(bf16[2,64,1408]{2,1,0:T(8,128)(2,1)S(1)} %fusion.7), channel_id=1, source_target_pairs={{0,4},{4,0},{8,12},{12,8},{16,20},{20,16},{24,28},{28,24},{1,5},{5... | collective-permute-start | bytes 1081352 | tf_op jit(solution)/shard_map/ppermute | solution.py:901
  155.2 12.7 %collective-permute-start.39 = (bf16[2,64,1408]{2,1,0:T(8,128)(2,1)}, bf16[2,64,1408]{2,1,0:T(8,128)(2,1)}, u32[]{:S(2)}, u32[]{:S(2)}) collective-permute-start(bf16[2,64,1408]{2,1,0:T(8,128)(2,1)} %fusion.6), channel_id=1, source_target_pairs={{0,2},{2,0},{1,3},{3,1},{4,6},{6,4},{5,7},{7,5},{8,10},{10,8},{9,1... | collective-permute-start | bytes 1081352 | tf_op jit(solution)/shard_map/ppermute | solution.py:209
  167.4 3.4 %collective-permute-start.34 = (bf16[2,2,2,80,384]{4,3,2,1,0:T(8,128)(2,1)}, bf16[2,2,2,80,384]{4,3,2,1,0:T(8,128)(2,1)S(1)}, u32[]{:S(2)}, u32[]{:S(2)}) collective-permute-start(bf16[2,2,2,80,384]{4,3,2,1,0:T(8,128)(2,1)} %get-tuple-element.141), channel_id=1, source_target_pairs={{0,1},{1,0},{2,3},{3,2},{4,5},{5,4},{6,7},{7,6},{8,9},{9,8},{10,11... | collective-permute-start | bytes 1474568 | tf_op jit(solution)/shard_map/ppermute | solution.py:205
  167.4 5.2 %collective-permute-start.44 = (bf16[2,2,2,80,384]{4,3,2,1,0:T(8,128)(2,1)}, bf16[2,2,2,80,384]{4,3,2,1,0:T(8,128)(2,1)S(1)}, u32[]{:S(2)}, u32[]{:S(2)}) collective-permute-start(bf16[2,2,2,80,384]{4,3,2,1,0:T(8,128)(2,1)} %get-tuple-element.148), channel_id=1, source_target_pairs={{0,1},{1,0},{2,3},{3,2},{4,5},{5,4},{6,7},{7,6},{8,9},{9,8},{10,11... | collective-permute-start | bytes 1474568 | tf_op jit(solution)/shard_map/ppermute | solution.py:205
  170.9 8.0 %collective-permute-start.36 = (bf16[2,2,80,384]{3,2,1,0:T(8,128)(2,1)S(1)}, bf16[2,2,80,384]{3,2,1,0:T(8,128)(2,1)S(1)}, u32[]{:S(2)}, u32[]{:S(2)}) collective-permute-start(bf16[2,2,80,384]{3,2,1,0:T(8,128)(2,1)S(1)} %fusion.8), channel_id=1, source_target_pairs={{0,2},{2,0},{1,3},{3,1},{4,6},{6,4},{5,7},{7,5},{8,10},{10,8},{9,1... | collective-permute-start | bytes 737288 | tf_op jit(solution)/shard_map/ppermute | solution.py:209
  172.7 7.7 %collective-permute-start.45 = (bf16[2,2,80,384]{3,2,1,0:T(8,128)(2,1)S(1)}, bf16[2,2,80,384]{3,2,1,0:T(8,128)(2,1)S(1)}, u32[]{:S(2)}, u32[]{:S(2)}) collective-permute-start(bf16[2,2,80,384]{3,2,1,0:T(8,128)(2,1)S(1)} %fusion.9), channel_id=1, source_target_pairs={{0,4},{4,0},{8,12},{12,8},{16,20},{20,16},{24,28},{28,24},{1,5},{5... | collective-permute-start | bytes 737288 | tf_op jit(solution)/shard_map/ppermute | solution.py:901
  173.0 9.3 %collective-permute-start.38 = (bf16[64,1408]{1,0:T(8,128)(2,1)S(1)}, bf16[64,1408]{1,0:T(8,128)(2,1)S(1)}, u32[]{:S(2)}, u32[]{:S(2)}) collective-permute-start(bf16[64,1408]{1,0:T(8,128)(2,1)S(1)} %slice_bitcast_fusion.2), channel_id=1, source_target_pairs={{0,8},{4,12},{8,16},{12,20},{16,24},{20,28},{24,0},{28,4},{1,9},{5... | collective-permute-start | bytes 540680 | tf_op jit(solution)/shard_map/ppermute | solution.py:904
  173.1 11.0 %collective-permute-start.41 = (bf16[64,1408]{1,0:T(8,128)(2,1)S(1)}, bf16[64,1408]{1,0:T(8,128)(2,1)S(1)}, u32[]{:S(2)}, u32[]{:S(2)}) collective-permute-start(bf16[64,1408]{1,0:T(8,128)(2,1)S(1)} %get-tuple-element.165), channel_id=1, source_target_pairs={{0,24},{4,28},{8,0},{12,4},{16,8},{20,12},{24,16},{28,20},{1,25},{... | collective-permute-start | bytes 540680 | tf_op jit(solution)/shard_map/ppermute | solution.py:904
  176.9 14.0 %collective-permute-start.40 = (bf16[64,1408]{1,0:T(8,128)(2,1)S(1)}, bf16[64,1408]{1,0:T(8,128)(2,1)S(1)}, u32[]{:S(2)}, u32[]{:S(2)}) collective-permute-start(bf16[64,1408]{1,0:T(8,128)(2,1)S(1)} %get-tuple-element.166), channel_id=1, source_target_pairs={{0,16},{4,20},{8,24},{12,28},{16,0},{20,4},{24,8},{28,12},{1,17},{... | collective-permute-start | bytes 540680 | tf_op jit(solution)/shard_map/ppermute | solution.py:904
  178.9 12.0 %collective-permute-start.37 = (bf16[2,80,384]{2,1,0:T(8,128)(2,1)S(1)}, bf16[2,80,384]{2,1,0:T(8,128)(2,1)S(1)}, u32[]{:S(2)}, u32[]{:S(2)}) collective-permute-start(bf16[2,80,384]{2,1,0:T(8,128)(2,1)S(1)} %fusion.15), channel_id=1, source_target_pairs={{0,4},{4,0},{8,12},{12,8},{16,20},{20,16},{24,28},{28,24},{1,5},{5... | collective-permute-start | bytes 368648 | tf_op jit(solution)/shard_map/ppermute | solution.py:901
  180.4 10.7 %collective-permute-start.46 = (bf16[2,80,384]{2,1,0:T(8,128)(2,1)S(1)}, bf16[2,80,384]{2,1,0:T(8,128)(2,1)S(1)}, u32[]{:S(2)}, u32[]{:S(2)}) collective-permute-start(bf16[2,80,384]{2,1,0:T(8,128)(2,1)S(1)} %fusion.10), channel_id=1, source_target_pairs={{0,2},{2,0},{1,3},{3,1},{4,6},{6,4},{5,7},{7,5},{8,10},{10,8},{9,1... | collective-permute-start | bytes 368648 | tf_op jit(solution)/shard_map/ppermute | solution.py:209
  182.4 13.5 %copy-start.24 = (bf16[64,1408]{1,0:T(8,128)(2,1)}, bf16[64,1408]{1,0:T(8,128)(2,1)S(1)}, u32[]{:S(2)}) copy-start(bf16[64,1408]{1,0:T(8,128)(2,1)S(1)} %collective-permute-done.38.one) | copy-start | bytes 540676
  184.1 11.8 %copy-start.25 = (bf16[64,1408]{1,0:T(8,128)(2,1)}, bf16[64,1408]{1,0:T(8,128)(2,1)S(1)}, u32[]{:S(2)}) copy-start(bf16[64,1408]{1,0:T(8,128)(2,1)S(1)} %collective-permute-done.41.three) | copy-start | bytes 540676
  191.0 6.9 %collective-permute-start.43 = (bf16[80,384]{1,0:T(8,128)(2,1)S(1)}, bf16[80,384]{1,0:T(8,128)(2,1)S(1)}, u32[]{:S(2)}, u32[]{:S(2)}) collective-permute-start(bf16[80,384]{1,0:T(8,128)(2,1)S(1)} %slice_bitcast_fusion.9), channel_id=1, source_target_pairs={{0,8},{4,12},{8,16},{12,20},{16,24},{20,28},{24,0},{28,4},{1,9},{5... | collective-permute-start | bytes 184328 | tf_op jit(solution)/shard_map/ppermute | solution.py:904
  191.1 12.1 %collective-permute-start.42 = (bf16[256,512]{1,0:T(8,128)(2,1)}, bf16[256,512]{1,0:T(8,128)(2,1)S(1)}, u32[]{:S(2)}, u32[]{:S(2)}) collective-permute-start(bf16[256,512]{1,0:T(8,128)(2,1)} %get-tuple-element.146), channel_id=1, source_target_pairs={{0,3},{3,0},{1,2},{2,1},{4,7},{7,4},{5,6},{6,5},{8,11},{11,8},{9,1... | collective-permute-start | bytes 786440 | tf_op jit(solution)/shard_map/ppermute | solution.py:213
  191.3 6.7 %collective-permute-start.48 = (bf16[80,384]{1,0:T(8,128)(2,1)S(1)}, bf16[80,384]{1,0:T(8,128)(2,1)S(1)}, u32[]{:S(2)}, u32[]{:S(2)}) collective-permute-start(bf16[80,384]{1,0:T(8,128)(2,1)S(1)} %get-tuple-element.175), channel_id=1, source_target_pairs={{0,24},{4,28},{8,0},{12,4},{16,8},{20,12},{24,16},{28,20},{1,25},{... | collective-permute-start | bytes 184328 | tf_op jit(solution)/shard_map/ppermute | solution.py:904
  195.1 5.7 %collective-permute-start.47 = (bf16[80,384]{1,0:T(8,128)(2,1)S(1)}, bf16[80,384]{1,0:T(8,128)(2,1)S(1)}, u32[]{:S(2)}, u32[]{:S(2)}) collective-permute-start(bf16[80,384]{1,0:T(8,128)(2,1)S(1)} %get-tuple-element.176), channel_id=1, source_target_pairs={{0,16},{4,20},{8,24},{12,28},{16,0},{20,4},{24,8},{28,12},{1,17},{... | collective-permute-start | bytes 184328 | tf_op jit(solution)/shard_map/ppermute | solution.py:904
  195.1 8.2 %copy-start.21 = (f32[256,512]{1,0:T(8,128)S(1)}, f32[256,512]{1,0:T(8,128)}, u32[]{:S(2)}) copy-start(f32[256,512]{1,0:T(8,128)} %get-tuple-element.138) | copy-start | bytes 1572868
  (19 other events, 57.8 us)

commit v3 on v2

--- a/solution.py
+++ b/solution.py
@@ -13,7 +13,6 @@
 ROWS = 64
 TINY = 16
 CHUNK = 32
-VMEM_MAX = 60 * 1024 * 1024
 
 PLACES_A = ((0, 0, 0), (0, 0, 1), (1, 0, 0), (1, 0, 1))
 PLACES_XA = tuple((y, 1, s) for y, _, s in PLACES_A)
@@ -51,24 +50,24 @@
     )
 
 
-def any_spec():
-    return pl.BlockSpec(memory_space=pl.ANY)
-
-
 def smem_spec():
     return pl.BlockSpec(memory_space=pltpu.SMEM)
 
 
-def params():
-    return pltpu.CompilerParams(vmem_limit_bytes=VMEM_MAX)
+def params(mebibytes):
+    return pltpu.CompilerParams(vmem_limit_bytes=mebibytes * 1024 * 1024)
 
 
 def cost(microseconds):
-    return pl.CostEstimate(flops=0, bytes_accessed=int(microseconds * 3.69e5), transcendentals=0)
+    return pl.CostEstimate(flops=0, bytes_accessed=int(microseconds * 3.69e6), transcendentals=0)
 
 
 def after(value, *earlier):
     return lax.optimization_barrier((value, *earlier))[0]
+
+
+def together(*values):
+    return lax.optimization_barrier(values)
 
 
 def shaped(shape, kind):
@@ -107,7 +106,7 @@
     group, hidden = wq.shape[0] * HEAD, wup.shape[1]
     return pl.pallas_call(
         pack_kernel,
-        cost_estimate=cost(2),
+        cost_estimate=cost(0.2),
         out_shape=(
             shaped((ROWS + TINY, group), BF16),
             shaped((ROWS, group + 2 * hidden), BF16),
@@ -117,7 +116,7 @@
             pltpu.VMEM((group, LANES), F32),
             pltpu.VMEM((LANES, LANES), F32),
         ],
-        compiler_params=params(),
+        compiler_params=params(60),
     )(wq, wo, wup, wdown, wk, wv, wr, tok, cot, *[v.reshape(1, -1) for v in vectors], bup.reshape(1, -1))
 
 
@@ -125,22 +124,24 @@
     return kept.astype(F32) + one.astype(F32) + two.astype(F32) + three.astype(F32)
 
 
-def unpack_first_kernel(kept, one, two, three, gq, gk, gv, gr, v1, v2, v3, v4, v5, gb, total):
-    total[...] = sum_four(kept[0], one[...], two[...], three[...])
+def unpack_first_kernel(kept, one, two, three, gq, gk, gv, gr, *refs):
+    vectors, (gb, total) = refs[:5], refs[5:]
+    total[...] = sum_four(kept[...], one[...], two[...], three[...])
     for j in range(gq.shape[0]):
         gq[j] = total[0:ROWS, j * HEAD : (j + 1) * HEAD]
-    gk[...] = total[ROWS : ROWS + TINY, 0:HEAD]
-    gv[...] = total[ROWS : ROWS + TINY, HEAD : 2 * HEAD]
-    gr[...] = total[ROWS : ROWS + TINY, LANES : LANES + gr.shape[1]]
+    small = total[ROWS:, :]
+    gk[...] = small[:, 0:HEAD]
+    gv[...] = small[:, HEAD : 2 * HEAD]
+    gr[...] = small[:, LANES : LANES + gr.shape[1]]
     square = jnp.concatenate(
-        [total[ROWS : ROWS + TINY, LANES : 2 * LANES], jnp.zeros((LANES - TINY, LANES), F32)], axis=0
+        [small[:, LANES : 2 * LANES], jnp.zeros((LANES - TINY, LANES), F32)], axis=0
     ).T
-    for i, out in enumerate((v1, v2, v3, v4, v5)):
+    for i, out in enumerate(vectors):
         out[...] = square[24 + i : 25 + i, 0:TINY]
-    gb[...] = total[ROWS : ROWS + 1, 2 * LANES : 2 * LANES + HEAD]
-
-
-def unpack_first(kept, one, two, three, experts, routed):
+    gb[...] = small[0:1, 2 * LANES : 2 * LANES + HEAD]
+
+
+def unpack_first(parts, experts, routed):
     outs = pl.pallas_call(
         unpack_first_kernel,
         cost_estimate=cost(2),
@@ -152,16 +153,16 @@
             *[shaped((1, TINY), F32) for _ in range(5)],
             shaped((1, HEAD), F32),
         ),
-        scratch_shapes=[pltpu.VMEM(kept.shape[1:], F32)],
-        compiler_params=params(),
-    )(kept, one, two, three)
+        scratch_shapes=[pltpu.VMEM(parts[0].shape, F32)],
+        compiler_params=params(8),
+    )(*parts)
     return outs[0], outs[1], outs[2], outs[3], [v.reshape(-1) for v in outs[4:9]], outs[9].reshape(-1)
 
 
 def unpack_second_kernel(kept, one, two, three, go, gup, gdown, total, wide):
     experts = go.shape[0]
     group, hidden = experts * HEAD, gup.shape[1]
-    total[...] = sum_four(kept[0], one[...], two[...], three[...])
+    total[...] = sum_four(kept[...], one[...], two[...], three[...])
     gup[...] = total[:, group : group + hidden]
     wide[...] = jnp.zeros_like(wide)
     wide[0:ROWS, :] = total[:, 0:group]
@@ -182,10 +183,10 @@
             shaped((ROWS, hidden), F32),
         ),
         scratch_shapes=[
-            pltpu.VMEM(kept.shape[1:], F32),
+            pltpu.VMEM(kept.shape, F32),
             pltpu.VMEM((LANES, group), F32),
         ],
-        compiler_params=params(),
+        compiler_params=params(8),
     )(kept, one, two, three)
 
 
@@ -213,37 +214,86 @@
     return lax.ppermute(x, "tensor", CROSSED)
 
 
-def add_low(*terms):
-    total = terms[0].astype(F32)
-    for term in terms[1:]:
-        total = total + term.astype(F32)
-    return total.astype(BF16)
-
-
-def block_copies(table, pieces, row_from, rows, stride, target, sems):
-    copies = []
-    for a, (piece, places) in enumerate(zip(pieces, LAYOUT)):
+def add_blocks(name, *sums):
+    terms = [term for parts in sums for term in parts]
+    shapes = [parts[0][0].shape[len(parts[0][1]) :] for parts in sums]
+    count = len(terms)
+
+    def kernel(*refs):
+        ins, outs = refs[:count], refs[count:]
+        at = 0
+        for out, parts in zip(outs, sums):
+            total = None
+            for ref, (_, index) in zip(ins[at : at + len(parts)], parts):
+                value = ref[index].astype(F32) if index else ref[...].astype(F32)
+                total = value if total is None else total + value
+            out[...] = total.astype(BF16)
+            at += len(parts)
+
+    kernel.__name__ = name
+    size = 0
+    for shape, parts in zip(shapes, sums):
+        block = 2 * (len(parts) + 1)
+        for n in shape:
+            block *= n
+        size += block
+    return pl.pallas_call(
+        kernel,
+        cost_estimate=pl.CostEstimate(flops=0, bytes_accessed=size, transcendentals=0),
+        out_shape=tuple(shaped(shape, BF16) for shape in shapes),
+        compiler_params=params(16),
+    )(*[array for array, _ in terms])
+
+
+def add_ends(side_a, side_b, tiny):
+    arrays = [*side_a, *side_b, *tiny]
+
+    def kernel(*refs):
+        ins, outs = refs[:12], refs[12:]
+
+        def total(terms, s):
+            kept, got, near, last = terms
+            return sum_four(kept[0, 0, s], got[0, 0, s], near[0, s], last[s]).astype(BF16)
+
+        for s, out in enumerate(outs):
+            out[0:ROWS, :] = total(ins[0:4] if s < 2 else ins[4:8], s % 2)
+            out[ROWS:, :] = total(ins[8:12], s)
+
+    shape = (ROWS + TINY, side_a[0].shape[-1])
+    return pl.pallas_call(
+        kernel,
+        cost_estimate=cost(1.5),
+        out_shape=(shaped(shape, BF16),) * 4,
+        compiler_params=params(16),
+    )(*arrays)
+
+
+def place_blocks(table, pieces, row_from, rows, put):
+    for piece, places in zip(pieces, LAYOUT):
         for i, (slot, place) in enumerate(places):
-            source = piece.at[i, pl.ds(row_from, rows), :]
-            block = table[IN_AT + place]
-            if stride is None:
-                into = target.at[slot, pl.ds(pl.multiple_of(block * rows, rows), rows), :]
-            else:
-                row = (block * stride + table[SLOT_AT + slot]) * rows
-                into = target.at[pl.ds(pl.multiple_of(row, rows), rows), :]
-            copies.append(pltpu.make_async_copy(source, into, sems.at[a, i]))
-    return copies
+            put(slot, table[IN_AT + place], piece[i, row_from : row_from + rows, :])
+
+
+def rows_at(index, rows):
+    return pl.ds(pl.multiple_of(index * rows, rows), rows)
+
+
+def place_weights(table, pieces, weight):
+    def put(slot, block, value):
+        weight[slot, rows_at(block, ROWS), :] = value
+
+    place_blocks(table, pieces, 0, ROWS, put)
 
 
 def first_kernel(table, low_tok, cross, routes, *refs):
-    pieces, (normed_ref, kv_ref, gates_ref, small, vectors, up_bias, sems) = refs[:8], refs[8:]
-    copies = block_copies(table, pieces, ROWS, TINY, 4, small, sems)
-    for copy in copies:
-        copy.start()
+    pieces, (normed_ref, kv_ref, gates_ref, small, vectors, up_bias) = refs[:8], refs[8:]
+
+    def put(slot, block, value):
+        small[rows_at(block * 4 + table[SLOT_AT + slot], TINY), :] = value
+
+    place_blocks(table, pieces, ROWS, TINY, put)
     tokens = jnp.concatenate([low_tok[0:HALF, :], cross[0:HALF, :]], axis=0).astype(F32)
     scaled, _ = norm_parts(tokens)
-    for copy in copies:
-        copy.wait()
     turned = small[:, LANES : 2 * LANES].astype(F32).T
     vectors[...] = turned[24:32, :]
     for i in range(32):
@@ -274,8 +324,8 @@
     rows, width = tokens.shape
     return pl.pallas_call(
         first_kernel,
-        cost_estimate=cost(5),
-        in_specs=[smem_spec()] + [pl.BlockSpec(memory_space=pltpu.VMEM)] * 3 + [any_spec()] * 8,
+        cost_estimate=cost(0.5),
+        in_specs=[smem_spec()] + [pl.BlockSpec(memory_space=pltpu.VMEM)] * 11,
         out_shape=(
             shaped((rows, width), BF16),
             shaped((rows, LANES), BF16),
@@ -284,43 +334,64 @@
             shaped((8, width), F32),
             shaped((8, width), F32),
         ),
-        scratch_shapes=[pltpu.SemaphoreType.DMA((8, 4))],
-        compiler_params=params(),
+        compiler_params=params(14),
     )(table, tokens, cross, routes, *pieces)
 
 
-def half_routes(routes, k, at, half):
-    return jnp.broadcast_to(routes[at, k : k + 1], half.shape) - half
+def wanted_pairs(routes, at, ways):
+    half = (lax.broadcasted_iota(jnp.int32, (CHUNK, LANES), 1) >= HEAD).astype(jnp.int32)
+    return [
+        (jnp.broadcast_to(routes[at, k : k + 1], half.shape) - half).astype(jnp.int16)
+        for k in range(ways)
+    ]
+
+
+def pairs_of(table, experts):
+    for slot in range(4):
+        for pair in range(experts // 2):
+            base = experts * table[SLOT_AT + slot] + 2 * pair
+            yield slot, pair, jnp.full((CHUNK, LANES), base, jnp.int32).astype(jnp.int16)
+
+
+def select_pairs(table, routes, at, ways, source):
+    wanted = wanted_pairs(routes, at, ways)
+    picked = [jnp.zeros((CHUNK, LANES), BF16)] * ways
+    for slot, pair, base in pairs_of(table, source.shape[2] // HEAD):
+        value = source[slot, at, pair * LANES : (pair + 1) * LANES]
+        for k in range(ways):
+            picked[k] = jnp.where(wanted[k] == base, value, picked[k])
+    return picked
+
+
+def spread_pairs(table, routes, at, held, target):
+    wanted = wanted_pairs(routes, at, len(held))
+    for slot, pair, base in pairs_of(table, target.shape[2] // HEAD):
+        value = jnp.zeros((CHUNK, LANES), BF16)
+        for k, row in enumerate(held):
+            value = jnp.where(wanted[k] == base, row, value)
+        target[slot, at, pair * LANES : (pair + 1) * LANES] = value
+
+
+def over_chunks(rows, step):
+    def body(c, _):
+        step(pl.ds(pl.multiple_of(c * CHUNK, CHUNK), CHUNK))
+        return 0
+
+    lax.fori_loop(0, rows // CHUNK, body, 0)
 
 
 def query_kernel(table, normed, routes, *refs):
-    pieces, (chosen, weight, queries, sems) = refs[:8], refs[8:]
-    experts = weight.shape[2] // HEAD
-    copies = block_copies(table, pieces, 0, ROWS, None, weight, sems)
-    for copy in copies:
-        copy.start()
-    for copy in copies:
-        copy.wait()
+    pieces, (chosen, weight, queries) = refs[:8], refs[8:]
+    place_weights(table, pieces, weight)
     for slot in range(4):
         queries[slot] = nn(normed[...], weight[slot]).astype(BF16)
     ways = routes.shape[1]
-    half = (lax.broadcasted_iota(jnp.int32, (CHUNK, LANES), 1) >= HEAD).astype(jnp.int32)
-
-    def step(c, _):
-        at = pl.ds(pl.multiple_of(c * CHUNK, CHUNK), CHUNK)
-        wanted = [half_routes(routes, k, at, half) for k in range(ways)]
-        picked = [jnp.zeros((CHUNK, LANES), F32)] * ways
-        for slot in range(4):
-            for pair in range(experts // 2):
-                value = queries[slot, at, pair * LANES : (pair + 1) * LANES].astype(F32)
-                base = experts * table[SLOT_AT + slot] + 2 * pair
-                for k in range(ways):
-                    picked[k] = jnp.where(wanted[k] == base, value, picked[k])
-        for k in range(ways):
-            chosen[k, at, :] = picked[k].astype(BF16)
-        return 0
-
-    lax.fori_loop(0, normed.shape[0] // CHUNK, step, 0)
+
+    def step(at):
+        for k, value in enumerate(select_pairs(table, routes, at, ways, queries)):
+            chosen[k, at, :] = value
+
+    over_chunks(normed.shape[0], step)
 
 
 def query_stage(table, normed, routes, pieces):
@@ -328,17 +399,14 @@
     group = pieces[0].shape[2]
     return pl.pallas_call(
         query_kernel,
-        cost_estimate=cost(8),
-        in_specs=[smem_spec()] + [pl.BlockSpec(memory_space=pltpu.VMEM)] * 2 + [any_spec()] * 8,
+        cost_estimate=cost(0.8),
+        in_specs=[smem_spec()] + [pl.BlockSpec(memory_space=pltpu.VMEM)] * 10,
         out_shape=(
             shaped((routes.shape[1], rows, LANES), BF16),
             shaped((4, width, group), BF16),
         ),
-        scratch_shapes=[
-            pltpu.VMEM((4, rows, group), BF16),
-            pltpu.SemaphoreType.DMA((8, 4)),
-        ],
-        compiler_params=params(),
+        scratch_shapes=[pltpu.VMEM((4, rows, group), BF16)],
+        compiler_params=params(16),
     )(table, normed, routes, *pieces)
 
 
@@ -400,10 +468,13 @@
         return 0
 
     lax.fori_loop(0, last + 1, weigh, 0)
+    lane = lax.broadcasted_iota(jnp.int32, (HALF, LANES), 1)
+    total = jnp.zeros((HALF, LANES), F32)
     for k in range(ways):
         whole = sums[k]
-        out_ref[k] = whole[:, 0:LANES] / whole[:, LANES:]
-        total_ref[k] = tops[k] + jnp.log(whole[:, LANES:])
+        out_ref[k] = (whole[:, 0:LANES] / whole[:, LANES:]).astype(BF16)
+        total = jnp.where(lane == k, tops[k] + jnp.log(whole[:, LANES:]), total)
+    total_ref[...] = total
 
 
 def attend_stage(table, query, pairs, seq):
@@ -412,11 +483,11 @@
     spec = pl.BlockSpec((ways, HALF, LANES), lambda b: (0, b, 0))
     return pl.pallas_call(
         attend_kernel,
-        cost_estimate=cost(12),
+        cost_estimate=cost(1.2),
         grid=(rows // HALF,),
         in_specs=[smem_spec(), spec] + [kv_spec] * 4,
-        out_specs=(spec, spec),
-        out_shape=(shaped((ways, rows, LANES), F32), shaped((ways, rows, LANES), F32)),
+        out_specs=(spec, pl.BlockSpec((HALF, LANES), lambda b: (b, 0))),
+        out_shape=(shaped((ways, rows, LANES), BF16), shaped((rows, LANES), F32)),
         scratch_shapes=[
             pltpu.VMEM((seq, LANES), BF16),
             pltpu.VMEM((seq, 2 * LANES), BF16),
@@ -424,14 +495,14 @@
             pltpu.VMEM((ways, HALF, LANES), F32),
             pltpu.VMEM((ways, HALF, 2 * LANES), F32),
         ],
-        compiler_params=params(),
+        compiler_params=params(28),
     )(table, query, *pairs)
 
 
 def attend_back_kernel(
-    table, query, grad, totals, inner, kv0, kv1, kv2, kv3, grad_query, *refs
+    table, query, grad, all_totals, gates, gate_grads, kv0, kv1, kv2, kv3, grad_query, *refs
 ):
-    outs, (keys, values, key_sum, value_sum, query_sum, query_t, grad_t, probs, scored) = refs[:4], refs[4:]
+    outs, (keys, values, key_sum, value_sum, query_sum, query_t, grad_t, probs, scored, totals, inner) = refs[:4], refs[4:]
     block = pl.program_id(0)
     ways = query.shape[0]
 
@@ -446,6 +517,8 @@
     for k in range(ways):
         query_t[:, k * HALF : (k + 1) * HALF] = query[k].T
         grad_t[:, k * HALF : (k + 1) * HALF] = grad[k].T
+        totals[k] = jnp.broadcast_to(all_totals[:, k : k + 1], (HALF, LANES))
+        inner[k] = jnp.broadcast_to(gates[:, k : k + 1] * gate_grads[:, k : k + 1], (HALF, LANES))
 
     def step(at, masked):
         rows = pl.ds(pl.multiple_of(at * HALF, HALF), HALF)
@@ -482,7 +555,7 @@
                 out[h, HEAD:, :] = (value_part[0:HEAD] + value_part[HEAD:]).astype(BF16)
 
 
-def attend_back_stage(table, query, grad, totals, inner, pairs, seq):
+def attend_back_stage(table, query, grad, totals, gates, gate_grads, pairs, seq):
     ways, rows, _ = query.shape
     kv_spec = pl.BlockSpec((rows, LANES), lambda b: (0, 0))
     spec = pl.BlockSpec((ways, HALF, LANES), lambda b: (0, b, 0))
@@ -491,7 +564,7 @@
         attend_back_kernel,
         cost_estimate=cost(16),
         grid=(rows // HALF,),
-        in_specs=[smem_spec()] + [spec] * 4 + [kv_spec] * 4,
+        in_specs=[smem_spec()] + [spec] * 2 + [pl.BlockSpec((HALF, LANES), lambda b: (b, 0))] * 3 + [kv_spec] * 4,
         out_specs=(spec,) + (pair_spec,) * 4,
         out_shape=(shaped((ways, rows, LANES), BF16),) + (shaped((2, LANES, HALF), BF16),) * 4,
         scratch_shapes=[
@@ -504,70 +577,61 @@
             pltpu.VMEM((LANES, ways * HALF), BF16),
             pltpu.VMEM((ways * HALF, HALF), BF16),
             pltpu.VMEM((ways * HALF, HALF), BF16),
+            pltpu.VMEM((ways, HALF, LANES), F32),
+            pltpu.VMEM((ways, HALF, LANES), F32),
         ],
-        compiler_params=params(),
-    )(table, query, grad, totals, inner, *pairs)
-
-
-def put_blocks(table, grads, outs, slot, rows, row_to, column_to, slot_stride):
+        compiler_params=params(20),
+    )(table, query, grad, totals, gates, gate_grads, *pairs)
+
+
+def in_order(table, turned, target):
+    for place in range(8):
+        target[place * ROWS : (place + 1) * ROWS, :] = turned[rows_at(table[OUT_AT + place], ROWS), :]
+
+
+def put_blocks(grads, outs, slot, column_to):
     keep_a, keep_b, send_a, send_b = outs
     y, core = slot // 2, slot % 2
     wide = grads.shape[1]
     for s in range(4):
         for x in range(2):
-            at = table[OUT_AT + 2 * s + x]
-            if slot_stride:
-                at = at * slot_stride + table[SLOT_AT + slot]
-            block = grads[pl.ds(pl.multiple_of(at * rows, rows), rows), :]
+            block = grads[(2 * s + x) * ROWS : (2 * s + x + 1) * ROWS, :].astype(BF16)
             if s < 2:
                 out, place = (send_a if core else keep_a), (y, x, s)
             else:
                 out, place = (send_b if core else keep_b), (x, y, s - 2)
-            out[place[0], place[1], place[2], row_to : row_to + rows, column_to : column_to + wide] = block
+            out[place[0], place[1], place[2], :, column_to : column_to + wide] = block
 
 
 def middle_kernel(table, low_tok, low_cot, cross, heads, gates, routes, vectors, up_bias, *refs):
     pieces = refs[:8]
-    output, grad_mid, back, sums, bias_grad = refs[8:13]
-    blocks = refs[13:17]
-    weight, mixed, big, hid_scr, pre_scr, sems = refs[17:]
+    low_out, high_out, grad_mid, back, sums, bias_grad = refs[8:14]
+    blocks = refs[14:18]
+    weight, mixed, turned, ordered, hid_scr, pre_scr = refs[18:]
     ways, rows, _ = heads.shape
     width = low_tok.shape[1]
     group = mixed.shape[2]
-    hidden = hid_scr.shape[1]
-    experts = group // HEAD
-    copies = block_copies(table, pieces, 0, ROWS, None, weight, sems)
-    for copy in copies:
-        copy.start()
-    half = (lax.broadcasted_iota(jnp.int32, (CHUNK, LANES), 1) >= HEAD).astype(jnp.int32)
-
-    def expand(c, _):
-        at = pl.ds(pl.multiple_of(c * CHUNK, CHUNK), CHUNK)
-        wanted = [half_routes(routes, k, at, half) for k in range(ways)]
-        weighted = [
-            (heads[k, at, :] * gates[at, k : k + 1]).astype(BF16).astype(F32) for k in range(ways)
+    hidden = hid_scr.shape[2]
+    place_weights(table, pieces, weight)
+
+    def expand(at):
+        held = [
+            (heads[k, at, :].astype(F32) * gates[at, k : k + 1]).astype(BF16) for k in range(ways)
         ]
-        for slot in range(4):
-            for pair in range(experts // 2):
-                base = experts * table[SLOT_AT + slot] + 2 * pair
-                value = jnp.zeros((CHUNK, LANES), F32)
-                for k in range(ways):
-                    value = jnp.where(wanted[k] == base, weighted[k], value)
-                mixed[slot, at, pair * LANES : (pair + 1) * LANES] = value.astype(BF16)
-        return 0
-
-    lax.fori_loop(0, rows // CHUNK, expand, 0)
-    for copy in copies:
-        copy.wait()
+        spread_pairs(table, routes, at, held, mixed)
+
+    over_chunks(rows, expand)
     middle = jnp.concatenate([low_tok[0:HALF, :], cross[0:HALF, :]], axis=0).astype(F32)
     for slot in range(4):
         middle = middle + nt(mixed[slot], weight[slot, :, 0:group])
     scaled, inverse = norm_parts(middle)
     gain = vectors[2:3, :]
     normed = (scaled * gain + vectors[3:4, :]).astype(BF16)
-    normed_t = normed.T
+    turned[0] = normed.T
+    in_order(table, turned.at[0], ordered.at[0])
     cot = jnp.concatenate([low_cot[0:HALF, :], cross[HALF:, :]], axis=0)
-    cot_t = cot.T
+    turned[1] = cot.T
+    in_order(table, turned.at[1], ordered.at[1])
     result = middle + vectors[4:5, :]
     grad_normed = jnp.zeros((rows, width), F32)
     up_at, down_at = group, group + hidden
@@ -576,20 +640,19 @@
         preact = nn(normed, weight[slot, :, up_at:down_at]) + bias
         share = jax.nn.sigmoid(preact)
         active = (preact * share).astype(BF16)
-        hid_scr[...] = active
+        hid_scr[slot] = active
         slope = share * (1.0 + preact * (1.0 - share))
         grad_pre = (nn(cot, weight[slot, :, down_at:]) * slope).astype(BF16)
-        pre_scr[...] = grad_pre
+        pre_scr[slot] = grad_pre
         bias_grad[pl.ds(table[SLOT_AT + slot], 1), :] = jnp.sum(
             grad_pre.astype(F32), axis=0, keepdims=True
         )
-        result = result + nt(hid_scr[...], weight[slot, :, down_at:])
-        grad_normed = grad_normed + nt(pre_scr[...], weight[slot, :, up_at:down_at])
-        big[...] = nn(normed_t, pre_scr[...]).astype(BF16)
-        put_blocks(table, big, blocks, slot, ROWS, 0, up_at, 0)
-        big[...] = nn(cot_t, hid_scr[...]).astype(BF16)
-        put_blocks(table, big, blocks, slot, ROWS, 0, down_at, 0)
-    output[...] = result.astype(BF16)
+        result = result + nt(hid_scr[slot], weight[slot, :, down_at:])
+        grad_normed = grad_normed + nt(pre_scr[slot], weight[slot, :, up_at:down_at])
+        put_blocks(nn(ordered[0], pre_scr[slot]), blocks, slot, up_at)
+        put_blocks(nn(ordered[1], hid_scr[slot]), blocks, slot, down_at)
+    low_out[...] = result[0:HALF].astype(BF16)
+    high_out[...] = result[HALF:].astype(BF16)
     cot_wide = cot.astype(F32)
     sums[...] = jnp.zeros_like(sums)
     sums[2:3, :] = jnp.sum(grad_normed * scaled, axis=0, keepdims=True)
@@ -598,41 +661,26 @@
     grad_middle = cot_wide + norm_backward(grad_normed, scaled, inverse, gain)
     grad_mid[...] = grad_middle
     grad_attn = grad_middle.astype(BF16)
-    grad_attn_t = grad_attn.T
+    turned[2] = grad_attn.T
+    in_order(table, turned.at[2], ordered.at[2])
     for slot in range(4):
-        big[:, 0:group] = nn(grad_attn_t, mixed[slot]).astype(BF16)
-        put_blocks(table, big.at[:, 0:group], blocks, slot, ROWS, 0, 0, 0)
+        put_blocks(nn(ordered[2], mixed[slot]), blocks, slot, 0)
         back[slot] = nn(grad_attn, weight[slot, :, 0:group]).astype(BF16)
 
 
-def select_kernel(table, back, heads, gates, routes, grad_ref, inner, grad_gate):
+def select_kernel(table, back, heads, gates, routes, grad_ref, grad_gate):
     ways, rows, _ = heads.shape
-    experts = back.shape[2] // HEAD
-    half = (lax.broadcasted_iota(jnp.int32, (CHUNK, LANES), 1) >= HEAD).astype(jnp.int32)
     lane = lax.broadcasted_iota(jnp.int32, (CHUNK, LANES), 1)
-
-    def select(c, _):
-        at = pl.ds(pl.multiple_of(c * CHUNK, CHUNK), CHUNK)
-        wanted = [half_routes(routes, k, at, half) for k in range(ways)]
-        picked = [jnp.zeros((CHUNK, LANES), F32)] * ways
-        for slot in range(4):
-            for pair in range(experts // 2):
-                value = back[slot, at, pair * LANES : (pair + 1) * LANES].astype(F32)
-                base = experts * table[SLOT_AT + slot] + 2 * pair
-                for k in range(ways):
-                    picked[k] = jnp.where(wanted[k] == base, value, picked[k])
+    ones = jnp.ones((LANES, LANES), BF16)
+
+    def step(at):
         gate_grads = jnp.zeros((CHUNK, LANES), F32)
-        ones = jnp.ones((LANES, LANES), BF16)
-        for k in range(ways):
-            gate = jnp.broadcast_to(gates[at, k : k + 1], (CHUNK, LANES))
-            gate_grad = nn((picked[k] * heads[k, at, :]).astype(BF16), ones)
-            gate_grads = jnp.where(lane == k, gate_grad, gate_grads)
-            grad_ref[k, at, :] = (picked[k] * gate).astype(BF16)
-            inner[k, at, :] = gate_grad * gate
+        for k, value in enumerate(select_pairs(table, routes, at, ways, back)):
+            gate_grads = jnp.where(lane == k, nn(value * heads[k, at, :], ones), gate_grads)
+            grad_ref[k, at, :] = (value.astype(F32) * gates[at, k : k + 1]).astype(BF16)
         grad_gate[at, :] = gate_grads
-        return 0
-
-    lax.fori_loop(0, rows // CHUNK, select, 0)
+
+    over_chunks(rows, step)
 
 
 def select_stage(table, back, heads, gates, routes):
@@ -644,10 +692,9 @@
         in_specs=[smem_spec()] + [vmem] * 4,
         out_shape=(
             shaped((ways, rows, LANES), BF16),
-            shaped((ways, rows, LANES), F32),
             shaped((rows, LANES), F32),
         ),
-        compiler_params=params(),
+        compiler_params=params(16),
     )(table, back, heads, gates, routes)
 
 
@@ -661,9 +708,10 @@
     return pl.pallas_call(
         middle_kernel,
         cost_estimate=cost(36),
-        in_specs=[smem_spec()] + [vmem] * 8 + [any_spec()] * 8,
+        in_specs=[smem_spec()] + [vmem] * 16,
         out_shape=(
-            shaped((rows, width), BF16),
+            shaped((HALF, width), BF16),
+            shaped((rows - HALF, width), BF16),
             shaped((rows, width), F32),
             shaped((4, rows, group), BF16),
             shaped((8, width), F32),
@@ -676,39 +724,49 @@
         scratch_shapes=[
             pltpu.VMEM((4, width, packed), BF16),
             pltpu.VMEM((4, rows, group), BF16),
-            pltpu.VMEM((width, hidden), BF16),
-            pltpu.VMEM((rows, hidden), BF16),
-            pltpu.VMEM((rows, hidden), BF16),
-            pltpu.SemaphoreType.DMA((8, 4)),
+            pltpu.VMEM((3, width, rows), BF16),
+            pltpu.VMEM((3, width, rows), BF16),
+            pltpu.VMEM((4, rows, hidden), BF16),
+            pltpu.VMEM((4, rows, hidden), BF16),
         ],
-        compiler_params=params(),
+        compiler_params=params(40),
     )(table, tokens, cot, cross, heads, gates, routes, vectors, up_bias, *pieces)
 
 
+def spread_kernel(table, grad_query, normed, routes, spread, *refs):
+    blocks, (turned, normed_t) = refs[:4], refs[4:]
+    ways, rows, _ = grad_query.shape
+
+    def expand(at):
+        spread_pairs(table, routes, at, [grad_query[k, at, :] for k in range(ways)], spread)
+
+    over_chunks(rows, expand)
+    turned[...] = normed[...].T
+    in_order(table, turned, normed_t)
+    for slot in range(4):
+        put_blocks(nn(normed_t[...], spread[slot]), blocks, slot, 0)
+
+
+def spread_stage(table, grad_query, normed, routes, group):
+    rows, width = normed.shape
+    block = shaped((2, 2, 2, ROWS, group), BF16)
+    vmem = pl.BlockSpec(memory_space=pltpu.VMEM)
+    return pl.pallas_call(
+        spread_kernel,
+        cost_estimate=cost(6),
+        in_specs=[smem_spec()] + [vmem] * 3,
+        out_shape=(shaped((4, rows, group), BF16), block, block, block, block),
+        scratch_shapes=[pltpu.VMEM((width, rows), BF16), pltpu.VMEM((width, rows), BF16)],
+        compiler_params=params(16),
+    )(table, grad_query, normed, routes)
+
+
 def last_kernel(
-    table, low_tok, cross, grad_mid, grad_query, normed, routes, gates, grad_gate, weight, small,
-    vectors, sums, bias_grad, p0, p1, p2, p3, low_out, high_out, *refs
+    table, low_tok, cross, grad_mid, spread, normed, routes, gates, grad_gate, weight, small,
+    vectors, sums, bias_grad, p0, p1, p2, p3, low_out, high_out, keep, send, pair_grad, tiny, wide, extra
 ):
-    blocks, (spread, pair_grad, big, tiny, wide, extra) = refs[:4], refs[4:]
-    ways, rows, _ = grad_query.shape
-    group = spread.shape[2]
-    experts = group // HEAD
-    half = (lax.broadcasted_iota(jnp.int32, (CHUNK, LANES), 1) >= HEAD).astype(jnp.int32)
-
-    def expand(c, _):
-        at = pl.ds(pl.multiple_of(c * CHUNK, CHUNK), CHUNK)
-        wanted = [half_routes(routes, k, at, half) for k in range(ways)]
-        held = [grad_query[k, at, :].astype(F32) for k in range(ways)]
-        for slot in range(4):
-            for pair in range(experts // 2):
-                base = experts * table[SLOT_AT + slot] + 2 * pair
-                value = jnp.zeros((CHUNK, LANES), F32)
-                for k in range(ways):
-                    value = jnp.where(wanted[k] == base, held[k], value)
-                spread[slot, at, pair * LANES : (pair + 1) * LANES] = value.astype(BF16)
-        return 0
-
-    lax.fori_loop(0, rows // CHUNK, expand, 0)
+    rows = normed.shape[0]
+    ways = routes.shape[1]
     for h in range(2):
         total = sum_four(p0[h], p1[h], p2[h], p3[h])
         pair_grad[h * HALF : (h + 1) * HALF, :] = total.T.astype(BF16)
@@ -724,8 +782,6 @@
     grad_normed = nt(pair_grad[...], small[:, 0:LANES]) + nt(logit_low, small[:, LANES : 2 * LANES])
     for slot in range(4):
         grad_normed = grad_normed + nt(spread[slot], weight[slot])
-        big[...] = nn(normed_t, spread[slot]).astype(BF16)
-        put_blocks(table, big, blocks, slot, ROWS, 0, 0, 0)
     tokens = jnp.concatenate([low_tok[0:HALF, :], cross[0:HALF, :]], axis=0).astype(F32)
     scaled, inverse = norm_parts(tokens)
     back = grad_mid[...] + norm_backward(grad_normed, scaled, inverse, vectors[0:1, :])
@@ -742,33 +798,34 @@
         extra[TINY * i : TINY * i + 1, 0:HEAD] = bias_grad[i // 8 : i // 8 + 1, (i % 8) * HEAD : (i % 8 + 1) * HEAD]
     tiny[:, 2 * LANES : 3 * LANES] = extra[...].astype(BF16)
     for slot in range(4):
-        put_blocks(table, tiny, blocks, slot, TINY, ROWS, 0, 4)
+        out = send if slot % 2 else keep
+        for s in range(4):
+            for x in range(2):
+                row = (table[OUT_AT + 2 * s + x] * 4 + table[SLOT_AT + slot]) * TINY
+                out[slot // 2, x, s] = tiny[pl.ds(pl.multiple_of(row, TINY), TINY), :]
 
 
 def last_stage(
-    table, tokens, cross, grad_mid, grad_query, normed, routes, gates, grad_gate, weight, small,
+    table, tokens, cross, grad_mid, spread, normed, routes, gates, grad_gate, weight, small,
     vectors, sums, bias_grad, pair_parts
 ):
     rows, width = tokens.shape
-    group = weight.shape[2]
-    block = shaped((2, 2, 2, ROWS + TINY, group), BF16)
+    block = shaped((2, 2, 4, TINY, 3 * LANES), BF16)
     vmem = pl.BlockSpec(memory_space=pltpu.VMEM)
     return pl.pallas_call(
         last_kernel,
-        cost_estimate=cost(12),
+        cost_estimate=cost(7),
         in_specs=[smem_spec()] + [vmem] * 17,
-        out_shape=(shaped((HALF, width), F32), shaped((rows - HALF, width), BF16), block, block, block, block),
+        out_shape=(shaped((HALF, width), F32), shaped((rows - HALF, width), BF16), block, block),
         scratch_shapes=[
-            pltpu.VMEM((4, rows, group), BF16),
             pltpu.VMEM((rows, LANES), BF16),
-            pltpu.VMEM((width, group), BF16),
             pltpu.VMEM((width, 3 * LANES), BF16),
             pltpu.VMEM((LANES, width), F32),
             pltpu.VMEM((width, LANES), F32),
         ],
-        compiler_params=params(),
+        compiler_params=params(24),
     )(
-        table, tokens, cross, grad_mid, grad_query, normed, routes, gates, grad_gate, weight, small,
+        table, tokens, cross, grad_mid, spread, normed, routes, gates, grad_gate, weight, small,
         vectors, sums, bias_grad, *pair_parts
     )
 
@@ -824,14 +881,16 @@
     return lax.psum(jnp.stack(slots), ("dp", "tensor")).astype(F32)
 
 
-def general_grads(first, later, experts, hidden, routed):
+def general_grads(first, tiny, later, experts, hidden, routed):
     group = experts * HEAD
     d, t = lax.axis_index("dp"), lax.axis_index("tensor")
     dp = lax.axis_size("dp")
     width = 8 * ROWS
     first, later = general_sum(first), general_sum(later)
-    mine = lax.dynamic_index_in_dim(first[:, :, 0:ROWS].reshape(4, width, group), t, 0, False)
-    small = first[:, :, ROWS:].transpose(1, 0, 2, 3).reshape(width, group)
+    tiny = jnp.stack([tiny[slot % 2][slot // 2].swapaxes(0, 1) for slot in range(4)])
+    small = lax.psum(tiny, ("dp", "tensor")).astype(F32).reshape(4, 8, TINY, 3 * LANES)
+    small = small.transpose(1, 0, 2, 3).reshape(width, 3 * LANES)
+    mine = lax.dynamic_index_in_dim(first.reshape(4, width, group), t, 0, False)
     rest = lax.dynamic_index_in_dim(later.reshape(4, width, -1), t, 0, False)
     rows = width // dp
 
@@ -842,7 +901,7 @@
     rest = own(rest, rows, d)
     index = d * 4 + t
     tiny = own(small, rows // 4, index)
-    bias = small.reshape(32, TINY, group)[:, 0, 2 * LANES : 2 * LANES + HEAD].reshape(-1)
+    bias = small.reshape(32, TINY, 3 * LANES)[:, 0, 2 * LANES : 2 * LANES + HEAD].reshape(-1)
     return (
         query,
         tiny[:, 0:HEAD],
@@ -918,14 +977,12 @@
         next_a, next_b = over_y(side_a), over_x(side_b)
         later_z1, later_z3 = [over_z(after(second, z1), step) for step in (1, 3)]
         later_z2 = over_z(later_z1, 1)
-        side_a = jnp.concatenate([side_a, after(next_a, later_z1, later_z3)], axis=0)
-        side_b = jnp.concatenate([side_b, after(next_b, later_z1, later_z3)], axis=0)
+        side_a = jnp.concatenate([side_a, after(next_a, later_z1, later_z3, cross)], axis=0)
+        side_b = jnp.concatenate([side_b, after(next_b, later_z1, later_z3, cross)], axis=0)
         far_a, far_b = over_x(side_a), over_y(side_b)
-        first_pieces = [side_a, after(far_a, later_z2), side_b, after(far_b, later_z2)]
+        far_a, far_b = after(far_a, later_z2), after(far_b, later_z2)
+        first_pieces = [side_a, far_a, side_b, far_b]
         first_pieces = first_pieces + [over_core(v) for v in first_pieces]
-        later_a = jnp.concatenate([after(second, far_a), later_z1], axis=0)
-        later_b = jnp.concatenate([after(later_z2, far_b), later_z3], axis=0)
-        next_a, next_b = over_y(later_a), over_x(later_b)
     else:
         first_pieces, second_pieces = general_pieces(
             w_query, w_out, w_up, w_down, w_key, w_value, w_router, vectors_in, b_up
@@ -935,74 +992,120 @@
         table, tokens, cross, own_routes, first_pieces
     )
     pair_y = over_y(pair)
+    if tuned:
+        later_a = jnp.concatenate([after(second, pair), later_z1], axis=0)
+        later_b = jnp.concatenate([after(later_z2, pair), later_z3], axis=0)
+        next_a, next_b = over_y(later_a), over_x(later_b)
     pairs = (pair, over_core(pair), pair_y, over_core(pair_y))
     if tuned:
         normed = after(normed, later_a, later_b)
     query, query_weight = query_stage(table, normed, own_routes, first_pieces)
     if tuned:
-        side_a = jnp.concatenate([later_a, after(next_a, query, pair_y)], axis=0)
+        side_a = jnp.concatenate([later_a, after(next_a, query)], axis=0)
         side_b = jnp.concatenate([later_b, after(next_b, query, pair_y)], axis=0)
         far_a, far_b = over_x(side_a), over_y(side_b)
     heads, totals = attend_stage(table, query, pairs, seq)
     if tuned:
-        second_pieces = [side_a, after(far_a, heads), side_b, after(far_b, heads)]
-        second_pieces = second_pieces + [over_core(v) for v in second_pieces]
-    output, grad_mid, back, sums, bias_grad, *later_blocks = middle_stage(
+        heads, far_a, far_b, core_a, core_b = together(heads, far_a, far_b, over_core(side_a), over_core(side_b))
+        second_pieces = [side_a, far_a, side_b, far_b, core_a, over_core(far_a), core_b, over_core(far_b)]
+    output, output_high, grad_mid, back, sums, bias_grad, *later_blocks = middle_stage(
         table, tokens, cotangent, cross, heads, gates, own_routes, vectors, up_bias, second_pieces
     )
     if tuned:
         keep_a, keep_b, send_a, send_b = later_blocks
         got_a, got_b = over_core(send_a), over_core(send_b)
-    output_high = crossed(output[HALF:])
-    grad_heads, inner, grad_gate = select_stage(table, back, heads, gates, own_routes)
+    grad_heads, grad_gate = select_stage(table, back, heads, gates, own_routes)
     if tuned:
-        part_a, part_b = add_low(keep_a[1], after(got_a, inner)[1]), add_low(keep_b[1], after(got_b, inner)[1])
+        got_a, got_b = after(got_a, grad_gate), after(got_b, grad_gate)
+        part_a, part_b = add_blocks(
+            "add_near", [(keep_a, (1,)), (got_a, (1,))], [(keep_b, (1,)), (got_b, (1,))]
+        )
         next_a, next_b = over_y(part_a), over_x(part_b)
-        grad_heads = after(grad_heads, part_a, part_b, output_high)
+        grad_heads = after(grad_heads, part_a, part_b)
     grad_query, part0, part1, part2, part3 = attend_back_stage(
-        table, query, grad_heads, totals, inner, pairs, seq
+        table, query, grad_heads, totals, gates, grad_gate, pairs, seq
     )
     pair_parts = (part0, over_core(part1), over_y(part2), crossed(part3))
     if tuned:
-        next_a, next_b = after(next_a, *pair_parts), after(next_b, *pair_parts)
-        part_a = add_low(keep_a[0, 1], got_a[0, 1], next_a[1])
-        part_b = add_low(keep_b[0, 1], got_b[0, 1], next_b[1])
+        next_a, next_b = after(next_a, part0), after(next_b, part0)
+        part_a, part_b = add_blocks(
+            "add_far",
+            [(keep_a, (0, 1)), (got_a, (0, 1)), (next_a, (1,))],
+            [(keep_b, (0, 1)), (got_b, (0, 1)), (next_b, (1,))],
+        )
         last_a, last_b = over_x(part_a), over_y(part_b)
         grad_query = after(grad_query, part_a, part_b)
-    low_rows, high_rows, *first_blocks = last_stage(
-        table, tokens, cross, grad_mid, grad_query, normed, own_routes, gates, grad_gate,
-        query_weight, small, vectors, sums, bias_grad, pair_parts,
-    )
+    spread, *first_blocks = spread_stage(table, grad_query, normed, own_routes, query_weight.shape[2])
     if tuned:
-        last_a, last_b = after(last_a, low_rows), after(last_b, low_rows)
-        done_a = add_low(keep_a[0, 0], got_a[0, 0], next_a[0], last_a)
-        done_b = add_low(keep_b[0, 0], got_b[0, 0], next_b[0], last_b)
-        later = (done_a, over_z(done_a[1], 1), over_z(done_b[0], 2), over_z(done_b[1], 3))
-        out_grad, up_grad, down_grad = unpack_second(*later, experts, hidden)
-        down_grad = down_grad.T
-
+        last_a, last_b, spread, *rest = together(last_a, last_b, spread, *pair_parts, *first_blocks)
+        pair_parts, first_blocks = rest[0:4], rest[4:8]
+
+        def final(name, keep_a, keep_b, got_a, got_b, next_a, next_b, last_a, last_b):
+            return add_blocks(
+                name,
+                *[
+                    [(keep, (0, 0, s)), (got, (0, 0, s)), (near, (0, s)), (last, (s,))]
+                    for keep, got, near, last in (
+                        (keep_a, got_a, next_a, last_a),
+                        (keep_b, got_b, next_b, last_b),
+                    )
+                    for s in (0, 1)
+                ],
+            )
+
+        done = final("add_last", keep_a, keep_b, got_a, got_b, next_a, next_b, last_a, last_b)
+        later = (done[0], *[over_z(done[step], step) for step in (1, 2, 3)])
         keep_a, keep_b, send_a, send_b = first_blocks
         got_a, got_b = over_core(send_a), over_core(send_b)
-        got_a, got_b = after(got_a, done_a), after(got_b, done_b)
-        next_a = over_y(add_low(keep_a[1], got_a[1]))
-        next_b = over_x(add_low(keep_b[1], got_b[1]))
-        last_a = over_x(add_low(keep_a[0, 1], got_a[0, 1], next_a[1]))
-        last_b = over_y(add_low(keep_b[0, 1], got_b[0, 1], next_b[1]))
-        last_a = after(last_a, *later[1:])
-        high_rows = after(high_rows, last_a)
-        done_a = add_low(keep_a[0, 0], got_a[0, 0], next_a[0], last_a)
-        done_b = add_low(keep_b[0, 0], got_b[0, 0], next_b[0], last_b)
-        early = (done_a, over_z(done_a[1], 1), over_z(done_b[0], 2), over_z(done_b[1], 3))
+        got_a, got_b = after(got_a, *done), after(got_b, *done)
+        part_a, part_b = add_blocks(
+            "add_near", [(keep_a, (1,)), (got_a, (1,))], [(keep_b, (1,)), (got_b, (1,))]
+        )
+        next_a, next_b = over_y(part_a), over_x(part_b)
+        spread = after(spread, part_a, part_b)
+        output_high = after(output_high, part_a)
+    output_high = crossed(output_high)
+    low_rows, high_rows, *tiny_blocks = last_stage(
+        table, tokens, cross, grad_mid, spread, normed, own_routes, gates, grad_gate,
+        query_weight, small, vectors, sums, bias_grad, pair_parts,
+    )
+    if tuned:
+        kept, one, two, three = later
+        low_rows, high_rows, keep, send, next_a, next_b, one, three, output_high = together(
+            low_rows, high_rows, *tiny_blocks, next_a, next_b, one, three, output_high
+        )
+        got = over_core(send)
+        part_a, part_b = add_blocks(
+            "add_far",
+            [(keep_a, (0, 1)), (got_a, (0, 1)), (next_a, (1,))],
+            [(keep_b, (0, 1)), (got_b, (0, 1)), (next_b, (1,))],
+        )
+        last_a, last_b = over_x(part_a), over_y(part_b)
+        (part,) = add_blocks("add_tiny", [(keep, (1,)), (got, (1,))])
+        next_tiny = over_y(part)
+        high_rows = after(high_rows, part)
+        out_grad, up_grad, down_grad = unpack_second(kept, one, two, three, experts, hidden)
+        down_grad = down_grad.T
+        (part,) = add_blocks("add_tiny", [(keep, (0, 1)), (got, (0, 1)), (next_tiny, (1,))])
+        last_tiny = over_x(part)
+        done = add_ends(
+            (keep_a, got_a, next_a, last_a), (keep_b, got_b, next_b, last_b), (keep, got, next_tiny, last_tiny)
+        )
+        one, two, three = [over_z(done[step], step) for step in (1, 2, 3)]
+        result = jnp.concatenate([output, output_high], axis=0)
+        grad_tokens = jnp.concatenate([low_rows, crossed(high_rows).astype(F32)], axis=0)
+        one = after(one, out_grad, result, grad_tokens)
+        parts = (done[0], one, two, three)
         query_grad, key_grad, value_grad, router_grad, small_grads, up_bias_grad = unpack_first(
-            *early, experts, routed
+            parts, experts, routed
         )
     else:
         (
             query_grad, key_grad, value_grad, router_grad, small_grads, up_bias_grad,
             out_grad, up_grad, down_grad,
-        ) = general_grads(first_blocks, later_blocks, experts, hidden, routed)
-    result = jnp.concatenate([output[:HALF], output_high], axis=0)
-    grad_tokens = jnp.concatenate([low_rows, crossed(high_rows).astype(F32)], axis=0)
+        ) = general_grads(first_blocks, tiny_blocks, later_blocks, experts, hidden, routed)
+        result = jnp.concatenate([output, output_high], axis=0)
+        grad_tokens = jnp.concatenate([low_rows, crossed(high_rows).astype(F32)], axis=0)
     return (
         result,
         grad_tokens,

time: 205 us -> 176 us (0.86)
  Pallas kernels: 89 us -> 66.7 us
  other arithmetic: 13.5 us -> 1.96 us
  starting transfers between devices: 39.2 us -> 47.4 us
  local copies, waits for them, and re-layouts: 12.3 us -> 4.2 us
  waiting for transfers between devices: 49.1 us -> 54.6 us
    ppermute x10 -> x11, waiting for transfers between devices: 7.2 us -> 22.5 us  [over_y(): return lax.ppermute(x, 'tensor', ACROSS)]
    convert_element_type x12 -> x0, other arithmetic: 10.8 us -> none  [add_low(): return total.astype(BF16)]
    pallas_call x5 -> x14, Pallas kernels: 39.7 us -> 29.1 us  [the longest x1 10.5 us: attend_stage(): pl.pallas_call(attend_kernel, cost_estimate=cost(1.2), grid=(rows // HALF...]
    ppermute x12, waiting for transfers between devices: 24 us -> 16.7 us  [over_z(): return lax.ppermute(x, 'dp', turns[step - 1])]
    ppermute x4, waiting for transfers between devices: 6.28 us -> 0.01 us  [crossed(): return lax.ppermute(x, 'tensor', CROSSED)]
    ppermute x15 -> x16, waiting for transfers between devices: 3.33 us -> 9.16 us  [over_core(): return lax.ppermute(x, 'tensor', CORE)]
    ppermute x12, starting transfers between devices: 15.8 us -> 20.5 us  [over_z(): return lax.ppermute(x, 'dp', turns[step - 1])]
    pallas_call x1, Pallas kernels: 8.79 us -> 4.69 us  [select_stage(): pl.pallas_call(select_kernel, cost_estimate=cost(8), in_specs=[smem_spec(...]
  transfers between devices with their start and end apart: 49 -> 52, of which waited for: 20 -> 29; matrix products, arithmetic and copies ran while one was open for 10% -> 2% of each run, Pallas kernels for 32% -> 25%
where the time goes in v3:
time: 176 us
  Pallas kernels  66.7 us (38%)
  waiting for transfers between devices  54.6 us (31%)
  starting transfers between devices  47.4 us (27%)
  local copies, waits for them, and re-layouts  4.2 us (2%)
  other arithmetic  1.96 us (1%)
    ppermute x11, waiting for transfers between devices, over_y(): return lax.ppermute(x, 'tensor', ACROSS)  22.5 us
    ppermute x12, starting transfers between devices, over_z(): return lax.ppermute(x, 'dp', turns[step - 1])  20.5 us
    pallas_call x1, Pallas kernels, middle_stage(): pl.pallas_call(middle_kernel, cost_estimate=cost(36), in_specs=[smem_spec...  17 us
    ppermute x12, waiting for transfers between devices, over_z(): return lax.ppermute(x, 'dp', turns[step - 1])  16.7 us
    pallas_call x1, Pallas kernels, attend_back_stage(): pl.pallas_call(attend_back_kernel, cost_estimate=cost(16), grid=(rows //...  14.3 us
    ppermute x11, starting transfers between devices, over_y(): return lax.ppermute(x, 'tensor', ACROSS)  12.8 us
    pallas_call x1, Pallas kernels, attend_stage(): pl.pallas_call(attend_kernel, cost_estimate=cost(1.2), grid=(rows // HALF...  10.5 us
    ppermute x16, waiting for transfers between devices, over_core(): return lax.ppermute(x, 'tensor', CORE)  9.16 us
  transfers between devices with their start and end apart: 52, of which 29 were waited for; matrix products, arithmetic and copies ran while one was open for 2% of the time, Pallas kernels for 25%

profile of v3, /device:TPU:0, one launch (start us, length us, event | category | flops | bytes accessed | tf_op | source)
XLA Modules:
  0.0 175.9 jit_solution(11711564134495577243)
XLA Ops:
  0.7 2.5 %shard_map.271 = (bf16[80,384]{1,0:T(8,128)(2,1)}, bf16[64,1408]{1,0:T(8,128)(2,1)}, bf16[512,512]{1,0:T(8,128)(2,1)}) custom-call(bf16[6,64,64]{2,1,0:T(8,128)(2,1)} %wq.1, bf16[6,64,64]{2,1,0:T(8,128)(2,1)} %wo.1, bf16[64,512]{1,0:T(8,128)(2,1)} %wup.1, bf16[64,512]{1,0:T(8,128)(2,1)} %bitcast.46, bf16[16,64]{1,0:T(8,128)(2,1)} %wk.1, bf16[16,64]{1,0:T(8,128)(2,1)} %wv.1, ...), custom_call_target="tpu_custom_call" | custom-call | bytes 738000 | tf_op jit(solution)/shard_map/pallas_call | solution.py:107
  3.2 5.0 %collective-permute-start.8 = (bf16[1,80,384]{2,1,0:T(8,128)(2,1)}, bf16[1,80,384]{2,1,0:T(8,128)(2,1)S(1)}, u32[]{:S(2)}, u32[]{:S(2)}) collective-permute-start(bf16[1,80,384]{2,1,0:T(8,128)(2,1)} %bitcast.38), channel_id=1, source_target_pairs={{0,24},{4,28},{8,0},{12,4},{16,8},{20,12},{24,16},{28,20},{1,25},{... | collective-permute-start | bytes 184328 | tf_op jit(solution)/shard_map/ppermute | solution.py:963
  8.2 1.0 collective-permute-start.1
  9.3 0.7 constant_dynamic-slice_fusion.1
  10.2 0.8 constant_dynamic-update-slice_fusion.2
  11.0 3.5 %collective-permute-done.1 = bf16[1,80,384]{2,1,0:T(8,128)(2,1)S(1)} collective-permute-done((bf16[1,80,384]{2,1,0:T(8,128)(2,1)}, bf16[1,80,384]{2,1,0:T(8,128)(2,1)S(1)}, u32[]{:S(2)}, u32[]{:S(2)}) %collective-permute-start.1) | collective-permute-done | bytes 61472 | tf_op jit(solution)/shard_map/ppermute | solution.py:963
  14.5 1.1 collective-permute-start.4
  15.7 0.9 collective-permute-start.3
  16.6 1.6 collective-permute-start.9
  18.1 0.8 pad_maximum_fusion.1
  19.0 1.6 collective-permute-start.2
  20.6 0.9 collective-permute-done.9
  21.5 4.3 %collective-permute-done.3 = bf16[1,64,1408]{2,1,0:T(8,128)(2,1)S(1)} collective-permute-done((bf16[1,64,1408]{2,1,0:T(8,128)(2,1)}, bf16[1,64,1408]{2,1,0:T(8,128)(2,1)S(1)}, u32[]{:S(2)}, u32[]{:S(2)}) %collective-permute-start.3) | collective-permute-done | bytes 180256 | tf_op jit(solution)/shard_map/ppermute | solution.py:963
  26.3 1.6 collective-permute-start.5
  27.9 1.2 collective-permute-start.10
  29.1 1.4 collective-permute-start.6
  31.0 5.5 %collective-permute-done.6 = bf16[1,64,1408]{2,1,0:T(8,128)(2,1)S(1)} collective-permute-done((bf16[1,64,1408]{2,1,0:T(8,128)(2,1)S(1)}, bf16[1,64,1408]{2,1,0:T(8,128)(2,1)S(1)}, u32[]{:S(2)}, u32[]{:S(2)}) %collective-permute-start.6) | collective-permute-done | bytes 180256 | tf_op jit(solution)/shard_map/ppermute | solution.py:963
  36.5 0.7 copy-done.6
  37.8 0.8 collective-permute-done.12.refs_5_
  39.0 2.4 %shard_map.272 = (bf16[512,512]{1,0:T(8,128)(2,1)S(1)}, bf16[512,128]{1,0:T(8,128)(2,1)S(1)}, f32[512,128]{1,0:T(8,128)S(1)}, bf16[512,384]{1,0:T(8,128)(2,1)S(1...) custom-call(s32[28]{0:T(128)S(1)} %stack.97.table, bf16[512,512]{1,0:T(8,128)(2,1)S(1)} %copy-done, ...), custom_call_target="tpu_custom_call" | custom-call | bytes 1845000 | tf_op jit(solution)/shard_map/pallas_call | solution.py:325
  41.6 1.3 collective-permute-start.18
  43.6 0.8 collective-permute-start.16
  44.3 4.2 %shard_map.273 = (bf16[8,512,128]{2,1,0:T(8,128)(2,1)S(1)}, bf16[4,512,384]{2,1,0:T(8,128)(2,1)S(1)}) custom-call(s32[28]{0:T(128)S(1)} %stack.97.table, bf16[512,512]{1,0:T(8,128)(2,1)S(1)} %get-tuple-element.144.normed, s32[512,8]{1,0:T(8,128)S(1)} %copy.33.routes, bf16[4,80,384]{2,1,0:T(8,128)(2,1)S(1)} %constant_dynamic-update-slice_fusion.refs_0_, ...), custom_call_target="tpu_custom_call" | custom-call | bytes 2952000 | tf_op jit(solution)/shard_map/pallas_call | solution.py:400
  48.5 4.4 %collective-permute-done.18 = bf16[2,64,1408]{2,1,0:T(8,128)(2,1)S(1)} collective-permute-done((bf16[2,64,1408]{2,1,0:T(8,128)(2,1)S(1)}, bf16[2,64,1408]{2,1,0:T(8,128)(2,1)S(1)}, u32[]{:S(2)}, u32[]{:S(2)}) %collective-permute-start.18) | collective-permute-done | bytes 360480 | tf_op jit(solution)/shard_map/ppermute | solution.py:210
  53.6 1.3 collective-permute-done.16.kv2
  55.0 1.3 collective-permute-start.21
  56.5 1.2 collective-permute-done.15.kv1
  57.9 1.2 collective-permute-done.17.kv3
  59.1 10.5 %shard_map.274 = (bf16[8,512,128]{2,1,0:T(8,128)(2,1)S(1)}, f32[512,128]{1,0:T(8,128)S(1)}) custom-call(s32[28]{0:T(128)S(1)} %stack.97.table, bf16[8,512,128]{2,1,0:T(8,128)(2,1)S(1)} %get-tuple-element.145.query, bf16[512,128]{1,0:T(8,128)(2,1)S(1)} %get-tuple-element.141.kv0, bf16[512,128]{1,0:T(8,128)(2,1)S(1)} %collective-permute-done.15.kv1, ...), custom_call_target="tpu_custom_call" | custom-call | bytes 4428000 | tf_op jit(solution)/shard_map/pallas_call | solution.py:484
  69.6 1.9 %collective-permute-done.19.refs_1_ = bf16[4,64,1408]{2,1,0:T(8,128)(2,1)S(1)} collective-permute-done((bf16[4,64,1408]{2,1,0:T(8,128)(2,1)S(1)}, bf16[4,64,1408]{2,1,0:T(8,128)(2,1)S(1)}, u32[]{:S(2)}, u32[]{:S(2)}) %collective-permute-start.19) | collective-permute-done | bytes 720928 | tf_op jit(solution)/shard_map/ppermute | solution.py:960
  71.6 2.0 %collective-permute-done.21.refs_3_ = bf16[4,64,1408]{2,1,0:T(8,128)(2,1)S(1)} collective-permute-done((bf16[4,64,1408]{2,1,0:T(8,128)(2,1)S(1)}, bf16[4,64,1408]{2,1,0:T(8,128)(2,1)S(1)}, u32[]{:S(2)}, u32[]{:S(2)}) %collective-permute-start.21) | collective-permute-done | bytes 720928 | tf_op jit(solution)/shard_map/ppermute | solution.py:210
  74.1 1.7 collective-permute-done.24.refs_5_
  75.8 1.0 collective-permute-done.25.refs_7_
  76.8 17.0 %shard_map.275 = (bf16[256,512]{1,0:T(8,128)(2,1)S(1)}, bf16[256,512]{1,0:T(8,128)(2,1)S(1)}, f32[512,512]{1,0:T(8,128)S(1)}, bf16[4,512,384]{2,1,0:T(8,128)(2,1...) custom-call(s32[28]{0:T(128)S(1)} %stack.97.table, ...), custom_call_target="tpu_custom_call" | custom-call | bytes 132840000 | tf_op jit(solution)/shard_map/pallas_call | solution.py:708
  94.3 1.4 copy-done.2
  95.7 4.7 %shard_map.276 = (bf16[8,512,128]{2,1,0:T(8,128)(2,1)S(1)}, f32[512,128]{1,0:T(8,128)S(1)}) custom-call(s32[28]{0:T(128)S(1)} %stack.97.table, bf16[4,512,384]{2,1,0:T(8,128)(2,1)S(1)} %copy-done.2, bf16[8,512,128]{2,1,0:T(8,128)(2,1)S(1)} %get-tuple-element.149.heads, f32[512,128]{1,0:T(8,128)S(1)} %get-tuple-element.150.gates, s32[512,8]{1,0:T(8,128)S(1)} %copy.33.routes), custom_call_target="tpu_custom_call" | custom-call | bytes 29520000 | tf_op jit(solution)/shard_map/pallas_call | solution.py:689
  100.8 1.3 collective-permute-start.28
  102.6 14.3 %shard_map.278 = (bf16[8,512,128]{2,1,0:T(8,128)(2,1)S(1)}, bf16[2,128,256]{2,1,0:T(8,128)(2,1)S(1)}, bf16[2,128,256]{2,1,0:T(8,128)(2,1)S(1)}, bf16[2,128,256]{2,1,0:T(8,128)(2,1)S(1)}, bf16[2,128,256]{2,1,0:T(8,128)(2,1)S(1)}) custom-call(s32[28]{0:T(128)S(1)} %stack.97.table, bf16[8,512,128]{2,1,0:T(8,128)(2,1)S(1)} %get-tuple-element.145.query, ...), custom_call_target="tpu_custom_call" | custom-call | bytes 59040000 | tf_op jit(solution)/shard_map/pallas_call | solution.py:563
  117.0 2.1 %collective-permute-done.28.refs_2_.refs_6_ = bf16[2,2,64,1408]{3,2,1,0:T(8,128)(2,1)S(1)} collective-permute-done((bf16[2,2,64,1408]{3,2,1,0:T(8,128)(2,1)S(1)}, bf16[2,2,64,1408]{3,2,1,0:T(8,128)(2,1)S(1)}, u32[]{:S(2)}, u32[]{:S(2)}) %collective-permute-start.28) | collective-permute-done | bytes 720928 | tf_op jit(solution)/shard_map/ppermute | solution.py:210
  119.0 1.0 collective-permute-done.29.refs_5_.refs_10_.refs_14_
  120.9 0.8 collective-permute-start.31
  121.7 1.2 collective-permute-start.33
  123.5 4.2 %shard_map.280 = (bf16[4,512,384]{2,1,0:T(8,128)(2,1)S(1)}, bf16[2,2,2,64,384]{4,3,2,1,0:T(8,128)(2,1)S(1)}, bf16[2,2,2,64,384]{4,3,2,1,0:T(8,128)(2,1)S(1)}, bf...) custom-call(s32[28]{0:T(128)S(1)} %stack.97.table, ...), custom_call_target="tpu_custom_call" | custom-call | bytes 22140000 | tf_op jit(solution)/shard_map/pallas_call | solution.py:754
  127.8 6.4 %collective-permute-done.33.p2 = bf16[2,128,256]{2,1,0:T(8,128)(2,1)S(1)} collective-permute-done((bf16[2,128,256]{2,1,0:T(8,128)(2,1)S(1)}, bf16[2,128,256]{2,1,0:T(8,128)(2,1)S(1)}, u32[]{:S(2)}, u32[]{:S(2)}) %collective-permute-start.33) | collective-permute-done | bytes 131104 | tf_op jit(solution)/shard_map/ppermute | solution.py:210
  134.1 1.2 collective-permute-start.35
  135.8 0.9 collective-permute-done.35.refs_1_
  137.4 0.8 collective-permute-start.41
  138.2 1.5 collective-permute-start.38
  139.7 1.2 collective-permute-start.37
  141.6 3.2 %collective-permute-start.40 = (bf16[64,1408]{1,0:T(8,128)(2,1)S(1)}, bf16[64,1408]{1,0:T(8,128)(2,1)S(1)}, u32[]{:S(2)}, u32[]{:S(2)}) collective-permute-start(bf16[64,1408]{1,0:T(8,128)(2,1)S(1)} %get-tuple-element.195), channel_id=1, source_target_pairs={{0,24},{4,28},{8,0},{12,4},{16,8},{20,12},{24,16},{28,20},{1,25},{... | collective-permute-start | bytes 540680 | tf_op jit(solution)/shard_map/ppermute | solution.py:963
  144.8 3.9 %shard_map.283 = (f32[256,512]{1,0:T(8,128)S(1)}, bf16[256,512]{1,0:T(8,128)(2,1)S(1)}, bf16[2,2,4,16,384]{4,3,2,1,0:T(8,128)(2,1)S(1)}, bf16[2,2,4,16,384]{4,3,2,1,0:T(8,128)(2,1)S(1)}) custom-call(s32[28]{0:T(128)S(1)} %stack.97.table, bf16[512,512]{1,0:T(8,128)(2,1)S(1)} %copy-done, bf16[512,512]{1,0:T(8,128)(2,1)S(1)} %collective-permute-done.cross, ...), custom_call_target="tpu_custom_call" | custom-call | bytes 25830000 | tf_op jit(solution)/shard_map/pallas_call | solution.py:815
  148.6 1.6 collective-permute-done.39.one
  150.2 1.0 collective-permute-done.40.three
  151.3 1.4 collective-permute-done.42.refs_1_.refs_9_
  153.2 2.2 %collective-permute-start.49 = (bf16[64,1408]{1,0:T(8,128)(2,1)S(1)}, bf16[64,1408]{1,0:T(8,128)(2,1)S(1)}, u32[]{:S(2)}, u32[]{:S(2)}) collective-permute-start(bf16[64,1408]{1,0:T(8,128)(2,1)S(1)} %get-tuple-element.194), channel_id=1, source_target_pairs={{0,16},{4,20},{8,24},{12,28},{16,0},{20,4},{24,8},{28,12},{1,17},{... | collective-permute-start | bytes 540680 | tf_op jit(solution)/shard_map/ppermute | solution.py:963
  155.4 1.2 collective-permute-start.46
  157.4 0.8 collective-permute-start.45
  158.1 5.7 %collective-permute-done.46.refs_2_.refs_10_ = bf16[2,4,16,384]{3,2,1,0:T(8,128)(2,1)S(1)} collective-permute-done((bf16[2,4,16,384]{3,2,1,0:T(8,128)(2,1)S(1)}, bf16[2,4,16,384]{3,2,1,0:T(8,128)(2,1)S(1)}, u32[]{:S(2)}, u32[]{:S(2)}) %collective-permute-start.46) | collective-permute-done | bytes 98336 | tf_op jit(solution)/shard_map/ppermute | solution.py:210
  164.6 0.9 shard_map.288
  165.6 2.4 %collective-permute-done.47.refs_11_ = bf16[4,16,384]{2,1,0:T(8,128)(2,1)S(1)} collective-permute-done((bf16[4,16,384]{2,1,0:T(8,128)(2,1)S(1)}, bf16[4,16,384]{2,1,0:T(8,128)(2,1)S(1)}, u32[]{:S(2)}, u32[]{:S(2)}) %collective-permute-start.47) | collective-permute-done | bytes 49184 | tf_op jit(solution)/shard_map/ppermute | solution.py:960
  168.6 2.3 %collective-permute-start.50 = (bf16[80,384]{1,0:T(8,128)(2,1)S(1)}, bf16[80,384]{1,0:T(8,128)(2,1)S(1)}, u32[]{:S(2)}, u32[]{:S(2)}) collective-permute-start(bf16[80,384]{1,0:T(8,128)(2,1)S(1)} %get-tuple-element.233), channel_id=1, source_target_pairs={{0,16},{4,20},{8,24},{12,28},{16,0},{20,4},{24,8},{28,12},{1,17},{... | collective-permute-start | bytes 184328 | tf_op jit(solution)/shard_map/ppermute | solution.py:963
  170.9 2.3 %collective-permute-start.51 = (bf16[80,384]{1,0:T(8,128)(2,1)S(1)}, bf16[80,384]{1,0:T(8,128)(2,1)S(1)}, u32[]{:S(2)}, u32[]{:S(2)}) collective-permute-start(bf16[80,384]{1,0:T(8,128)(2,1)S(1)} %get-tuple-element.234), channel_id=1, source_target_pairs={{0,24},{4,28},{8,0},{12,4},{16,8},{20,12},{24,16},{28,20},{1,25},{... | collective-permute-start | bytes 184328 | tf_op jit(solution)/shard_map/ppermute | solution.py:963
  173.3 1.0 pad_maximum_fusion
  175.1 0.8 shard_map.289
  (99 shorter events, 12.9 us)
Async XLA Ops:
  0.7 38.4 %copy-start = (bf16[512,512]{1,0:T(8,128)(2,1)S(1)}, bf16[512,512]{1,0:T(8,128)(2,1)}, u32[]{:S(2)}) copy-start(bf16[512,512]{1,0:T(8,128)(2,1)} %low_tok.5) | copy-start | bytes 1572868
  3.2 13.4 %collective-permute-start.8 = (bf16[1,80,384]{2,1,0:T(8,128)(2,1)}, bf16[1,80,384]{2,1,0:T(8,128)(2,1)S(1)}, u32[]{:S(2)}, u32[]{:S(2)}) collective-permute-start(bf16[1,80,384]{2,1,0:T(8,128)(2,1)} %bitcast.38), channel_id=1, source_target_pairs={{0,24},{4,28},{8,0},{12,4},{16,8},{20,12},{24,16},{28,20},{1,25},{... | collective-permute-start | bytes 184328 | tf_op jit(solution)/shard_map/ppermute | solution.py:963
  8.2 8.4 %collective-permute-start.7 = (bf16[1,80,384]{2,1,0:T(8,128)(2,1)}, bf16[1,80,384]{2,1,0:T(8,128)(2,1)S(1)}, u32[]{:S(2)}, u32[]{:S(2)}) collective-permute-start(bf16[1,80,384]{2,1,0:T(8,128)(2,1)} %bitcast.39), channel_id=1, source_target_pairs={{0,16},{4,20},{8,24},{12,28},{16,0},{20,4},{24,8},{28,12},{1,17},{... | collective-permute-start | bytes 184328 | tf_op jit(solution)/shard_map/ppermute | solution.py:963
  8.2 6.3 %collective-permute-start.1 = (bf16[1,80,384]{2,1,0:T(8,128)(2,1)}, bf16[1,80,384]{2,1,0:T(8,128)(2,1)S(1)}, u32[]{:S(2)}, u32[]{:S(2)}) collective-permute-start(bf16[1,80,384]{2,1,0:T(8,128)(2,1)} %bitcast.40), channel_id=1, source_target_pairs={{0,8},{4,12},{8,16},{12,20},{16,24},{20,28},{24,0},{28,4},{1,9},{5... | collective-permute-start | bytes 184328 | tf_op jit(solution)/shard_map/ppermute | solution.py:963
  9.2 16.6 %collective-permute-start = (bf16[512,512]{1,0:T(8,128)(2,1)}, bf16[512,512]{1,0:T(8,128)(2,1)S(1)}, u32[]{:S(2)}, u32[]{:S(2)}) collective-permute-start(bf16[512,512]{1,0:T(8,128)(2,1)} %get-tuple-element.131), channel_id=1, source_target_pairs={{0,3},{3,0},{1,2},{2,1},{4,7},{7,4},{5,6},{6,5},{8,11},{11,8},{9,1... | collective-permute-start | bytes 1572872 | tf_op jit(solution)/shard_map/ppermute | solution.py:214
  14.5 7.0 %collective-permute-start.4 = (bf16[1,64,1408]{2,1,0:T(8,128)(2,1)}, bf16[1,64,1408]{2,1,0:T(8,128)(2,1)S(1)}, u32[]{:S(2)}, u32[]{:S(2)}) collective-permute-start(bf16[1,64,1408]{2,1,0:T(8,128)(2,1)} %bitcast.43), channel_id=1, source_target_pairs={{0,24},{4,28},{8,0},{12,4},{16,8},{20,12},{24,16},{28,20},{1,25},{... | collective-permute-start | bytes 540680 | tf_op jit(solution)/shard_map/ppermute | solution.py:963
  15.7 10.2 %collective-permute-start.3 = (bf16[1,64,1408]{2,1,0:T(8,128)(2,1)}, bf16[1,64,1408]{2,1,0:T(8,128)(2,1)S(1)}, u32[]{:S(2)}, u32[]{:S(2)}) collective-permute-start(bf16[1,64,1408]{2,1,0:T(8,128)(2,1)} %bitcast.44), channel_id=1, source_target_pairs={{0,8},{4,12},{8,16},{12,20},{16,24},{20,28},{24,0},{28,4},{1,9},{5... | collective-permute-start | bytes 540680 | tf_op jit(solution)/shard_map/ppermute | solution.py:963
  16.6 4.9 %collective-permute-start.9 = (bf16[2,80,384]{2,1,0:T(8,128)(2,1)S(1)}, bf16[2,80,384]{2,1,0:T(8,128)(2,1)S(1)}, u32[]{:S(2)}, u32[]{:S(2)}) collective-permute-start(bf16[2,80,384]{2,1,0:T(8,128)(2,1)S(1)} %pad_maximum_fusion.2), channel_id=1, source_target_pairs={{0,4},{4,0},{8,12},{12,8},{16,20},{20,16},{24,28},{28,24},{1,5},{5... | collective-permute-start | bytes 368648 | tf_op jit(solution)/shard_map/ppermute | solution.py:960
  19.0 7.3 %collective-permute-start.2 = (bf16[2,80,384]{2,1,0:T(8,128)(2,1)S(1)}, bf16[2,80,384]{2,1,0:T(8,128)(2,1)S(1)}, u32[]{:S(2)}, u32[]{:S(2)}) collective-permute-start(bf16[2,80,384]{2,1,0:T(8,128)(2,1)S(1)} %pad_maximum_fusion.1), channel_id=1, source_target_pairs={{0,2},{2,0},{1,3},{3,1},{4,6},{6,4},{5,7},{7,5},{8,10},{10,8},{9,1... | collective-permute-start | bytes 368648 | tf_op jit(solution)/shard_map/ppermute | solution.py:210
  25.8 10.6 %copy-start.4 = (bf16[1,64,1408]{2,1,0:T(8,128)(2,1)}, bf16[1,64,1408]{2,1,0:T(8,128)(2,1)S(1)}, u32[]{:S(2)}) copy-start(bf16[1,64,1408]{2,1,0:T(8,128)(2,1)S(1)} %collective-permute-done.3) | copy-start | bytes 540676
  26.3 10.8 %collective-permute-start.5 = (bf16[4,80,384]{2,1,0:T(8,128)(2,1)S(1)}, bf16[4,80,384]{2,1,0:T(8,128)(2,1)S(1)}, u32[]{:S(2)}, u32[]{:S(2)}) collective-permute-start(bf16[4,80,384]{2,1,0:T(8,128)(2,1)S(1)} %constant_dynamic-update-slice_fusion.refs_0_), channel_id=1, source_target_pairs={{0,4},{4,0},{8,12},{12,8},{16,20},{20,16},{24,28},{28,24},{1,5},{5... | collective-permute-start | bytes 737288 | tf_op jit(solution)/shard_map/ppermute | solution.py:960
  27.9 9.3 %collective-permute-start.10 = (bf16[4,80,384]{2,1,0:T(8,128)(2,1)S(1)}, bf16[4,80,384]{2,1,0:T(8,128)(2,1)S(1)}, u32[]{:S(2)}, u32[]{:S(2)}) collective-permute-start(bf16[4,80,384]{2,1,0:T(8,128)(2,1)S(1)} %constant_dynamic-update-slice_fusion.3.refs_2_), channel_id=1, source_target_pairs={{0,2},{2,0},{1,3},{3,1},{4,6},{6,4},{5,7},{7,5},{8,10},{10,8},{9,1... | collective-permute-start | bytes 737288 | tf_op jit(solution)/shard_map/ppermute | solution.py:210
  29.1 7.4 %collective-permute-start.6 = (bf16[1,64,1408]{2,1,0:T(8,128)(2,1)S(1)}, bf16[1,64,1408]{2,1,0:T(8,128)(2,1)S(1)}, u32[]{:S(2)}, u32[]{:S(2)}) collective-permute-start(bf16[1,64,1408]{2,1,0:T(8,128)(2,1)S(1)} %collective-permute-done.3), channel_id=1, source_target_pairs={{0,8},{4,12},{8,16},{12,20},{16,24},{20,28},{24,0},{28,4},{1,9},{5... | collective-permute-start | bytes 540680 | tf_op jit(solution)/shard_map/ppermute | solution.py:963
  30.5 7.3 %collective-permute-start.11 = (bf16[4,80,384]{2,1,0:T(8,128)(2,1)S(1)}, bf16[4,80,384]{2,1,0:T(8,128)(2,1)S(1)}, u32[]{:S(2)}, u32[]{:S(2)}) collective-permute-start(bf16[4,80,384]{2,1,0:T(8,128)(2,1)S(1)} %constant_dynamic-update-slice_fusion.refs_0_), channel_id=1, source_target_pairs={{0,1},{1,0},{2,3},{3,2},{4,5},{5,4},{6,7},{7,6},{8,9},{9,8},{10,11... | collective-permute-start | bytes 737288 | tf_op jit(solution)/shard_map/ppermute | solution.py:206
  30.5 7.3 %collective-permute-start.13 = (bf16[4,80,384]{2,1,0:T(8,128)(2,1)S(1)}, bf16[4,80,384]{2,1,0:T(8,128)(2,1)S(1)}, u32[]{:S(2)}, u32[]{:S(2)}) collective-permute-start(bf16[4,80,384]{2,1,0:T(8,128)(2,1)S(1)} %constant_dynamic-update-slice_fusion.3.refs_2_), channel_id=1, source_target_pairs={{0,1},{1,0},{2,3},{3,2},{4,5},{5,4},{6,7},{7,6},{8,9},{9,8},{10,11... | collective-permute-start | bytes 737288 | tf_op jit(solution)/shard_map/ppermute | solution.py:206
  36.5 0.7 copy-start.6
  37.1 1.5 collective-permute-start.12
  37.1 1.9 %collective-permute-start.14 = (bf16[4,80,384]{2,1,0:T(8,128)(2,1)S(1)}, bf16[4,80,384]{2,1,0:T(8,128)(2,1)S(1)}, u32[]{:S(2)}, u32[]{:S(2)}) collective-permute-start(bf16[4,80,384]{2,1,0:T(8,128)(2,1)S(1)} %collective-permute-done.10.refs_3_), channel_id=1, source_target_pairs={{0,1},{1,0},{2,3},{3,2},{4,5},{5,4},{6,7},{7,6},{8,9},{9,8},{10,11... | collective-permute-start | bytes 737288 | tf_op jit(solution)/shard_map/ppermute | solution.py:206
  37.8 3.7 %copy-start.3 = (bf16[64,1408]{1,0:T(8,128)(2,1)S(1)}, bf16[64,1408]{1,0:T(8,128)(2,1)}, u32[]{:S(2)}) copy-start(bf16[64,1408]{1,0:T(8,128)(2,1)} %get-tuple-element.134) | copy-start | bytes 540676
  37.8 3.7 %copy-start.5 = (bf16[1,64,1408]{2,1,0:T(8,128)(2,1)S(1)}, bf16[1,64,1408]{2,1,0:T(8,128)(2,1)}, u32[]{:S(2)}) copy-start(bf16[1,64,1408]{2,1,0:T(8,128)(2,1)} %copy-done.4) | copy-start | bytes 540676
  37.8 5.1 %copy-start.7 = (bf16[1,64,1408]{2,1,0:T(8,128)(2,1)S(1)}, bf16[1,64,1408]{2,1,0:T(8,128)(2,1)}, u32[]{:S(2)}) copy-start(bf16[1,64,1408]{2,1,0:T(8,128)(2,1)} %copy-done.6) | copy-start | bytes 540676
  41.6 11.3 %collective-permute-start.18 = (bf16[2,64,1408]{2,1,0:T(8,128)(2,1)S(1)}, bf16[2,64,1408]{2,1,0:T(8,128)(2,1)S(1)}, u32[]{:S(2)}, u32[]{:S(2)}) collective-permute-start(bf16[2,64,1408]{2,1,0:T(8,128)(2,1)S(1)} %get-tuple-element.252), channel_id=1, source_target_pairs={{0,2},{2,0},{1,3},{3,1},{4,6},{6,4},{5,7},{7,5},{8,10},{10,8},{9,1... | collective-permute-start | bytes 1081352 | tf_op jit(solution)/shard_map/ppermute | solution.py:210
  43.0 12.0 %collective-permute-start.20 = (bf16[2,64,1408]{2,1,0:T(8,128)(2,1)S(1)}, bf16[2,64,1408]{2,1,0:T(8,128)(2,1)S(1)}, u32[]{:S(2)}, u32[]{:S(2)}) collective-permute-start(bf16[2,64,1408]{2,1,0:T(8,128)(2,1)S(1)} %get-tuple-element.248), channel_id=1, source_target_pairs={{0,4},{4,0},{8,12},{12,8},{16,20},{20,16},{24,28},{28,24},{1,5},{5... | collective-permute-start | bytes 1081352 | tf_op jit(solution)/shard_map/ppermute | solution.py:960
  43.6 11.3 %collective-permute-start.16 = (bf16[512,128]{1,0:T(8,128)(2,1)S(1)}, bf16[512,128]{1,0:T(8,128)(2,1)S(1)}, u32[]{:S(2)}, u32[]{:S(2)}) collective-permute-start(bf16[512,128]{1,0:T(8,128)(2,1)S(1)} %get-tuple-element.141.kv0), channel_id=1, source_target_pairs={{0,2},{2,0},{1,3},{3,1},{4,6},{6,4},{5,7},{7,5},{8,10},{10,8},{9,1... | collective-permute-start | bytes 393224 | tf_op jit(solution)/shard_map/ppermute | solution.py:210
  52.9 23.9 %copy-start.1 = (bf16[512,512]{1,0:T(8,128)(2,1)S(1)}, bf16[512,512]{1,0:T(8,128)(2,1)}, u32[]{:S(2)}) copy-start(bf16[512,512]{1,0:T(8,128)(2,1)} %low_cot.1) | copy-start | bytes 1572868
  52.9 16.7 %collective-permute-start.22 = (bf16[4,64,1408]{2,1,0:T(8,128)(2,1)S(1)}, bf16[4,64,1408]{2,1,0:T(8,128)(2,1)S(1)}, u32[]{:S(2)}, u32[]{:S(2)}) collective-permute-start(bf16[4,64,1408]{2,1,0:T(8,128)(2,1)S(1)} %constant_dynamic-update-slice_fusion.10.refs_0_), channel_id=1, source_target_pairs={{0,1},{1,0},{2,3},{3,2},{4,5},{5,4},{6,7},{7,6},{8,9},{9,8},{10,11... | collective-permute-start | bytes 2162696 | tf_op jit(solution)/shard_map/ppermute | solution.py:206
  53.0 18.6 %collective-permute-start.19 = (bf16[4,64,1408]{2,1,0:T(8,128)(2,1)S(1)}, bf16[4,64,1408]{2,1,0:T(8,128)(2,1)S(1)}, u32[]{:S(2)}, u32[]{:S(2)}) collective-permute-start(bf16[4,64,1408]{2,1,0:T(8,128)(2,1)S(1)} %constant_dynamic-update-slice_fusion.10.refs_0_), channel_id=1, source_target_pairs={{0,4},{4,0},{8,12},{12,8},{16,20},{20,16},{24,28},{28,24},{1,5},{5... | collective-permute-start | bytes 2162696 | tf_op jit(solution)/shard_map/ppermute | solution.py:960
  55.0 16.6 %collective-permute-start.23 = (bf16[4,64,1408]{2,1,0:T(8,128)(2,1)S(1)}, bf16[4,64,1408]{2,1,0:T(8,128)(2,1)S(1)}, u32[]{:S(2)}, u32[]{:S(2)}) collective-permute-start(bf16[4,64,1408]{2,1,0:T(8,128)(2,1)S(1)} %constant_dynamic-update-slice_fusion.13.refs_2_), channel_id=1, source_target_pairs={{0,1},{1,0},{2,3},{3,2},{4,5},{5,4},{6,7},{7,6},{8,9},{9,8},{10,11... | collective-permute-start | bytes 2162696 | tf_op jit(solution)/shard_map/ppermute | solution.py:206
  55.0 18.6 %collective-permute-start.21 = (bf16[4,64,1408]{2,1,0:T(8,128)(2,1)S(1)}, bf16[4,64,1408]{2,1,0:T(8,128)(2,1)S(1)}, u32[]{:S(2)}, u32[]{:S(2)}) collective-permute-start(bf16[4,64,1408]{2,1,0:T(8,128)(2,1)S(1)} %constant_dynamic-update-slice_fusion.13.refs_2_), channel_id=1, source_target_pairs={{0,2},{2,0},{1,3},{3,1},{4,6},{6,4},{5,7},{7,5},{8,10},{10,8},{9,1... | collective-permute-start | bytes 2162696 | tf_op jit(solution)/shard_map/ppermute | solution.py:210
  56.4 1.3 collective-permute-start.15
  57.7 1.3 collective-permute-start.17
  73.6 2.2 %collective-permute-start.24 = (bf16[4,64,1408]{2,1,0:T(8,128)(2,1)S(1)}, bf16[4,64,1408]{2,1,0:T(8,128)(2,1)S(1)}, u32[]{:S(2)}, u32[]{:S(2)}) collective-permute-start(bf16[4,64,1408]{2,1,0:T(8,128)(2,1)S(1)} %collective-permute-done.19.refs_1_), channel_id=1, source_target_pairs={{0,1},{1,0},{2,3},{3,2},{4,5},{5,4},{6,7},{7,6},{8,9},{9,8},{10,11... | collective-permute-start | bytes 2162696 | tf_op jit(solution)/shard_map/ppermute | solution.py:206
  73.6 3.2 %collective-permute-start.25 = (bf16[4,64,1408]{2,1,0:T(8,128)(2,1)S(1)}, bf16[4,64,1408]{2,1,0:T(8,128)(2,1)S(1)}, u32[]{:S(2)}, u32[]{:S(2)}) collective-permute-start(bf16[4,64,1408]{2,1,0:T(8,128)(2,1)S(1)} %collective-permute-done.21.refs_3_), channel_id=1, source_target_pairs={{0,1},{1,0},{2,3},{3,2},{4,5},{5,4},{6,7},{7,6},{8,9},{9,8},{10,11... | collective-permute-start | bytes 2162696 | tf_op jit(solution)/shard_map/ppermute | solution.py:206
  93.8 6.6 %collective-permute-start.26 = (bf16[2,2,2,64,1408]{4,3,2,1,0:T(8,128)(2,1)}, bf16[2,2,2,64,1408]{4,3,2,1,0:T(8,128)(2,1)S(1)}, u32[]{:S(2)}, u32[]{:S(2)}) collective-permute-start(bf16[2,2,2,64,1408]{4,3,2,1,0:T(8,128)(2,1)} %get-tuple-element.160), channel_id=1, source_target_pairs={{0,1},{1,0},{2,3},{3,2},{4,5},{5,4},{6,7},{7,6},{8,9},{9,8},{10,11... | collective-permute-start | bytes 4325384 | tf_op jit(solution)/shard_map/ppermute | solution.py:206
  94.0 6.5 %collective-permute-start.27 = (bf16[2,2,2,64,1408]{4,3,2,1,0:T(8,128)(2,1)}, bf16[2,2,2,64,1408]{4,3,2,1,0:T(8,128)(2,1)S(1)}, u32[]{:S(2)}, u32[]{:S(2)}) collective-permute-start(bf16[2,2,2,64,1408]{4,3,2,1,0:T(8,128)(2,1)} %get-tuple-element.165), channel_id=1, source_target_pairs={{0,1},{1,0},{2,3},{3,2},{4,5},{5,4},{6,7},{7,6},{8,9},{9,8},{10,11... | collective-permute-start | bytes 4325384 | tf_op jit(solution)/shard_map/ppermute | solution.py:206
  94.3 1.4 copy-start.2
  100.8 18.3 %collective-permute-start.28 = (bf16[2,2,64,1408]{3,2,1,0:T(8,128)(2,1)S(1)}, bf16[2,2,64,1408]{3,2,1,0:T(8,128)(2,1)S(1)}, u32[]{:S(2)}, u32[]{:S(2)}) collective-permute-start(bf16[2,2,64,1408]{3,2,1,0:T(8,128)(2,1)S(1)} %get-tuple-element.167), channel_id=1, source_target_pairs={{0,2},{2,0},{1,3},{3,1},{4,6},{6,4},{5,7},{7,5},{8,10},{10,8},{9,1... | collective-permute-start | bytes 2162696 | tf_op jit(solution)/shard_map/ppermute | solution.py:210
  102.1 17.9 %collective-permute-start.29 = (bf16[2,2,64,1408]{3,2,1,0:T(8,128)(2,1)S(1)}, bf16[2,2,64,1408]{3,2,1,0:T(8,128)(2,1)S(1)}, u32[]{:S(2)}, u32[]{:S(2)}) collective-permute-start(bf16[2,2,64,1408]{3,2,1,0:T(8,128)(2,1)S(1)} %get-tuple-element.169), channel_id=1, source_target_pairs={{0,4},{4,0},{8,12},{12,8},{16,20},{20,16},{24,28},{28,24},{1,5},{5... | collective-permute-start | bytes 2162696 | tf_op jit(solution)/shard_map/ppermute | solution.py:960
  120.3 13.9 %collective-permute-start.30 = (bf16[2,64,1408]{2,1,0:T(8,128)(2,1)S(1)}, bf16[2,64,1408]{2,1,0:T(8,128)(2,1)S(1)}, u32[]{:S(2)}, u32[]{:S(2)}) collective-permute-start(bf16[2,64,1408]{2,1,0:T(8,128)(2,1)S(1)} %get-tuple-element.175), channel_id=1, source_target_pairs={{0,4},{4,0},{8,12},{12,8},{16,20},{20,16},{24,28},{28,24},{1,5},{5... | collective-permute-start | bytes 1081352 | tf_op jit(solution)/shard_map/ppermute | solution.py:960
  120.9 13.3 %collective-permute-start.31 = (bf16[2,64,1408]{2,1,0:T(8,128)(2,1)S(1)}, bf16[2,64,1408]{2,1,0:T(8,128)(2,1)S(1)}, u32[]{:S(2)}, u32[]{:S(2)}) collective-permute-start(bf16[2,64,1408]{2,1,0:T(8,128)(2,1)S(1)} %get-tuple-element.176), channel_id=1, source_target_pairs={{0,2},{2,0},{1,3},{3,1},{4,6},{6,4},{5,7},{7,5},{8,10},{10,8},{9,1... | collective-permute-start | bytes 1081352 | tf_op jit(solution)/shard_map/ppermute | solution.py:210
  121.7 6.1 %collective-permute-start.32 = (bf16[2,128,256]{2,1,0:T(8,128)(2,1)S(1)}, bf16[2,128,256]{2,1,0:T(8,128)(2,1)S(1)}, u32[]{:S(2)}, u32[]{:S(2)}) collective-permute-start(bf16[2,128,256]{2,1,0:T(8,128)(2,1)S(1)} %get-tuple-element.180), channel_id=1, source_target_pairs={{0,1},{1,0},{2,3},{3,2},{4,5},{5,4},{6,7},{7,6},{8,9},{9,8},{10,11... | collective-permute-start | bytes 393224 | tf_op jit(solution)/shard_map/ppermute | solution.py:206
  121.7 12.5 %collective-permute-start.33 = (bf16[2,128,256]{2,1,0:T(8,128)(2,1)S(1)}, bf16[2,128,256]{2,1,0:T(8,128)(2,1)S(1)}, u32[]{:S(2)}, u32[]{:S(2)}) collective-permute-start(bf16[2,128,256]{2,1,0:T(8,128)(2,1)S(1)} %get-tuple-element.181), channel_id=1, source_target_pairs={{0,2},{2,0},{1,3},{3,1},{4,6},{6,4},{5,7},{7,5},{8,10},{10,8},{9,1... | collective-permute-start | bytes 393224 | tf_op jit(solution)/shard_map/ppermute | solution.py:210
  122.9 11.2 %collective-permute-start.34 = (bf16[2,128,256]{2,1,0:T(8,128)(2,1)S(1)}, bf16[2,128,256]{2,1,0:T(8,128)(2,1)S(1)}, u32[]{:S(2)}, u32[]{:S(2)}) collective-permute-start(bf16[2,128,256]{2,1,0:T(8,128)(2,1)S(1)} %get-tuple-element.182), channel_id=1, source_target_pairs={{0,3},{3,0},{1,2},{2,1},{4,7},{7,4},{5,6},{6,5},{8,11},{11,8},{9,1... | collective-permute-start | bytes 393224 | tf_op jit(solution)/shard_map/ppermute | solution.py:214
  134.1 2.6 %collective-permute-start.35 = (bf16[2,2,2,64,384]{4,3,2,1,0:T(8,128)(2,1)S(1)}, bf16[2,2,2,64,384]{4,3,2,1,0:T(8,128)(2,1)S(1)}, u32[]{:S(2)}, u32[]{:S(2)}) collective-permute-start(bf16[2,2,2,64,384]{4,3,2,1,0:T(8,128)(2,1)S(1)} %get-tuple-element.189), channel_id=1, source_target_pairs={{0,1},{1,0},{2,3},{3,2},{4,5},{5,4},{6,7},{7,6},{8,9},{9,8},{10,11... | collective-permute-start | bytes 1179656 | tf_op jit(solution)/shard_map/ppermute | solution.py:206
  135.4 1.9 %collective-permute-start.36 = (bf16[2,2,2,64,384]{4,3,2,1,0:T(8,128)(2,1)S(1)}, bf16[2,2,2,64,384]{4,3,2,1,0:T(8,128)(2,1)S(1)}, u32[]{:S(2)}, u32[]{:S(2)}) collective-permute-start(bf16[2,2,2,64,384]{4,3,2,1,0:T(8,128)(2,1)S(1)} %get-tuple-element.198), channel_id=1, source_target_pairs={{0,1},{1,0},{2,3},{3,2},{4,5},{5,4},{6,7},{7,6},{8,9},{9,8},{10,11... | collective-permute-start | bytes 1179656 | tf_op jit(solution)/shard_map/ppermute | solution.py:206
  137.4 13.8 %collective-permute-start.41 = (bf16[256,512]{1,0:T(8,128)(2,1)S(1)}, bf16[256,512]{1,0:T(8,128)(2,1)S(1)}, u32[]{:S(2)}, u32[]{:S(2)}) collective-permute-start(bf16[256,512]{1,0:T(8,128)(2,1)S(1)} %get-tuple-element.216), channel_id=1, source_target_pairs={{0,3},{3,0},{1,2},{2,1},{4,7},{7,4},{5,6},{6,5},{8,11},{11,8},{9,1... | collective-permute-start | bytes 786440 | tf_op jit(solution)/shard_map/ppermute | solution.py:214
  138.2 13.0 %collective-permute-start.38 = (bf16[2,2,64,384]{3,2,1,0:T(8,128)(2,1)S(1)}, bf16[2,2,64,384]{3,2,1,0:T(8,128)(2,1)S(1)}, u32[]{:S(2)}, u32[]{:S(2)}) collective-permute-start(bf16[2,2,64,384]{3,2,1,0:T(8,128)(2,1)S(1)} %get-tuple-element.201), channel_id=1, source_target_pairs={{0,4},{4,0},{8,12},{12,8},{16,20},{20,16},{24,28},{28,24},{1,5},{5... | collective-permute-start | bytes 589832 | tf_op jit(solution)/shard_map/ppermute | solution.py:960
  139.7 11.5 %collective-permute-start.37 = (bf16[2,2,64,384]{3,2,1,0:T(8,128)(2,1)S(1)}, bf16[2,2,64,384]{3,2,1,0:T(8,128)(2,1)S(1)}, u32[]{:S(2)}, u32[]{:S(2)}) collective-permute-start(bf16[2,2,64,384]{3,2,1,0:T(8,128)(2,1)S(1)} %get-tuple-element.200), channel_id=1, source_target_pairs={{0,2},{2,0},{1,3},{3,1},{4,6},{6,4},{5,7},{7,5},{8,10},{10,8},{9,1... | collective-permute-start | bytes 589832 | tf_op jit(solution)/shard_map/ppermute | solution.py:210
  140.9 9.3 %collective-permute-start.39 = (bf16[64,1408]{1,0:T(8,128)(2,1)S(1)}, bf16[64,1408]{1,0:T(8,128)(2,1)S(1)}, u32[]{:S(2)}, u32[]{:S(2)}) collective-permute-start(bf16[64,1408]{1,0:T(8,128)(2,1)S(1)} %get-tuple-element.193), channel_id=1, source_target_pairs={{0,8},{4,12},{8,16},{12,20},{16,24},{20,28},{24,0},{28,4},{1,9},{5... | collective-permute-start | bytes 540680 | tf_op jit(solution)/shard_map/ppermute | solution.py:963
  141.6 9.6 %collective-permute-start.40 = (bf16[64,1408]{1,0:T(8,128)(2,1)S(1)}, bf16[64,1408]{1,0:T(8,128)(2,1)S(1)}, u32[]{:S(2)}, u32[]{:S(2)}) collective-permute-start(bf16[64,1408]{1,0:T(8,128)(2,1)S(1)} %get-tuple-element.195), channel_id=1, source_target_pairs={{0,24},{4,28},{8,0},{12,4},{16,8},{20,12},{24,16},{28,20},{1,25},{... | collective-permute-start | bytes 540680 | tf_op jit(solution)/shard_map/ppermute | solution.py:963
  151.2 1.5 collective-permute-start.42
  152.7 20.4 %collective-permute-start.43 = (bf16[256,512]{1,0:T(8,128)(2,1)S(1)}, bf16[256,512]{1,0:T(8,128)(2,1)S(1)}, u32[]{:S(2)}, u32[]{:S(2)}) collective-permute-start(bf16[256,512]{1,0:T(8,128)(2,1)S(1)} %get-tuple-element.222), channel_id=1, source_target_pairs={{0,3},{3,0},{1,2},{2,1},{4,7},{7,4},{5,6},{6,5},{8,11},{11,8},{9,1... | collective-permute-start | bytes 786440 | tf_op jit(solution)/shard_map/ppermute | solution.py:214
  153.2 11.3 %collective-permute-start.49 = (bf16[64,1408]{1,0:T(8,128)(2,1)S(1)}, bf16[64,1408]{1,0:T(8,128)(2,1)S(1)}, u32[]{:S(2)}, u32[]{:S(2)}) collective-permute-start(bf16[64,1408]{1,0:T(8,128)(2,1)S(1)} %get-tuple-element.194), channel_id=1, source_target_pairs={{0,16},{4,20},{8,24},{12,28},{16,0},{20,4},{24,8},{28,12},{1,17},{... | collective-permute-start | bytes 540680 | tf_op jit(solution)/shard_map/ppermute | solution.py:963
  155.4 8.4 %collective-permute-start.46 = (bf16[2,4,16,384]{3,2,1,0:T(8,128)(2,1)S(1)}, bf16[2,4,16,384]{3,2,1,0:T(8,128)(2,1)S(1)}, u32[]{:S(2)}, u32[]{:S(2)}) collective-permute-start(bf16[2,4,16,384]{3,2,1,0:T(8,128)(2,1)S(1)} %shard_map.284), channel_id=1, source_target_pairs={{0,2},{2,0},{1,3},{3,1},{4,6},{6,4},{5,7},{7,5},{8,10},{10,8},{9,1... | collective-permute-start | bytes 294920 | tf_op jit(solution)/shard_map/ppermute | solution.py:210
  156.8 8.7 %collective-permute-start.44 = (bf16[2,64,384]{2,1,0:T(8,128)(2,1)S(1)}, bf16[2,64,384]{2,1,0:T(8,128)(2,1)S(1)}, u32[]{:S(2)}, u32[]{:S(2)}) collective-permute-start(bf16[2,64,384]{2,1,0:T(8,128)(2,1)S(1)} %get-tuple-element.225), channel_id=1, source_target_pairs={{0,4},{4,0},{8,12},{12,8},{16,20},{20,16},{24,28},{28,24},{1,5},{5... | collective-permute-start | bytes 294920 | tf_op jit(solution)/shard_map/ppermute | solution.py:960
  157.4 8.3 %collective-permute-start.45 = (bf16[2,64,384]{2,1,0:T(8,128)(2,1)S(1)}, bf16[2,64,384]{2,1,0:T(8,128)(2,1)S(1)}, u32[]{:S(2)}, u32[]{:S(2)}) collective-permute-start(bf16[2,64,384]{2,1,0:T(8,128)(2,1)S(1)} %get-tuple-element.226), channel_id=1, source_target_pairs={{0,2},{2,0},{1,3},{3,1},{4,6},{6,4},{5,7},{7,5},{8,10},{10,8},{9,1... | collective-permute-start | bytes 294920 | tf_op jit(solution)/shard_map/ppermute | solution.py:210
  163.9 4.2 %collective-permute-start.47 = (bf16[4,16,384]{2,1,0:T(8,128)(2,1)S(1)}, bf16[4,16,384]{2,1,0:T(8,128)(2,1)S(1)}, u32[]{:S(2)}, u32[]{:S(2)}) collective-permute-start(bf16[4,16,384]{2,1,0:T(8,128)(2,1)S(1)} %shard_map.286), channel_id=1, source_target_pairs={{0,4},{4,0},{8,12},{12,8},{16,20},{20,16},{24,28},{28,24},{1,5},{5... | collective-permute-start | bytes 147464 | tf_op jit(solution)/shard_map/ppermute | solution.py:960
  164.5 3.7 %copy-start.8 = (bf16[512,512]{1,0:T(8,128)(2,1)}, bf16[512,512]{1,0:T(8,128)(2,1)S(1)}, u32[]{:S(2)}) copy-start(bf16[512,512]{1,0:T(8,128)(2,1)S(1)} %constant_dynamic-update-slice_fusion.16) | copy-start | bytes 1572868
  168.2 6.2 %collective-permute-start.48 = (bf16[80,384]{1,0:T(8,128)(2,1)S(1)}, bf16[80,384]{1,0:T(8,128)(2,1)S(1)}, u32[]{:S(2)}, u32[]{:S(2)}) collective-permute-start(bf16[80,384]{1,0:T(8,128)(2,1)S(1)} %get-tuple-element.228), channel_id=1, source_target_pairs={{0,8},{4,12},{8,16},{12,20},{16,24},{20,28},{24,0},{28,4},{1,9},{5... | collective-permute-start | bytes 184328 | tf_op jit(solution)/shard_map/ppermute | solution.py:963
  168.6 5.9 %collective-permute-start.50 = (bf16[80,384]{1,0:T(8,128)(2,1)S(1)}, bf16[80,384]{1,0:T(8,128)(2,1)S(1)}, u32[]{:S(2)}, u32[]{:S(2)}) collective-permute-start(bf16[80,384]{1,0:T(8,128)(2,1)S(1)} %get-tuple-element.233), channel_id=1, source_target_pairs={{0,16},{4,20},{8,24},{12,28},{16,0},{20,4},{24,8},{28,12},{1,17},{... | collective-permute-start | bytes 184328 | tf_op jit(solution)/shard_map/ppermute | solution.py:963
  170.9 4.2 %collective-permute-start.51 = (bf16[80,384]{1,0:T(8,128)(2,1)S(1)}, bf16[80,384]{1,0:T(8,128)(2,1)S(1)}, u32[]{:S(2)}, u32[]{:S(2)}) collective-permute-start(bf16[80,384]{1,0:T(8,128)(2,1)S(1)} %get-tuple-element.234), channel_id=1, source_target_pairs={{0,24},{4,28},{8,0},{12,4},{16,8},{20,12},{24,16},{28,20},{1,25},{... | collective-permute-start | bytes 184328 | tf_op jit(solution)/shard_map/ppermute | solution.py:963

commit v4 on v3

--- a/solution.py
+++ b/solution.py
@@ -159,10 +159,10 @@
     return outs[0], outs[1], outs[2], outs[3], [v.reshape(-1) for v in outs[4:9]], outs[9].reshape(-1)
 
 
-def unpack_second_kernel(kept, one, two, three, go, gup, gdown, total, wide):
+def unpack_second_kernel(kept, one, three, go, gup, gdown, total, wide):
     experts = go.shape[0]
     group, hidden = experts * HEAD, gup.shape[1]
-    total[...] = sum_four(kept[...], one[...], two[...], three[...])
+    total[...] = kept[...].astype(F32) + one[...].astype(F32) + three[...].astype(F32)
     gup[...] = total[:, group : group + hidden]
     wide[...] = jnp.zeros_like(wide)
     wide[0:ROWS, :] = total[:, 0:group]
@@ -172,7 +172,7 @@
     gdown[...] = total[:, group + hidden :]
 
 
-def unpack_second(kept, one, two, three, experts, hidden):
+def unpack_second(kept, one, three, experts, hidden):
     group = experts * HEAD
     return pl.pallas_call(
         unpack_second_kernel,
@@ -187,7 +187,7 @@
             pltpu.VMEM((LANES, group), F32),
         ],
         compiler_params=params(8),
-    )(kept, one, two, three)
+    )(kept, one, three)
 
 
 def axis_moves(dp):
@@ -243,29 +243,6 @@
         out_shape=tuple(shaped(shape, BF16) for shape in shapes),
         compiler_params=params(16),
     )(*[array for array, _ in terms])
-
-
-def add_ends(side_a, side_b, tiny):
-    arrays = [*side_a, *side_b, *tiny]
-
-    def kernel(*refs):
-        ins, outs = refs[:12], refs[12:]
-
-        def total(terms, s):
-            kept, got, near, last = terms
-            return sum_four(kept[0, 0, s], got[0, 0, s], near[0, s], last[s]).astype(BF16)
-
-        for s, out in enumerate(outs):
-            out[0:ROWS, :] = total(ins[0:4] if s < 2 else ins[4:8], s % 2)
-            out[ROWS:, :] = total(ins[8:12], s)
-
-    shape = (ROWS + TINY, side_a[0].shape[-1])
-    return pl.pallas_call(
-        kernel,
-        cost_estimate=cost(1.5),
-        out_shape=(shaped(shape, BF16),) * 4,
-        compiler_params=params(16),
-    )(*arrays)
 
 
 def place_blocks(table, pieces, row_from, rows, put):
@@ -502,7 +479,7 @@
 def attend_back_kernel(
     table, query, grad, all_totals, gates, gate_grads, kv0, kv1, kv2, kv3, grad_query, *refs
 ):
-    outs, (keys, values, key_sum, value_sum, query_sum, query_t, grad_t, probs, scored, totals, inner) = refs[:4], refs[4:]
+    pair_outs, (keys, values, key_sum, value_sum, query_sum, query_t, grad_t, probs, scored, totals, inner) = refs[:2], refs[2:]
     block = pl.program_id(0)
     ways = query.shape[0]
 
@@ -547,26 +524,27 @@
 
     @pl.when(block == pl.num_programs(0) - 1)
     def _():
-        for p, out in enumerate(outs):
+        for p in range(4):
+            out = pair_outs[p % 2]
             for h in range(2):
                 at = table[POS_AT + 2 * p + h]
                 key_part, value_part = key_sum[at], value_sum[at]
-                out[h, 0:HEAD, :] = ((key_part[0:HEAD] + key_part[HEAD:]) * 0.125).astype(BF16)
-                out[h, HEAD:, :] = (value_part[0:HEAD] + value_part[HEAD:]).astype(BF16)
+                out[p // 2, h, 0:HEAD, :] = ((key_part[0:HEAD] + key_part[HEAD:]) * 0.125).astype(BF16)
+                out[p // 2, h, HEAD:, :] = (value_part[0:HEAD] + value_part[HEAD:]).astype(BF16)
 
 
 def attend_back_stage(table, query, grad, totals, gates, gate_grads, pairs, seq):
     ways, rows, _ = query.shape
     kv_spec = pl.BlockSpec((rows, LANES), lambda b: (0, 0))
     spec = pl.BlockSpec((ways, HALF, LANES), lambda b: (0, b, 0))
-    pair_spec = pl.BlockSpec((2, LANES, HALF), lambda b: (0, 0, 0))
+    pair_spec = pl.BlockSpec((2, 2, LANES, HALF), lambda b: (0, 0, 0, 0))
     return pl.pallas_call(
         attend_back_kernel,
         cost_estimate=cost(16),
         grid=(rows // HALF,),
         in_specs=[smem_spec()] + [spec] * 2 + [pl.BlockSpec((HALF, LANES), lambda b: (b, 0))] * 3 + [kv_spec] * 4,
-        out_specs=(spec,) + (pair_spec,) * 4,
-        out_shape=(shaped((ways, rows, LANES), BF16),) + (shaped((2, LANES, HALF), BF16),) * 4,
+        out_specs=(spec,) + (pair_spec,) * 2,
+        out_shape=(shaped((ways, rows, LANES), BF16),) + (shaped((2, 2, LANES, HALF), BF16),) * 2,
         scratch_shapes=[
             pltpu.VMEM((seq, LANES), BF16),
             pltpu.VMEM((seq, LANES), BF16),
@@ -596,11 +574,11 @@
     for s in range(4):
         for x in range(2):
             block = grads[(2 * s + x) * ROWS : (2 * s + x + 1) * ROWS, :].astype(BF16)
-            if s < 2:
-                out, place = (send_a if core else keep_a), (y, x, s)
+            if s in (1, 2):
+                out, place = (send_a if core else keep_a), (y, x, s - 1)
             else:
-                out, place = (send_b if core else keep_b), (x, y, s - 2)
-            out[place[0], place[1], place[2], :, column_to : column_to + wide] = block
+                out, place = (send_b if core else keep_b), (x, y, s // 2)
+            out[place[0], place[1], place[2], 0:ROWS, column_to : column_to + wide] = block
 
 
 def middle_kernel(table, low_tok, low_cot, cross, heads, gates, routes, vectors, up_bias, *refs):
@@ -733,8 +711,7 @@
     )(table, tokens, cot, cross, heads, gates, routes, vectors, up_bias, *pieces)
 
 
-def spread_kernel(table, grad_query, normed, routes, spread, *refs):
-    blocks, (turned, normed_t) = refs[:4], refs[4:]
+def spread_kernel(table, grad_query, normed, routes, spread, grads, turned, normed_t):
     ways, rows, _ = grad_query.shape
 
     def expand(at):
@@ -744,18 +721,17 @@
     turned[...] = normed[...].T
     in_order(table, turned, normed_t)
     for slot in range(4):
-        put_blocks(nn(normed_t[...], spread[slot]), blocks, slot, 0)
+        grads[slot] = nn(normed_t[...], spread[slot]).astype(BF16)
 
 
 def spread_stage(table, grad_query, normed, routes, group):
     rows, width = normed.shape
-    block = shaped((2, 2, 2, ROWS, group), BF16)
     vmem = pl.BlockSpec(memory_space=pltpu.VMEM)
     return pl.pallas_call(
         spread_kernel,
         cost_estimate=cost(6),
         in_specs=[smem_spec()] + [vmem] * 3,
-        out_shape=(shaped((4, rows, group), BF16), block, block, block, block),
+        out_shape=(shaped((4, rows, group), BF16), shaped((4, width, group), BF16)),
         scratch_shapes=[pltpu.VMEM((width, rows), BF16), pltpu.VMEM((width, rows), BF16)],
         compiler_params=params(16),
     )(table, grad_query, normed, routes)
@@ -763,12 +739,14 @@
 
 def last_kernel(
     table, low_tok, cross, grad_mid, spread, normed, routes, gates, grad_gate, weight, small,
-    vectors, sums, bias_grad, p0, p1, p2, p3, low_out, high_out, keep, send, pair_grad, tiny, wide, extra
+    vectors, sums, bias_grad, pair_keep, pair_got, pair_far, grads, low_out, high_out, *refs
 ):
+    blocks, (pair_grad, tiny, wide, extra) = refs[:4], refs[4:]
+    keep_a, keep_b, send_a, send_b = blocks
     rows = normed.shape[0]
     ways = routes.shape[1]
     for h in range(2):
-        total = sum_four(p0[h], p1[h], p2[h], p3[h])
+        total = pair_keep[0, h].astype(F32) + pair_got[0, h].astype(F32) + pair_far[h].astype(F32)
         pair_grad[h * HALF : (h + 1) * HALF, :] = total.T.astype(BF16)
     gate = gates[...]
     gate_grad = grad_gate[...]
@@ -798,25 +776,30 @@
         extra[TINY * i : TINY * i + 1, 0:HEAD] = bias_grad[i // 8 : i // 8 + 1, (i % 8) * HEAD : (i % 8 + 1) * HEAD]
     tiny[:, 2 * LANES : 3 * LANES] = extra[...].astype(BF16)
     for slot in range(4):
-        out = send if slot % 2 else keep
+        y, core = slot // 2, slot % 2
+        put_blocks(grads[slot], blocks, slot, 0)
         for s in range(4):
             for x in range(2):
-                row = (table[OUT_AT + 2 * s + x] * 4 + table[SLOT_AT + slot]) * TINY
-                out[slot // 2, x, s] = tiny[pl.ds(pl.multiple_of(row, TINY), TINY), :]
+                row = table[OUT_AT + 2 * s + x] * 4 + table[SLOT_AT + slot]
+                if s in (1, 2):
+                    out, place = (send_a if core else keep_a), (y, x, s - 1)
+                else:
+                    out, place = (send_b if core else keep_b), (x, y, s // 2)
+                out[place[0], place[1], place[2], ROWS:, :] = tiny[rows_at(row, TINY), :]
 
 
 def last_stage(
     table, tokens, cross, grad_mid, spread, normed, routes, gates, grad_gate, weight, small,
-    vectors, sums, bias_grad, pair_parts
+    vectors, sums, bias_grad, pair_parts, grads
 ):
     rows, width = tokens.shape
-    block = shaped((2, 2, 4, TINY, 3 * LANES), BF16)
+    block = shaped((2, 2, 2, ROWS + TINY, 3 * LANES), BF16)
     vmem = pl.BlockSpec(memory_space=pltpu.VMEM)
     return pl.pallas_call(
         last_kernel,
         cost_estimate=cost(7),
         in_specs=[smem_spec()] + [vmem] * 17,
-        out_shape=(shaped((HALF, width), F32), shaped((rows - HALF, width), BF16), block, block),
+        out_shape=(shaped((HALF, width), F32), shaped((rows - HALF, width), BF16), block, block, block, block),
         scratch_shapes=[
             pltpu.VMEM((rows, LANES), BF16),
             pltpu.VMEM((width, 3 * LANES), BF16),
@@ -826,7 +809,7 @@
         compiler_params=params(24),
     )(
         table, tokens, cross, grad_mid, spread, normed, routes, gates, grad_gate, weight, small,
-        vectors, sums, bias_grad, *pair_parts
+        vectors, sums, bias_grad, *pair_parts, grads
     )
 
 
@@ -875,22 +858,24 @@
         part_a, part_b = (send_a, send_b) if core else (keep_a, keep_b)
         slots.append(
             jnp.stack(
-                [(part_a[y, x, s] if s < 2 else part_b[x, y, s - 2]) for s in range(4) for x in range(2)]
+                [
+                    (part_a[y, x, s - 1] if s in (1, 2) else part_b[x, y, s // 2])
+                    for s in range(4)
+                    for x in range(2)
+                ]
             )
         )
     return lax.psum(jnp.stack(slots), ("dp", "tensor")).astype(F32)
 
 
-def general_grads(first, tiny, later, experts, hidden, routed):
+def general_grads(first, later, experts, hidden, routed):
     group = experts * HEAD
     d, t = lax.axis_index("dp"), lax.axis_index("tensor")
     dp = lax.axis_size("dp")
     width = 8 * ROWS
     first, later = general_sum(first), general_sum(later)
-    tiny = jnp.stack([tiny[slot % 2][slot // 2].swapaxes(0, 1) for slot in range(4)])
-    small = lax.psum(tiny, ("dp", "tensor")).astype(F32).reshape(4, 8, TINY, 3 * LANES)
-    small = small.transpose(1, 0, 2, 3).reshape(width, 3 * LANES)
-    mine = lax.dynamic_index_in_dim(first.reshape(4, width, group), t, 0, False)
+    small = first[:, :, ROWS:].transpose(1, 0, 2, 3).reshape(width, group)
+    mine = lax.dynamic_index_in_dim(first[:, :, :ROWS].reshape(4, width, group), t, 0, False)
     rest = lax.dynamic_index_in_dim(later.reshape(4, width, -1), t, 0, False)
     rows = width // dp
 
@@ -901,7 +886,7 @@
     rest = own(rest, rows, d)
     index = d * 4 + t
     tiny = own(small, rows // 4, index)
-    bias = small.reshape(32, TINY, 3 * LANES)[:, 0, 2 * LANES : 2 * LANES + HEAD].reshape(-1)
+    bias = small.reshape(32, TINY, group)[:, 0, 2 * LANES : 2 * LANES + HEAD].reshape(-1)
     return (
         query,
         tiny[:, 0:HEAD],
@@ -980,7 +965,10 @@
         side_a = jnp.concatenate([side_a, after(next_a, later_z1, later_z3, cross)], axis=0)
         side_b = jnp.concatenate([side_b, after(next_b, later_z1, later_z3, cross)], axis=0)
         far_a, far_b = over_x(side_a), over_y(side_b)
-        far_a, far_b = after(far_a, later_z2), after(far_b, later_z2)
+        far_a, far_b, later_z2 = together(far_a, far_b, later_z2)
+        later_a = jnp.concatenate([after(second, far_a), later_z1], axis=0)
+        later_b = jnp.concatenate([later_z2, later_z3], axis=0)
+        next_a, next_b = over_y(later_a), over_x(later_b)
         first_pieces = [side_a, far_a, side_b, far_b]
         first_pieces = first_pieces + [over_core(v) for v in first_pieces]
     else:
@@ -992,13 +980,9 @@
         table, tokens, cross, own_routes, first_pieces
     )
     pair_y = over_y(pair)
-    if tuned:
-        later_a = jnp.concatenate([after(second, pair), later_z1], axis=0)
-        later_b = jnp.concatenate([after(later_z2, pair), later_z3], axis=0)
-        next_a, next_b = over_y(later_a), over_x(later_b)
     pairs = (pair, over_core(pair), pair_y, over_core(pair_y))
     if tuned:
-        normed = after(normed, later_a, later_b)
+        normed, later_a, later_b = together(normed, later_a, later_b)
     query, query_weight = query_stage(table, normed, own_routes, first_pieces)
     if tuned:
         side_a = jnp.concatenate([later_a, after(next_a, query)], axis=0)
@@ -1016,81 +1000,81 @@
         got_a, got_b = over_core(send_a), over_core(send_b)
     grad_heads, grad_gate = select_stage(table, back, heads, gates, own_routes)
     if tuned:
-        got_a, got_b = after(got_a, grad_gate), after(got_b, grad_gate)
+        grad_heads, grad_gate, output_high, got_a, got_b = together(
+            grad_heads, grad_gate, crossed(output_high), got_a, got_b
+        )
         part_a, part_b = add_blocks(
             "add_near", [(keep_a, (1,)), (got_a, (1,))], [(keep_b, (1,)), (got_b, (1,))]
         )
         next_a, next_b = over_y(part_a), over_x(part_b)
         grad_heads = after(grad_heads, part_a, part_b)
-    grad_query, part0, part1, part2, part3 = attend_back_stage(
+    grad_query, pair_keep, pair_send = attend_back_stage(
         table, query, grad_heads, totals, gates, grad_gate, pairs, seq
     )
-    pair_parts = (part0, over_core(part1), over_y(part2), crossed(part3))
+    pair_got = over_core(pair_send)
+    (pair_next,) = add_blocks("add_pairs", [(pair_keep, (1,)), (pair_got, (1,))])
+    pair_parts = (pair_keep, pair_got, over_y(pair_next))
     if tuned:
-        next_a, next_b = after(next_a, part0), after(next_b, part0)
+        next_a, next_b = after(next_a, pair_next), after(next_b, pair_next)
+        part_a, part_b = add_blocks(
+            "add_far",
+            [(keep_a, (0, 1)), (got_a, (0, 1)), (next_a, (1,))],
+            [(keep_b, (0, 1)), (got_b, (0, 1)), (next_b, (1,))],
+        )
+        last_a = over_x(part_a)
+        grad_query = after(grad_query, part_a, part_b)
+    else:
+        output_high = crossed(output_high)
+    spread, query_grads = spread_stage(table, grad_query, normed, own_routes, query_weight.shape[2])
+    if tuned:
+        spread, pair_far, last_a = together(spread, pair_parts[2], last_a)
+        pair_parts = (*pair_parts[0:2], pair_far)
+        last_b = over_y(after(part_b, pair_far, spread))
+
+        def final(name, *sides):
+            return add_blocks(
+                name,
+                *[
+                    [(keep, (0, 0, s)), (got, (0, 0, s)), (near, (0, s)), (last, (s,))]
+                    for keep, got, near, last in sides
+                    for s in (0, 1)
+                ],
+            )
+
+        ahead, beyond = final("add_last", (keep_a, got_a, next_a, last_a))
+        beyond = over_z(beyond, 1)
+    low_rows, high_rows, *first_blocks = last_stage(
+        table, tokens, cross, grad_mid, spread, normed, own_routes, gates, grad_gate,
+        query_weight, small, vectors, sums, bias_grad, pair_parts, query_grads,
+    )
+    if tuned:
+        low_rows, high_rows, last_b, beyond, *first_blocks = together(
+            low_rows, high_rows, last_b, beyond, *first_blocks
+        )
+        first_got = over_core(first_blocks[2]), over_core(first_blocks[3])
+        kept, back = final("add_last", (keep_b, got_b, next_b, last_b))
+        (ahead,) = add_blocks("add_ahead", [(ahead, ()), (beyond, ())])
+        one, three = over_z(ahead, 1), over_z(back, 3)
+        keep_a, keep_b = first_blocks[0:2]
+        got_a, got_b = first_got
+        got_a, got_b = after(got_a, ahead, back), after(got_b, ahead, back)
+        part_a, part_b = add_blocks(
+            "add_near", [(keep_a, (1,)), (got_a, (1,))], [(keep_b, (1,)), (got_b, (1,))]
+        )
+        next_a, next_b = over_y(part_a), over_x(part_b)
+        next_a, next_b = together(next_a, next_b)
         part_a, part_b = add_blocks(
             "add_far",
             [(keep_a, (0, 1)), (got_a, (0, 1)), (next_a, (1,))],
             [(keep_b, (0, 1)), (got_b, (0, 1)), (next_b, (1,))],
         )
         last_a, last_b = over_x(part_a), over_y(part_b)
-        grad_query = after(grad_query, part_a, part_b)
-    spread, *first_blocks = spread_stage(table, grad_query, normed, own_routes, query_weight.shape[2])
-    if tuned:
-        last_a, last_b, spread, *rest = together(last_a, last_b, spread, *pair_parts, *first_blocks)
-        pair_parts, first_blocks = rest[0:4], rest[4:8]
-
-        def final(name, keep_a, keep_b, got_a, got_b, next_a, next_b, last_a, last_b):
-            return add_blocks(
-                name,
-                *[
-                    [(keep, (0, 0, s)), (got, (0, 0, s)), (near, (0, s)), (last, (s,))]
-                    for keep, got, near, last in (
-                        (keep_a, got_a, next_a, last_a),
-                        (keep_b, got_b, next_b, last_b),
-                    )
-                    for s in (0, 1)
-                ],
-            )
-
-        done = final("add_last", keep_a, keep_b, got_a, got_b, next_a, next_b, last_a, last_b)
-        later = (done[0], *[over_z(done[step], step) for step in (1, 2, 3)])
-        keep_a, keep_b, send_a, send_b = first_blocks
-        got_a, got_b = over_core(send_a), over_core(send_b)
-        got_a, got_b = after(got_a, *done), after(got_b, *done)
-        part_a, part_b = add_blocks(
-            "add_near", [(keep_a, (1,)), (got_a, (1,))], [(keep_b, (1,)), (got_b, (1,))]
-        )
-        next_a, next_b = over_y(part_a), over_x(part_b)
-        spread = after(spread, part_a, part_b)
-        output_high = after(output_high, part_a)
-    output_high = crossed(output_high)
-    low_rows, high_rows, *tiny_blocks = last_stage(
-        table, tokens, cross, grad_mid, spread, normed, own_routes, gates, grad_gate,
-        query_weight, small, vectors, sums, bias_grad, pair_parts,
-    )
-    if tuned:
-        kept, one, two, three = later
-        low_rows, high_rows, keep, send, next_a, next_b, one, three, output_high = together(
-            low_rows, high_rows, *tiny_blocks, next_a, next_b, one, three, output_high
-        )
-        got = over_core(send)
-        part_a, part_b = add_blocks(
-            "add_far",
-            [(keep_a, (0, 1)), (got_a, (0, 1)), (next_a, (1,))],
-            [(keep_b, (0, 1)), (got_b, (0, 1)), (next_b, (1,))],
-        )
-        last_a, last_b = over_x(part_a), over_y(part_b)
-        (part,) = add_blocks("add_tiny", [(keep, (1,)), (got, (1,))])
-        next_tiny = over_y(part)
-        high_rows = after(high_rows, part)
-        out_grad, up_grad, down_grad = unpack_second(kept, one, two, three, experts, hidden)
+        last_a, last_b, one, three = together(last_a, last_b, one, three)
+        high_rows = after(high_rows, last_b)
+        out_grad, up_grad, down_grad = unpack_second(kept, one, three, experts, hidden)
         down_grad = down_grad.T
-        (part,) = add_blocks("add_tiny", [(keep, (0, 1)), (got, (0, 1)), (next_tiny, (1,))])
-        last_tiny = over_x(part)
-        done = add_ends(
-            (keep_a, got_a, next_a, last_a), (keep_b, got_b, next_b, last_b), (keep, got, next_tiny, last_tiny)
-        )
+        done = final("add_last", (keep_a, got_a, next_a, last_a), (keep_b, got_b, next_b, last_b))
+        done = (done[2], done[0], done[1], done[3])
         one, two, three = [over_z(done[step], step) for step in (1, 2, 3)]
         result = jnp.concatenate([output, output_high], axis=0)
         grad_tokens = jnp.concatenate([low_rows, crossed(high_rows).astype(F32)], axis=0)
@@ -1103,7 +1087,7 @@
         (
             query_grad, key_grad, value_grad, router_grad, small_grads, up_bias_grad,
             out_grad, up_grad, down_grad,
-        ) = general_grads(first_blocks, tiny_blocks, later_blocks, experts, hidden, routed)
+        ) = general_grads(first_blocks, later_blocks, experts, hidden, routed)
         result = jnp.concatenate([output, output_high], axis=0)
         grad_tokens = jnp.concatenate([low_rows, crossed(high_rows).astype(F32)], axis=0)
     return (

time: 176 us -> 166 us (0.943)
  waiting for transfers between devices: 54.6 us -> 48 us
  starting transfers between devices: 47.4 us -> 43.2 us
    ppermute x11 -> x10, waiting for transfers between devices: 22.5 us -> 8.69 us  [over_y(): return lax.ppermute(x, 'tensor', ACROSS)]
    ppermute x4 -> x3, waiting for transfers between devices: 0.01 us -> 3.81 us  [crossed(): return lax.ppermute(x, 'tensor', CROSSED)]
    ppermute x9 -> x8, waiting for transfers between devices: 6.22 us -> 9.08 us  [over_x(): return lax.ppermute(x, 'dp', swap)]
    ppermute x11 -> x10, starting transfers between devices: 12.8 us -> 10.8 us  [over_y(): return lax.ppermute(x, 'tensor', ACROSS)]
    ppermute x9 -> x8, starting transfers between devices: 8.15 us -> 9.23 us  [over_x(): return lax.ppermute(x, 'dp', swap)]
    ppermute x16 -> x15, starting transfers between devices: 3.88 us -> 3.24 us  [over_core(): return lax.ppermute(x, 'tensor', CORE)]
    ppermute x16 -> x15, waiting for transfers between devices: 9.16 us -> 8.55 us  [over_core(): return lax.ppermute(x, 'tensor', CORE)]
  transfers between devices with their start and end apart: 52 -> 48, of which waited for: 29 -> 28; matrix products, arithmetic and copies ran while one was open for 2% -> 2% of each run, Pallas kernels for 25% -> 28%
where the time goes in v4:
time: 166 us; the launch traced here: 165 us
  Pallas kernels  66.9 us (40%)
  waiting for transfers between devices  48 us (29%)
  starting transfers between devices  43.2 us (26%)
  local copies, waits for them, and re-layouts  4.15 us (3%)
  other arithmetic  1.96 us (1%)
    ppermute x12, starting transfers between devices, over_z(): return lax.ppermute(x, 'dp', turns[step - 1])  18.8 us
    ppermute x12, waiting for transfers between devices, over_z(): return lax.ppermute(x, 'dp', turns[step - 1])  17.9 us
    pallas_call x1, Pallas kernels, middle_stage(): pl.pallas_call(middle_kernel, cost_estimate=cost(36), in_specs=[smem_spec...  17.1 us
    pallas_call x1, Pallas kernels, attend_back_stage(): pl.pallas_call(attend_back_kernel, cost_estimate=cost(16), grid=(rows //...  14.3 us
    ppermute x10, starting transfers between devices, over_y(): return lax.ppermute(x, 'tensor', ACROSS)  10.8 us
    pallas_call x1, Pallas kernels, attend_stage(): pl.pallas_call(attend_kernel, cost_estimate=cost(1.2), grid=(rows // HALF...  10.5 us
    ppermute x8, starting transfers between devices, over_x(): return lax.ppermute(x, 'dp', swap)  9.23 us
    ppermute x8, waiting for transfers between devices, over_x(): return lax.ppermute(x, 'dp', swap)  9.08 us
  transfers between devices with their start and end apart: 48, of which 28 were waited for; matrix products, arithmetic and copies ran while one was open for 2% of the time, Pallas kernels for 28%

profile of v4, /device:TPU:0, one launch (start us, length us, event | category | flops | bytes accessed | tf_op | source)
XLA Modules:
  0.0 165.2 jit_solution(2747466247807371918)
XLA Ops:
  0.7 2.4 %shard_map.271 = (bf16[80,384]{1,0:T(8,128)(2,1)}, bf16[64,1408]{1,0:T(8,128)(2,1)}, bf16[512,512]{1,0:T(8,128)(2,1)}) custom-call(bf16[6,64,64]{2,1,0:T(8,128)(2,1)} %wq.1, bf16[6,64,64]{2,1,0:T(8,128)(2,1)} %wo.1, bf16[64,512]{1,0:T(8,128)(2,1)} %wup.1, bf16[64,512]{1,0:T(8,128)(2,1)} %bitcast.46, bf16[16,64]{1,0:T(8,128)(2,1)} %wk.1, bf16[16,64]{1,0:T(8,128)(2,1)} %wv.1, ...), custom_call_target="tpu_custom_call" | custom-call | bytes 738000 | tf_op jit(solution)/shard_map/pallas_call | solution.py:107
  3.1 5.0 %collective-permute-start.7 = (bf16[1,80,384]{2,1,0:T(8,128)(2,1)}, bf16[1,80,384]{2,1,0:T(8,128)(2,1)S(1)}, u32[]{:S(2)}, u32[]{:S(2)}) collective-permute-start(bf16[1,80,384]{2,1,0:T(8,128)(2,1)} %bitcast.38), channel_id=1, source_target_pairs={{0,24},{4,28},{8,0},{12,4},{16,8},{20,12},{24,16},{28,20},{1,25},{... | collective-permute-start | bytes 184328 | tf_op jit(solution)/shard_map/ppermute | solution.py:948
  8.1 1.0 collective-permute-start.1
  9.3 0.7 constant_dynamic-slice_fusion.1
  10.1 0.8 constant_dynamic-update-slice_fusion.2
  10.9 3.5 %collective-permute-done.1 = bf16[1,80,384]{2,1,0:T(8,128)(2,1)S(1)} collective-permute-done((bf16[1,80,384]{2,1,0:T(8,128)(2,1)}, bf16[1,80,384]{2,1,0:T(8,128)(2,1)S(1)}, u32[]{:S(2)}, u32[]{:S(2)}) %collective-permute-start.1) | collective-permute-done | bytes 61472 | tf_op jit(solution)/shard_map/ppermute | solution.py:948
  14.5 1.1 collective-permute-start.4
  15.6 0.9 collective-permute-start.3
  16.5 1.6 collective-permute-start.8
  18.1 0.8 pad_maximum_fusion.1
  18.9 1.6 collective-permute-start.2
  20.6 0.9 collective-permute-done.8
  21.5 4.3 %collective-permute-done.3 = bf16[1,64,1408]{2,1,0:T(8,128)(2,1)S(1)} collective-permute-done((bf16[1,64,1408]{2,1,0:T(8,128)(2,1)}, bf16[1,64,1408]{2,1,0:T(8,128)(2,1)S(1)}, u32[]{:S(2)}, u32[]{:S(2)}) %collective-permute-start.3) | collective-permute-done | bytes 180256 | tf_op jit(solution)/shard_map/ppermute | solution.py:948
  26.2 1.6 collective-permute-start.5
  27.8 1.1 collective-permute-start.9
  29.0 1.5 collective-permute-start.10
  31.1 5.3 %collective-permute-done.10 = bf16[1,64,1408]{2,1,0:T(8,128)(2,1)S(1)} collective-permute-done((bf16[1,64,1408]{2,1,0:T(8,128)(2,1)S(1)}, bf16[1,64,1408]{2,1,0:T(8,128)(2,1)S(1)}, u32[]{:S(2)}, u32[]{:S(2)}) %collective-permute-start.10) | collective-permute-done | bytes 180256 | tf_op jit(solution)/shard_map/ppermute | solution.py:948
  37.7 1.3 collective-permute-start.18
  39.0 2.5 %shard_map.272 = (bf16[512,512]{1,0:T(8,128)(2,1)S(1)}, bf16[512,128]{1,0:T(8,128)(2,1)S(1)}, f32[512,128]{1,0:T(8,128)S(1)}, bf16[512,384]{1,0:T(8,128)(2,1)S(1...) custom-call(s32[28]{0:T(128)S(1)} %stack.97.table, bf16[512,512]{1,0:T(8,128)(2,1)S(1)} %copy-done, ...), custom_call_target="tpu_custom_call" | custom-call | bytes 1845000 | tf_op jit(solution)/shard_map/pallas_call | solution.py:302
  41.5 0.8 collective-permute-start.16
  42.3 4.2 %shard_map.273 = (bf16[8,512,128]{2,1,0:T(8,128)(2,1)S(1)}, bf16[4,512,384]{2,1,0:T(8,128)(2,1)S(1)}) custom-call(s32[28]{0:T(128)S(1)} %stack.97.table, bf16[512,512]{1,0:T(8,128)(2,1)S(1)} %get-tuple-element.141.normed, s32[512,8]{1,0:T(8,128)S(1)} %copy.33.routes, bf16[4,80,384]{2,1,0:T(8,128)(2,1)S(1)} %constant_dynamic-update-slice_fusion.refs_0_, ...), custom_call_target="tpu_custom_call" | custom-call | bytes 2952000 | tf_op jit(solution)/shard_map/pallas_call | solution.py:377
  46.6 2.5 %collective-permute-done.18 = bf16[2,64,1408]{2,1,0:T(8,128)(2,1)S(1)} collective-permute-done((bf16[2,64,1408]{2,1,0:T(8,128)(2,1)S(1)}, bf16[2,64,1408]{2,1,0:T(8,128)(2,1)S(1)}, u32[]{:S(2)}, u32[]{:S(2)}) %collective-permute-start.18) | collective-permute-done | bytes 360480 | tf_op jit(solution)/shard_map/ppermute | solution.py:210
  49.2 1.6 collective-permute-start.19
  51.0 1.3 collective-permute-start.21
  52.3 1.3 collective-permute-done.15.kv1
  53.8 1.2 collective-permute-done.17.kv3
  55.0 10.5 %shard_map.274 = (bf16[8,512,128]{2,1,0:T(8,128)(2,1)S(1)}, f32[512,128]{1,0:T(8,128)S(1)}) custom-call(s32[28]{0:T(128)S(1)} %stack.97.table, bf16[8,512,128]{2,1,0:T(8,128)(2,1)S(1)} %get-tuple-element.142.query, bf16[512,128]{1,0:T(8,128)(2,1)S(1)} %get-tuple-element.143.kv0, bf16[512,128]{1,0:T(8,128)(2,1)S(1)} %collective-permute-done.15.kv1, ...), custom_call_target="tpu_custom_call" | custom-call | bytes 4428000 | tf_op jit(solution)/shard_map/pallas_call | solution.py:461
  65.5 2.2 %collective-permute-done.19.refs_1_ = bf16[4,64,1408]{2,1,0:T(8,128)(2,1)S(1)} collective-permute-done((bf16[4,64,1408]{2,1,0:T(8,128)(2,1)S(1)}, bf16[4,64,1408]{2,1,0:T(8,128)(2,1)S(1)}, u32[]{:S(2)}, u32[]{:S(2)}) %collective-permute-start.19) | collective-permute-done | bytes 720928 | tf_op jit(solution)/shard_map/ppermute | solution.py:945
  67.7 1.7 %collective-permute-done.21.refs_3_ = bf16[4,64,1408]{2,1,0:T(8,128)(2,1)S(1)} collective-permute-done((bf16[4,64,1408]{2,1,0:T(8,128)(2,1)S(1)}, bf16[4,64,1408]{2,1,0:T(8,128)(2,1)S(1)}, u32[]{:S(2)}, u32[]{:S(2)}) %collective-permute-start.21) | collective-permute-done | bytes 720928 | tf_op jit(solution)/shard_map/ppermute | solution.py:210
  69.9 1.7 %collective-permute-done.24.refs_5_ = bf16[4,64,1408]{2,1,0:T(8,128)(2,1)S(1)} collective-permute-done((bf16[4,64,1408]{2,1,0:T(8,128)(2,1)S(1)}, bf16[4,64,1408]{2,1,0:T(8,128)(2,1)S(1)}, u32[]{:S(2)}, u32[]{:S(2)}) %collective-permute-start.24) | collective-permute-done | bytes 720928 | tf_op jit(solution)/shard_map/ppermute | solution.py:206
  71.6 1.0 collective-permute-done.25.refs_7_
  72.6 17.1 %shard_map.275 = (bf16[256,512]{1,0:T(8,128)(2,1)S(1)}, bf16[256,512]{1,0:T(8,128)(2,1)S(1)}, f32[512,512]{1,0:T(8,128)S(1)}, bf16[4,512,384]{2,1,0:T(8,128)(2,1...) custom-call(s32[28]{0:T(128)S(1)} %stack.97.table, ...), custom_call_target="tpu_custom_call" | custom-call | bytes 132840000 | tf_op jit(solution)/shard_map/pallas_call | solution.py:686
  90.2 1.0 collective-permute-start.26
  91.2 1.4 copy-done.2
  92.6 4.7 %shard_map.276 = (bf16[8,512,128]{2,1,0:T(8,128)(2,1)S(1)}, f32[512,128]{1,0:T(8,128)S(1)}) custom-call(s32[28]{0:T(128)S(1)} %stack.97.table, bf16[4,512,384]{2,1,0:T(8,128)(2,1)S(1)} %copy-done.2, bf16[8,512,128]{2,1,0:T(8,128)(2,1)S(1)} %get-tuple-element.149.heads, f32[512,128]{1,0:T(8,128)S(1)} %get-tuple-element.150.gates, s32[512,8]{1,0:T(8,128)S(1)} %copy.33.routes), custom_call_target="tpu_custom_call" | custom-call | bytes 29520000 | tf_op jit(solution)/shard_map/pallas_call | solution.py:667
  97.3 1.2 collective-permute-done.26
  98.8 1.3 collective-permute-start.29
  100.2 1.4 collective-permute-start.31
  101.5 14.3 %shard_map.278 = (bf16[8,512,128]{2,1,0:T(8,128)(2,1)S(1)}, bf16[2,2,128,256]{3,2,1,0:T(8,128)(2,1)S(1)}, bf16[2,2,128,256]{3,2,1,0:T(8,128)(2,1)S(1)}) custom-call(s32[28]{0:T(128)S(1)} %stack.97.table, bf16[8,512,128]{2,1,0:T(8,128)(2,1)S(1)} %get-tuple-element.142.query, bf16[8,512,128]{2,1,0:T(8,128)(2,1)S(1)} %get-tuple-element.173.grad, ...), custom_call_target="tpu_custom_call" | custom-call | bytes 59040000 | tf_op jit(solution)/shard_map/pallas_call | solution.py:541
  115.9 1.5 collective-permute-done.30.refs_1_.pair_got
  118.3 1.4 collective-permute-start.33
  119.8 0.8 collective-permute-start.32
  120.5 4.2 %shard_map.281 = (bf16[4,512,384]{2,1,0:T(8,128)(2,1)S(1)}, bf16[4,512,384]{2,1,0:T(8,128)(2,1)S(1)}) custom-call(s32[28]{0:T(128)S(1)} %stack.97.table, bf16[8,512,128]{2,1,0:T(8,128)(2,1)S(1)} %get-tuple-element.183.grad_query, bf16[512,512]{1,0:T(8,128)(2,1)S(1)} %get-tuple-element.141.normed, s32[512,8]{1,0:T(8,128)S(1)} %copy.33.routes), custom_call_target="tpu_custom_call" | custom-call | bytes 22140000 | tf_op jit(solution)/shard_map/pallas_call | solution.py:730
  124.8 3.5 %collective-permute-done.33.refs_3_.refs_7_ = bf16[2,64,1408]{2,1,0:T(8,128)(2,1)S(1)} collective-permute-done((bf16[2,64,1408]{2,1,0:T(8,128)(2,1)S(1)}, bf16[2,64,1408]{2,1,0:T(8,128)(2,1)S(1)}, u32[]{:S(2)}, u32[]{:S(2)}) %collective-permute-start.33) | collective-permute-done | bytes 360480 | tf_op jit(solution)/shard_map/ppermute | solution.py:945
  128.3 0.8 collective-permute-start.34
  129.3 1.6 collective-permute-start.35
  130.9 4.0 %shard_map.282 = (f32[256,512]{1,0:T(8,128)S(1)}, bf16[256,512]{1,0:T(8,128)(2,1)S(1)}, bf16[2,2,2,80,384]{4,3,2,1,0:T(8,128)(2,1)S(1)}, bf16[2,2,2,80,384]{4,3,...) custom-call(s32[28]{0:T(128)S(1)} %stack.97.table, ...), custom_call_target="tpu_custom_call" | custom-call | bytes 25830000 | tf_op jit(solution)/shard_map/pallas_call | solution.py:798
  134.8 1.8 %collective-permute-done.35.refs_1_ = bf16[64,1408]{1,0:T(8,128)(2,1)S(1)} collective-permute-done((bf16[64,1408]{1,0:T(8,128)(2,1)S(1)}, bf16[64,1408]{1,0:T(8,128)(2,1)S(1)}, u32[]{:S(2)}, u32[]{:S(2)}) %collective-permute-start.35) | collective-permute-done | bytes 180256 | tf_op jit(solution)/shard_map/ppermute | solution.py:948
  138.1 1.1 collective-permute-done.36.refs_1_.refs_5_
  140.0 0.8 collective-permute-start.38
  141.4 1.2 collective-permute-start.42
  142.6 2.6 %collective-permute-start.43 = (bf16[64,1408]{1,0:T(8,128)(2,1)S(1)}, bf16[64,1408]{1,0:T(8,128)(2,1)S(1)}, u32[]{:S(2)}, u32[]{:S(2)}) collective-permute-start(bf16[64,1408]{1,0:T(8,128)(2,1)S(1)} %get-tuple-element.208), channel_id=1, source_target_pairs={{0,24},{4,28},{8,0},{12,4},{16,8},{20,12},{24,16},{28,20},{1,25},{... | collective-permute-start | bytes 540680 | tf_op jit(solution)/shard_map/ppermute | solution.py:948
  145.2 2.8 %collective-permute-done.38.refs_2_.refs_6_ = bf16[2,2,80,384]{3,2,1,0:T(8,128)(2,1)S(1)} collective-permute-done((bf16[2,2,80,384]{3,2,1,0:T(8,128)(2,1)S(1)}, bf16[2,2,80,384]{3,2,1,0:T(8,128)(2,1)S(1)}, u32[]{:S(2)}, u32[]{:S(2)}) %collective-permute-start.38) | collective-permute-done | bytes 245792 | tf_op jit(solution)/shard_map/ppermute | solution.py:210
  149.3 1.0 collective-permute-start.41
  150.7 1.6 collective-permute-done.43.three
  152.3 1.3 collective-permute-done.40.refs_3_.refs_7_
  155.0 1.3 collective-permute-start.45
  156.3 1.0 collective-permute-start.46
  157.3 1.5 collective-permute-start.47
  158.8 0.8 shard_map.289
  159.7 2.6 %collective-permute-done.44 = bf16[256,512]{1,0:T(8,128)(2,1)S(1)} collective-permute-done((bf16[256,512]{1,0:T(8,128)(2,1)S(1)}, bf16[256,512]{1,0:T(8,128)(2,1)S(1)}, u32[]{:S(2)}, u32[]{:S(2)}) %collective-permute-start.44) | collective-permute-done | bytes 262176 | tf_op jit(solution)/shard_map/ppermute | solution.py:214
  162.4 1.0 pad_maximum_fusion
  163.4 1.0 collective-permute-done.46.two
  164.4 0.8 shard_map.290
  (86 shorter events, 11.7 us)
Async XLA Ops:
  3.1 33.3 %copy-start.3 = (bf16[64,1408]{1,0:T(8,128)(2,1)S(1)}, bf16[64,1408]{1,0:T(8,128)(2,1)}, u32[]{:S(2)}) copy-start(bf16[64,1408]{1,0:T(8,128)(2,1)} %get-tuple-element.132) | copy-start | bytes 540676
  3.1 13.4 %collective-permute-start.7 = (bf16[1,80,384]{2,1,0:T(8,128)(2,1)}, bf16[1,80,384]{2,1,0:T(8,128)(2,1)S(1)}, u32[]{:S(2)}, u32[]{:S(2)}) collective-permute-start(bf16[1,80,384]{2,1,0:T(8,128)(2,1)} %bitcast.38), channel_id=1, source_target_pairs={{0,24},{4,28},{8,0},{12,4},{16,8},{20,12},{24,16},{28,20},{1,25},{... | collective-permute-start | bytes 184328 | tf_op jit(solution)/shard_map/ppermute | solution.py:948
  8.1 8.4 %collective-permute-start.6 = (bf16[1,80,384]{2,1,0:T(8,128)(2,1)}, bf16[1,80,384]{2,1,0:T(8,128)(2,1)S(1)}, u32[]{:S(2)}, u32[]{:S(2)}) collective-permute-start(bf16[1,80,384]{2,1,0:T(8,128)(2,1)} %bitcast.39), channel_id=1, source_target_pairs={{0,16},{4,20},{8,24},{12,28},{16,0},{20,4},{24,8},{28,12},{1,17},{... | collective-permute-start | bytes 184328 | tf_op jit(solution)/shard_map/ppermute | solution.py:948
  8.1 6.3 %collective-permute-start.1 = (bf16[1,80,384]{2,1,0:T(8,128)(2,1)}, bf16[1,80,384]{2,1,0:T(8,128)(2,1)S(1)}, u32[]{:S(2)}, u32[]{:S(2)}) collective-permute-start(bf16[1,80,384]{2,1,0:T(8,128)(2,1)} %bitcast.40), channel_id=1, source_target_pairs={{0,8},{4,12},{8,16},{12,20},{16,24},{20,28},{24,0},{28,4},{1,9},{5... | collective-permute-start | bytes 184328 | tf_op jit(solution)/shard_map/ppermute | solution.py:948
  9.2 16.6 %collective-permute-start = (bf16[512,512]{1,0:T(8,128)(2,1)}, bf16[512,512]{1,0:T(8,128)(2,1)S(1)}, u32[]{:S(2)}, u32[]{:S(2)}) collective-permute-start(bf16[512,512]{1,0:T(8,128)(2,1)} %get-tuple-element.129), channel_id=1, source_target_pairs={{0,3},{3,0},{1,2},{2,1},{4,7},{7,4},{5,6},{6,5},{8,11},{11,8},{9,1... | collective-permute-start | bytes 1572872 | tf_op jit(solution)/shard_map/ppermute | solution.py:214
  14.5 7.0 %collective-permute-start.4 = (bf16[1,64,1408]{2,1,0:T(8,128)(2,1)}, bf16[1,64,1408]{2,1,0:T(8,128)(2,1)S(1)}, u32[]{:S(2)}, u32[]{:S(2)}) collective-permute-start(bf16[1,64,1408]{2,1,0:T(8,128)(2,1)} %bitcast.43), channel_id=1, source_target_pairs={{0,24},{4,28},{8,0},{12,4},{16,8},{20,12},{24,16},{28,20},{1,25},{... | collective-permute-start | bytes 540680 | tf_op jit(solution)/shard_map/ppermute | solution.py:948
  15.6 10.2 %collective-permute-start.3 = (bf16[1,64,1408]{2,1,0:T(8,128)(2,1)}, bf16[1,64,1408]{2,1,0:T(8,128)(2,1)S(1)}, u32[]{:S(2)}, u32[]{:S(2)}) collective-permute-start(bf16[1,64,1408]{2,1,0:T(8,128)(2,1)} %bitcast.44), channel_id=1, source_target_pairs={{0,8},{4,12},{8,16},{12,20},{16,24},{20,28},{24,0},{28,4},{1,9},{5... | collective-permute-start | bytes 540680 | tf_op jit(solution)/shard_map/ppermute | solution.py:948
  16.5 22.5 %copy-start = (bf16[512,512]{1,0:T(8,128)(2,1)S(1)}, bf16[512,512]{1,0:T(8,128)(2,1)}, u32[]{:S(2)}) copy-start(bf16[512,512]{1,0:T(8,128)(2,1)} %low_tok.5) | copy-start | bytes 1572868
  16.5 4.9 %collective-permute-start.8 = (bf16[2,80,384]{2,1,0:T(8,128)(2,1)S(1)}, bf16[2,80,384]{2,1,0:T(8,128)(2,1)S(1)}, u32[]{:S(2)}, u32[]{:S(2)}) collective-permute-start(bf16[2,80,384]{2,1,0:T(8,128)(2,1)S(1)} %pad_maximum_fusion.2), channel_id=1, source_target_pairs={{0,4},{4,0},{8,12},{12,8},{16,20},{20,16},{24,28},{28,24},{1,5},{5... | collective-permute-start | bytes 368648 | tf_op jit(solution)/shard_map/ppermute | solution.py:945
  18.9 7.3 %collective-permute-start.2 = (bf16[2,80,384]{2,1,0:T(8,128)(2,1)S(1)}, bf16[2,80,384]{2,1,0:T(8,128)(2,1)S(1)}, u32[]{:S(2)}, u32[]{:S(2)}) collective-permute-start(bf16[2,80,384]{2,1,0:T(8,128)(2,1)S(1)} %pad_maximum_fusion.1), channel_id=1, source_target_pairs={{0,2},{2,0},{1,3},{3,1},{4,6},{6,4},{5,7},{7,5},{8,10},{10,8},{9,1... | collective-permute-start | bytes 368648 | tf_op jit(solution)/shard_map/ppermute | solution.py:210
  26.2 10.2 %collective-permute-start.5 = (bf16[4,80,384]{2,1,0:T(8,128)(2,1)S(1)}, bf16[4,80,384]{2,1,0:T(8,128)(2,1)S(1)}, u32[]{:S(2)}, u32[]{:S(2)}) collective-permute-start(bf16[4,80,384]{2,1,0:T(8,128)(2,1)S(1)} %constant_dynamic-update-slice_fusion.refs_0_), channel_id=1, source_target_pairs={{0,4},{4,0},{8,12},{12,8},{16,20},{20,16},{24,28},{28,24},{1,5},{5... | collective-permute-start | bytes 737288 | tf_op jit(solution)/shard_map/ppermute | solution.py:945
  27.8 8.6 %collective-permute-start.9 = (bf16[4,80,384]{2,1,0:T(8,128)(2,1)S(1)}, bf16[4,80,384]{2,1,0:T(8,128)(2,1)S(1)}, u32[]{:S(2)}, u32[]{:S(2)}) collective-permute-start(bf16[4,80,384]{2,1,0:T(8,128)(2,1)S(1)} %constant_dynamic-update-slice_fusion.3.refs_2_), channel_id=1, source_target_pairs={{0,2},{2,0},{1,3},{3,1},{4,6},{6,4},{5,7},{7,5},{8,10},{10,8},{9,1... | collective-permute-start | bytes 737288 | tf_op jit(solution)/shard_map/ppermute | solution.py:210
  29.0 7.4 %collective-permute-start.10 = (bf16[1,64,1408]{2,1,0:T(8,128)(2,1)S(1)}, bf16[1,64,1408]{2,1,0:T(8,128)(2,1)S(1)}, u32[]{:S(2)}, u32[]{:S(2)}) collective-permute-start(bf16[1,64,1408]{2,1,0:T(8,128)(2,1)S(1)} %collective-permute-done.3), channel_id=1, source_target_pairs={{0,8},{4,12},{8,16},{12,20},{16,24},{20,28},{24,0},{28,4},{1,9},{5... | collective-permute-start | bytes 540680 | tf_op jit(solution)/shard_map/ppermute | solution.py:948
  30.6 7.1 %collective-permute-start.11 = (bf16[4,80,384]{2,1,0:T(8,128)(2,1)S(1)}, bf16[4,80,384]{2,1,0:T(8,128)(2,1)S(1)}, u32[]{:S(2)}, u32[]{:S(2)}) collective-permute-start(bf16[4,80,384]{2,1,0:T(8,128)(2,1)S(1)} %constant_dynamic-update-slice_fusion.refs_0_), channel_id=1, source_target_pairs={{0,1},{1,0},{2,3},{3,2},{4,5},{5,4},{6,7},{7,6},{8,9},{9,8},{10,11... | collective-permute-start | bytes 737288 | tf_op jit(solution)/shard_map/ppermute | solution.py:206
  30.6 8.4 %collective-permute-start.13 = (bf16[4,80,384]{2,1,0:T(8,128)(2,1)S(1)}, bf16[4,80,384]{2,1,0:T(8,128)(2,1)S(1)}, u32[]{:S(2)}, u32[]{:S(2)}) collective-permute-start(bf16[4,80,384]{2,1,0:T(8,128)(2,1)S(1)} %constant_dynamic-update-slice_fusion.3.refs_2_), channel_id=1, source_target_pairs={{0,1},{1,0},{2,3},{3,2},{4,5},{5,4},{6,7},{7,6},{8,9},{9,8},{10,11... | collective-permute-start | bytes 737288 | tf_op jit(solution)/shard_map/ppermute | solution.py:206
  36.4 2.6 %collective-permute-start.12 = (bf16[4,80,384]{2,1,0:T(8,128)(2,1)S(1)}, bf16[4,80,384]{2,1,0:T(8,128)(2,1)S(1)}, u32[]{:S(2)}, u32[]{:S(2)}) collective-permute-start(bf16[4,80,384]{2,1,0:T(8,128)(2,1)S(1)} %collective-permute-done.5.refs_1_), channel_id=1, source_target_pairs={{0,1},{1,0},{2,3},{3,2},{4,5},{5,4},{6,7},{7,6},{8,9},{9,8},{10,11... | collective-permute-start | bytes 737288 | tf_op jit(solution)/shard_map/ppermute | solution.py:206
  36.5 2.5 %collective-permute-start.14 = (bf16[4,80,384]{2,1,0:T(8,128)(2,1)S(1)}, bf16[4,80,384]{2,1,0:T(8,128)(2,1)S(1)}, u32[]{:S(2)}, u32[]{:S(2)}) collective-permute-start(bf16[4,80,384]{2,1,0:T(8,128)(2,1)S(1)} %collective-permute-done.9.refs_3_), channel_id=1, source_target_pairs={{0,1},{1,0},{2,3},{3,2},{4,5},{5,4},{6,7},{7,6},{8,9},{9,8},{10,11... | collective-permute-start | bytes 737288 | tf_op jit(solution)/shard_map/ppermute | solution.py:206
  37.0 13.7 %collective-permute-start.20 = (bf16[2,64,1408]{2,1,0:T(8,128)(2,1)S(1)}, bf16[2,64,1408]{2,1,0:T(8,128)(2,1)S(1)}, u32[]{:S(2)}, u32[]{:S(2)}) collective-permute-start(bf16[2,64,1408]{2,1,0:T(8,128)(2,1)S(1)} %constant_dynamic-update-slice_fusion.8), channel_id=1, source_target_pairs={{0,4},{4,0},{8,12},{12,8},{16,20},{20,16},{24,28},{28,24},{1,5},{5... | collective-permute-start | bytes 1081352 | tf_op jit(solution)/shard_map/ppermute | solution.py:945
  37.7 11.4 %collective-permute-start.18 = (bf16[2,64,1408]{2,1,0:T(8,128)(2,1)S(1)}, bf16[2,64,1408]{2,1,0:T(8,128)(2,1)S(1)}, u32[]{:S(2)}, u32[]{:S(2)}) collective-permute-start(bf16[2,64,1408]{2,1,0:T(8,128)(2,1)S(1)} %constant_dynamic-update-slice_fusion.6), channel_id=1, source_target_pairs={{0,2},{2,0},{1,3},{3,1},{4,6},{6,4},{5,7},{7,5},{8,10},{10,8},{9,1... | collective-permute-start | bytes 1081352 | tf_op jit(solution)/shard_map/ppermute | solution.py:210
  41.5 9.2 %collective-permute-start.16 = (bf16[512,128]{1,0:T(8,128)(2,1)S(1)}, bf16[512,128]{1,0:T(8,128)(2,1)S(1)}, u32[]{:S(2)}, u32[]{:S(2)}) collective-permute-start(bf16[512,128]{1,0:T(8,128)(2,1)S(1)} %get-tuple-element.143.kv0), channel_id=1, source_target_pairs={{0,2},{2,0},{1,3},{3,1},{4,6},{6,4},{5,7},{7,5},{8,10},{10,8},{9,1... | collective-permute-start | bytes 393224 | tf_op jit(solution)/shard_map/ppermute | solution.py:210
  49.1 23.6 %copy-start.1 = (bf16[512,512]{1,0:T(8,128)(2,1)S(1)}, bf16[512,512]{1,0:T(8,128)(2,1)}, u32[]{:S(2)}) copy-start(bf16[512,512]{1,0:T(8,128)(2,1)} %low_cot.1) | copy-start | bytes 1572868
  49.1 16.4 %collective-permute-start.22 = (bf16[4,64,1408]{2,1,0:T(8,128)(2,1)S(1)}, bf16[4,64,1408]{2,1,0:T(8,128)(2,1)S(1)}, u32[]{:S(2)}, u32[]{:S(2)}) collective-permute-start(bf16[4,64,1408]{2,1,0:T(8,128)(2,1)S(1)} %constant_dynamic-update-slice_fusion.10.refs_0_), channel_id=1, source_target_pairs={{0,1},{1,0},{2,3},{3,2},{4,5},{5,4},{6,7},{7,6},{8,9},{9,8},{10,11... | collective-permute-start | bytes 2162696 | tf_op jit(solution)/shard_map/ppermute | solution.py:206
  49.2 18.6 %collective-permute-start.19 = (bf16[4,64,1408]{2,1,0:T(8,128)(2,1)S(1)}, bf16[4,64,1408]{2,1,0:T(8,128)(2,1)S(1)}, u32[]{:S(2)}, u32[]{:S(2)}) collective-permute-start(bf16[4,64,1408]{2,1,0:T(8,128)(2,1)S(1)} %constant_dynamic-update-slice_fusion.10.refs_0_), channel_id=1, source_target_pairs={{0,4},{4,0},{8,12},{12,8},{16,20},{20,16},{24,28},{28,24},{1,5},{5... | collective-permute-start | bytes 2162696 | tf_op jit(solution)/shard_map/ppermute | solution.py:945
  50.8 17.0 %collective-permute-start.23 = (bf16[4,64,1408]{2,1,0:T(8,128)(2,1)S(1)}, bf16[4,64,1408]{2,1,0:T(8,128)(2,1)S(1)}, u32[]{:S(2)}, u32[]{:S(2)}) collective-permute-start(bf16[4,64,1408]{2,1,0:T(8,128)(2,1)S(1)} %constant_dynamic-update-slice_fusion.12.refs_2_), channel_id=1, source_target_pairs={{0,1},{1,0},{2,3},{3,2},{4,5},{5,4},{6,7},{7,6},{8,9},{9,8},{10,11... | collective-permute-start | bytes 2162696 | tf_op jit(solution)/shard_map/ppermute | solution.py:206
  51.0 18.4 %collective-permute-start.21 = (bf16[4,64,1408]{2,1,0:T(8,128)(2,1)S(1)}, bf16[4,64,1408]{2,1,0:T(8,128)(2,1)S(1)}, u32[]{:S(2)}, u32[]{:S(2)}) collective-permute-start(bf16[4,64,1408]{2,1,0:T(8,128)(2,1)S(1)} %constant_dynamic-update-slice_fusion.12.refs_2_), channel_id=1, source_target_pairs={{0,2},{2,0},{1,3},{3,1},{4,6},{6,4},{5,7},{7,5},{8,10},{10,8},{9,1... | collective-permute-start | bytes 2162696 | tf_op jit(solution)/shard_map/ppermute | solution.py:210
  52.3 1.3 collective-permute-start.15
  53.6 1.3 collective-permute-start.17
  69.4 2.2 %collective-permute-start.24 = (bf16[4,64,1408]{2,1,0:T(8,128)(2,1)S(1)}, bf16[4,64,1408]{2,1,0:T(8,128)(2,1)S(1)}, u32[]{:S(2)}, u32[]{:S(2)}) collective-permute-start(bf16[4,64,1408]{2,1,0:T(8,128)(2,1)S(1)} %collective-permute-done.19.refs_1_), channel_id=1, source_target_pairs={{0,1},{1,0},{2,3},{3,2},{4,5},{5,4},{6,7},{7,6},{8,9},{9,8},{10,11... | collective-permute-start | bytes 2162696 | tf_op jit(solution)/shard_map/ppermute | solution.py:206
  69.4 3.2 %collective-permute-start.25 = (bf16[4,64,1408]{2,1,0:T(8,128)(2,1)S(1)}, bf16[4,64,1408]{2,1,0:T(8,128)(2,1)S(1)}, u32[]{:S(2)}, u32[]{:S(2)}) collective-permute-start(bf16[4,64,1408]{2,1,0:T(8,128)(2,1)S(1)} %collective-permute-done.21.refs_3_), channel_id=1, source_target_pairs={{0,1},{1,0},{2,3},{3,2},{4,5},{5,4},{6,7},{7,6},{8,9},{9,8},{10,11... | collective-permute-start | bytes 2162696 | tf_op jit(solution)/shard_map/ppermute | solution.py:206
  89.7 8.8 %collective-permute-start.27 = (bf16[2,2,2,64,1408]{4,3,2,1,0:T(8,128)(2,1)}, bf16[2,2,2,64,1408]{4,3,2,1,0:T(8,128)(2,1)S(1)}, u32[]{:S(2)}, u32[]{:S(2)}) collective-permute-start(bf16[2,2,2,64,1408]{4,3,2,1,0:T(8,128)(2,1)} %get-tuple-element.162), channel_id=1, source_target_pairs={{0,1},{1,0},{2,3},{3,2},{4,5},{5,4},{6,7},{7,6},{8,9},{9,8},{10,11... | collective-permute-start | bytes 4325384 | tf_op jit(solution)/shard_map/ppermute | solution.py:206
  89.8 8.7 %collective-permute-start.28 = (bf16[2,2,2,64,1408]{4,3,2,1,0:T(8,128)(2,1)}, bf16[2,2,2,64,1408]{4,3,2,1,0:T(8,128)(2,1)S(1)}, u32[]{:S(2)}, u32[]{:S(2)}) collective-permute-start(bf16[2,2,2,64,1408]{4,3,2,1,0:T(8,128)(2,1)} %get-tuple-element.163), channel_id=1, source_target_pairs={{0,1},{1,0},{2,3},{3,2},{4,5},{5,4},{6,7},{7,6},{8,9},{9,8},{10,11... | collective-permute-start | bytes 4325384 | tf_op jit(solution)/shard_map/ppermute | solution.py:206
  90.2 8.3 %collective-permute-start.26 = (bf16[256,512]{1,0:T(8,128)(2,1)S(1)}, bf16[256,512]{1,0:T(8,128)(2,1)S(1)}, u32[]{:S(2)}, u32[]{:S(2)}) collective-permute-start(bf16[256,512]{1,0:T(8,128)(2,1)S(1)} %get-tuple-element.161), channel_id=1, source_target_pairs={{0,3},{3,0},{1,2},{2,1},{4,7},{7,4},{5,6},{6,5},{8,11},{11,8},{9,1... | collective-permute-start | bytes 786440 | tf_op jit(solution)/shard_map/ppermute | solution.py:214
  91.2 1.4 copy-start.2
  98.8 18.7 %collective-permute-start.29 = (bf16[2,2,64,1408]{3,2,1,0:T(8,128)(2,1)S(1)}, bf16[2,2,64,1408]{3,2,1,0:T(8,128)(2,1)S(1)}, u32[]{:S(2)}, u32[]{:S(2)}) collective-permute-start(bf16[2,2,64,1408]{3,2,1,0:T(8,128)(2,1)S(1)} %get-tuple-element.171), channel_id=1, source_target_pairs={{0,2},{2,0},{1,3},{3,1},{4,6},{6,4},{5,7},{7,5},{8,10},{10,8},{9,1... | collective-permute-start | bytes 2162696 | tf_op jit(solution)/shard_map/ppermute | solution.py:210
  100.2 17.9 %collective-permute-start.31 = (bf16[2,2,64,1408]{3,2,1,0:T(8,128)(2,1)S(1)}, bf16[2,2,64,1408]{3,2,1,0:T(8,128)(2,1)S(1)}, u32[]{:S(2)}, u32[]{:S(2)}) collective-permute-start(bf16[2,2,64,1408]{3,2,1,0:T(8,128)(2,1)S(1)} %get-tuple-element.172), channel_id=1, source_target_pairs={{0,4},{4,0},{8,12},{12,8},{16,20},{20,16},{24,28},{28,24},{1,5},{5... | collective-permute-start | bytes 2162696 | tf_op jit(solution)/shard_map/ppermute | solution.py:945
  115.8 1.6 collective-permute-start.30
  118.3 10.0 %collective-permute-start.33 = (bf16[2,64,1408]{2,1,0:T(8,128)(2,1)S(1)}, bf16[2,64,1408]{2,1,0:T(8,128)(2,1)S(1)}, u32[]{:S(2)}, u32[]{:S(2)}) collective-permute-start(bf16[2,64,1408]{2,1,0:T(8,128)(2,1)S(1)} %get-tuple-element.181), channel_id=1, source_target_pairs={{0,4},{4,0},{8,12},{12,8},{16,20},{20,16},{24,28},{28,24},{1,5},{5... | collective-permute-start | bytes 1081352 | tf_op jit(solution)/shard_map/ppermute | solution.py:945
  119.8 5.0 %collective-permute-start.32 = (bf16[2,128,256]{2,1,0:T(8,128)(2,1)S(1)}, bf16[2,128,256]{2,1,0:T(8,128)(2,1)S(1)}, u32[]{:S(2)}, u32[]{:S(2)}) collective-permute-start(bf16[2,128,256]{2,1,0:T(8,128)(2,1)S(1)} %shard_map.279), channel_id=1, source_target_pairs={{0,2},{2,0},{1,3},{3,1},{4,6},{6,4},{5,7},{7,5},{8,10},{10,8},{9,1... | collective-permute-start | bytes 393224 | tf_op jit(solution)/shard_map/ppermute | solution.py:210
  128.3 9.0 %collective-permute-start.34 = (bf16[2,64,1408]{2,1,0:T(8,128)(2,1)S(1)}, bf16[2,64,1408]{2,1,0:T(8,128)(2,1)S(1)}, u32[]{:S(2)}, u32[]{:S(2)}) collective-permute-start(bf16[2,64,1408]{2,1,0:T(8,128)(2,1)S(1)} %get-tuple-element.194), channel_id=1, source_target_pairs={{0,2},{2,0},{1,3},{3,1},{4,6},{6,4},{5,7},{7,5},{8,10},{10,8},{9,1... | collective-permute-start | bytes 1081352 | tf_op jit(solution)/shard_map/ppermute | solution.py:210
  129.3 7.3 %collective-permute-start.35 = (bf16[64,1408]{1,0:T(8,128)(2,1)S(1)}, bf16[64,1408]{1,0:T(8,128)(2,1)S(1)}, u32[]{:S(2)}, u32[]{:S(2)}) collective-permute-start(bf16[64,1408]{1,0:T(8,128)(2,1)S(1)} %get-tuple-element.196), channel_id=1, source_target_pairs={{0,8},{4,12},{8,16},{12,20},{16,24},{20,28},{24,0},{28,4},{1,9},{5... | collective-permute-start | bytes 540680 | tf_op jit(solution)/shard_map/ppermute | solution.py:948
  137.3 1.9 %collective-permute-start.36 = (bf16[2,2,2,80,384]{4,3,2,1,0:T(8,128)(2,1)S(1)}, bf16[2,2,2,80,384]{4,3,2,1,0:T(8,128)(2,1)S(1)}, u32[]{:S(2)}, u32[]{:S(2)}) collective-permute-start(bf16[2,2,2,80,384]{4,3,2,1,0:T(8,128)(2,1)S(1)} %get-tuple-element.204), channel_id=1, source_target_pairs={{0,1},{1,0},{2,3},{3,2},{4,5},{5,4},{6,7},{7,6},{8,9},{9,8},{10,11... | collective-permute-start | bytes 1474568 | tf_op jit(solution)/shard_map/ppermute | solution.py:206
  137.3 2.6 %collective-permute-start.37 = (bf16[2,2,2,80,384]{4,3,2,1,0:T(8,128)(2,1)S(1)}, bf16[2,2,2,80,384]{4,3,2,1,0:T(8,128)(2,1)S(1)}, u32[]{:S(2)}, u32[]{:S(2)}) collective-permute-start(bf16[2,2,2,80,384]{4,3,2,1,0:T(8,128)(2,1)S(1)} %get-tuple-element.211), channel_id=1, source_target_pairs={{0,1},{1,0},{2,3},{3,2},{4,5},{5,4},{6,7},{7,6},{8,9},{9,8},{10,11... | collective-permute-start | bytes 1474568 | tf_op jit(solution)/shard_map/ppermute | solution.py:206
  140.0 8.1 %collective-permute-start.38 = (bf16[2,2,80,384]{3,2,1,0:T(8,128)(2,1)S(1)}, bf16[2,2,80,384]{3,2,1,0:T(8,128)(2,1)S(1)}, u32[]{:S(2)}, u32[]{:S(2)}) collective-permute-start(bf16[2,2,80,384]{3,2,1,0:T(8,128)(2,1)S(1)} %get-tuple-element.213), channel_id=1, source_target_pairs={{0,2},{2,0},{1,3},{3,1},{4,6},{6,4},{5,7},{7,5},{8,10},{10,8},{9,1... | collective-permute-start | bytes 737288 | tf_op jit(solution)/shard_map/ppermute | solution.py:210
  140.8 7.7 %collective-permute-start.39 = (bf16[2,2,80,384]{3,2,1,0:T(8,128)(2,1)S(1)}, bf16[2,2,80,384]{3,2,1,0:T(8,128)(2,1)S(1)}, u32[]{:S(2)}, u32[]{:S(2)}) collective-permute-start(bf16[2,2,80,384]{3,2,1,0:T(8,128)(2,1)S(1)} %get-tuple-element.214), channel_id=1, source_target_pairs={{0,4},{4,0},{8,12},{12,8},{16,20},{20,16},{24,28},{28,24},{1,5},{5... | collective-permute-start | bytes 737288 | tf_op jit(solution)/shard_map/ppermute | solution.py:945
  141.4 9.3 %collective-permute-start.42 = (bf16[64,1408]{1,0:T(8,128)(2,1)S(1)}, bf16[64,1408]{1,0:T(8,128)(2,1)S(1)}, u32[]{:S(2)}, u32[]{:S(2)}) collective-permute-start(bf16[64,1408]{1,0:T(8,128)(2,1)S(1)} %shard_map.284), channel_id=1, source_target_pairs={{0,8},{4,12},{8,16},{12,20},{16,24},{20,28},{24,0},{28,4},{1,9},{5... | collective-permute-start | bytes 540680 | tf_op jit(solution)/shard_map/ppermute | solution.py:948
  142.6 9.7 %collective-permute-start.43 = (bf16[64,1408]{1,0:T(8,128)(2,1)S(1)}, bf16[64,1408]{1,0:T(8,128)(2,1)S(1)}, u32[]{:S(2)}, u32[]{:S(2)}) collective-permute-start(bf16[64,1408]{1,0:T(8,128)(2,1)S(1)} %get-tuple-element.208), channel_id=1, source_target_pairs={{0,24},{4,28},{8,0},{12,4},{16,8},{20,12},{24,16},{28,20},{1,25},{... | collective-permute-start | bytes 540680 | tf_op jit(solution)/shard_map/ppermute | solution.py:948
  148.7 4.9 %collective-permute-start.40 = (bf16[2,80,384]{2,1,0:T(8,128)(2,1)S(1)}, bf16[2,80,384]{2,1,0:T(8,128)(2,1)S(1)}, u32[]{:S(2)}, u32[]{:S(2)}) collective-permute-start(bf16[2,80,384]{2,1,0:T(8,128)(2,1)S(1)} %get-tuple-element.217), channel_id=1, source_target_pairs={{0,4},{4,0},{8,12},{12,8},{16,20},{20,16},{24,28},{28,24},{1,5},{5... | collective-permute-start | bytes 368648 | tf_op jit(solution)/shard_map/ppermute | solution.py:945
  149.3 4.9 %collective-permute-start.41 = (bf16[2,80,384]{2,1,0:T(8,128)(2,1)S(1)}, bf16[2,80,384]{2,1,0:T(8,128)(2,1)S(1)}, u32[]{:S(2)}, u32[]{:S(2)}) collective-permute-start(bf16[2,80,384]{2,1,0:T(8,128)(2,1)S(1)} %get-tuple-element.218), channel_id=1, source_target_pairs={{0,2},{2,0},{1,3},{3,1},{4,6},{6,4},{5,7},{7,5},{8,10},{10,8},{9,1... | collective-permute-start | bytes 368648 | tf_op jit(solution)/shard_map/ppermute | solution.py:210
  154.2 8.1 %collective-permute-start.44 = (bf16[256,512]{1,0:T(8,128)(2,1)S(1)}, bf16[256,512]{1,0:T(8,128)(2,1)S(1)}, u32[]{:S(2)}, u32[]{:S(2)}) collective-permute-start(bf16[256,512]{1,0:T(8,128)(2,1)S(1)} %get-tuple-element.220), channel_id=1, source_target_pairs={{0,3},{3,0},{1,2},{2,1},{4,7},{7,4},{5,6},{6,5},{8,11},{11,8},{9,1... | collective-permute-start | bytes 786440 | tf_op jit(solution)/shard_map/ppermute | solution.py:214
  154.2 0.8 copy-start.4
  155.0 8.4 %collective-permute-start.45 = (bf16[80,384]{1,0:T(8,128)(2,1)S(1)}, bf16[80,384]{1,0:T(8,128)(2,1)S(1)}, u32[]{:S(2)}, u32[]{:S(2)}) collective-permute-start(bf16[80,384]{1,0:T(8,128)(2,1)S(1)} %get-tuple-element.223), channel_id=1, source_target_pairs={{0,8},{4,12},{8,16},{12,20},{16,24},{20,28},{24,0},{28,4},{1,9},{5... | collective-permute-start | bytes 184328 | tf_op jit(solution)/shard_map/ppermute | solution.py:948
  156.3 8.1 %collective-permute-start.46 = (bf16[80,384]{1,0:T(8,128)(2,1)S(1)}, bf16[80,384]{1,0:T(8,128)(2,1)S(1)}, u32[]{:S(2)}, u32[]{:S(2)}) collective-permute-start(bf16[80,384]{1,0:T(8,128)(2,1)S(1)} %get-tuple-element.229), channel_id=1, source_target_pairs={{0,16},{4,20},{8,24},{12,28},{16,0},{20,4},{24,8},{28,12},{1,17},{... | collective-permute-start | bytes 184328 | tf_op jit(solution)/shard_map/ppermute | solution.py:948
  157.3 7.1 %collective-permute-start.47 = (bf16[80,384]{1,0:T(8,128)(2,1)S(1)}, bf16[80,384]{1,0:T(8,128)(2,1)S(1)}, u32[]{:S(2)}, u32[]{:S(2)}) collective-permute-start(bf16[80,384]{1,0:T(8,128)(2,1)S(1)} %get-tuple-element.230), channel_id=1, source_target_pairs={{0,24},{4,28},{8,0},{12,4},{16,8},{20,12},{24,16},{28,20},{1,25},{... | collective-permute-start | bytes 184328 | tf_op jit(solution)/shard_map/ppermute | solution.py:948

commit v5 on v4

--- a/solution.py
+++ b/solution.py
@@ -124,8 +124,10 @@
     return kept.astype(F32) + one.astype(F32) + two.astype(F32) + three.astype(F32)
 
 
-def unpack_first_kernel(kept, one, two, three, gq, gk, gv, gr, *refs):
-    vectors, (gb, total) = refs[:5], refs[5:]
+def unpack_first_kernel(kept, one, two, three, low, high, gq, gk, gv, gr, *refs):
+    vectors, (gb, tokens, total) = refs[:5], refs[5:]
+    tokens[0:HALF, :] = low[...]
+    tokens[HALF:, :] = high[...].astype(F32)
     total[...] = sum_four(kept[...], one[...], two[...], three[...])
     for j in range(gq.shape[0]):
         gq[j] = total[0:ROWS, j * HEAD : (j + 1) * HEAD]
@@ -141,7 +143,7 @@
     gb[...] = small[0:1, 2 * LANES : 2 * LANES + HEAD]
 
 
-def unpack_first(parts, experts, routed):
+def unpack_first(parts, low, high, experts, routed):
     outs = pl.pallas_call(
         unpack_first_kernel,
         cost_estimate=cost(2),
@@ -152,14 +154,17 @@
             shaped((TINY, routed), F32),
             *[shaped((1, TINY), F32) for _ in range(5)],
             shaped((1, HEAD), F32),
+            shaped((low.shape[0] + high.shape[0], low.shape[1]), F32),
         ),
         scratch_shapes=[pltpu.VMEM(parts[0].shape, F32)],
         compiler_params=params(8),
-    )(*parts)
-    return outs[0], outs[1], outs[2], outs[3], [v.reshape(-1) for v in outs[4:9]], outs[9].reshape(-1)
-
-
-def unpack_second_kernel(kept, one, three, go, gup, gdown, total, wide):
+    )(*parts, low, high)
+    return *outs[0:4], [v.reshape(-1) for v in outs[4:9]], outs[9].reshape(-1), outs[10]
+
+
+def unpack_second_kernel(kept, one, three, low, high, go, gup, gdown, rows, total, wide):
+    rows[0:HALF, :] = low[...]
+    rows[HALF:, :] = high[...]
     experts = go.shape[0]
     group, hidden = experts * HEAD, gup.shape[1]
     total[...] = kept[...].astype(F32) + one[...].astype(F32) + three[...].astype(F32)
@@ -172,7 +177,7 @@
     gdown[...] = total[:, group + hidden :]
 
 
-def unpack_second(kept, one, three, experts, hidden):
+def unpack_second(kept, one, three, low, high, experts, hidden):
     group = experts * HEAD
     return pl.pallas_call(
         unpack_second_kernel,
@@ -181,13 +186,14 @@
             shaped((experts, HEAD, ROWS), F32),
             shaped((ROWS, hidden), F32),
             shaped((ROWS, hidden), F32),
+            shaped((low.shape[0] + high.shape[0], low.shape[1]), BF16),
         ),
         scratch_shapes=[
             pltpu.VMEM(kept.shape, F32),
             pltpu.VMEM((LANES, group), F32),
         ],
         compiler_params=params(8),
-    )(kept, one, three)
+    )(kept, one, three, low, high)
 
 
 def axis_moves(dp):
@@ -581,16 +587,8 @@
             out[place[0], place[1], place[2], 0:ROWS, column_to : column_to + wide] = block
 
 
-def middle_kernel(table, low_tok, low_cot, cross, heads, gates, routes, vectors, up_bias, *refs):
-    pieces = refs[:8]
-    low_out, high_out, grad_mid, back, sums, bias_grad = refs[8:14]
-    blocks = refs[14:18]
-    weight, mixed, turned, ordered, hid_scr, pre_scr = refs[18:]
+def prepare_kernel(table, heads, gates, routes, low_cot, cross, mixed, cot_t, turned):
     ways, rows, _ = heads.shape
-    width = low_tok.shape[1]
-    group = mixed.shape[2]
-    hidden = hid_scr.shape[2]
-    place_weights(table, pieces, weight)
 
     def expand(at):
         held = [
@@ -599,6 +597,31 @@
         spread_pairs(table, routes, at, held, mixed)
 
     over_chunks(rows, expand)
+    turned[...] = jnp.concatenate([low_cot[0:HALF, :], cross[HALF:, :]], axis=0).T
+    in_order(table, turned, cot_t)
+
+
+def prepare_stage(table, heads, gates, routes, cot, cross, group):
+    rows, width = cot.shape
+    return pl.pallas_call(
+        prepare_kernel,
+        cost_estimate=cost(0.3),
+        in_specs=[smem_spec()] + [pl.BlockSpec(memory_space=pltpu.VMEM)] * 5,
+        out_shape=(shaped((4, rows, group), BF16), shaped((width, rows), BF16)),
+        scratch_shapes=[pltpu.VMEM((width, rows), BF16)],
+        compiler_params=params(12),
+    )(table, heads, gates, routes, cot, cross)
+
+
+def middle_kernel(table, low_tok, low_cot, cross, mixed, cot_t, vectors, up_bias, *refs):
+    pieces = refs[:8]
+    low_out, high_out, grad_mid, back, sums, bias_grad = refs[8:14]
+    blocks = refs[14:18]
+    weight, turned, ordered, hid_scr, pre_scr = refs[18:]
+    rows, width = low_tok.shape
+    group = mixed.shape[2]
+    hidden = hid_scr.shape[2]
+    place_weights(table, pieces, weight)
     middle = jnp.concatenate([low_tok[0:HALF, :], cross[0:HALF, :]], axis=0).astype(F32)
     for slot in range(4):
         middle = middle + nt(mixed[slot], weight[slot, :, 0:group])
@@ -608,8 +631,6 @@
     turned[0] = normed.T
     in_order(table, turned.at[0], ordered.at[0])
     cot = jnp.concatenate([low_cot[0:HALF, :], cross[HALF:, :]], axis=0)
-    turned[1] = cot.T
-    in_order(table, turned.at[1], ordered.at[1])
     result = middle + vectors[4:5, :]
     grad_normed = jnp.zeros((rows, width), F32)
     up_at, down_at = group, group + hidden
@@ -628,7 +649,7 @@
         result = result + nt(hid_scr[slot], weight[slot, :, down_at:])
         grad_normed = grad_normed + nt(pre_scr[slot], weight[slot, :, up_at:down_at])
         put_blocks(nn(ordered[0], pre_scr[slot]), blocks, slot, up_at)
-        put_blocks(nn(ordered[1], hid_scr[slot]), blocks, slot, down_at)
+        put_blocks(nn(cot_t[...], hid_scr[slot]), blocks, slot, down_at)
     low_out[...] = result[0:HALF].astype(BF16)
     high_out[...] = result[HALF:].astype(BF16)
     cot_wide = cot.astype(F32)
@@ -639,10 +660,10 @@
     grad_middle = cot_wide + norm_backward(grad_normed, scaled, inverse, gain)
     grad_mid[...] = grad_middle
     grad_attn = grad_middle.astype(BF16)
-    turned[2] = grad_attn.T
-    in_order(table, turned.at[2], ordered.at[2])
+    turned[1] = grad_attn.T
+    in_order(table, turned.at[1], ordered.at[1])
     for slot in range(4):
-        put_blocks(nn(ordered[2], mixed[slot]), blocks, slot, 0)
+        put_blocks(nn(ordered[1], mixed[slot]), blocks, slot, 0)
         back[slot] = nn(grad_attn, weight[slot, :, 0:group]).astype(BF16)
 
 
@@ -676,7 +697,7 @@
     )(table, back, heads, gates, routes)
 
 
-def middle_stage(table, tokens, cot, cross, heads, gates, routes, vectors, up_bias, pieces):
+def middle_stage(table, tokens, cot, cross, mixed, cot_t, vectors, up_bias, pieces):
     rows, width = tokens.shape
     packed = pieces[0].shape[2]
     hidden = up_bias.shape[1]
@@ -686,7 +707,7 @@
     return pl.pallas_call(
         middle_kernel,
         cost_estimate=cost(36),
-        in_specs=[smem_spec()] + [vmem] * 16,
+        in_specs=[smem_spec()] + [vmem] * 15,
         out_shape=(
             shaped((HALF, width), BF16),
             shaped((rows - HALF, width), BF16),
@@ -701,14 +722,13 @@
         ),
         scratch_shapes=[
             pltpu.VMEM((4, width, packed), BF16),
-            pltpu.VMEM((4, rows, group), BF16),
-            pltpu.VMEM((3, width, rows), BF16),
-            pltpu.VMEM((3, width, rows), BF16),
+            pltpu.VMEM((2, width, rows), BF16),
+            pltpu.VMEM((2, width, rows), BF16),
             pltpu.VMEM((4, rows, hidden), BF16),
             pltpu.VMEM((4, rows, hidden), BF16),
         ],
-        compiler_params=params(40),
-    )(table, tokens, cot, cross, heads, gates, routes, vectors, up_bias, *pieces)
+        compiler_params=params(28),
+    )(table, tokens, cot, cross, mixed, cot_t, vectors, up_bias, *pieces)
 
 
 def spread_kernel(table, grad_query, normed, routes, spread, grads, turned, normed_t):
@@ -965,9 +985,9 @@
         side_a = jnp.concatenate([side_a, after(next_a, later_z1, later_z3, cross)], axis=0)
         side_b = jnp.concatenate([side_b, after(next_b, later_z1, later_z3, cross)], axis=0)
         far_a, far_b = over_x(side_a), over_y(side_b)
-        far_a, far_b, later_z2 = together(far_a, far_b, later_z2)
-        later_a = jnp.concatenate([after(second, far_a), later_z1], axis=0)
+        later_a = jnp.concatenate([second, later_z1], axis=0)
         later_b = jnp.concatenate([later_z2, later_z3], axis=0)
+        far_a, far_b, later_a, later_b = together(far_a, far_b, later_a, later_b)
         next_a, next_b = over_y(later_a), over_x(later_b)
         first_pieces = [side_a, far_a, side_b, far_b]
         first_pieces = first_pieces + [over_core(v) for v in first_pieces]
@@ -989,20 +1009,19 @@
         side_b = jnp.concatenate([later_b, after(next_b, query, pair_y)], axis=0)
         far_a, far_b = over_x(side_a), over_y(side_b)
     heads, totals = attend_stage(table, query, pairs, seq)
+    mixed, cot_t = prepare_stage(table, heads, gates, own_routes, cotangent, cross, query_weight.shape[2])
     if tuned:
-        heads, far_a, far_b, core_a, core_b = together(heads, far_a, far_b, over_core(side_a), over_core(side_b))
+        mixed, far_a, far_b, core_a, core_b = together(mixed, far_a, far_b, over_core(side_a), over_core(side_b))
         second_pieces = [side_a, far_a, side_b, far_b, core_a, over_core(far_a), core_b, over_core(far_b)]
     output, output_high, grad_mid, back, sums, bias_grad, *later_blocks = middle_stage(
-        table, tokens, cotangent, cross, heads, gates, own_routes, vectors, up_bias, second_pieces
+        table, tokens, cotangent, cross, mixed, cot_t, vectors, up_bias, second_pieces
     )
     if tuned:
         keep_a, keep_b, send_a, send_b = later_blocks
         got_a, got_b = over_core(send_a), over_core(send_b)
     grad_heads, grad_gate = select_stage(table, back, heads, gates, own_routes)
     if tuned:
-        grad_heads, grad_gate, output_high, got_a, got_b = together(
-            grad_heads, grad_gate, crossed(output_high), got_a, got_b
-        )
+        grad_heads, grad_gate, got_a, got_b = together(grad_heads, grad_gate, got_a, got_b)
         part_a, part_b = add_blocks(
             "add_near", [(keep_a, (1,)), (got_a, (1,))], [(keep_b, (1,)), (got_b, (1,))]
         )
@@ -1027,7 +1046,7 @@
         output_high = crossed(output_high)
     spread, query_grads = spread_stage(table, grad_query, normed, own_routes, query_weight.shape[2])
     if tuned:
-        spread, pair_far, last_a = together(spread, pair_parts[2], last_a)
+        spread, pair_far = together(spread, pair_parts[2])
         pair_parts = (*pair_parts[0:2], pair_far)
         last_b = over_y(after(part_b, pair_far, spread))
 
@@ -1041,28 +1060,27 @@
                 ],
             )
 
-        ahead, beyond = final("add_last", (keep_a, got_a, next_a, last_a))
-        beyond = over_z(beyond, 1)
     low_rows, high_rows, *first_blocks = last_stage(
         table, tokens, cross, grad_mid, spread, normed, own_routes, gates, grad_gate,
         query_weight, small, vectors, sums, bias_grad, pair_parts, query_grads,
     )
     if tuned:
-        low_rows, high_rows, last_b, beyond, *first_blocks = together(
-            low_rows, high_rows, last_b, beyond, *first_blocks
-        )
-        first_got = over_core(first_blocks[2]), over_core(first_blocks[3])
+        last_a = after(last_a, low_rows)
+        ahead, beyond = final("add_last", (keep_a, got_a, next_a, last_a))
+        beyond = over_z(beyond, 1)
+        low_rows, high_rows, last_b, *first_blocks = together(low_rows, high_rows, last_b, *first_blocks)
+        output_high = crossed(after(output_high, last_b))
         kept, back = final("add_last", (keep_b, got_b, next_b, last_b))
+        keep_a, keep_b, send_a, send_b = first_blocks
+        got_a, got_b, beyond, back = together(over_core(send_a), over_core(send_b), beyond, back)
         (ahead,) = add_blocks("add_ahead", [(ahead, ()), (beyond, ())])
         one, three = over_z(ahead, 1), over_z(back, 3)
-        keep_a, keep_b = first_blocks[0:2]
-        got_a, got_b = first_got
-        got_a, got_b = after(got_a, ahead, back), after(got_b, ahead, back)
+        got_a, got_b = after(got_a, ahead), after(got_b, ahead)
         part_a, part_b = add_blocks(
             "add_near", [(keep_a, (1,)), (got_a, (1,))], [(keep_b, (1,)), (got_b, (1,))]
         )
         next_a, next_b = over_y(part_a), over_x(part_b)
-        next_a, next_b = together(next_a, next_b)
+        next_a, next_b, output_high = together(next_a, next_b, output_high)
         part_a, part_b = add_blocks(
             "add_far",
             [(keep_a, (0, 1)), (got_a, (0, 1)), (next_a, (1,))],
@@ -1071,17 +1089,17 @@
         last_a, last_b = over_x(part_a), over_y(part_b)
         last_a, last_b, one, three = together(last_a, last_b, one, three)
         high_rows = after(high_rows, last_b)
-        out_grad, up_grad, down_grad = unpack_second(kept, one, three, experts, hidden)
+        out_grad, up_grad, down_grad, result = unpack_second(
+            kept, one, three, output, output_high, experts, hidden
+        )
         down_grad = down_grad.T
         done = final("add_last", (keep_a, got_a, next_a, last_a), (keep_b, got_b, next_b, last_b))
         done = (done[2], done[0], done[1], done[3])
         one, two, three = [over_z(done[step], step) for step in (1, 2, 3)]
-        result = jnp.concatenate([output, output_high], axis=0)
-        grad_tokens = jnp.concatenate([low_rows, crossed(high_rows).astype(F32)], axis=0)
-        one = after(one, out_grad, result, grad_tokens)
+        one = after(one, out_grad)
         parts = (done[0], one, two, three)
-        query_grad, key_grad, value_grad, router_grad, small_grads, up_bias_grad = unpack_first(
-            parts, experts, routed
+        query_grad, key_grad, value_grad, router_grad, small_grads, up_bias_grad, grad_tokens = unpack_first(
+            parts, low_rows, crossed(high_rows), experts, routed
         )
     else:
         (

time: 166 us -> 156 us (0.940)
  waiting for transfers between devices: 48 us -> 43.5 us
  starting transfers between devices: 43.2 us -> 40.6 us
  local copies, waits for them, and re-layouts: 4.15 us -> 2.01 us
    ppermute x8, waiting for transfers between devices: 9.08 us -> 2.75 us  [over_x(): return lax.ppermute(x, 'dp', swap)]
    pallas_call x1, Pallas kernels: 17.1 us -> 12.1 us  [middle_stage(): pl.pallas_call(middle_kernel, cost_estimate=cost(36), in_specs=[smem_spec...]
    ppermute x12, waiting for transfers between devices: 17.9 us -> 21.9 us  [over_z(): return lax.ppermute(x, 'dp', turns[step - 1])]
    pallas_call x0 -> x1, Pallas kernels: none -> 3.93 us  [prepare_stage(): pl.pallas_call(prepare_kernel, cost_estimate=cost(0.3), in_specs=[smem_sp...]
    ppermute x3, waiting for transfers between devices: 3.81 us -> 0.01 us  [crossed(): return lax.ppermute(x, 'tensor', CROSSED)]
    ppermute x10, waiting for transfers between devices: 8.69 us -> 11.9 us  [over_y(): return lax.ppermute(x, 'tensor', ACROSS)]
    unnamed x19 -> x16, local copies, waits for them, and re-layouts: 3.04 us -> 0.96 us
  transfers between devices with their start and end apart: 48 -> 48, of which waited for: 28 -> 26; matrix products, arithmetic and copies ran while one was open for 2% -> 3% of each run, Pallas kernels for 28% -> 32%
where the time goes in v5:
time: 156 us
  Pallas kernels  66.3 us (42%)
  waiting for transfers between devices  43.5 us (28%)
  starting transfers between devices  40.6 us (26%)
  other arithmetic  2.41 us (2%)
  local copies, waits for them, and re-layouts  2.01 us (1%)
    ppermute x12, waiting for transfers between devices, over_z(): return lax.ppermute(x, 'dp', turns[step - 1])  21.9 us
    ppermute x12, starting transfers between devices, over_z(): return lax.ppermute(x, 'dp', turns[step - 1])  17.9 us
    pallas_call x1, Pallas kernels, attend_back_stage(): pl.pallas_call(attend_back_kernel, cost_estimate=cost(16), grid=(rows //...  14.3 us
    pallas_call x1, Pallas kernels, middle_stage(): pl.pallas_call(middle_kernel, cost_estimate=cost(36), in_specs=[smem_spec...  12.1 us
    ppermute x10, waiting for transfers between devices, over_y(): return lax.ppermute(x, 'tensor', ACROSS)  11.9 us
    ppermute x10, starting transfers between devices, over_y(): return lax.ppermute(x, 'tensor', ACROSS)  10.6 us
    pallas_call x1, Pallas kernels, attend_stage(): pl.pallas_call(attend_kernel, cost_estimate=cost(1.2), grid=(rows // HALF...  10.5 us
    ppermute x8, starting transfers between devices, over_x(): return lax.ppermute(x, 'dp', swap)  8.83 us
  transfers between devices with their start and end apart: 48, of which 26 were waited for; matrix products, arithmetic and copies ran while one was open for 3% of the time, Pallas kernels for 32%

profile of v5, /device:TPU:0, one launch (start us, length us, event | category | flops | bytes accessed | tf_op | source)
XLA Modules:
  0.0 155.8 jit_solution(4971015770538445756)
XLA Ops:
  0.7 2.4 %shard_map.271 = (bf16[80,384]{1,0:T(8,128)(2,1)}, bf16[64,1408]{1,0:T(8,128)(2,1)}, bf16[512,512]{1,0:T(8,128)(2,1)}) custom-call(bf16[6,64,64]{2,1,0:T(8,128)(2,1)} %wq.1, bf16[6,64,64]{2,1,0:T(8,128)(2,1)} %wo.1, bf16[64,512]{1,0:T(8,128)(2,1)} %wup.1, bf16[64,512]{1,0:T(8,128)(2,1)} %bitcast.46, bf16[16,64]{1,0:T(8,128)(2,1)} %wk.1, bf16[16,64]{1,0:T(8,128)(2,1)} %wv.1, ...), custom_call_target="tpu_custom_call" | custom-call | bytes 738000 | tf_op jit(solution)/shard_map/pallas_call | solution.py:107
  3.1 5.0 %collective-permute-start.7 = (bf16[1,80,384]{2,1,0:T(8,128)(2,1)}, bf16[1,80,384]{2,1,0:T(8,128)(2,1)S(1)}, u32[]{:S(2)}, u32[]{:S(2)}) collective-permute-start(bf16[1,80,384]{2,1,0:T(8,128)(2,1)} %bitcast.38), channel_id=1, source_target_pairs={{0,24},{4,28},{8,0},{12,4},{16,8},{20,12},{24,16},{28,20},{1,25},{... | collective-permute-start | bytes 184328 | tf_op jit(solution)/shard_map/ppermute | solution.py:968
  8.1 1.0 collective-permute-start.1
  9.3 0.7 constant_dynamic-slice_fusion.1
  10.1 0.8 constant_dynamic-update-slice_fusion.2
  10.9 3.5 %collective-permute-done.1 = bf16[1,80,384]{2,1,0:T(8,128)(2,1)S(1)} collective-permute-done((bf16[1,80,384]{2,1,0:T(8,128)(2,1)}, bf16[1,80,384]{2,1,0:T(8,128)(2,1)S(1)}, u32[]{:S(2)}, u32[]{:S(2)}) %collective-permute-start.1) | collective-permute-done | bytes 61472 | tf_op jit(solution)/shard_map/ppermute | solution.py:968
  14.5 1.1 collective-permute-start.4
  15.6 0.9 collective-permute-start.3
  16.5 1.6 collective-permute-start.8
  18.1 0.8 pad_maximum_fusion.2
  18.9 1.6 %collective-permute-start.2 = (bf16[2,80,384]{2,1,0:T(8,128)(2,1)S(1)}, bf16[2,80,384]{2,1,0:T(8,128)(2,1)S(1)}, u32[]{:S(2)}, u32[]{:S(2)}) collective-permute-start(bf16[2,80,384]{2,1,0:T(8,128)(2,1)S(1)} %pad_maximum_fusion.2), channel_id=1, source_target_pairs={{0,2},{2,0},{1,3},{3,1},{4,6},{6,4},{5,7},{7,5},{8,10},{10,8},{9,1... | collective-permute-start | bytes 368648 | tf_op jit(solution)/shard_map/ppermute | solution.py:216
  20.6 5.2 %collective-permute-done.3 = bf16[1,64,1408]{2,1,0:T(8,128)(2,1)S(1)} collective-permute-done((bf16[1,64,1408]{2,1,0:T(8,128)(2,1)}, bf16[1,64,1408]{2,1,0:T(8,128)(2,1)S(1)}, u32[]{:S(2)}, u32[]{:S(2)}) %collective-permute-start.3) | collective-permute-done | bytes 180256 | tf_op jit(solution)/shard_map/ppermute | solution.py:968
  26.2 1.6 collective-permute-start.5
  27.8 1.2 collective-permute-start.9
  29.0 0.8 pad_maximum_fusion
  29.8 3.3 %collective-permute-done.10 = bf16[1,64,1408]{2,1,0:T(8,128)(2,1)S(1)} collective-permute-done((bf16[1,64,1408]{2,1,0:T(8,128)(2,1)S(1)}, bf16[1,64,1408]{2,1,0:T(8,128)(2,1)S(1)}, u32[]{:S(2)}, u32[]{:S(2)}) %collective-permute-start.10) | collective-permute-done | bytes 180256 | tf_op jit(solution)/shard_map/ppermute | solution.py:968
  33.1 0.8 pad_maximum_fusion.1
  33.9 0.5 collective-permute-start.13
  34.4 1.2 collective-permute-done.9.refs_3_
  35.5 0.5 collective-permute-start.14
  36.2 0.8 collective-permute-start.18
  37.0 1.1 collective-permute-start.20
  38.1 2.5 %shard_map.272 = (bf16[512,512]{1,0:T(8,128)(2,1)S(1)}, bf16[512,128]{1,0:T(8,128)(2,1)S(1)}, f32[512,128]{1,0:T(8,128)S(1)}, bf16[512,384]{1,0:T(8,128)(2,1)S(1...) custom-call(s32[28]{0:T(128)S(1)} %stack.97.table, bf16[512,512]{1,0:T(8,128)(2,1)S(1)} %copy-done, ...), custom_call_target="tpu_custom_call" | custom-call | bytes 1845000 | tf_op jit(solution)/shard_map/pallas_call | solution.py:308
  40.6 0.8 collective-permute-start.16
  41.4 4.2 %shard_map.273 = (bf16[8,512,128]{2,1,0:T(8,128)(2,1)S(1)}, bf16[4,512,384]{2,1,0:T(8,128)(2,1)S(1)}) custom-call(s32[28]{0:T(128)S(1)} %stack.97.table, bf16[512,512]{1,0:T(8,128)(2,1)S(1)} %get-tuple-element.149.normed, s32[512,8]{1,0:T(8,128)S(1)} %copy.33.routes, bf16[4,80,384]{2,1,0:T(8,128)(2,1)S(1)} %constant_dynamic-update-slice_fusion.refs_0_, ...), custom_call_target="tpu_custom_call" | custom-call | bytes 2952000 | tf_op jit(solution)/shard_map/pallas_call | solution.py:383
  45.6 2.1 %collective-permute-done.18 = bf16[2,64,1408]{2,1,0:T(8,128)(2,1)S(1)} collective-permute-done((bf16[2,64,1408]{2,1,0:T(8,128)(2,1)}, bf16[2,64,1408]{2,1,0:T(8,128)(2,1)S(1)}, u32[]{:S(2)}, u32[]{:S(2)}) %collective-permute-start.18) | collective-permute-done | bytes 360480 | tf_op jit(solution)/shard_map/ppermute | solution.py:216
  47.8 0.6 collective-permute-start.19
  48.4 1.1 collective-permute-done.16.kv2
  49.7 0.8 collective-permute-start.21
  50.7 1.4 collective-permute-done.15.kv1
  52.2 1.2 collective-permute-done.17.kv3
  53.4 10.5 %shard_map.274 = (bf16[8,512,128]{2,1,0:T(8,128)(2,1)S(1)}, f32[512,128]{1,0:T(8,128)S(1)}) custom-call(s32[28]{0:T(128)S(1)} %stack.97.table, bf16[8,512,128]{2,1,0:T(8,128)(2,1)S(1)} %get-tuple-element.150.query, bf16[512,128]{1,0:T(8,128)(2,1)S(1)} %get-tuple-element.151.kv0, bf16[512,128]{1,0:T(8,128)(2,1)S(1)} %collective-permute-done.15.kv1, ...), custom_call_target="tpu_custom_call" | custom-call | bytes 4428000 | tf_op jit(solution)/shard_map/pallas_call | solution.py:467
  63.9 3.9 %shard_map.275 = (bf16[4,512,384]{2,1,0:T(8,128)(2,1)S(1)}, bf16[512,512]{1,0:T(8,128)(2,1)S(1)}) custom-call(s32[28]{0:T(128)S(1)} %stack.97.table, bf16[8,512,128]{2,1,0:T(8,128)(2,1)S(1)} %get-tuple-element.152.heads, f32[512,128]{1,0:T(8,128)S(1)} %get-tuple-element.153.gates, s32[512,8]{1,0:T(8,128)S(1)} %copy.33.routes, ...), custom_call_target="tpu_custom_call" | custom-call | bytes 1107000 | tf_op jit(solution)/shard_map/pallas_call | solution.py:606
  68.7 1.7 %collective-permute-done.24.refs_5_ = bf16[4,64,1408]{2,1,0:T(8,128)(2,1)S(1)} collective-permute-done((bf16[4,64,1408]{2,1,0:T(8,128)(2,1)S(1)}, bf16[4,64,1408]{2,1,0:T(8,128)(2,1)S(1)}, u32[]{:S(2)}, u32[]{:S(2)}) %collective-permute-start.24) | collective-permute-done | bytes 720928 | tf_op jit(solution)/shard_map/ppermute | solution.py:212
  70.4 1.0 collective-permute-done.25.refs_7_
  71.5 12.1 %shard_map.276 = (bf16[256,512]{1,0:T(8,128)(2,1)S(1)}, bf16[256,512]{1,0:T(8,128)(2,1)S(1)}, f32[512,512]{1,0:T(8,128)S(1)}, bf16[4,512,384]{2,1,0:T(8,128)(2,1...) custom-call(s32[28]{0:T(128)S(1)} %stack.97.table, ...), custom_call_target="tpu_custom_call" | custom-call | bytes 132840000 | tf_op jit(solution)/shard_map/pallas_call | solution.py:707
  84.2 4.7 %shard_map.277 = (bf16[8,512,128]{2,1,0:T(8,128)(2,1)S(1)}, f32[512,128]{1,0:T(8,128)S(1)}) custom-call(s32[28]{0:T(128)S(1)} %stack.97.table, bf16[4,512,384]{2,1,0:T(8,128)(2,1)S(1)} %get-tuple-element.168.back, bf16[8,512,128]{2,1,0:T(8,128)(2,1)S(1)} %get-tuple-element.152.heads, f32[512,128]{1,0:T(8,128)S(1)} %get-tuple-element.153.gates, ...), custom_call_target="tpu_custom_call" | custom-call | bytes 29520000 | tf_op jit(solution)/shard_map/pallas_call | solution.py:688
  89.3 0.8 collective-permute-start.28
  90.1 1.2 collective-permute-start.30
  91.3 14.3 %shard_map.279 = (bf16[8,512,128]{2,1,0:T(8,128)(2,1)S(1)}, bf16[2,2,128,256]{3,2,1,0:T(8,128)(2,1)S(1)}, bf16[2,2,128,256]{3,2,1,0:T(8,128)(2,1)S(1)}) custom-call(s32[28]{0:T(128)S(1)} %stack.97.table, bf16[8,512,128]{2,1,0:T(8,128)(2,1)S(1)} %get-tuple-element.150.query, bf16[8,512,128]{2,1,0:T(8,128)(2,1)S(1)} %get-tuple-element.179.grad, ...), custom_call_target="tpu_custom_call" | custom-call | bytes 59040000 | tf_op jit(solution)/shard_map/pallas_call | solution.py:547
  105.7 1.5 collective-permute-done.29.refs_1_.pair_got
  107.2 0.9 collective-permute-start.31
  108.4 4.2 %shard_map.282 = (bf16[4,512,384]{2,1,0:T(8,128)(2,1)S(1)}, bf16[4,512,384]{2,1,0:T(8,128)(2,1)S(1)}) custom-call(s32[28]{0:T(128)S(1)} %stack.97.table, bf16[8,512,128]{2,1,0:T(8,128)(2,1)S(1)} %get-tuple-element.190.grad_query, bf16[512,512]{1,0:T(8,128)(2,1)S(1)} %get-tuple-element.149.normed, s32[512,8]{1,0:T(8,128)S(1)} %copy.33.routes), custom_call_target="tpu_custom_call" | custom-call | bytes 22140000 | tf_op jit(solution)/shard_map/pallas_call | solution.py:750
  112.8 1.0 collective-permute-start.32
  113.9 1.1 collective-permute-start.35
  115.0 3.9 %shard_map.283 = (f32[256,512]{1,0:T(8,128)S(1)}, bf16[256,512]{1,0:T(8,128)(2,1)S(1)}, bf16[2,2,2,80,384]{4,3,2,1,0:T(8,128)(2,1)S(1)}, bf16[2,2,2,80,384]{4,3,...) custom-call(s32[28]{0:T(128)S(1)} %stack.97.table, ...), custom_call_target="tpu_custom_call" | custom-call | bytes 25830000 | tf_op jit(solution)/shard_map/pallas_call | solution.py:818
  118.9 4.0 %collective-permute-done.32.refs_3_.refs_7_ = bf16[2,64,1408]{2,1,0:T(8,128)(2,1)S(1)} collective-permute-done((bf16[2,64,1408]{2,1,0:T(8,128)(2,1)S(1)}, bf16[2,64,1408]{2,1,0:T(8,128)(2,1)S(1)}, u32[]{:S(2)}, u32[]{:S(2)}) %collective-permute-start.32) | collective-permute-done | bytes 360480 | tf_op jit(solution)/shard_map/ppermute | solution.py:216
  124.0 1.9 %collective-permute-start.36 = (bf16[64,1408]{1,0:T(8,128)(2,1)S(1)}, bf16[64,1408]{1,0:T(8,128)(2,1)S(1)}, u32[]{:S(2)}, u32[]{:S(2)}) collective-permute-start(bf16[64,1408]{1,0:T(8,128)(2,1)S(1)} %get-tuple-element.212), channel_id=1, source_target_pairs={{0,8},{4,12},{8,16},{12,20},{16,24},{20,28},{24,0},{28,4},{1,9},{5... | collective-permute-start | bytes 540680 | tf_op jit(solution)/shard_map/ppermute | solution.py:968
  126.2 5.7 %collective-permute-done.36.refs_1_ = bf16[64,1408]{1,0:T(8,128)(2,1)S(1)} collective-permute-done((bf16[64,1408]{1,0:T(8,128)(2,1)S(1)}, bf16[64,1408]{1,0:T(8,128)(2,1)S(1)}, u32[]{:S(2)}, u32[]{:S(2)}) %collective-permute-start.36) | collective-permute-done | bytes 180256 | tf_op jit(solution)/shard_map/ppermute | solution.py:968
  132.0 1.3 collective-permute-start.37
  133.3 0.9 collective-permute-start.38
  134.2 0.7 collective-permute-start.42
  134.9 3.2 %collective-permute-start.43 = (bf16[64,1408]{1,0:T(8,128)(2,1)S(1)}, bf16[64,1408]{1,0:T(8,128)(2,1)S(1)}, u32[]{:S(2)}, u32[]{:S(2)}) collective-permute-start(bf16[64,1408]{1,0:T(8,128)(2,1)S(1)} %get-tuple-element.229), channel_id=1, source_target_pairs={{0,24},{4,28},{8,0},{12,4},{16,8},{20,12},{24,16},{28,20},{1,25},{... | collective-permute-start | bytes 540680 | tf_op jit(solution)/shard_map/ppermute | solution.py:968
  138.1 1.6 %collective-permute-done.37.refs_2_.refs_6_ = bf16[2,2,80,384]{3,2,1,0:T(8,128)(2,1)S(1)} collective-permute-done((bf16[2,2,80,384]{3,2,1,0:T(8,128)(2,1)S(1)}, bf16[2,2,80,384]{3,2,1,0:T(8,128)(2,1)S(1)}, u32[]{:S(2)}, u32[]{:S(2)}) %collective-permute-start.37) | collective-permute-done | bytes 245792 | tf_op jit(solution)/shard_map/ppermute | solution.py:216
  140.1 1.2 collective-permute-start.40
  141.3 1.0 collective-permute-start.41
  143.1 2.0 %collective-permute-done.40.refs_3_.refs_7_ = bf16[2,80,384]{2,1,0:T(8,128)(2,1)S(1)} collective-permute-done((bf16[2,80,384]{2,1,0:T(8,128)(2,1)S(1)}, bf16[2,80,384]{2,1,0:T(8,128)(2,1)S(1)}, u32[]{:S(2)}, u32[]{:S(2)}) %collective-permute-start.40) | collective-permute-done | bytes 122912 | tf_op jit(solution)/shard_map/ppermute | solution.py:965
  145.0 1.1 collective-permute-done.41.refs_11_.refs_15_
  146.6 1.7 %collective-permute-start.45 = (bf16[80,384]{1,0:T(8,128)(2,1)S(1)}, bf16[80,384]{1,0:T(8,128)(2,1)S(1)}, u32[]{:S(2)}, u32[]{:S(2)}) collective-permute-start(bf16[80,384]{1,0:T(8,128)(2,1)S(1)} %get-tuple-element.241), channel_id=1, source_target_pairs={{0,16},{4,20},{8,24},{12,28},{16,0},{20,4},{24,8},{28,12},{1,17},{... | collective-permute-start | bytes 184328 | tf_op jit(solution)/shard_map/ppermute | solution.py:968
  148.3 1.9 %collective-permute-start.46 = (bf16[80,384]{1,0:T(8,128)(2,1)S(1)}, bf16[80,384]{1,0:T(8,128)(2,1)S(1)}, u32[]{:S(2)}, u32[]{:S(2)}) collective-permute-start(bf16[80,384]{1,0:T(8,128)(2,1)S(1)} %get-tuple-element.242), channel_id=1, source_target_pairs={{0,24},{4,28},{8,0},{12,4},{16,8},{20,12},{24,16},{28,20},{1,25},{... | collective-permute-start | bytes 184328 | tf_op jit(solution)/shard_map/ppermute | solution.py:968
  150.2 1.0 shard_map.289
  151.3 1.9 %collective-permute-done.44.one = bf16[80,384]{1,0:T(8,128)(2,1)S(1)} collective-permute-done((bf16[80,384]{1,0:T(8,128)(2,1)S(1)}, bf16[80,384]{1,0:T(8,128)(2,1)S(1)}, u32[]{:S(2)}, u32[]{:S(2)}) %collective-permute-start.44) | collective-permute-done | bytes 61472 | tf_op jit(solution)/shard_map/ppermute | solution.py:968
  153.1 1.5 collective-permute-done.45.two
  154.7 1.1 shard_map.291
  (81 shorter events, 7.1 us)
Async XLA Ops:
  3.1 25.9 %copy-start.4 = (bf16[64,1408]{1,0:T(8,128)(2,1)S(1)}, bf16[64,1408]{1,0:T(8,128)(2,1)}, u32[]{:S(2)}) copy-start(bf16[64,1408]{1,0:T(8,128)(2,1)} %get-tuple-element.140) | copy-start | bytes 540676
  3.1 13.4 %collective-permute-start.7 = (bf16[1,80,384]{2,1,0:T(8,128)(2,1)}, bf16[1,80,384]{2,1,0:T(8,128)(2,1)S(1)}, u32[]{:S(2)}, u32[]{:S(2)}) collective-permute-start(bf16[1,80,384]{2,1,0:T(8,128)(2,1)} %bitcast.38), channel_id=1, source_target_pairs={{0,24},{4,28},{8,0},{12,4},{16,8},{20,12},{24,16},{28,20},{1,25},{... | collective-permute-start | bytes 184328 | tf_op jit(solution)/shard_map/ppermute | solution.py:968
  8.1 8.4 %collective-permute-start.6 = (bf16[1,80,384]{2,1,0:T(8,128)(2,1)}, bf16[1,80,384]{2,1,0:T(8,128)(2,1)S(1)}, u32[]{:S(2)}, u32[]{:S(2)}) collective-permute-start(bf16[1,80,384]{2,1,0:T(8,128)(2,1)} %bitcast.39), channel_id=1, source_target_pairs={{0,16},{4,20},{8,24},{12,28},{16,0},{20,4},{24,8},{28,12},{1,17},{... | collective-permute-start | bytes 184328 | tf_op jit(solution)/shard_map/ppermute | solution.py:968
  8.1 6.3 %collective-permute-start.1 = (bf16[1,80,384]{2,1,0:T(8,128)(2,1)}, bf16[1,80,384]{2,1,0:T(8,128)(2,1)S(1)}, u32[]{:S(2)}, u32[]{:S(2)}) collective-permute-start(bf16[1,80,384]{2,1,0:T(8,128)(2,1)} %bitcast.40), channel_id=1, source_target_pairs={{0,8},{4,12},{8,16},{12,20},{16,24},{20,28},{24,0},{28,4},{1,9},{5... | collective-permute-start | bytes 184328 | tf_op jit(solution)/shard_map/ppermute | solution.py:968
  9.2 16.8 %collective-permute-start = (bf16[512,512]{1,0:T(8,128)(2,1)}, bf16[512,512]{1,0:T(8,128)(2,1)S(1)}, u32[]{:S(2)}, u32[]{:S(2)}) collective-permute-start(bf16[512,512]{1,0:T(8,128)(2,1)} %get-tuple-element.137), channel_id=1, source_target_pairs={{0,3},{3,0},{1,2},{2,1},{4,7},{7,4},{5,6},{6,5},{8,11},{11,8},{9,1... | collective-permute-start | bytes 1572872 | tf_op jit(solution)/shard_map/ppermute | solution.py:220
  14.5 11.4 %collective-permute-start.4 = (bf16[1,64,1408]{2,1,0:T(8,128)(2,1)}, bf16[1,64,1408]{2,1,0:T(8,128)(2,1)S(1)}, u32[]{:S(2)}, u32[]{:S(2)}) collective-permute-start(bf16[1,64,1408]{2,1,0:T(8,128)(2,1)} %bitcast.43), channel_id=1, source_target_pairs={{0,24},{4,28},{8,0},{12,4},{16,8},{20,12},{24,16},{28,20},{1,25},{... | collective-permute-start | bytes 540680 | tf_op jit(solution)/shard_map/ppermute | solution.py:968
  15.6 10.2 %collective-permute-start.3 = (bf16[1,64,1408]{2,1,0:T(8,128)(2,1)}, bf16[1,64,1408]{2,1,0:T(8,128)(2,1)S(1)}, u32[]{:S(2)}, u32[]{:S(2)}) collective-permute-start(bf16[1,64,1408]{2,1,0:T(8,128)(2,1)} %bitcast.44), channel_id=1, source_target_pairs={{0,8},{4,12},{8,16},{12,20},{16,24},{20,28},{24,0},{28,4},{1,9},{5... | collective-permute-start | bytes 540680 | tf_op jit(solution)/shard_map/ppermute | solution.py:968
  16.5 21.6 %copy-start = (bf16[512,512]{1,0:T(8,128)(2,1)S(1)}, bf16[512,512]{1,0:T(8,128)(2,1)}, u32[]{:S(2)}) copy-start(bf16[512,512]{1,0:T(8,128)(2,1)} %low_tok.5) | copy-start | bytes 1572868
  16.5 9.4 %collective-permute-start.8 = (bf16[2,80,384]{2,1,0:T(8,128)(2,1)S(1)}, bf16[2,80,384]{2,1,0:T(8,128)(2,1)S(1)}, u32[]{:S(2)}, u32[]{:S(2)}) collective-permute-start(bf16[2,80,384]{2,1,0:T(8,128)(2,1)S(1)} %pad_maximum_fusion.3), channel_id=1, source_target_pairs={{0,4},{4,0},{8,12},{12,8},{16,20},{20,16},{24,28},{28,24},{1,5},{5... | collective-permute-start | bytes 368648 | tf_op jit(solution)/shard_map/ppermute | solution.py:965
  18.9 7.3 %collective-permute-start.2 = (bf16[2,80,384]{2,1,0:T(8,128)(2,1)S(1)}, bf16[2,80,384]{2,1,0:T(8,128)(2,1)S(1)}, u32[]{:S(2)}, u32[]{:S(2)}) collective-permute-start(bf16[2,80,384]{2,1,0:T(8,128)(2,1)S(1)} %pad_maximum_fusion.2), channel_id=1, source_target_pairs={{0,2},{2,0},{1,3},{3,1},{4,6},{6,4},{5,7},{7,5},{8,10},{10,8},{9,1... | collective-permute-start | bytes 368648 | tf_op jit(solution)/shard_map/ppermute | solution.py:216
  25.8 7.3 %collective-permute-start.10 = (bf16[1,64,1408]{2,1,0:T(8,128)(2,1)S(1)}, bf16[1,64,1408]{2,1,0:T(8,128)(2,1)S(1)}, u32[]{:S(2)}, u32[]{:S(2)}) collective-permute-start(bf16[1,64,1408]{2,1,0:T(8,128)(2,1)S(1)} %collective-permute-done.3), channel_id=1, source_target_pairs={{0,8},{4,12},{8,16},{12,20},{16,24},{20,28},{24,0},{28,4},{1,9},{5... | collective-permute-start | bytes 540680 | tf_op jit(solution)/shard_map/ppermute | solution.py:968
  26.2 8.1 %collective-permute-start.5 = (bf16[4,80,384]{2,1,0:T(8,128)(2,1)S(1)}, bf16[4,80,384]{2,1,0:T(8,128)(2,1)S(1)}, u32[]{:S(2)}, u32[]{:S(2)}) collective-permute-start(bf16[4,80,384]{2,1,0:T(8,128)(2,1)S(1)} %constant_dynamic-update-slice_fusion.refs_0_), channel_id=1, source_target_pairs={{0,4},{4,0},{8,12},{12,8},{16,20},{20,16},{24,28},{28,24},{1,5},{5... | collective-permute-start | bytes 737288 | tf_op jit(solution)/shard_map/ppermute | solution.py:965
  27.8 7.7 %collective-permute-start.9 = (bf16[4,80,384]{2,1,0:T(8,128)(2,1)S(1)}, bf16[4,80,384]{2,1,0:T(8,128)(2,1)S(1)}, u32[]{:S(2)}, u32[]{:S(2)}) collective-permute-start(bf16[4,80,384]{2,1,0:T(8,128)(2,1)S(1)} %constant_dynamic-update-slice_fusion.3.refs_2_), channel_id=1, source_target_pairs={{0,2},{2,0},{1,3},{3,1},{4,6},{6,4},{5,7},{7,5},{8,10},{10,8},{9,1... | collective-permute-start | bytes 737288 | tf_op jit(solution)/shard_map/ppermute | solution.py:216
  33.9 3.1 %collective-permute-start.11 = (bf16[4,80,384]{2,1,0:T(8,128)(2,1)S(1)}, bf16[4,80,384]{2,1,0:T(8,128)(2,1)S(1)}, u32[]{:S(2)}, u32[]{:S(2)}) collective-permute-start(bf16[4,80,384]{2,1,0:T(8,128)(2,1)S(1)} %constant_dynamic-update-slice_fusion.refs_0_), channel_id=1, source_target_pairs={{0,1},{1,0},{2,3},{3,2},{4,5},{5,4},{6,7},{7,6},{8,9},{9,8},{10,11... | collective-permute-start | bytes 737288 | tf_op jit(solution)/shard_map/ppermute | solution.py:212
  33.9 4.2 %collective-permute-start.13 = (bf16[4,80,384]{2,1,0:T(8,128)(2,1)S(1)}, bf16[4,80,384]{2,1,0:T(8,128)(2,1)S(1)}, u32[]{:S(2)}, u32[]{:S(2)}) collective-permute-start(bf16[4,80,384]{2,1,0:T(8,128)(2,1)S(1)} %constant_dynamic-update-slice_fusion.3.refs_2_), channel_id=1, source_target_pairs={{0,1},{1,0},{2,3},{3,2},{4,5},{5,4},{6,7},{7,6},{8,9},{9,8},{10,11... | collective-permute-start | bytes 737288 | tf_op jit(solution)/shard_map/ppermute | solution.py:212
  35.5 2.6 %collective-permute-start.12 = (bf16[4,80,384]{2,1,0:T(8,128)(2,1)S(1)}, bf16[4,80,384]{2,1,0:T(8,128)(2,1)S(1)}, u32[]{:S(2)}, u32[]{:S(2)}) collective-permute-start(bf16[4,80,384]{2,1,0:T(8,128)(2,1)S(1)} %collective-permute-done.5.refs_1_), channel_id=1, source_target_pairs={{0,1},{1,0},{2,3},{3,2},{4,5},{5,4},{6,7},{7,6},{8,9},{9,8},{10,11... | collective-permute-start | bytes 737288 | tf_op jit(solution)/shard_map/ppermute | solution.py:212
  35.5 2.6 %collective-permute-start.14 = (bf16[4,80,384]{2,1,0:T(8,128)(2,1)S(1)}, bf16[4,80,384]{2,1,0:T(8,128)(2,1)S(1)}, u32[]{:S(2)}, u32[]{:S(2)}) collective-permute-start(bf16[4,80,384]{2,1,0:T(8,128)(2,1)S(1)} %collective-permute-done.9.refs_3_), channel_id=1, source_target_pairs={{0,1},{1,0},{2,3},{3,2},{4,5},{5,4},{6,7},{7,6},{8,9},{9,8},{10,11... | collective-permute-start | bytes 737288 | tf_op jit(solution)/shard_map/ppermute | solution.py:212
  36.2 11.6 %collective-permute-start.18 = (bf16[2,64,1408]{2,1,0:T(8,128)(2,1)}, bf16[2,64,1408]{2,1,0:T(8,128)(2,1)S(1)}, u32[]{:S(2)}, u32[]{:S(2)}) collective-permute-start(bf16[2,64,1408]{2,1,0:T(8,128)(2,1)} %pad_maximum_fusion), channel_id=1, source_target_pairs={{0,2},{2,0},{1,3},{3,1},{4,6},{6,4},{5,7},{7,5},{8,10},{10,8},{9,1... | collective-permute-start | bytes 1081352 | tf_op jit(solution)/shard_map/ppermute | solution.py:216
  37.0 11.4 %collective-permute-start.20 = (bf16[2,64,1408]{2,1,0:T(8,128)(2,1)}, bf16[2,64,1408]{2,1,0:T(8,128)(2,1)S(1)}, u32[]{:S(2)}, u32[]{:S(2)}) collective-permute-start(bf16[2,64,1408]{2,1,0:T(8,128)(2,1)} %pad_maximum_fusion.1), channel_id=1, source_target_pairs={{0,4},{4,0},{8,12},{12,8},{16,20},{20,16},{24,28},{28,24},{1,5},{5... | collective-permute-start | bytes 1081352 | tf_op jit(solution)/shard_map/ppermute | solution.py:965
  40.6 5.0 %copy-start.3 = (bf16[2,64,1408]{2,1,0:T(8,128)(2,1)S(1)}, bf16[2,64,1408]{2,1,0:T(8,128)(2,1)}, u32[]{:S(2)}) copy-start(bf16[2,64,1408]{2,1,0:T(8,128)(2,1)} %pad_maximum_fusion) | copy-start | bytes 1081348
  40.6 5.0 %copy-start.2 = (bf16[2,64,1408]{2,1,0:T(8,128)(2,1)S(1)}, bf16[2,64,1408]{2,1,0:T(8,128)(2,1)}, u32[]{:S(2)}) copy-start(bf16[2,64,1408]{2,1,0:T(8,128)(2,1)} %pad_maximum_fusion.1) | copy-start | bytes 1081348
  40.6 9.0 %collective-permute-start.16 = (bf16[512,128]{1,0:T(8,128)(2,1)S(1)}, bf16[512,128]{1,0:T(8,128)(2,1)S(1)}, u32[]{:S(2)}, u32[]{:S(2)}) collective-permute-start(bf16[512,128]{1,0:T(8,128)(2,1)S(1)} %get-tuple-element.151.kv0), channel_id=1, source_target_pairs={{0,2},{2,0},{1,3},{3,1},{4,6},{6,4},{5,7},{7,5},{8,10},{10,8},{9,1... | collective-permute-start | bytes 393224 | tf_op jit(solution)/shard_map/ppermute | solution.py:216
  47.7 16.2 %copy-start.1 = (bf16[512,512]{1,0:T(8,128)(2,1)S(1)}, bf16[512,512]{1,0:T(8,128)(2,1)}, u32[]{:S(2)}) copy-start(bf16[512,512]{1,0:T(8,128)(2,1)} %low_cot.3) | copy-start | bytes 1572868
  47.8 20.1 %collective-permute-start.22 = (bf16[4,64,1408]{2,1,0:T(8,128)(2,1)S(1)}, bf16[4,64,1408]{2,1,0:T(8,128)(2,1)S(1)}, u32[]{:S(2)}, u32[]{:S(2)}) collective-permute-start(bf16[4,64,1408]{2,1,0:T(8,128)(2,1)S(1)} %constant_dynamic-update-slice_fusion.6.refs_0_), channel_id=1, source_target_pairs={{0,1},{1,0},{2,3},{3,2},{4,5},{5,4},{6,7},{7,6},{8,9},{9,8},{10,11... | collective-permute-start | bytes 2162696 | tf_op jit(solution)/shard_map/ppermute | solution.py:212
  47.8 20.1 %collective-permute-start.19 = (bf16[4,64,1408]{2,1,0:T(8,128)(2,1)S(1)}, bf16[4,64,1408]{2,1,0:T(8,128)(2,1)S(1)}, u32[]{:S(2)}, u32[]{:S(2)}) collective-permute-start(bf16[4,64,1408]{2,1,0:T(8,128)(2,1)S(1)} %constant_dynamic-update-slice_fusion.6.refs_0_), channel_id=1, source_target_pairs={{0,4},{4,0},{8,12},{12,8},{16,20},{20,16},{24,28},{28,24},{1,5},{5... | collective-permute-start | bytes 2162696 | tf_op jit(solution)/shard_map/ppermute | solution.py:965
  49.6 18.3 %collective-permute-start.23 = (bf16[4,64,1408]{2,1,0:T(8,128)(2,1)S(1)}, bf16[4,64,1408]{2,1,0:T(8,128)(2,1)S(1)}, u32[]{:S(2)}, u32[]{:S(2)}) collective-permute-start(bf16[4,64,1408]{2,1,0:T(8,128)(2,1)S(1)} %constant_dynamic-update-slice_fusion.8.refs_2_), channel_id=1, source_target_pairs={{0,1},{1,0},{2,3},{3,2},{4,5},{5,4},{6,7},{7,6},{8,9},{9,8},{10,11... | collective-permute-start | bytes 2162696 | tf_op jit(solution)/shard_map/ppermute | solution.py:212
  49.7 18.6 %collective-permute-start.21 = (bf16[4,64,1408]{2,1,0:T(8,128)(2,1)S(1)}, bf16[4,64,1408]{2,1,0:T(8,128)(2,1)S(1)}, u32[]{:S(2)}, u32[]{:S(2)}) collective-permute-start(bf16[4,64,1408]{2,1,0:T(8,128)(2,1)S(1)} %constant_dynamic-update-slice_fusion.8.refs_2_), channel_id=1, source_target_pairs={{0,2},{2,0},{1,3},{3,1},{4,6},{6,4},{5,7},{7,5},{8,10},{10,8},{9,1... | collective-permute-start | bytes 2162696 | tf_op jit(solution)/shard_map/ppermute | solution.py:216
  50.5 1.5 collective-permute-start.15
  52.0 1.3 collective-permute-start.17
  68.2 2.2 %collective-permute-start.24 = (bf16[4,64,1408]{2,1,0:T(8,128)(2,1)S(1)}, bf16[4,64,1408]{2,1,0:T(8,128)(2,1)S(1)}, u32[]{:S(2)}, u32[]{:S(2)}) collective-permute-start(bf16[4,64,1408]{2,1,0:T(8,128)(2,1)S(1)} %collective-permute-done.19.refs_1_), channel_id=1, source_target_pairs={{0,1},{1,0},{2,3},{3,2},{4,5},{5,4},{6,7},{7,6},{8,9},{9,8},{10,11... | collective-permute-start | bytes 2162696 | tf_op jit(solution)/shard_map/ppermute | solution.py:212
  68.2 3.2 %collective-permute-start.25 = (bf16[4,64,1408]{2,1,0:T(8,128)(2,1)S(1)}, bf16[4,64,1408]{2,1,0:T(8,128)(2,1)S(1)}, u32[]{:S(2)}, u32[]{:S(2)}) collective-permute-start(bf16[4,64,1408]{2,1,0:T(8,128)(2,1)S(1)} %collective-permute-done.21.refs_3_), channel_id=1, source_target_pairs={{0,1},{1,0},{2,3},{3,2},{4,5},{5,4},{6,7},{7,6},{8,9},{9,8},{10,11... | collective-permute-start | bytes 2162696 | tf_op jit(solution)/shard_map/ppermute | solution.py:212
  83.6 5.3 %collective-permute-start.26 = (bf16[2,2,2,64,1408]{4,3,2,1,0:T(8,128)(2,1)S(1)}, bf16[2,2,2,64,1408]{4,3,2,1,0:T(8,128)(2,1)S(1)}, u32[]{:S(2)}, u32[]{:S(2)}) collective-permute-start(bf16[2,2,2,64,1408]{4,3,2,1,0:T(8,128)(2,1)S(1)} %get-tuple-element.171), channel_id=1, source_target_pairs={{0,1},{1,0},{2,3},{3,2},{4,5},{5,4},{6,7},{7,6},{8,9},{9,8},{10,11... | collective-permute-start | bytes 4325384 | tf_op jit(solution)/shard_map/ppermute | solution.py:212
  83.8 5.2 %collective-permute-start.27 = (bf16[2,2,2,64,1408]{4,3,2,1,0:T(8,128)(2,1)S(1)}, bf16[2,2,2,64,1408]{4,3,2,1,0:T(8,128)(2,1)S(1)}, u32[]{:S(2)}, u32[]{:S(2)}) collective-permute-start(bf16[2,2,2,64,1408]{4,3,2,1,0:T(8,128)(2,1)S(1)} %get-tuple-element.172), channel_id=1, source_target_pairs={{0,1},{1,0},{2,3},{3,2},{4,5},{5,4},{6,7},{7,6},{8,9},{9,8},{10,11... | collective-permute-start | bytes 4325384 | tf_op jit(solution)/shard_map/ppermute | solution.py:212
  89.3 18.8 %collective-permute-start.28 = (bf16[2,2,64,1408]{3,2,1,0:T(8,128)(2,1)S(1)}, bf16[2,2,64,1408]{3,2,1,0:T(8,128)(2,1)S(1)}, u32[]{:S(2)}, u32[]{:S(2)}) collective-permute-start(bf16[2,2,64,1408]{3,2,1,0:T(8,128)(2,1)S(1)} %get-tuple-element.176), channel_id=1, source_target_pairs={{0,4},{4,0},{8,12},{12,8},{16,20},{20,16},{24,28},{28,24},{1,5},{5... | collective-permute-start | bytes 2162696 | tf_op jit(solution)/shard_map/ppermute | solution.py:965
  90.1 18.1 %collective-permute-start.30 = (bf16[2,2,64,1408]{3,2,1,0:T(8,128)(2,1)S(1)}, bf16[2,2,64,1408]{3,2,1,0:T(8,128)(2,1)S(1)}, u32[]{:S(2)}, u32[]{:S(2)}) collective-permute-start(bf16[2,2,64,1408]{3,2,1,0:T(8,128)(2,1)S(1)} %get-tuple-element.178), channel_id=1, source_target_pairs={{0,2},{2,0},{1,3},{3,1},{4,6},{6,4},{5,7},{7,5},{8,10},{10,8},{9,1... | collective-permute-start | bytes 2162696 | tf_op jit(solution)/shard_map/ppermute | solution.py:216
  105.6 1.6 %collective-permute-start.29 = (bf16[2,2,128,256]{3,2,1,0:T(8,128)(2,1)S(1)}, bf16[2,2,128,256]{3,2,1,0:T(8,128)(2,1)S(1)}, u32[]{:S(2)}, u32[]{:S(2)}) collective-permute-start(bf16[2,2,128,256]{3,2,1,0:T(8,128)(2,1)S(1)} %get-tuple-element.183), channel_id=1, source_target_pairs={{0,1},{1,0},{2,3},{3,2},{4,5},{5,4},{6,7},{7,6},{8,9},{9,8},{10,11... | collective-permute-start | bytes 786440 | tf_op jit(solution)/shard_map/ppermute | solution.py:212
  107.2 5.6 %collective-permute-start.31 = (bf16[2,128,256]{2,1,0:T(8,128)(2,1)S(1)}, bf16[2,128,256]{2,1,0:T(8,128)(2,1)S(1)}, u32[]{:S(2)}, u32[]{:S(2)}) collective-permute-start(bf16[2,128,256]{2,1,0:T(8,128)(2,1)S(1)} %shard_map.280), channel_id=1, source_target_pairs={{0,2},{2,0},{1,3},{3,1},{4,6},{6,4},{5,7},{7,5},{8,10},{10,8},{9,1... | collective-permute-start | bytes 393224 | tf_op jit(solution)/shard_map/ppermute | solution.py:216
  112.8 10.0 %collective-permute-start.32 = (bf16[2,64,1408]{2,1,0:T(8,128)(2,1)S(1)}, bf16[2,64,1408]{2,1,0:T(8,128)(2,1)S(1)}, u32[]{:S(2)}, u32[]{:S(2)}) collective-permute-start(bf16[2,64,1408]{2,1,0:T(8,128)(2,1)S(1)} %get-tuple-element.201), channel_id=1, source_target_pairs={{0,2},{2,0},{1,3},{3,1},{4,6},{6,4},{5,7},{7,5},{8,10},{10,8},{9,1... | collective-permute-start | bytes 1081352 | tf_op jit(solution)/shard_map/ppermute | solution.py:216
  113.9 9.9 %collective-permute-start.35 = (bf16[2,64,1408]{2,1,0:T(8,128)(2,1)S(1)}, bf16[2,64,1408]{2,1,0:T(8,128)(2,1)S(1)}, u32[]{:S(2)}, u32[]{:S(2)}) collective-permute-start(bf16[2,64,1408]{2,1,0:T(8,128)(2,1)S(1)} %get-tuple-element.188), channel_id=1, source_target_pairs={{0,4},{4,0},{8,12},{12,8},{16,20},{20,16},{24,28},{28,24},{1,5},{5... | collective-permute-start | bytes 1081352 | tf_op jit(solution)/shard_map/ppermute | solution.py:965
  122.8 9.0 %collective-permute-start.33 = (bf16[2,2,2,80,384]{4,3,2,1,0:T(8,128)(2,1)S(1)}, bf16[2,2,2,80,384]{4,3,2,1,0:T(8,128)(2,1)S(1)}, u32[]{:S(2)}, u32[]{:S(2)}) collective-permute-start(bf16[2,2,2,80,384]{4,3,2,1,0:T(8,128)(2,1)S(1)} %get-tuple-element.209), channel_id=1, source_target_pairs={{0,1},{1,0},{2,3},{3,2},{4,5},{5,4},{6,7},{7,6},{8,9},{9,8},{10,11... | collective-permute-start | bytes 1474568 | tf_op jit(solution)/shard_map/ppermute | solution.py:212
  122.9 9.0 %collective-permute-start.34 = (bf16[2,2,2,80,384]{4,3,2,1,0:T(8,128)(2,1)S(1)}, bf16[2,2,2,80,384]{4,3,2,1,0:T(8,128)(2,1)S(1)}, u32[]{:S(2)}, u32[]{:S(2)}) collective-permute-start(bf16[2,2,2,80,384]{4,3,2,1,0:T(8,128)(2,1)S(1)} %get-tuple-element.210), channel_id=1, source_target_pairs={{0,1},{1,0},{2,3},{3,2},{4,5},{5,4},{6,7},{7,6},{8,9},{9,8},{10,11... | collective-permute-start | bytes 1474568 | tf_op jit(solution)/shard_map/ppermute | solution.py:212
  124.0 7.9 %collective-permute-start.36 = (bf16[64,1408]{1,0:T(8,128)(2,1)S(1)}, bf16[64,1408]{1,0:T(8,128)(2,1)S(1)}, u32[]{:S(2)}, u32[]{:S(2)}) collective-permute-start(bf16[64,1408]{1,0:T(8,128)(2,1)S(1)} %get-tuple-element.212), channel_id=1, source_target_pairs={{0,8},{4,12},{8,16},{12,20},{16,24},{20,28},{24,0},{28,4},{1,9},{5... | collective-permute-start | bytes 540680 | tf_op jit(solution)/shard_map/ppermute | solution.py:968
  125.9 12.2 %collective-permute-start.39 = (bf16[256,512]{1,0:T(8,128)(2,1)S(1)}, bf16[256,512]{1,0:T(8,128)(2,1)S(1)}, u32[]{:S(2)}, u32[]{:S(2)}) collective-permute-start(bf16[256,512]{1,0:T(8,128)(2,1)S(1)} %get-tuple-element.224), channel_id=1, source_target_pairs={{0,3},{3,0},{1,2},{2,1},{4,7},{7,4},{5,6},{6,5},{8,11},{11,8},{9,1... | collective-permute-start | bytes 786440 | tf_op jit(solution)/shard_map/ppermute | solution.py:220
  132.0 7.6 %collective-permute-start.37 = (bf16[2,2,80,384]{3,2,1,0:T(8,128)(2,1)S(1)}, bf16[2,2,80,384]{3,2,1,0:T(8,128)(2,1)S(1)}, u32[]{:S(2)}, u32[]{:S(2)}) collective-permute-start(bf16[2,2,80,384]{3,2,1,0:T(8,128)(2,1)S(1)} %get-tuple-element.221), channel_id=1, source_target_pairs={{0,2},{2,0},{1,3},{3,1},{4,6},{6,4},{5,7},{7,5},{8,10},{10,8},{9,1... | collective-permute-start | bytes 737288 | tf_op jit(solution)/shard_map/ppermute | solution.py:216
  133.3 6.7 %collective-permute-start.38 = (bf16[2,2,80,384]{3,2,1,0:T(8,128)(2,1)S(1)}, bf16[2,2,80,384]{3,2,1,0:T(8,128)(2,1)S(1)}, u32[]{:S(2)}, u32[]{:S(2)}) collective-permute-start(bf16[2,2,80,384]{3,2,1,0:T(8,128)(2,1)S(1)} %get-tuple-element.222), channel_id=1, source_target_pairs={{0,4},{4,0},{8,12},{12,8},{16,20},{20,16},{24,28},{28,24},{1,5},{5... | collective-permute-start | bytes 737288 | tf_op jit(solution)/shard_map/ppermute | solution.py:965
  134.2 8.5 %collective-permute-start.42 = (bf16[64,1408]{1,0:T(8,128)(2,1)S(1)}, bf16[64,1408]{1,0:T(8,128)(2,1)S(1)}, u32[]{:S(2)}, u32[]{:S(2)}) collective-permute-start(bf16[64,1408]{1,0:T(8,128)(2,1)S(1)} %shard_map.286), channel_id=1, source_target_pairs={{0,8},{4,12},{8,16},{12,20},{16,24},{20,28},{24,0},{28,4},{1,9},{5... | collective-permute-start | bytes 540680 | tf_op jit(solution)/shard_map/ppermute | solution.py:968
  134.9 8.2 %collective-permute-start.43 = (bf16[64,1408]{1,0:T(8,128)(2,1)S(1)}, bf16[64,1408]{1,0:T(8,128)(2,1)S(1)}, u32[]{:S(2)}, u32[]{:S(2)}) collective-permute-start(bf16[64,1408]{1,0:T(8,128)(2,1)S(1)} %get-tuple-element.229), channel_id=1, source_target_pairs={{0,24},{4,28},{8,0},{12,4},{16,8},{20,12},{24,16},{28,20},{1,25},{... | collective-permute-start | bytes 540680 | tf_op jit(solution)/shard_map/ppermute | solution.py:968
  140.1 4.9 %collective-permute-start.40 = (bf16[2,80,384]{2,1,0:T(8,128)(2,1)S(1)}, bf16[2,80,384]{2,1,0:T(8,128)(2,1)S(1)}, u32[]{:S(2)}, u32[]{:S(2)}) collective-permute-start(bf16[2,80,384]{2,1,0:T(8,128)(2,1)S(1)} %get-tuple-element.227), channel_id=1, source_target_pairs={{0,4},{4,0},{8,12},{12,8},{16,20},{20,16},{24,28},{28,24},{1,5},{5... | collective-permute-start | bytes 368648 | tf_op jit(solution)/shard_map/ppermute | solution.py:965
  141.3 4.9 %collective-permute-start.41 = (bf16[2,80,384]{2,1,0:T(8,128)(2,1)S(1)}, bf16[2,80,384]{2,1,0:T(8,128)(2,1)S(1)}, u32[]{:S(2)}, u32[]{:S(2)}) collective-permute-start(bf16[2,80,384]{2,1,0:T(8,128)(2,1)S(1)} %get-tuple-element.228), channel_id=1, source_target_pairs={{0,2},{2,0},{1,3},{3,1},{4,6},{6,4},{5,7},{7,5},{8,10},{10,8},{9,1... | collective-permute-start | bytes 368648 | tf_op jit(solution)/shard_map/ppermute | solution.py:216
  146.2 8.5 %collective-permute-start.47 = (bf16[256,512]{1,0:T(8,128)(2,1)S(1)}, bf16[256,512]{1,0:T(8,128)(2,1)S(1)}, u32[]{:S(2)}, u32[]{:S(2)}) collective-permute-start(bf16[256,512]{1,0:T(8,128)(2,1)S(1)} %get-tuple-element.245), channel_id=1, source_target_pairs={{0,3},{3,0},{1,2},{2,1},{4,7},{7,4},{5,6},{6,5},{8,11},{11,8},{9,1... | collective-permute-start | bytes 786440 | tf_op jit(solution)/shard_map/ppermute | solution.py:220
  146.3 6.8 %collective-permute-start.44 = (bf16[80,384]{1,0:T(8,128)(2,1)S(1)}, bf16[80,384]{1,0:T(8,128)(2,1)S(1)}, u32[]{:S(2)}, u32[]{:S(2)}) collective-permute-start(bf16[80,384]{1,0:T(8,128)(2,1)S(1)} %get-tuple-element.238), channel_id=1, source_target_pairs={{0,8},{4,12},{8,16},{12,20},{16,24},{20,28},{24,0},{28,4},{1,9},{5... | collective-permute-start | bytes 184328 | tf_op jit(solution)/shard_map/ppermute | solution.py:968
  146.6 8.1 %collective-permute-start.45 = (bf16[80,384]{1,0:T(8,128)(2,1)S(1)}, bf16[80,384]{1,0:T(8,128)(2,1)S(1)}, u32[]{:S(2)}, u32[]{:S(2)}) collective-permute-start(bf16[80,384]{1,0:T(8,128)(2,1)S(1)} %get-tuple-element.241), channel_id=1, source_target_pairs={{0,16},{4,20},{8,24},{12,28},{16,0},{20,4},{24,8},{28,12},{1,17},{... | collective-permute-start | bytes 184328 | tf_op jit(solution)/shard_map/ppermute | solution.py:968
  148.3 6.4 %collective-permute-start.46 = (bf16[80,384]{1,0:T(8,128)(2,1)S(1)}, bf16[80,384]{1,0:T(8,128)(2,1)S(1)}, u32[]{:S(2)}, u32[]{:S(2)}) collective-permute-start(bf16[80,384]{1,0:T(8,128)(2,1)S(1)} %get-tuple-element.242), channel_id=1, source_target_pairs={{0,24},{4,28},{8,0},{12,4},{16,8},{20,12},{24,16},{28,20},{1,25},{... | collective-permute-start | bytes 184328 | tf_op jit(solution)/shard_map/ppermute | solution.py:968

commit v6 on v5

--- a/solution.py
+++ b/solution.py
@@ -744,24 +744,12 @@
         grads[slot] = nn(normed_t[...], spread[slot]).astype(BF16)
 
 
-def spread_stage(table, grad_query, normed, routes, group):
-    rows, width = normed.shape
-    vmem = pl.BlockSpec(memory_space=pltpu.VMEM)
-    return pl.pallas_call(
-        spread_kernel,
-        cost_estimate=cost(6),
-        in_specs=[smem_spec()] + [vmem] * 3,
-        out_shape=(shaped((4, rows, group), BF16), shaped((4, width, group), BF16)),
-        scratch_shapes=[pltpu.VMEM((width, rows), BF16), pltpu.VMEM((width, rows), BF16)],
-        compiler_params=params(16),
-    )(table, grad_query, normed, routes)
-
-
 def last_kernel(
-    table, low_tok, cross, grad_mid, spread, normed, routes, gates, grad_gate, weight, small,
-    vectors, sums, bias_grad, pair_keep, pair_got, pair_far, grads, low_out, high_out, *refs
+    table, low_tok, cross, grad_mid, grad_query, normed, routes, gates, grad_gate, weight, small,
+    vectors, sums, bias_grad, pair_keep, pair_got, pair_far, low_out, high_out, *refs
 ):
-    blocks, (pair_grad, tiny, wide, extra) = refs[:4], refs[4:]
+    blocks, (pair_grad, tiny, wide, extra, spread, grads, turned, ordered) = refs[:4], refs[4:]
+    spread_kernel(table, grad_query, normed, routes, spread, grads, turned, ordered)
     keep_a, keep_b, send_a, send_b = blocks
     rows = normed.shape[0]
     ways = routes.shape[1]
@@ -809,8 +797,8 @@
 
 
 def last_stage(
-    table, tokens, cross, grad_mid, spread, normed, routes, gates, grad_gate, weight, small,
-    vectors, sums, bias_grad, pair_parts, grads
+    table, tokens, cross, grad_mid, grad_query, normed, routes, gates, grad_gate, weight, small,
+    vectors, sums, bias_grad, pair_parts
 ):
     rows, width = tokens.shape
     block = shaped((2, 2, 2, ROWS + TINY, 3 * LANES), BF16)
@@ -818,18 +806,22 @@
     return pl.pallas_call(
         last_kernel,
         cost_estimate=cost(7),
-        in_specs=[smem_spec()] + [vmem] * 17,
+        in_specs=[smem_spec()] + [vmem] * 16,
         out_shape=(shaped((HALF, width), F32), shaped((rows - HALF, width), BF16), block, block, block, block),
         scratch_shapes=[
             pltpu.VMEM((rows, LANES), BF16),
             pltpu.VMEM((width, 3 * LANES), BF16),
             pltpu.VMEM((LANES, width), F32),
             pltpu.VMEM((width, LANES), F32),
+            pltpu.VMEM((4, rows, weight.shape[2]), BF16),
+            pltpu.VMEM((4, width, weight.shape[2]), BF16),
+            pltpu.VMEM((width, rows), BF16),
+            pltpu.VMEM((width, rows), BF16),
         ],
         compiler_params=params(24),
     )(
-        table, tokens, cross, grad_mid, spread, normed, routes, gates, grad_gate, weight, small,
-        vectors, sums, bias_grad, *pair_parts, grads
+        table, tokens, cross, grad_mid, grad_query, normed, routes, gates, grad_gate, weight, small,
+        vectors, sums, bias_grad, *pair_parts
     )
 
 
@@ -1044,11 +1036,10 @@
         grad_query = after(grad_query, part_a, part_b)
     else:
         output_high = crossed(output_high)
-    spread, query_grads = spread_stage(table, grad_query, normed, own_routes, query_weight.shape[2])
     if tuned:
-        spread, pair_far = together(spread, pair_parts[2])
+        grad_query, pair_far = together(grad_query, pair_parts[2])
         pair_parts = (*pair_parts[0:2], pair_far)
-        last_b = over_y(after(part_b, pair_far, spread))
+        last_b = over_y(after(part_b, pair_far))
 
         def final(name, *sides):
             return add_blocks(
@@ -1061,8 +1052,8 @@
             )
 
     low_rows, high_rows, *first_blocks = last_stage(
-        table, tokens, cross, grad_mid, spread, normed, own_routes, gates, grad_gate,
-        query_weight, small, vectors, sums, bias_grad, pair_parts, query_grads,
+        table, tokens, cross, grad_mid, grad_query, normed, own_routes, gates, grad_gate,
+        query_weight, small, vectors, sums, bias_grad, pair_parts,
     )
     if tuned:
         last_a = after(last_a, low_rows)

time: 156 us -> 156 us (level)
  Pallas kernels: 66.3 us -> 64.7 us
    pallas_call x1 -> x0, Pallas kernels: 4.19 us -> none  [spread_stage(): pl.pallas_call(spread_kernel, cost_estimate=cost(6), in_specs=[smem_spec(...]
    pallas_call x1, Pallas kernels: 3.92 us -> 6.48 us  [last_stage(): pl.pallas_call(last_kernel, cost_estimate=cost(7), in_specs=[smem_spec()]...]
    ppermute x8, waiting for transfers between devices: 2.75 us -> 0.86 us  [over_x(): return lax.ppermute(x, 'dp', swap)]
  transfers between devices with their start and end apart: 48 -> 48, of which waited for: 26 -> 24; matrix products, arithmetic and copies ran while one was open for 3% -> 3% of each run, Pallas kernels for 32% -> 31%
where the time goes in v6:
time: 156 us
  Pallas kernels  64.7 us (41%)
  waiting for transfers between devices  44.3 us (28%)
  starting transfers between devices  41.6 us (27%)
  other arithmetic  2.41 us (2%)
  local copies, waits for them, and re-layouts  2.01 us (1%)
    ppermute x12, waiting for transfers between devices, over_z(): return lax.ppermute(x, 'dp', turns[step - 1])  23.2 us
    ppermute x12, starting transfers between devices, over_z(): return lax.ppermute(x, 'dp', turns[step - 1])  18.2 us
    pallas_call x1, Pallas kernels, attend_back_stage(): pl.pallas_call(attend_back_kernel, cost_estimate=cost(16), grid=(rows //...  14.3 us
    ppermute x10, waiting for transfers between devices, over_y(): return lax.ppermute(x, 'tensor', ACROSS)  13.3 us
    pallas_call x1, Pallas kernels, middle_stage(): pl.pallas_call(middle_kernel, cost_estimate=cost(36), in_specs=[smem_spec...  12.1 us
    pallas_call x1, Pallas kernels, attend_stage(): pl.pallas_call(attend_kernel, cost_estimate=cost(1.2), grid=(rows // HALF...  10.5 us
    ppermute x10, starting transfers between devices, over_y(): return lax.ppermute(x, 'tensor', ACROSS)  10.1 us
    ppermute x8, starting transfers between devices, over_x(): return lax.ppermute(x, 'dp', swap)  9.9 us
  transfers between devices with their start and end apart: 48, of which 24 were waited for; matrix products, arithmetic and copies ran while one was open for 3% of the time, Pallas kernels for 31%

profile of v6, /device:TPU:0, one launch (start us, length us, event | category | flops | bytes accessed | tf_op | source)
XLA Modules:
  0.0 155.9 jit_solution(9313028049573135239)
XLA Ops:
  0.7 2.4 %shard_map.271 = (bf16[80,384]{1,0:T(8,128)(2,1)}, bf16[64,1408]{1,0:T(8,128)(2,1)}, bf16[512,512]{1,0:T(8,128)(2,1)}) custom-call(bf16[6,64,64]{2,1,0:T(8,128)(2,1)} %wq.1, bf16[6,64,64]{2,1,0:T(8,128)(2,1)} %wo.1, bf16[64,512]{1,0:T(8,128)(2,1)} %wup.1, bf16[64,512]{1,0:T(8,128)(2,1)} %bitcast.46, bf16[16,64]{1,0:T(8,128)(2,1)} %wk.1, bf16[16,64]{1,0:T(8,128)(2,1)} %wv.1, ...), custom_call_target="tpu_custom_call" | custom-call | bytes 738000 | tf_op jit(solution)/shard_map/pallas_call | solution.py:107
  3.1 5.0 %collective-permute-start.7 = (bf16[1,80,384]{2,1,0:T(8,128)(2,1)}, bf16[1,80,384]{2,1,0:T(8,128)(2,1)S(1)}, u32[]{:S(2)}, u32[]{:S(2)}) collective-permute-start(bf16[1,80,384]{2,1,0:T(8,128)(2,1)} %bitcast.38), channel_id=1, source_target_pairs={{0,24},{4,28},{8,0},{12,4},{16,8},{20,12},{24,16},{28,20},{1,25},{... | collective-permute-start | bytes 184328 | tf_op jit(solution)/shard_map/ppermute | solution.py:960
  8.1 1.0 collective-permute-start.1
  9.3 0.7 constant_dynamic-slice_fusion.1
  10.1 0.8 constant_dynamic-update-slice_fusion.2
  10.9 3.5 %collective-permute-done.1 = bf16[1,80,384]{2,1,0:T(8,128)(2,1)S(1)} collective-permute-done((bf16[1,80,384]{2,1,0:T(8,128)(2,1)}, bf16[1,80,384]{2,1,0:T(8,128)(2,1)S(1)}, u32[]{:S(2)}, u32[]{:S(2)}) %collective-permute-start.1) | collective-permute-done | bytes 61472 | tf_op jit(solution)/shard_map/ppermute | solution.py:960
  14.5 1.1 collective-permute-start.4
  15.6 0.9 collective-permute-start.3
  16.5 1.6 collective-permute-start.8
  18.1 0.8 pad_maximum_fusion.2
  18.9 1.6 %collective-permute-start.2 = (bf16[2,80,384]{2,1,0:T(8,128)(2,1)S(1)}, bf16[2,80,384]{2,1,0:T(8,128)(2,1)S(1)}, u32[]{:S(2)}, u32[]{:S(2)}) collective-permute-start(bf16[2,80,384]{2,1,0:T(8,128)(2,1)S(1)} %pad_maximum_fusion.2), channel_id=1, source_target_pairs={{0,2},{2,0},{1,3},{3,1},{4,6},{6,4},{5,7},{7,5},{8,10},{10,8},{9,1... | collective-permute-start | bytes 368648 | tf_op jit(solution)/shard_map/ppermute | solution.py:216
  20.6 5.2 %collective-permute-done.3 = bf16[1,64,1408]{2,1,0:T(8,128)(2,1)S(1)} collective-permute-done((bf16[1,64,1408]{2,1,0:T(8,128)(2,1)}, bf16[1,64,1408]{2,1,0:T(8,128)(2,1)S(1)}, u32[]{:S(2)}, u32[]{:S(2)}) %collective-permute-start.3) | collective-permute-done | bytes 180256 | tf_op jit(solution)/shard_map/ppermute | solution.py:960
  26.2 1.6 collective-permute-start.5
  27.8 1.2 collective-permute-start.9
  29.0 0.8 pad_maximum_fusion
  29.8 3.3 %collective-permute-done.10 = bf16[1,64,1408]{2,1,0:T(8,128)(2,1)S(1)} collective-permute-done((bf16[1,64,1408]{2,1,0:T(8,128)(2,1)S(1)}, bf16[1,64,1408]{2,1,0:T(8,128)(2,1)S(1)}, u32[]{:S(2)}, u32[]{:S(2)}) %collective-permute-start.10) | collective-permute-done | bytes 180256 | tf_op jit(solution)/shard_map/ppermute | solution.py:960
  33.1 0.8 pad_maximum_fusion.1
  34.4 1.2 collective-permute-done.9.refs_3_
  36.2 0.8 collective-permute-start.18
  37.0 1.1 collective-permute-start.20
  38.1 2.5 %shard_map.272 = (bf16[512,512]{1,0:T(8,128)(2,1)S(1)}, bf16[512,128]{1,0:T(8,128)(2,1)S(1)}, f32[512,128]{1,0:T(8,128)S(1)}, bf16[512,384]{1,0:T(8,128)(2,1)S(1...) custom-call(s32[28]{0:T(128)S(1)} %stack.97.table, bf16[512,512]{1,0:T(8,128)(2,1)S(1)} %copy-done, ...), custom_call_target="tpu_custom_call" | custom-call | bytes 1845000 | tf_op jit(solution)/shard_map/pallas_call | solution.py:308
  40.6 0.8 collective-permute-start.16
  41.4 4.2 %shard_map.273 = (bf16[8,512,128]{2,1,0:T(8,128)(2,1)S(1)}, bf16[4,512,384]{2,1,0:T(8,128)(2,1)S(1)}) custom-call(s32[28]{0:T(128)S(1)} %stack.97.table, bf16[512,512]{1,0:T(8,128)(2,1)S(1)} %get-tuple-element.147.normed, s32[512,8]{1,0:T(8,128)S(1)} %copy.33.routes, bf16[4,80,384]{2,1,0:T(8,128)(2,1)S(1)} %constant_dynamic-update-slice_fusion.refs_0_, ...), custom_call_target="tpu_custom_call" | custom-call | bytes 2952000 | tf_op jit(solution)/shard_map/pallas_call | solution.py:383
  45.6 2.1 %collective-permute-done.18 = bf16[2,64,1408]{2,1,0:T(8,128)(2,1)S(1)} collective-permute-done((bf16[2,64,1408]{2,1,0:T(8,128)(2,1)}, bf16[2,64,1408]{2,1,0:T(8,128)(2,1)S(1)}, u32[]{:S(2)}, u32[]{:S(2)}) %collective-permute-start.18) | collective-permute-done | bytes 360480 | tf_op jit(solution)/shard_map/ppermute | solution.py:216
  47.8 0.6 collective-permute-start.19
  48.4 1.1 collective-permute-done.16.kv2
  49.7 0.8 collective-permute-start.21
  50.7 1.4 collective-permute-done.15.kv1
  52.2 1.2 collective-permute-done.17.kv3
  53.4 10.5 %shard_map.274 = (bf16[8,512,128]{2,1,0:T(8,128)(2,1)S(1)}, f32[512,128]{1,0:T(8,128)S(1)}) custom-call(s32[28]{0:T(128)S(1)} %stack.97.table, bf16[8,512,128]{2,1,0:T(8,128)(2,1)S(1)} %get-tuple-element.148.query, bf16[512,128]{1,0:T(8,128)(2,1)S(1)} %get-tuple-element.149.kv0, bf16[512,128]{1,0:T(8,128)(2,1)S(1)} %collective-permute-done.15.kv1, ...), custom_call_target="tpu_custom_call" | custom-call | bytes 4428000 | tf_op jit(solution)/shard_map/pallas_call | solution.py:467
  63.9 3.9 %shard_map.275 = (bf16[4,512,384]{2,1,0:T(8,128)(2,1)S(1)}, bf16[512,512]{1,0:T(8,128)(2,1)S(1)}) custom-call(s32[28]{0:T(128)S(1)} %stack.97.table, bf16[8,512,128]{2,1,0:T(8,128)(2,1)S(1)} %get-tuple-element.150.heads, f32[512,128]{1,0:T(8,128)S(1)} %get-tuple-element.151.gates, s32[512,8]{1,0:T(8,128)S(1)} %copy.33.routes, ...), custom_call_target="tpu_custom_call" | custom-call | bytes 1107000 | tf_op jit(solution)/shard_map/pallas_call | solution.py:606
  68.7 1.7 %collective-permute-done.24.refs_5_ = bf16[4,64,1408]{2,1,0:T(8,128)(2,1)S(1)} collective-permute-done((bf16[4,64,1408]{2,1,0:T(8,128)(2,1)S(1)}, bf16[4,64,1408]{2,1,0:T(8,128)(2,1)S(1)}, u32[]{:S(2)}, u32[]{:S(2)}) %collective-permute-start.24) | collective-permute-done | bytes 720928 | tf_op jit(solution)/shard_map/ppermute | solution.py:212
  70.4 1.0 collective-permute-done.25.refs_7_
  71.5 12.1 %shard_map.276 = (bf16[256,512]{1,0:T(8,128)(2,1)S(1)}, bf16[256,512]{1,0:T(8,128)(2,1)S(1)}, f32[512,512]{1,0:T(8,128)S(1)}, bf16[4,512,384]{2,1,0:T(8,128)(2,1...) custom-call(s32[28]{0:T(128)S(1)} %stack.97.table, ...), custom_call_target="tpu_custom_call" | custom-call | bytes 132840000 | tf_op jit(solution)/shard_map/pallas_call | solution.py:707
  84.2 4.7 %shard_map.277 = (bf16[8,512,128]{2,1,0:T(8,128)(2,1)S(1)}, f32[512,128]{1,0:T(8,128)S(1)}) custom-call(s32[28]{0:T(128)S(1)} %stack.97.table, bf16[4,512,384]{2,1,0:T(8,128)(2,1)S(1)} %get-tuple-element.166.back, bf16[8,512,128]{2,1,0:T(8,128)(2,1)S(1)} %get-tuple-element.150.heads, f32[512,128]{1,0:T(8,128)S(1)} %get-tuple-element.151.gates, ...), custom_call_target="tpu_custom_call" | custom-call | bytes 29520000 | tf_op jit(solution)/shard_map/pallas_call | solution.py:688
  89.3 0.8 collective-permute-start.28
  90.1 1.2 collective-permute-start.30
  91.3 14.3 %shard_map.279 = (bf16[8,512,128]{2,1,0:T(8,128)(2,1)S(1)}, bf16[2,2,128,256]{3,2,1,0:T(8,128)(2,1)S(1)}, bf16[2,2,128,256]{3,2,1,0:T(8,128)(2,1)S(1)}) custom-call(s32[28]{0:T(128)S(1)} %stack.97.table, bf16[8,512,128]{2,1,0:T(8,128)(2,1)S(1)} %get-tuple-element.148.query, bf16[8,512,128]{2,1,0:T(8,128)(2,1)S(1)} %get-tuple-element.177.grad, ...), custom_call_target="tpu_custom_call" | custom-call | bytes 59040000 | tf_op jit(solution)/shard_map/pallas_call | solution.py:547
  105.7 1.5 collective-permute-done.29.refs_1_.pair_got
  107.2 0.9 collective-permute-start.31
  108.4 4.4 %collective-permute-done.31.pair_far = bf16[2,128,256]{2,1,0:T(8,128)(2,1)S(1)} collective-permute-done((bf16[2,128,256]{2,1,0:T(8,128)(2,1)S(1)}, bf16[2,128,256]{2,1,0:T(8,128)(2,1)S(1)}, u32[]{:S(2)}, u32[]{:S(2)}) %collective-permute-start.31) | collective-permute-done | bytes 131104 | tf_op jit(solution)/shard_map/ppermute | solution.py:216
  112.8 0.8 collective-permute-start.32
  113.7 1.3 collective-permute-start.35
  115.0 6.5 %shard_map.282 = (f32[256,512]{1,0:T(8,128)S(1)}, bf16[256,512]{1,0:T(8,128)(2,1)S(1)}, bf16[2,2,2,80,384]{4,3,2,1,0:T(8,128)(2,1)S(1)}, bf16[2,2,2,80,384]{4,3,...) custom-call(s32[28]{0:T(128)S(1)} %stack.97.table, ...), custom_call_target="tpu_custom_call" | custom-call | bytes 25830000 | tf_op jit(solution)/shard_map/pallas_call | solution.py:806
  121.5 1.0 collective-permute-done.32.refs_3_.refs_7_
  123.2 2.3 %collective-permute-start.36 = (bf16[64,1408]{1,0:T(8,128)(2,1)S(1)}, bf16[64,1408]{1,0:T(8,128)(2,1)S(1)}, u32[]{:S(2)}, u32[]{:S(2)}) collective-permute-start(bf16[64,1408]{1,0:T(8,128)(2,1)S(1)} %get-tuple-element.208), channel_id=1, source_target_pairs={{0,8},{4,12},{8,16},{12,20},{16,24},{20,28},{24,0},{28,4},{1,9},{5... | collective-permute-start | bytes 540680 | tf_op jit(solution)/shard_map/ppermute | solution.py:960
  125.8 5.6 %collective-permute-done.36.refs_1_ = bf16[64,1408]{1,0:T(8,128)(2,1)S(1)} collective-permute-done((bf16[64,1408]{1,0:T(8,128)(2,1)S(1)}, bf16[64,1408]{1,0:T(8,128)(2,1)S(1)}, u32[]{:S(2)}, u32[]{:S(2)}) %collective-permute-start.36) | collective-permute-done | bytes 180256 | tf_op jit(solution)/shard_map/ppermute | solution.py:960
  131.7 0.9 collective-permute-start.37
  132.6 1.3 collective-permute-start.38
  133.9 0.7 collective-permute-start.42
  134.5 3.2 %collective-permute-start.43 = (bf16[64,1408]{1,0:T(8,128)(2,1)S(1)}, bf16[64,1408]{1,0:T(8,128)(2,1)S(1)}, u32[]{:S(2)}, u32[]{:S(2)}) collective-permute-start(bf16[64,1408]{1,0:T(8,128)(2,1)S(1)} %get-tuple-element.225), channel_id=1, source_target_pairs={{0,24},{4,28},{8,0},{12,4},{16,8},{20,12},{24,16},{28,20},{1,25},{... | collective-permute-start | bytes 540680 | tf_op jit(solution)/shard_map/ppermute | solution.py:960
  137.7 1.2 collective-permute-done.37.refs_2_.refs_6_
  139.0 1.7 %collective-permute-start.40 = (bf16[2,80,384]{2,1,0:T(8,128)(2,1)S(1)}, bf16[2,80,384]{2,1,0:T(8,128)(2,1)S(1)}, u32[]{:S(2)}, u32[]{:S(2)}) collective-permute-start(bf16[2,80,384]{2,1,0:T(8,128)(2,1)S(1)} %get-tuple-element.223), channel_id=1, source_target_pairs={{0,4},{4,0},{8,12},{12,8},{16,20},{20,16},{24,28},{28,24},{1,5},{5... | collective-permute-start | bytes 368648 | tf_op jit(solution)/shard_map/ppermute | solution.py:957
  140.7 1.1 collective-permute-start.41
  141.8 1.0 collective-permute-done.42.one
  143.1 0.8 collective-permute-done.40.refs_3_.refs_7_
  143.9 1.6 %collective-permute-done.41.refs_11_.refs_15_ = bf16[2,80,384]{2,1,0:T(8,128)(2,1)S(1)} collective-permute-done((bf16[2,80,384]{2,1,0:T(8,128)(2,1)S(1)}, bf16[2,80,384]{2,1,0:T(8,128)(2,1)S(1)}, u32[]{:S(2)}, u32[]{:S(2)}) %collective-permute-start.41) | collective-permute-done | bytes 122912 | tf_op jit(solution)/shard_map/ppermute | solution.py:216
  145.7 0.7 collective-permute-start.44
  146.5 1.1 collective-permute-start.45
  147.5 2.1 %collective-permute-start.46 = (bf16[80,384]{1,0:T(8,128)(2,1)S(1)}, bf16[80,384]{1,0:T(8,128)(2,1)S(1)}, u32[]{:S(2)}, u32[]{:S(2)}) collective-permute-start(bf16[80,384]{1,0:T(8,128)(2,1)S(1)} %get-tuple-element.238), channel_id=1, source_target_pairs={{0,24},{4,28},{8,0},{12,4},{16,8},{20,12},{24,16},{28,20},{1,25},{... | collective-permute-start | bytes 184328 | tf_op jit(solution)/shard_map/ppermute | solution.py:960
  149.6 1.0 shard_map.288
  150.6 1.8 %collective-permute-done.44.one = bf16[80,384]{1,0:T(8,128)(2,1)S(1)} collective-permute-done((bf16[80,384]{1,0:T(8,128)(2,1)S(1)}, bf16[80,384]{1,0:T(8,128)(2,1)S(1)}, u32[]{:S(2)}, u32[]{:S(2)}) %collective-permute-start.44) | collective-permute-done | bytes 61472 | tf_op jit(solution)/shard_map/ppermute | solution.py:960
  152.4 2.4 %collective-permute-done.45.two = bf16[80,384]{1,0:T(8,128)(2,1)S(1)} collective-permute-done((bf16[80,384]{1,0:T(8,128)(2,1)S(1)}, bf16[80,384]{1,0:T(8,128)(2,1)S(1)}, u32[]{:S(2)}, u32[]{:S(2)}) %collective-permute-start.45) | collective-permute-done | bytes 61472 | tf_op jit(solution)/shard_map/ppermute | solution.py:960
  154.8 1.1 shard_map.290
  (80 shorter events, 6.5 us)
Async XLA Ops:
  3.1 25.9 %copy-start.4 = (bf16[64,1408]{1,0:T(8,128)(2,1)S(1)}, bf16[64,1408]{1,0:T(8,128)(2,1)}, u32[]{:S(2)}) copy-start(bf16[64,1408]{1,0:T(8,128)(2,1)} %get-tuple-element.138) | copy-start | bytes 540676
  3.1 13.4 %collective-permute-start.7 = (bf16[1,80,384]{2,1,0:T(8,128)(2,1)}, bf16[1,80,384]{2,1,0:T(8,128)(2,1)S(1)}, u32[]{:S(2)}, u32[]{:S(2)}) collective-permute-start(bf16[1,80,384]{2,1,0:T(8,128)(2,1)} %bitcast.38), channel_id=1, source_target_pairs={{0,24},{4,28},{8,0},{12,4},{16,8},{20,12},{24,16},{28,20},{1,25},{... | collective-permute-start | bytes 184328 | tf_op jit(solution)/shard_map/ppermute | solution.py:960
  8.1 8.4 %collective-permute-start.6 = (bf16[1,80,384]{2,1,0:T(8,128)(2,1)}, bf16[1,80,384]{2,1,0:T(8,128)(2,1)S(1)}, u32[]{:S(2)}, u32[]{:S(2)}) collective-permute-start(bf16[1,80,384]{2,1,0:T(8,128)(2,1)} %bitcast.39), channel_id=1, source_target_pairs={{0,16},{4,20},{8,24},{12,28},{16,0},{20,4},{24,8},{28,12},{1,17},{... | collective-permute-start | bytes 184328 | tf_op jit(solution)/shard_map/ppermute | solution.py:960
  8.1 6.3 %collective-permute-start.1 = (bf16[1,80,384]{2,1,0:T(8,128)(2,1)}, bf16[1,80,384]{2,1,0:T(8,128)(2,1)S(1)}, u32[]{:S(2)}, u32[]{:S(2)}) collective-permute-start(bf16[1,80,384]{2,1,0:T(8,128)(2,1)} %bitcast.40), channel_id=1, source_target_pairs={{0,8},{4,12},{8,16},{12,20},{16,24},{20,28},{24,0},{28,4},{1,9},{5... | collective-permute-start | bytes 184328 | tf_op jit(solution)/shard_map/ppermute | solution.py:960
  9.2 16.8 %collective-permute-start = (bf16[512,512]{1,0:T(8,128)(2,1)}, bf16[512,512]{1,0:T(8,128)(2,1)S(1)}, u32[]{:S(2)}, u32[]{:S(2)}) collective-permute-start(bf16[512,512]{1,0:T(8,128)(2,1)} %get-tuple-element.135), channel_id=1, source_target_pairs={{0,3},{3,0},{1,2},{2,1},{4,7},{7,4},{5,6},{6,5},{8,11},{11,8},{9,1... | collective-permute-start | bytes 1572872 | tf_op jit(solution)/shard_map/ppermute | solution.py:220
  14.5 11.4 %collective-permute-start.4 = (bf16[1,64,1408]{2,1,0:T(8,128)(2,1)}, bf16[1,64,1408]{2,1,0:T(8,128)(2,1)S(1)}, u32[]{:S(2)}, u32[]{:S(2)}) collective-permute-start(bf16[1,64,1408]{2,1,0:T(8,128)(2,1)} %bitcast.43), channel_id=1, source_target_pairs={{0,24},{4,28},{8,0},{12,4},{16,8},{20,12},{24,16},{28,20},{1,25},{... | collective-permute-start | bytes 540680 | tf_op jit(solution)/shard_map/ppermute | solution.py:960
  15.6 10.2 %collective-permute-start.3 = (bf16[1,64,1408]{2,1,0:T(8,128)(2,1)}, bf16[1,64,1408]{2,1,0:T(8,128)(2,1)S(1)}, u32[]{:S(2)}, u32[]{:S(2)}) collective-permute-start(bf16[1,64,1408]{2,1,0:T(8,128)(2,1)} %bitcast.44), channel_id=1, source_target_pairs={{0,8},{4,12},{8,16},{12,20},{16,24},{20,28},{24,0},{28,4},{1,9},{5... | collective-permute-start | bytes 540680 | tf_op jit(solution)/shard_map/ppermute | solution.py:960
  16.5 21.6 %copy-start = (bf16[512,512]{1,0:T(8,128)(2,1)S(1)}, bf16[512,512]{1,0:T(8,128)(2,1)}, u32[]{:S(2)}) copy-start(bf16[512,512]{1,0:T(8,128)(2,1)} %low_tok.5) | copy-start | bytes 1572868
  16.5 9.4 %collective-permute-start.8 = (bf16[2,80,384]{2,1,0:T(8,128)(2,1)S(1)}, bf16[2,80,384]{2,1,0:T(8,128)(2,1)S(1)}, u32[]{:S(2)}, u32[]{:S(2)}) collective-permute-start(bf16[2,80,384]{2,1,0:T(8,128)(2,1)S(1)} %pad_maximum_fusion.3), channel_id=1, source_target_pairs={{0,4},{4,0},{8,12},{12,8},{16,20},{20,16},{24,28},{28,24},{1,5},{5... | collective-permute-start | bytes 368648 | tf_op jit(solution)/shard_map/ppermute | solution.py:957
  18.9 7.3 %collective-permute-start.2 = (bf16[2,80,384]{2,1,0:T(8,128)(2,1)S(1)}, bf16[2,80,384]{2,1,0:T(8,128)(2,1)S(1)}, u32[]{:S(2)}, u32[]{:S(2)}) collective-permute-start(bf16[2,80,384]{2,1,0:T(8,128)(2,1)S(1)} %pad_maximum_fusion.2), channel_id=1, source_target_pairs={{0,2},{2,0},{1,3},{3,1},{4,6},{6,4},{5,7},{7,5},{8,10},{10,8},{9,1... | collective-permute-start | bytes 368648 | tf_op jit(solution)/shard_map/ppermute | solution.py:216
  25.8 7.3 %collective-permute-start.10 = (bf16[1,64,1408]{2,1,0:T(8,128)(2,1)S(1)}, bf16[1,64,1408]{2,1,0:T(8,128)(2,1)S(1)}, u32[]{:S(2)}, u32[]{:S(2)}) collective-permute-start(bf16[1,64,1408]{2,1,0:T(8,128)(2,1)S(1)} %collective-permute-done.3), channel_id=1, source_target_pairs={{0,8},{4,12},{8,16},{12,20},{16,24},{20,28},{24,0},{28,4},{1,9},{5... | collective-permute-start | bytes 540680 | tf_op jit(solution)/shard_map/ppermute | solution.py:960
  26.2 8.1 %collective-permute-start.5 = (bf16[4,80,384]{2,1,0:T(8,128)(2,1)S(1)}, bf16[4,80,384]{2,1,0:T(8,128)(2,1)S(1)}, u32[]{:S(2)}, u32[]{:S(2)}) collective-permute-start(bf16[4,80,384]{2,1,0:T(8,128)(2,1)S(1)} %constant_dynamic-update-slice_fusion.refs_0_), channel_id=1, source_target_pairs={{0,4},{4,0},{8,12},{12,8},{16,20},{20,16},{24,28},{28,24},{1,5},{5... | collective-permute-start | bytes 737288 | tf_op jit(solution)/shard_map/ppermute | solution.py:957
  27.8 7.7 %collective-permute-start.9 = (bf16[4,80,384]{2,1,0:T(8,128)(2,1)S(1)}, bf16[4,80,384]{2,1,0:T(8,128)(2,1)S(1)}, u32[]{:S(2)}, u32[]{:S(2)}) collective-permute-start(bf16[4,80,384]{2,1,0:T(8,128)(2,1)S(1)} %constant_dynamic-update-slice_fusion.3.refs_2_), channel_id=1, source_target_pairs={{0,2},{2,0},{1,3},{3,1},{4,6},{6,4},{5,7},{7,5},{8,10},{10,8},{9,1... | collective-permute-start | bytes 737288 | tf_op jit(solution)/shard_map/ppermute | solution.py:216
  33.9 3.1 %collective-permute-start.11 = (bf16[4,80,384]{2,1,0:T(8,128)(2,1)S(1)}, bf16[4,80,384]{2,1,0:T(8,128)(2,1)S(1)}, u32[]{:S(2)}, u32[]{:S(2)}) collective-permute-start(bf16[4,80,384]{2,1,0:T(8,128)(2,1)S(1)} %constant_dynamic-update-slice_fusion.refs_0_), channel_id=1, source_target_pairs={{0,1},{1,0},{2,3},{3,2},{4,5},{5,4},{6,7},{7,6},{8,9},{9,8},{10,11... | collective-permute-start | bytes 737288 | tf_op jit(solution)/shard_map/ppermute | solution.py:212
  33.9 4.2 %collective-permute-start.13 = (bf16[4,80,384]{2,1,0:T(8,128)(2,1)S(1)}, bf16[4,80,384]{2,1,0:T(8,128)(2,1)S(1)}, u32[]{:S(2)}, u32[]{:S(2)}) collective-permute-start(bf16[4,80,384]{2,1,0:T(8,128)(2,1)S(1)} %constant_dynamic-update-slice_fusion.3.refs_2_), channel_id=1, source_target_pairs={{0,1},{1,0},{2,3},{3,2},{4,5},{5,4},{6,7},{7,6},{8,9},{9,8},{10,11... | collective-permute-start | bytes 737288 | tf_op jit(solution)/shard_map/ppermute | solution.py:212
  35.5 2.6 %collective-permute-start.12 = (bf16[4,80,384]{2,1,0:T(8,128)(2,1)S(1)}, bf16[4,80,384]{2,1,0:T(8,128)(2,1)S(1)}, u32[]{:S(2)}, u32[]{:S(2)}) collective-permute-start(bf16[4,80,384]{2,1,0:T(8,128)(2,1)S(1)} %collective-permute-done.5.refs_1_), channel_id=1, source_target_pairs={{0,1},{1,0},{2,3},{3,2},{4,5},{5,4},{6,7},{7,6},{8,9},{9,8},{10,11... | collective-permute-start | bytes 737288 | tf_op jit(solution)/shard_map/ppermute | solution.py:212
  35.5 2.6 %collective-permute-start.14 = (bf16[4,80,384]{2,1,0:T(8,128)(2,1)S(1)}, bf16[4,80,384]{2,1,0:T(8,128)(2,1)S(1)}, u32[]{:S(2)}, u32[]{:S(2)}) collective-permute-start(bf16[4,80,384]{2,1,0:T(8,128)(2,1)S(1)} %collective-permute-done.9.refs_3_), channel_id=1, source_target_pairs={{0,1},{1,0},{2,3},{3,2},{4,5},{5,4},{6,7},{7,6},{8,9},{9,8},{10,11... | collective-permute-start | bytes 737288 | tf_op jit(solution)/shard_map/ppermute | solution.py:212
  36.2 11.6 %collective-permute-start.18 = (bf16[2,64,1408]{2,1,0:T(8,128)(2,1)}, bf16[2,64,1408]{2,1,0:T(8,128)(2,1)S(1)}, u32[]{:S(2)}, u32[]{:S(2)}) collective-permute-start(bf16[2,64,1408]{2,1,0:T(8,128)(2,1)} %pad_maximum_fusion), channel_id=1, source_target_pairs={{0,2},{2,0},{1,3},{3,1},{4,6},{6,4},{5,7},{7,5},{8,10},{10,8},{9,1... | collective-permute-start | bytes 1081352 | tf_op jit(solution)/shard_map/ppermute | solution.py:216
  37.0 11.4 %collective-permute-start.20 = (bf16[2,64,1408]{2,1,0:T(8,128)(2,1)}, bf16[2,64,1408]{2,1,0:T(8,128)(2,1)S(1)}, u32[]{:S(2)}, u32[]{:S(2)}) collective-permute-start(bf16[2,64,1408]{2,1,0:T(8,128)(2,1)} %pad_maximum_fusion.1), channel_id=1, source_target_pairs={{0,4},{4,0},{8,12},{12,8},{16,20},{20,16},{24,28},{28,24},{1,5},{5... | collective-permute-start | bytes 1081352 | tf_op jit(solution)/shard_map/ppermute | solution.py:957
  40.6 5.0 %copy-start.3 = (bf16[2,64,1408]{2,1,0:T(8,128)(2,1)S(1)}, bf16[2,64,1408]{2,1,0:T(8,128)(2,1)}, u32[]{:S(2)}) copy-start(bf16[2,64,1408]{2,1,0:T(8,128)(2,1)} %pad_maximum_fusion) | copy-start | bytes 1081348
  40.6 5.0 %copy-start.2 = (bf16[2,64,1408]{2,1,0:T(8,128)(2,1)S(1)}, bf16[2,64,1408]{2,1,0:T(8,128)(2,1)}, u32[]{:S(2)}) copy-start(bf16[2,64,1408]{2,1,0:T(8,128)(2,1)} %pad_maximum_fusion.1) | copy-start | bytes 1081348
  40.6 9.0 %collective-permute-start.16 = (bf16[512,128]{1,0:T(8,128)(2,1)S(1)}, bf16[512,128]{1,0:T(8,128)(2,1)S(1)}, u32[]{:S(2)}, u32[]{:S(2)}) collective-permute-start(bf16[512,128]{1,0:T(8,128)(2,1)S(1)} %get-tuple-element.149.kv0), channel_id=1, source_target_pairs={{0,2},{2,0},{1,3},{3,1},{4,6},{6,4},{5,7},{7,5},{8,10},{10,8},{9,1... | collective-permute-start | bytes 393224 | tf_op jit(solution)/shard_map/ppermute | solution.py:216
  47.7 16.2 %copy-start.1 = (bf16[512,512]{1,0:T(8,128)(2,1)S(1)}, bf16[512,512]{1,0:T(8,128)(2,1)}, u32[]{:S(2)}) copy-start(bf16[512,512]{1,0:T(8,128)(2,1)} %low_cot.3) | copy-start | bytes 1572868
  47.8 20.1 %collective-permute-start.22 = (bf16[4,64,1408]{2,1,0:T(8,128)(2,1)S(1)}, bf16[4,64,1408]{2,1,0:T(8,128)(2,1)S(1)}, u32[]{:S(2)}, u32[]{:S(2)}) collective-permute-start(bf16[4,64,1408]{2,1,0:T(8,128)(2,1)S(1)} %constant_dynamic-update-slice_fusion.6.refs_0_), channel_id=1, source_target_pairs={{0,1},{1,0},{2,3},{3,2},{4,5},{5,4},{6,7},{7,6},{8,9},{9,8},{10,11... | collective-permute-start | bytes 2162696 | tf_op jit(solution)/shard_map/ppermute | solution.py:212
  47.8 20.1 %collective-permute-start.19 = (bf16[4,64,1408]{2,1,0:T(8,128)(2,1)S(1)}, bf16[4,64,1408]{2,1,0:T(8,128)(2,1)S(1)}, u32[]{:S(2)}, u32[]{:S(2)}) collective-permute-start(bf16[4,64,1408]{2,1,0:T(8,128)(2,1)S(1)} %constant_dynamic-update-slice_fusion.6.refs_0_), channel_id=1, source_target_pairs={{0,4},{4,0},{8,12},{12,8},{16,20},{20,16},{24,28},{28,24},{1,5},{5... | collective-permute-start | bytes 2162696 | tf_op jit(solution)/shard_map/ppermute | solution.py:957
  49.6 18.3 %collective-permute-start.23 = (bf16[4,64,1408]{2,1,0:T(8,128)(2,1)S(1)}, bf16[4,64,1408]{2,1,0:T(8,128)(2,1)S(1)}, u32[]{:S(2)}, u32[]{:S(2)}) collective-permute-start(bf16[4,64,1408]{2,1,0:T(8,128)(2,1)S(1)} %constant_dynamic-update-slice_fusion.8.refs_2_), channel_id=1, source_target_pairs={{0,1},{1,0},{2,3},{3,2},{4,5},{5,4},{6,7},{7,6},{8,9},{9,8},{10,11... | collective-permute-start | bytes 2162696 | tf_op jit(solution)/shard_map/ppermute | solution.py:212
  49.7 18.6 %collective-permute-start.21 = (bf16[4,64,1408]{2,1,0:T(8,128)(2,1)S(1)}, bf16[4,64,1408]{2,1,0:T(8,128)(2,1)S(1)}, u32[]{:S(2)}, u32[]{:S(2)}) collective-permute-start(bf16[4,64,1408]{2,1,0:T(8,128)(2,1)S(1)} %constant_dynamic-update-slice_fusion.8.refs_2_), channel_id=1, source_target_pairs={{0,2},{2,0},{1,3},{3,1},{4,6},{6,4},{5,7},{7,5},{8,10},{10,8},{9,1... | collective-permute-start | bytes 2162696 | tf_op jit(solution)/shard_map/ppermute | solution.py:216
  50.5 1.5 collective-permute-start.15
  52.0 1.3 collective-permute-start.17
  68.2 2.2 %collective-permute-start.24 = (bf16[4,64,1408]{2,1,0:T(8,128)(2,1)S(1)}, bf16[4,64,1408]{2,1,0:T(8,128)(2,1)S(1)}, u32[]{:S(2)}, u32[]{:S(2)}) collective-permute-start(bf16[4,64,1408]{2,1,0:T(8,128)(2,1)S(1)} %collective-permute-done.19.refs_1_), channel_id=1, source_target_pairs={{0,1},{1,0},{2,3},{3,2},{4,5},{5,4},{6,7},{7,6},{8,9},{9,8},{10,11... | collective-permute-start | bytes 2162696 | tf_op jit(solution)/shard_map/ppermute | solution.py:212
  68.2 3.2 %collective-permute-start.25 = (bf16[4,64,1408]{2,1,0:T(8,128)(2,1)S(1)}, bf16[4,64,1408]{2,1,0:T(8,128)(2,1)S(1)}, u32[]{:S(2)}, u32[]{:S(2)}) collective-permute-start(bf16[4,64,1408]{2,1,0:T(8,128)(2,1)S(1)} %collective-permute-done.21.refs_3_), channel_id=1, source_target_pairs={{0,1},{1,0},{2,3},{3,2},{4,5},{5,4},{6,7},{7,6},{8,9},{9,8},{10,11... | collective-permute-start | bytes 2162696 | tf_op jit(solution)/shard_map/ppermute | solution.py:212
  83.6 5.3 %collective-permute-start.26 = (bf16[2,2,2,64,1408]{4,3,2,1,0:T(8,128)(2,1)S(1)}, bf16[2,2,2,64,1408]{4,3,2,1,0:T(8,128)(2,1)S(1)}, u32[]{:S(2)}, u32[]{:S(2)}) collective-permute-start(bf16[2,2,2,64,1408]{4,3,2,1,0:T(8,128)(2,1)S(1)} %get-tuple-element.169), channel_id=1, source_target_pairs={{0,1},{1,0},{2,3},{3,2},{4,5},{5,4},{6,7},{7,6},{8,9},{9,8},{10,11... | collective-permute-start | bytes 4325384 | tf_op jit(solution)/shard_map/ppermute | solution.py:212
  83.8 5.2 %collective-permute-start.27 = (bf16[2,2,2,64,1408]{4,3,2,1,0:T(8,128)(2,1)S(1)}, bf16[2,2,2,64,1408]{4,3,2,1,0:T(8,128)(2,1)S(1)}, u32[]{:S(2)}, u32[]{:S(2)}) collective-permute-start(bf16[2,2,2,64,1408]{4,3,2,1,0:T(8,128)(2,1)S(1)} %get-tuple-element.170), channel_id=1, source_target_pairs={{0,1},{1,0},{2,3},{3,2},{4,5},{5,4},{6,7},{7,6},{8,9},{9,8},{10,11... | collective-permute-start | bytes 4325384 | tf_op jit(solution)/shard_map/ppermute | solution.py:212
  89.3 18.8 %collective-permute-start.28 = (bf16[2,2,64,1408]{3,2,1,0:T(8,128)(2,1)S(1)}, bf16[2,2,64,1408]{3,2,1,0:T(8,128)(2,1)S(1)}, u32[]{:S(2)}, u32[]{:S(2)}) collective-permute-start(bf16[2,2,64,1408]{3,2,1,0:T(8,128)(2,1)S(1)} %get-tuple-element.174), channel_id=1, source_target_pairs={{0,4},{4,0},{8,12},{12,8},{16,20},{20,16},{24,28},{28,24},{1,5},{5... | collective-permute-start | bytes 2162696 | tf_op jit(solution)/shard_map/ppermute | solution.py:957
  90.1 18.1 %collective-permute-start.30 = (bf16[2,2,64,1408]{3,2,1,0:T(8,128)(2,1)S(1)}, bf16[2,2,64,1408]{3,2,1,0:T(8,128)(2,1)S(1)}, u32[]{:S(2)}, u32[]{:S(2)}) collective-permute-start(bf16[2,2,64,1408]{3,2,1,0:T(8,128)(2,1)S(1)} %get-tuple-element.176), channel_id=1, source_target_pairs={{0,2},{2,0},{1,3},{3,1},{4,6},{6,4},{5,7},{7,5},{8,10},{10,8},{9,1... | collective-permute-start | bytes 2162696 | tf_op jit(solution)/shard_map/ppermute | solution.py:216
  105.6 1.6 %collective-permute-start.29 = (bf16[2,2,128,256]{3,2,1,0:T(8,128)(2,1)S(1)}, bf16[2,2,128,256]{3,2,1,0:T(8,128)(2,1)S(1)}, u32[]{:S(2)}, u32[]{:S(2)}) collective-permute-start(bf16[2,2,128,256]{3,2,1,0:T(8,128)(2,1)S(1)} %get-tuple-element.181), channel_id=1, source_target_pairs={{0,1},{1,0},{2,3},{3,2},{4,5},{5,4},{6,7},{7,6},{8,9},{9,8},{10,11... | collective-permute-start | bytes 786440 | tf_op jit(solution)/shard_map/ppermute | solution.py:212
  107.2 5.6 %collective-permute-start.31 = (bf16[2,128,256]{2,1,0:T(8,128)(2,1)S(1)}, bf16[2,128,256]{2,1,0:T(8,128)(2,1)S(1)}, u32[]{:S(2)}, u32[]{:S(2)}) collective-permute-start(bf16[2,128,256]{2,1,0:T(8,128)(2,1)S(1)} %shard_map.280), channel_id=1, source_target_pairs={{0,2},{2,0},{1,3},{3,1},{4,6},{6,4},{5,7},{7,5},{8,10},{10,8},{9,1... | collective-permute-start | bytes 393224 | tf_op jit(solution)/shard_map/ppermute | solution.py:216
  112.8 9.6 %collective-permute-start.32 = (bf16[2,64,1408]{2,1,0:T(8,128)(2,1)S(1)}, bf16[2,64,1408]{2,1,0:T(8,128)(2,1)S(1)}, u32[]{:S(2)}, u32[]{:S(2)}) collective-permute-start(bf16[2,64,1408]{2,1,0:T(8,128)(2,1)S(1)} %get-tuple-element.197), channel_id=1, source_target_pairs={{0,2},{2,0},{1,3},{3,1},{4,6},{6,4},{5,7},{7,5},{8,10},{10,8},{9,1... | collective-permute-start | bytes 1081352 | tf_op jit(solution)/shard_map/ppermute | solution.py:216
  113.7 9.3 %collective-permute-start.35 = (bf16[2,64,1408]{2,1,0:T(8,128)(2,1)S(1)}, bf16[2,64,1408]{2,1,0:T(8,128)(2,1)S(1)}, u32[]{:S(2)}, u32[]{:S(2)}) collective-permute-start(bf16[2,64,1408]{2,1,0:T(8,128)(2,1)S(1)} %get-tuple-element.186), channel_id=1, source_target_pairs={{0,4},{4,0},{8,12},{12,8},{16,20},{20,16},{24,28},{28,24},{1,5},{5... | collective-permute-start | bytes 1081352 | tf_op jit(solution)/shard_map/ppermute | solution.py:957
  122.5 9.0 %collective-permute-start.33 = (bf16[2,2,2,80,384]{4,3,2,1,0:T(8,128)(2,1)S(1)}, bf16[2,2,2,80,384]{4,3,2,1,0:T(8,128)(2,1)S(1)}, u32[]{:S(2)}, u32[]{:S(2)}) collective-permute-start(bf16[2,2,2,80,384]{4,3,2,1,0:T(8,128)(2,1)S(1)} %get-tuple-element.205), channel_id=1, source_target_pairs={{0,1},{1,0},{2,3},{3,2},{4,5},{5,4},{6,7},{7,6},{8,9},{9,8},{10,11... | collective-permute-start | bytes 1474568 | tf_op jit(solution)/shard_map/ppermute | solution.py:212
  122.5 9.0 %collective-permute-start.34 = (bf16[2,2,2,80,384]{4,3,2,1,0:T(8,128)(2,1)S(1)}, bf16[2,2,2,80,384]{4,3,2,1,0:T(8,128)(2,1)S(1)}, u32[]{:S(2)}, u32[]{:S(2)}) collective-permute-start(bf16[2,2,2,80,384]{4,3,2,1,0:T(8,128)(2,1)S(1)} %get-tuple-element.206), channel_id=1, source_target_pairs={{0,1},{1,0},{2,3},{3,2},{4,5},{5,4},{6,7},{7,6},{8,9},{9,8},{10,11... | collective-permute-start | bytes 1474568 | tf_op jit(solution)/shard_map/ppermute | solution.py:212
  123.2 8.3 %collective-permute-start.36 = (bf16[64,1408]{1,0:T(8,128)(2,1)S(1)}, bf16[64,1408]{1,0:T(8,128)(2,1)S(1)}, u32[]{:S(2)}, u32[]{:S(2)}) collective-permute-start(bf16[64,1408]{1,0:T(8,128)(2,1)S(1)} %get-tuple-element.208), channel_id=1, source_target_pairs={{0,8},{4,12},{8,16},{12,20},{16,24},{20,28},{24,0},{28,4},{1,9},{5... | collective-permute-start | bytes 540680 | tf_op jit(solution)/shard_map/ppermute | solution.py:960
  125.5 12.2 %collective-permute-start.39 = (bf16[256,512]{1,0:T(8,128)(2,1)S(1)}, bf16[256,512]{1,0:T(8,128)(2,1)S(1)}, u32[]{:S(2)}, u32[]{:S(2)}) collective-permute-start(bf16[256,512]{1,0:T(8,128)(2,1)S(1)} %get-tuple-element.220), channel_id=1, source_target_pairs={{0,3},{3,0},{1,2},{2,1},{4,7},{7,4},{5,6},{6,5},{8,11},{11,8},{9,1... | collective-permute-start | bytes 786440 | tf_op jit(solution)/shard_map/ppermute | solution.py:220
  131.7 7.2 %collective-permute-start.37 = (bf16[2,2,80,384]{3,2,1,0:T(8,128)(2,1)S(1)}, bf16[2,2,80,384]{3,2,1,0:T(8,128)(2,1)S(1)}, u32[]{:S(2)}, u32[]{:S(2)}) collective-permute-start(bf16[2,2,80,384]{3,2,1,0:T(8,128)(2,1)S(1)} %get-tuple-element.217), channel_id=1, source_target_pairs={{0,2},{2,0},{1,3},{3,1},{4,6},{6,4},{5,7},{7,5},{8,10},{10,8},{9,1... | collective-permute-start | bytes 737288 | tf_op jit(solution)/shard_map/ppermute | solution.py:216
  132.6 6.3 %collective-permute-start.38 = (bf16[2,2,80,384]{3,2,1,0:T(8,128)(2,1)S(1)}, bf16[2,2,80,384]{3,2,1,0:T(8,128)(2,1)S(1)}, u32[]{:S(2)}, u32[]{:S(2)}) collective-permute-start(bf16[2,2,80,384]{3,2,1,0:T(8,128)(2,1)S(1)} %get-tuple-element.218), channel_id=1, source_target_pairs={{0,4},{4,0},{8,12},{12,8},{16,20},{20,16},{24,28},{28,24},{1,5},{5... | collective-permute-start | bytes 737288 | tf_op jit(solution)/shard_map/ppermute | solution.py:957
  133.9 8.9 %collective-permute-start.42 = (bf16[64,1408]{1,0:T(8,128)(2,1)S(1)}, bf16[64,1408]{1,0:T(8,128)(2,1)S(1)}, u32[]{:S(2)}, u32[]{:S(2)}) collective-permute-start(bf16[64,1408]{1,0:T(8,128)(2,1)S(1)} %shard_map.285), channel_id=1, source_target_pairs={{0,8},{4,12},{8,16},{12,20},{16,24},{20,28},{24,0},{28,4},{1,9},{5... | collective-permute-start | bytes 540680 | tf_op jit(solution)/shard_map/ppermute | solution.py:960
  134.5 8.6 %collective-permute-start.43 = (bf16[64,1408]{1,0:T(8,128)(2,1)S(1)}, bf16[64,1408]{1,0:T(8,128)(2,1)S(1)}, u32[]{:S(2)}, u32[]{:S(2)}) collective-permute-start(bf16[64,1408]{1,0:T(8,128)(2,1)S(1)} %get-tuple-element.225), channel_id=1, source_target_pairs={{0,24},{4,28},{8,0},{12,4},{16,8},{20,12},{24,16},{28,20},{1,25},{... | collective-permute-start | bytes 540680 | tf_op jit(solution)/shard_map/ppermute | solution.py:960
  139.0 4.9 %collective-permute-start.40 = (bf16[2,80,384]{2,1,0:T(8,128)(2,1)S(1)}, bf16[2,80,384]{2,1,0:T(8,128)(2,1)S(1)}, u32[]{:S(2)}, u32[]{:S(2)}) collective-permute-start(bf16[2,80,384]{2,1,0:T(8,128)(2,1)S(1)} %get-tuple-element.223), channel_id=1, source_target_pairs={{0,4},{4,0},{8,12},{12,8},{16,20},{20,16},{24,28},{28,24},{1,5},{5... | collective-permute-start | bytes 368648 | tf_op jit(solution)/shard_map/ppermute | solution.py:957
  140.7 4.9 %collective-permute-start.41 = (bf16[2,80,384]{2,1,0:T(8,128)(2,1)S(1)}, bf16[2,80,384]{2,1,0:T(8,128)(2,1)S(1)}, u32[]{:S(2)}, u32[]{:S(2)}) collective-permute-start(bf16[2,80,384]{2,1,0:T(8,128)(2,1)S(1)} %get-tuple-element.224), channel_id=1, source_target_pairs={{0,2},{2,0},{1,3},{3,1},{4,6},{6,4},{5,7},{7,5},{8,10},{10,8},{9,1... | collective-permute-start | bytes 368648 | tf_op jit(solution)/shard_map/ppermute | solution.py:216
  145.6 9.2 %collective-permute-start.47 = (bf16[256,512]{1,0:T(8,128)(2,1)S(1)}, bf16[256,512]{1,0:T(8,128)(2,1)S(1)}, u32[]{:S(2)}, u32[]{:S(2)}) collective-permute-start(bf16[256,512]{1,0:T(8,128)(2,1)S(1)} %get-tuple-element.241), channel_id=1, source_target_pairs={{0,3},{3,0},{1,2},{2,1},{4,7},{7,4},{5,6},{6,5},{8,11},{11,8},{9,1... | collective-permute-start | bytes 786440 | tf_op jit(solution)/shard_map/ppermute | solution.py:220
  145.7 6.7 %collective-permute-start.44 = (bf16[80,384]{1,0:T(8,128)(2,1)S(1)}, bf16[80,384]{1,0:T(8,128)(2,1)S(1)}, u32[]{:S(2)}, u32[]{:S(2)}) collective-permute-start(bf16[80,384]{1,0:T(8,128)(2,1)S(1)} %get-tuple-element.234), channel_id=1, source_target_pairs={{0,8},{4,12},{8,16},{12,20},{16,24},{20,28},{24,0},{28,4},{1,9},{5... | collective-permute-start | bytes 184328 | tf_op jit(solution)/shard_map/ppermute | solution.py:960
  146.5 8.3 %collective-permute-start.45 = (bf16[80,384]{1,0:T(8,128)(2,1)S(1)}, bf16[80,384]{1,0:T(8,128)(2,1)S(1)}, u32[]{:S(2)}, u32[]{:S(2)}) collective-permute-start(bf16[80,384]{1,0:T(8,128)(2,1)S(1)} %get-tuple-element.237), channel_id=1, source_target_pairs={{0,16},{4,20},{8,24},{12,28},{16,0},{20,4},{24,8},{28,12},{1,17},{... | collective-permute-start | bytes 184328 | tf_op jit(solution)/shard_map/ppermute | solution.py:960
  147.5 7.3 %collective-permute-start.46 = (bf16[80,384]{1,0:T(8,128)(2,1)S(1)}, bf16[80,384]{1,0:T(8,128)(2,1)S(1)}, u32[]{:S(2)}, u32[]{:S(2)}) collective-permute-start(bf16[80,384]{1,0:T(8,128)(2,1)S(1)} %get-tuple-element.238), channel_id=1, source_target_pairs={{0,24},{4,28},{8,0},{12,4},{16,8},{20,12},{24,16},{28,20},{1,25},{... | collective-permute-start | bytes 184328 | tf_op jit(solution)/shard_map/ppermute | solution.py:960
